TPU v7x, 32 devices: a whole 2x2x4 slice. The times are simulated.
32 devices in a mesh: ctx: 8 (over z, core), head: 4 (over y, x).
Axes of the slice: x: 2, y: 2, z: 4, core: 2. Of those that a mesh axis runs over, the one named last changes fastest.
Arguments:
- tokens: bfloat16 [2048, 2048], P('ctx'), may hold values from -15 to 15
- w_qkv: bfloat16 [3, 2048, 2048], P(None, None, 'head'), may hold values from -0.9943689 to 0.9943689
- w_out: bfloat16 [2048, 2048], P('head'), may hold values from -0.125 to 0.125
- w_dec: bfloat16 [2048, 12, 256], P(None, None, 'head'), may hold values from -0.125 to 0.125
Outputs:
- field: float32 [2048, 8, 256], P('ctx', None, 'head')
All inputs are finite; a program needn't handle non-finite values.
Results may differ from a plain program's by a relative error of at most 0.011.
Values may be sent and summed in bfloat16 or wider, within the bound.
No kernel may reach another device: no remote copies, remote signals or barrier semaphores. Data moves between devices by JAX's collectives and lax.ppermute only.
A program may use at most 64 MiB of HBM per device.

v0:
```python
import math

import jax
import jax.numpy as jnp
from jax import lax
from jax.sharding import PartitionSpec as P

HD = 64
PATCH = 8
OV = 2


eps = 1e-05


def passed_along(value, axis, steps):
    count = lax.axis_size(axis)
    pairs = [(source, (source + steps) % count) for source in range(count)]
    return lax.ppermute(value, axis, pairs)


def rms_scale(values):
    return values * lax.rsqrt(jnp.mean(values * values, axis=-1, keepdims=True) + eps)


def body(tokens, w_qkv, w_out, w_dec):
    rows = tokens.shape[0]
    local_heads = w_qkv.shape[2] // HD
    xf = tokens.astype(jnp.float32)
    normed = rms_scale(xf).astype(jnp.bfloat16)
    projected = jnp.einsum("td,kdc->ktc", normed, w_qkv, preferred_element_type=jnp.float32).astype(
        jnp.bfloat16
    )
    queries = projected[0].reshape(rows, local_heads, HD)
    keyvals = projected[1:]
    scale = HD ** (-0.5)

    def block_update(carry, block):
        best, total, accum = carry
        keys = block[0].reshape(-1, local_heads, HD)
        values = block[1].reshape(-1, local_heads, HD)
        scores = (
            jnp.einsum("thd,rhd->thr", queries, keys, preferred_element_type=jnp.float32) * scale
        )
        fresh = jnp.maximum(best, jnp.max(scores, axis=-1))
        shrink = jnp.exp(best - fresh)
        weights = jnp.exp(scores - fresh[..., None])
        total = total * shrink + jnp.sum(weights, axis=-1)
        accum = accum * shrink[..., None] + jnp.einsum(
            "thr,rhd->thd", weights.astype(jnp.bfloat16), values, preferred_element_type=jnp.float32
        )
        return (fresh, total, accum)

    initial = (
        jnp.full((rows, local_heads), -1e30, jnp.float32),
        jnp.zeros((rows, local_heads), jnp.float32),
        jnp.zeros((rows, local_heads, HD), jnp.float32),
    )
    piece = lax.all_gather(keyvals, "ctx", axis=1, tiled=True)
    length = piece.shape[1]
    span = math.gcd(length, 1024)

    def one_block(index, inner):
        block = lax.dynamic_slice_in_dim(piece, index * span, span, 1)
        return block_update(inner, block)

    best, total, accum = lax.fori_loop(0, length // span, one_block, initial)
    attended = (accum / total[..., None]).astype(jnp.bfloat16).reshape(rows, local_heads * HD)
    partial_out = jnp.dot(attended, w_out, preferred_element_type=jnp.float32)
    mixed = lax.psum(partial_out.astype(jnp.bfloat16), "head").astype(jnp.float32)
    hidden = rms_scale(xf + mixed).astype(jnp.bfloat16)
    extended = jnp.dot(
        hidden, w_dec.reshape(w_dec.shape[0], -1), preferred_element_type=jnp.float32
    )
    extended = extended.reshape(rows, w_dec.shape[1], w_dec.shape[2])
    from_before = passed_along(extended[:, PATCH + OV :].astype(jnp.bfloat16), "ctx", 1).astype(
        jnp.float32
    )
    from_after = passed_along(extended[:, :OV].astype(jnp.bfloat16), "ctx", -1).astype(jnp.float32)
    middle = extended[:, OV : OV + PATCH]
    field = jnp.concatenate(
        [
            middle[:, :OV] + from_before,
            middle[:, OV : PATCH - OV],
            middle[:, PATCH - OV :] + from_after,
        ],
        axis=1,
    )
    return field


def solution(mesh):
    return jax.shard_map(
        body,
        mesh=mesh,
        in_specs=(P("ctx", None), P(None, None, "head"), P("head", None), P(None, None, "head")),
        out_specs=P("ctx", None, "head"),
        check_vma=False,
    )
```

profile of v0, /device:TPU:0, one launch (start us, length us, event | category | flops | bytes accessed | tf_op | source)
XLA Modules:
  0.0 166.6 jit_solution(2205606966415838868)
XLA Ops:
  6.5 1.7 fusion.17
  8.2 5.0 %fusion.19 = bf16[3,256,512]{2,1,0:T(8,128)(2,1)S(1)} fusion(bf16[3,2048,512]{2,1,0:T(8,128)(2,1)} %param.7, bf16[256,2048]{1,0:T(8,128)(2,1)} %param.6, f32[256]{0:T(256)S(1)} %add_rsqrt_fusion.1), kind=kOutput, calls=%fused_computation.29 | convolution fusion | flops 1612578816 | bytes 8127488 | tf_op jit(solution)/shard_map/td,kdc->ktc/dot_general | solution.py:31
  13.2 0.9 copy-done.4
  14.1 0.8 slice.50
  14.9 0.0 all-reduce.2.cloned.1.call-start
  15.0 1.7 %slice.51 = bf16[1,256,512]{2,1,0:T(8,128)(2,1)} slice(bf16[3,256,512]{2,1,0:T(8,128)(2,1)} %copy-done.4), slice={[0:1], [0:256], [0:512]} | slice | bytes 524288 | tf_op jit(solution)/shard_map/slice | solution.py:34
  16.7 1.1 copy.9
  17.7 47.2 %all-gather.2.cloned.1.call-done = bf16[2,2048,512]{2,1,0:T(8,128)(2,1)} async-done(((bf16[2,256,512]{2,1,0:T(8,128)(2,1)}), bf16[2,2048,512]{2,1,0:T(8,128)(2,1)}) %all-gather.2.cloned.1.call-update) | async-done | bytes 4194320 | tf_op jit(solution)/shard_map/all_gather | solution.py:59
  64.9 27.8 %while.18 = (s32[]{:T(128)}, f32[256,8]{0,1:T(8,128)S(1)}, f32[256,8]{0,1:T(8,128)S(1)}, f32[256,8,64]{0,2,1:T(8,128)}, bf16[2,2048,512]{2,1,0:T(8,128)(2,1)}, /...) while((s32[]{:T(128)}, f32[256,8]{0,1:T(8,128)S(1)}, ...), condition=%wide.region_4.0_spmd.clone, body=%wide.region_1.0_spmd.clone.sunk | while | flops 554051584 | bytes 45482260 | solution.py:67
  64.9 3.0 %constant_dynamic-slice_fusion.3 = (bf16[1,1024,512]{2,1,0:T(8,128)(2,1)}, bf16[1,1024,512]{2,1,0:T(8,128)(2,1)}) fusion(bf16[2,2048,512]{2,1,0:T(8,128)(2,1)} %get-tuple-element.249, s32[]{:T(128)S(6)} %add.98, s32[]{:T(128)S(6)} %select_n.9), kind=kLoop, calls=%fused_computation.16.clone.1 | loop fusion | bytes 4194312 | tf_op jit(solution)/shard_map/while/body/eval_jaxpr/slice | solution.py:41
  67.9 2.3 %copy.17 = bf16[1,1024,512]{1,2,0:T(8,128)(2,1)} copy(bf16[1,1024,512]{2,1,0:T(8,128)(2,1)} %get-tuple-element.217) | data formatting | bytes 2097152 | tf_op jit(solution)/shard_map/while
  70.2 2.3 %copy.18 = bf16[1,1024,512]{1,2,0:T(8,128)(2,1)} copy(bf16[1,1024,512]{2,1,0:T(8,128)(2,1)} %get-tuple-element.221) | data formatting | bytes 2097152 | tf_op jit(solution)/shard_map/while
  72.4 2.5 %bitcast_reduce_fusion.2 = (f32[256,8]{0,1:T(8,128)S(1)}, f32[8,1024,256]{2,1,0:T(8,128)S(1)}) fusion(bf16[1024,8,64]{0,2,1:T(8,128)(2,1)} %bitcast.66, bf16[256,8,64]{0,2,1:T(8,128)(2,1)S(1)} %get-tuple-element.250), kind=kOutput, calls=%fused_computation.1.clone.1 | convolution fusion | flops 272627712 | bytes 9707520 | tf_op jit(solution)/shard_map/while/body/eval_jaxpr/thd,rhd->thr/dot_general | solution.py:43
  75.0 1.4 fusion.45
  76.4 1.6 fusion.47
  78.1 0.8 copy-done.3
  78.8 3.0 %constant_dynamic-slice_fusion.3 = (bf16[1,1024,512]{2,1,0:T(8,128)(2,1)}, bf16[1,1024,512]{2,1,0:T(8,128)(2,1)}) fusion(bf16[2,2048,512]{2,1,0:T(8,128)(2,1)} %get-tuple-element.249, s32[]{:T(128)S(6)} %add.98, s32[]{:T(128)S(6)} %select_n.9), kind=kLoop, calls=%fused_computation.16.clone.1 | loop fusion | bytes 4194312 | tf_op jit(solution)/shard_map/while/body/eval_jaxpr/slice | solution.py:41
  81.8 2.3 %copy.17 = bf16[1,1024,512]{1,2,0:T(8,128)(2,1)} copy(bf16[1,1024,512]{2,1,0:T(8,128)(2,1)} %get-tuple-element.217) | data formatting | bytes 2097152 | tf_op jit(solution)/shard_map/while
  84.1 2.3 %copy.18 = bf16[1,1024,512]{1,2,0:T(8,128)(2,1)} copy(bf16[1,1024,512]{2,1,0:T(8,128)(2,1)} %get-tuple-element.221) | data formatting | bytes 2097152 | tf_op jit(solution)/shard_map/while
  86.4 2.5 %bitcast_reduce_fusion.2 = (f32[256,8]{0,1:T(8,128)S(1)}, f32[8,1024,256]{2,1,0:T(8,128)S(1)}) fusion(bf16[1024,8,64]{0,2,1:T(8,128)(2,1)} %bitcast.66, bf16[256,8,64]{0,2,1:T(8,128)(2,1)S(1)} %get-tuple-element.250), kind=kOutput, calls=%fused_computation.1.clone.1 | convolution fusion | flops 272627712 | bytes 9707520 | tf_op jit(solution)/shard_map/while/body/eval_jaxpr/thd,rhd->thr/dot_general | solution.py:43
  88.9 1.4 fusion.45
  90.4 1.6 fusion.47
  92.0 0.8 copy-done.3
  92.7 1.1 divide_convert_fusion
  93.8 3.3 %convolution_convert_fusion = bf16[256,2048]{1,0:T(8,128)(2,1)} fusion(bf16[256,512]{0,1:T(8,128)(2,1)S(1)} %bitcast.68, bf16[512,2048]{1,0:T(8,128)(2,1)} %param.8), kind=kOutput, calls=%fused_computation.23 | convolution fusion | flops 537395200 | bytes 3407872 | tf_op jit(solution)/shard_map/dot_general | solution.py:69
  97.2 51.4 %all-reduce.2.cloned.1.call-done = bf16[256,2048]{1,0:T(8,128)(2,1)} async-done(((bf16[256,2048]{1,0:T(8,128)(2,1)}), bf16[256,2048]{1,0:T(8,128)(2,1)}) %all-reduce.2.cloned.1.call-update) | async-done | bytes 1048592 | tf_op jit(solution)/shard_map/psum | solution.py:70
  148.6 2.0 %multiply_reduce_fusion = f32[256]{0:T(256)S(1)} fusion(bf16[256,2048]{1,0:T(8,128)(2,1)} %all-reduce.2.cloned.1.call-done, bf16[256,2048]{1,0:T(8,128)(2,1)} %param.6), kind=kLoop, calls=%fused_computation.27 | loop fusion | flops 2621184 | bytes 2098176 | tf_op jit(solution)/shard_map/reduce_sum | solution.py:23
  150.6 2.6 %fusion.27 = (bf16[256,12,64]{0,2,1:T(8,128)(2,1)S(1)}, f32[256,12,64]{0,2,1:T(8,128)S(1)}) fusion(bf16[2048,12,64]{0,2,1:T(8,128)(2,1)S(1)} %copy-done, bf16[256,2048]{1,0:T(8,128)(2,1)} %all-reduce.2.cloned.1.call-done, bf16[256,2048]{1,0:T(8,128)(2,1)} %param.6, f32[256]{0:T(256)S(1)} %add_rsqrt_fusion), kind=kOutput, calls=%fused_computation.41 | convolution fusion | flops 808124416 | bytes 6423552 | tf_op jit(solution)/shard_map/dot_general | solution.py:72
  153.3 0.1 collective-permute-start
  153.3 3.5 %collective-permute-start.1 = (bf16[256,2,64]{0,2,1:T(8,128)(2,1)S(1)}, bf16[256,2,64]{0,2,1:T(8,128)(2,1)S(1)}, u32[]{:S(2)}, u32[]{:S(2)}) collective-permute-start(bf16[256,2,64]{0,2,1:T(8,128)(2,1)S(1)} %get-tuple-element.171), channel_id=1, source_target_pairs={{0,28},{4,0},{8,4},{12,8},{16,12},{20,16},{24,20},{28,24},{1,29},{... | collective-permute-start | bytes 196616 | tf_op jit(solution)/shard_map/ppermute | solution.py:19
  156.9 2.0 %collective-permute-done = bf16[256,2,64]{0,2,1:T(8,128)(2,1)S(1)} collective-permute-done((bf16[256,2,64]{0,2,1:T(8,128)(2,1)S(1)}, bf16[256,2,64]{0,2,1:T(8,128)(2,1)S(1)}, u32[]{:S(2)}, u32[]{:S(2)}) %collective-permute-start) | collective-permute-done | bytes 65568 | tf_op jit(solution)/shard_map/ppermute | solution.py:19
  159.0 0.8 pad_maximum_fusion
  (31 shorter events, 0.2 us)
Async XLA Ops:
  6.5 144.1 %copy-start = (bf16[2048,12,64]{0,2,1:T(8,128)(2,1)S(1)}, bf16[2048,12,64]{0,2,1:T(8,128)(2,1)}, u32[]{:S(2)}) copy-start(bf16[2048,12,64]{0,2,1:T(8,128)(2,1)} %param.9) | copy-start | bytes 9437188
  6.5 58.4 %all-gather.2.cloned.1.call-start = ((), (), s32[]{:S(2)}) async-start(), calls=%async_computation | async-start | bytes 4718592 | tf_op jit(solution)/shard_map/all_gather | solution.py:59
  13.2 0.9 copy-start.4
  14.9 133.7 %all-reduce.2.cloned.1.call-start = ((), (), s32[]{:S(2)}) async-start(), calls=%async_computation.1 | async-start | bytes 2097152 | tf_op jit(solution)/shard_map/psum | solution.py:70
  75.0 1.4 copy-start.1
  75.0 1.4 copy-start.2
  78.0 0.8 copy-start.3
  88.9 1.4 copy-start.1
  88.9 1.4 copy-start.2
  92.0 0.8 copy-start.3
  153.3 5.6 %collective-permute-start = (bf16[256,2,64]{0,2,1:T(8,128)(2,1)S(1)}, bf16[256,2,64]{0,2,1:T(8,128)(2,1)S(1)}, u32[]{:S(2)}, u32[]{:S(2)}) collective-permute-start(bf16[256,2,64]{0,2,1:T(8,128)(2,1)S(1)} %get-tuple-element.170), channel_id=1, source_target_pairs={{0,4},{4,8},{8,12},{12,16},{16,20},{20,24},{24,28},{28,0},{1,5},{5... | collective-permute-start | bytes 196616 | tf_op jit(solution)/shard_map/ppermute | solution.py:19
  153.3 5.6 %collective-permute-start.1 = (bf16[256,2,64]{0,2,1:T(8,128)(2,1)S(1)}, bf16[256,2,64]{0,2,1:T(8,128)(2,1)S(1)}, u32[]{:S(2)}, u32[]{:S(2)}) collective-permute-start(bf16[256,2,64]{0,2,1:T(8,128)(2,1)S(1)} %get-tuple-element.171), channel_id=1, source_target_pairs={{0,28},{4,0},{8,4},{12,8},{16,12},{20,16},{24,20},{28,24},{1,29},{... | collective-permute-start | bytes 196616 | tf_op jit(solution)/shard_map/ppermute | solution.py:19
Sparse Core Ops, SparseCore 0:
  15.0 49.8 all-gather.1
  97.3 51.2 all-reduce.1
where the time goes:
time: 167 us
  waiting for transfers between devices  101 us (60%)
  local copies, waits for them, and re-layouts  21.1 us (13%)
  matrix products  19.2 us (11%)
  between operations  13.5 us (8%)
  other arithmetic  8.36 us (5%)
  starting transfers between devices  3.63 us (2%)
    psum x1, waiting for transfers between devices, body(): lax.psum(partial_out.astype(jnp.bfloat16), 'head').astype(jnp.float32)  51.4 us
    all_gather x1, waiting for transfers between devices, body(): piece = lax.all_gather(keyvals, 'ctx', axis=1, tiled=True)  47.2 us
    while x18, local copies, waits for them, and re-layouts  10.6 us
    slice x2, local copies, waits for them, and re-layouts, block_update(): values = block[1].reshape(-1, local_heads, HD)  6.02 us
    dot_general x2, matrix products, block_update(): jnp.einsum('thd,rhd->thr', queries, keys, preferred_element_type=jnp.floa...  5.08 us
    dot_general x1, matrix products, body(): jnp.einsum('td,kdc->ktc', normed, w_qkv, preferred_element_type=jnp.float32)  4.96 us
    reduce_sum x2, other arithmetic, rms_scale(): jnp.mean(values * values, axis=-1, keepdims=True) + eps  3.62 us
    ppermute x2, starting transfers between devices, passed_along(): return lax.ppermute(value, axis, pairs)  3.59 us
  transfers between devices with their start and end apart: 4, of which 3 were waited for; matrix products, arithmetic and copies ran while one was open for 2% of the time, Pallas kernels for 0%

commit v1 on v0

v1 whole, which is shorter than its diff:
```python
import functools
import math

import jax
import jax.numpy as jnp
from jax import lax
from jax.experimental import pallas as pl
from jax.experimental.pallas import tpu as pltpu
from jax.sharding import PartitionSpec as P

HD = 64
PATCH = 8
OV = 2
LANES = 128

eps = 1e-05
bf16 = jnp.bfloat16
f32 = jnp.float32


def passed_along(value, axis, steps):
    count = lax.axis_size(axis)
    pairs = [(source, (source + steps) % count) for source in range(count)]
    return lax.ppermute(value, axis, pairs)


def swapped(value, axis, bits):
    count = lax.axis_size(axis)
    return lax.ppermute(value, axis, [(i, i ^ bits) for i in range(count)])


def rms_scale(values):
    return values * lax.rsqrt(jnp.mean(values * values, axis=-1, keepdims=True) + eps)


def qkv_kernel(pos, x_ref, w_ref, kva, kvb, qa, qb, scale_ref):
    step = pl.program_id(0)

    @pl.when(step == 0)
    def _():
        x = x_ref[...].astype(f32)
        scale_ref[...] = lax.rsqrt(jnp.mean(x * x, axis=-1, keepdims=True) + eps)

    out = jnp.dot(x_ref[...], w_ref[0], preferred_element_type=f32) * scale_ref[...]
    odd = pos[1]

    @pl.when(step < 2)
    def _():
        kv = out.astype(bf16)

        @pl.when(odd == 0)
        def _():
            kva[step] = kv[:, :LANES]
            kvb[step] = kv[:, LANES:]

        @pl.when(odd == 1)
        def _():
            kvb[step] = kv[:, :LANES]
            kva[step] = kv[:, LANES:]

    @pl.when(step == 2)
    def _():
        q = (out * (HD ** (-0.5) * math.log2(math.e))).astype(bf16)

        @pl.when(odd == 0)
        def _():
            qa[...] = q[:, :LANES]
            qb[...] = q[:, LANES:]

        @pl.when(odd == 1)
        def _():
            qb[...] = q[:, :LANES]
            qa[...] = q[:, LANES:]


def project(pos, tokens, w_qkv):
    rows, width = tokens.shape
    whole2 = lambda i, pos: (0, 0)
    whole3 = lambda i, pos: (0, 0, 0)
    kv = jax.ShapeDtypeStruct((2, rows, LANES), bf16)
    q = jax.ShapeDtypeStruct((rows, LANES), bf16)
    return pl.pallas_call(
        qkv_kernel,
        grid_spec=pltpu.PrefetchScalarGridSpec(
            num_scalar_prefetch=1,
            grid=(3,),
            in_specs=[
                pl.BlockSpec((rows, width), whole2),
                pl.BlockSpec((1, width, 2 * LANES), lambda i, pos: (lax.rem(i + 1, 3), 0, pos[0])),
            ],
            out_specs=[
                pl.BlockSpec((2, rows, LANES), whole3),
                pl.BlockSpec((2, rows, LANES), whole3),
                pl.BlockSpec((rows, LANES), whole2),
                pl.BlockSpec((rows, LANES), whole2),
            ],
            scratch_shapes=[pltpu.VMEM((rows, 1), f32)],
        ),
        out_shape=[kv, kv, q, q],
        compiler_params=pltpu.CompilerParams(vmem_limit_bytes=24 * 2**20),
        name="project",
    )(pos, tokens, w_qkv)


def attention_kernel(tile, *refs):
    qs, kvs, outs = refs[:4], refs[4:12], refs[12:16]
    k_all, v_lo, v_hi = refs[16:19]
    rows = qs[0].shape[0]
    low = lax.broadcasted_iota(jnp.int32, (1, LANES), 1) < HD
    one = jnp.ones((), bf16)
    zero = jnp.zeros((), bf16)
    for i, kv in enumerate(kvs):
        part = pl.ds(i * rows, rows)
        k_all[part] = kv[0]
        v = kv[1]
        v_lo[part] = jnp.where(low, v, one)
        v_hi[part] = jnp.where(low, one, v)

    def weigh(q, v_ref):
        scores = lax.dot_general(q, k_all[...], (((1,), (1,)), ((), ())), preferred_element_type=f32)
        top = jnp.max(scores, axis=-1, keepdims=True)
        weights = jnp.exp2(scores - top).astype(bf16)
        return jnp.dot(weights, v_ref[...], preferred_element_type=f32)

    for q_ref, o_ref in zip(qs, outs):

        def one_tile(t, carry):
            part = pl.ds(pl.multiple_of(t * tile, tile), tile)
            q = q_ref[part]
            lo = weigh(jnp.where(low, q, zero), v_lo)
            hi = weigh(jnp.where(low, zero, q), v_hi)
            top = jnp.where(low, lo, hi)
            bottom = pltpu.roll(jnp.where(low, hi, lo), HD, 1)
            o_ref[part] = (top / bottom).astype(bf16)
            return carry

        lax.fori_loop(0, rows // tile, one_tile, 0)


def attend(qs, kvs):
    rows = qs[0].shape[0]
    keys = rows * len(kvs)
    vmem = pl.BlockSpec(memory_space=pltpu.VMEM)
    return pl.pallas_call(
        functools.partial(attention_kernel, 128),
        in_specs=[vmem] * (len(qs) + len(kvs)),
        out_specs=[vmem] * len(qs),
        out_shape=[jax.ShapeDtypeStruct(q.shape, bf16) for q in qs],
        scratch_shapes=[pltpu.VMEM((keys, LANES), bf16)] * 3,
        compiler_params=pltpu.CompilerParams(vmem_limit_bytes=32 * 2**20),
        name="attend",
    )(*qs, *kvs)


def decode_kernel(pos, x_ref, dec_ref, *refs):
    atts = refs[:16]
    own = refs[16]
    near, far = refs[17:23], refs[23:29]
    main, up, down = refs[29:32]
    att, total = refs[32:34]
    z, core = pos[0], pos[1]
    half = own.shape[0] // 2
    quarter = half // 2
    total[...] = x_ref[...].astype(f32)
    for r in range(4):
        for s in range(4):
            at = pl.multiple_of((z ^ s) * LANES, LANES)
            att[r, :, pl.ds(at, LANES)] = atts[4 * r + s][...]
    total[...] += jnp.dot(att[0], own[...], preferred_element_type=f32)
    for r in range(1, 4):
        for group, side in ((near, core), (far, 1 - core)):
            w = jnp.concatenate([group[2 * (r - 1)][...], group[2 * (r - 1) + 1][...]], axis=0)
            at = pl.multiple_of(side * half, half)
            total[...] += jnp.dot(att[r, :, pl.ds(at, half)], w, preferred_element_type=f32)
    hidden = rms_scale(total[...]).astype(bf16)
    ext = lax.dot_general(
        dec_ref[...], hidden, (((1,), (1,)), ((), ())), preferred_element_type=f32
    )
    cells = main.shape[0] // PATCH
    main[...] = ext[OV * cells : (OV + PATCH) * cells]
    down[...] = ext[: OV * cells].astype(bf16)
    up[...] = ext[(OV + PATCH) * cells :].astype(bf16)


def decode(pos, tokens, w_dec, atts, own, near, far):
    rows, width = tokens.shape
    wide = w_dec.shape[0]
    cells = wide // (PATCH + 2 * OV)
    vmem = pl.BlockSpec(memory_space=pltpu.VMEM)
    return pl.pallas_call(
        decode_kernel,
        in_specs=[pl.BlockSpec(memory_space=pltpu.SMEM)] + [vmem] * (3 + 16 + 12),
        out_specs=[vmem] * 3,
        out_shape=[
            jax.ShapeDtypeStruct((PATCH * cells, rows), f32),
            jax.ShapeDtypeStruct((OV * cells, rows), bf16),
            jax.ShapeDtypeStruct((OV * cells, rows), bf16),
        ],
        scratch_shapes=[pltpu.VMEM((4, rows, width // 4), bf16), pltpu.VMEM((rows, width), f32)],
        compiler_params=pltpu.CompilerParams(vmem_limit_bytes=40 * 2**20),
        name="decode",
    )(pos, tokens, w_dec, *atts, own, *near, *far)


def fast_body(tokens, w_qkv, w_out, w_dec):
    rows = tokens.shape[0]
    ctx = lax.axis_index("ctx")
    z, core = ctx // 2, ctx % 2
    far_pos = jnp.stack([(z // 2) ^ 1, z % 2])
    near_pos = jnp.stack([z // 2, z % 2])

    half = w_out.shape[0] // 2
    quarter = half // 2
    mine = lax.dynamic_slice_in_dim(w_out, core * half, half, 0)
    first, second = mine[:quarter], mine[quarter:]
    x_first, y_second = swapped(first, "head", 1), swapped(second, "head", 2)

    kv2, kv3, q2, q3 = project(far_pos, tokens, w_qkv)
    kv2r, kv3r = swapped(kv2, "ctx", 4), swapped(kv3, "ctx", 6)
    kv0, kv1, q0, q1 = project(near_pos, tokens, w_qkv)
    kv1r = swapped(kv1, "ctx", 2)
    q2r, q3r, q1r = swapped(q2, "ctx", 4), swapped(q3, "ctx", 6), swapped(q1, "ctx", 2)

    x_second, y_first = swapped(second, "head", 1), swapped(first, "head", 2)
    diag_first, diag_second = swapped(x_first, "head", 2), swapped(y_second, "head", 1)
    near = [x_first, x_second, y_first, y_second, diag_first, diag_second]
    far = [swapped(part, "ctx", 1) for part in near]

    kvs = [kv0, kv1r, kv2r, kv3r]
    kvs = kvs + [swapped(kv, "ctx", 1) for kv in kvs]
    o0, o1, o2, o3 = attend([q0, q1r, q2r, q3r], kvs)
    att0 = [o0, swapped(o1, "ctx", 2), swapped(o2, "ctx", 4), swapped(o3, "ctx", 6)]
    att1 = [swapped(part, "head", 1) for part in att0]
    att2 = [swapped(part, "head", 2) for part in att0]
    att3 = [swapped(att1[s], "head", 2) if s < 2 else swapped(att2[s], "head", 1) for s in range(4)]

    dec = w_dec.transpose(1, 2, 0)
    dec = dec.reshape(-1, dec.shape[2])
    main, up, down = decode(
        jnp.stack([z, core]), tokens, dec, att0 + att1 + att2 + att3, w_out, near, far
    )
    from_before = passed_along(up, "ctx", 1).astype(f32)
    from_after = passed_along(down, "ctx", -1).astype(f32)
    edge = up.shape[0]
    field = jnp.concatenate(
        [main[:edge] + from_before, main[edge:-edge], main[-edge:] + from_after], axis=0
    )
    return field.reshape(PATCH, -1, rows).transpose(2, 0, 1)


def general_body(tokens, w_qkv, w_out, w_dec):
    rows = tokens.shape[0]
    local_heads = w_qkv.shape[2] // HD
    xf = tokens.astype(f32)
    normed = rms_scale(xf).astype(bf16)
    projected = jnp.einsum("td,kdc->ktc", normed, w_qkv, preferred_element_type=f32).astype(bf16)
    queries = projected[0].reshape(rows, local_heads, HD)
    keyvals = projected[1:]
    scale = HD ** (-0.5)

    def block_update(carry, block):
        best, total, accum = carry
        keys = block[0].reshape(-1, local_heads, HD)
        values = block[1].reshape(-1, local_heads, HD)
        scores = jnp.einsum("thd,rhd->thr", queries, keys, preferred_element_type=f32) * scale
        fresh = jnp.maximum(best, jnp.max(scores, axis=-1))
        shrink = jnp.exp(best - fresh)
        weights = jnp.exp(scores - fresh[..., None])
        total = total * shrink + jnp.sum(weights, axis=-1)
        accum = accum * shrink[..., None] + jnp.einsum(
            "thr,rhd->thd", weights.astype(bf16), values, preferred_element_type=f32
        )
        return (fresh, total, accum)

    initial = (
        jnp.full((rows, local_heads), -1e30, f32),
        jnp.zeros((rows, local_heads), f32),
        jnp.zeros((rows, local_heads, HD), f32),
    )
    piece = lax.all_gather(keyvals, "ctx", axis=1, tiled=True)
    length = piece.shape[1]
    span = math.gcd(length, 1024)

    def one_block(index, inner):
        block = lax.dynamic_slice_in_dim(piece, index * span, span, 1)
        return block_update(inner, block)

    best, total, accum = lax.fori_loop(0, length // span, one_block, initial)
    attended = (accum / total[..., None]).astype(bf16).reshape(rows, local_heads * HD)
    partial_out = jnp.dot(attended, w_out, preferred_element_type=f32)
    mixed = lax.psum(partial_out.astype(bf16), "head").astype(f32)
    hidden = rms_scale(xf + mixed).astype(bf16)
    extended = jnp.dot(hidden, w_dec.reshape(w_dec.shape[0], -1), preferred_element_type=f32)
    extended = extended.reshape(rows, w_dec.shape[1], w_dec.shape[2])
    from_before = passed_along(extended[:, PATCH + OV :].astype(bf16), "ctx", 1).astype(f32)
    from_after = passed_along(extended[:, :OV].astype(bf16), "ctx", -1).astype(f32)
    middle = extended[:, OV : OV + PATCH]
    return jnp.concatenate(
        [
            middle[:, :OV] + from_before,
            middle[:, OV : PATCH - OV],
            middle[:, PATCH - OV :] + from_after,
        ],
        axis=1,
    )


def body(tokens, w_qkv, w_out, w_dec):
    fits = lax.axis_size("ctx") == 8 and lax.axis_size("head") == 4
    fits = fits and w_qkv.shape[2] == 4 * LANES and tokens.shape[0] % 256 == 0
    run = fast_body if fits else general_body
    return run(tokens, w_qkv, w_out, w_dec)


def solution(mesh):
    return jax.shard_map(
        body,
        mesh=mesh,
        in_specs=(P("ctx", None), P(None, None, "head"), P("head", None), P(None, None, "head")),
        out_specs=P("ctx", None, "head"),
        check_vma=False,
    )
```

time: 167 us -> 112 us (0.67)
  waiting for transfers between devices: 101 us -> 37.2 us
  starting transfers between devices: 3.63 us -> 43.9 us
  Pallas kernels: 0 us -> 21.1 us
  matrix products: 19.2 us -> 0 us
  between operations: 13.5 us -> 0.09 us
  local copies, waits for them, and re-layouts: 21.1 us -> 8.79 us
  other arithmetic: 8.36 us -> 1 us
    psum x1 -> x0, waiting for transfers between devices: 51.4 us -> none  [body(): lax.psum(partial_out.astype(jnp.bfloat16), 'head').astype(jnp.float32)]
    all_gather x1 -> x0, waiting for transfers between devices: 47.2 us -> none  [body(): piece = lax.all_gather(keyvals, 'ctx', axis=1, tiled=True)]
    ppermute x0 -> x37, starting transfers between devices: none -> 40.3 us  [swapped(): return lax.ppermute(value, axis, [(i, i ^ bits) for i in range(count)])]
    ppermute x0 -> x37, waiting for transfers between devices: none -> 34.9 us  [swapped(): return lax.ppermute(value, axis, [(i, i ^ bits) for i in range(count)])]
    pallas_call x0 -> x4, Pallas kernels: none -> 21.1 us  [the longest x1 10.6 us: attend(): pl.pallas_call(functools.partial(attention_kernel, 128), in_specs=[vmem]...]
    dot_general x7 -> x0, matrix products: 19.2 us -> none  [the longest x2 5.08 us: block_update(): jnp.einsum('thd,rhd->thr', queries, keys, preferred_element_type=jnp.floa...]
    while x18 -> x0, local copies, waits for them, and re-layouts: 10.6 us -> none
    slice x7 -> x2, local copies, waits for them, and re-layouts: 9.62 us -> 0.12 us  [the longest x1 0.1 us: fast_body(): first, second = (mine[:quarter], mine[quarter:])]
  transfers between devices with their start and end apart: 4 -> 39, of which waited for: 3 -> 21; matrix products, arithmetic and copies ran while one was open for 2% -> 0% of each run, Pallas kernels for 0% -> 12%
where the time goes in v1:
time: 112 us
  starting transfers between devices  43.9 us (39%)
  waiting for transfers between devices  37.2 us (33%)
  Pallas kernels  21.1 us (19%)
  local copies, waits for them, and re-layouts  8.79 us (8%)
    ppermute x37, starting transfers between devices, swapped(): return lax.ppermute(value, axis, [(i, i ^ bits) for i in range(count)])  40.3 us
    ppermute x37, waiting for transfers between devices, swapped(): return lax.ppermute(value, axis, [(i, i ^ bits) for i in range(count)])  34.9 us
    pallas_call x1, Pallas kernels, attend(): pl.pallas_call(functools.partial(attention_kernel, 128), in_specs=[vmem]...  10.6 us
    unnamed x20, local copies, waits for them, and re-layouts  8.67 us
    pallas_call x2, Pallas kernels, project(): pl.pallas_call(qkv_kernel, grid_spec=pltpu.PrefetchScalarGridSpec(num_sca...  6.34 us
    pallas_call x1, Pallas kernels, decode(): pl.pallas_call(decode_kernel, in_specs=[pl.BlockSpec(memory_space=pltpu.S...  4.18 us
    ppermute x2, starting transfers between devices, passed_along(): return lax.ppermute(value, axis, pairs)  3.6 us
    ppermute x2, waiting for transfers between devices, passed_along(): return lax.ppermute(value, axis, pairs)  2.29 us
  transfers between devices with their start and end apart: 39, of which 21 were waited for; matrix products, arithmetic and copies ran while one was open for 0% of the time, Pallas kernels for 12%

profile of v1, /device:TPU:0, one launch (start us, length us, event | category | flops | bytes accessed | tf_op | source)
XLA Modules:
  0.0 112.1 jit_solution(8398018620992844471)
XLA Ops:
  0.1 2.8 %copy-done = bf16[3,2048,512]{2,1,0:T(8,128)(2,1)S(1)} copy-done((bf16[3,2048,512]{2,1,0:T(8,128)(2,1)S(1)}, bf16[3,2048,512]{2,1,0:T(8,128)(2,1)}, u32[]{:S(2)}) %copy-start) | copy-done | bytes 6291480
  4.1 3.2 %project.2 = (bf16[2,256,128]{2,1,0:T(8,128)(2,1)S(1)}, bf16[2,256,128]{2,1,0:T(8,128)(2,1)}, bf16[256,128]{1,0:T(8,128)(2,1)S(1)}, bf16[256,128]{1,0:T(8,128)(2,1)}) custom-call(s32[2]{0:T(128)S(1)} %get-tuple-element.39.pos, bf16[256,2048]{1,0:T(8,128)(2,1)S(1)} %copy-done.2, bf16[3,2048,512]{2,1,0:T(8,128)(2,1)S(1)} %copy-done), custom_call_target="tpu_custom_call" | custom-call | tf_op jit(solution)/shard_map/project/pallas_call | solution.py:82
  7.9 3.0 %collective-permute-start = (bf16[256,128]{1,0:T(8,128)(2,1)}, bf16[256,128]{1,0:T(8,128)(2,1)}, u32[]{:S(2)}, u32[]{:S(2)}) collective-permute-start(bf16[256,128]{1,0:T(8,128)(2,1)} %get-tuple-element.21), channel_id=1, source_target_pairs={{0,8},{4,12},{8,0},{12,4},{16,24},{20,28},{24,16},{28,20},{1,9},{5... | collective-permute-start | bytes 196616 | tf_op jit(solution)/shard_map/ppermute | solution.py:29
  10.9 3.2 %project.3 = (bf16[2,256,128]{2,1,0:T(8,128)(2,1)S(1)}, bf16[2,256,128]{2,1,0:T(8,128)(2,1)S(1)}, bf16[256,128]{1,0:T(8,128)(2,1)}, bf16[256,128]{1,0:T(8,128)(2,1)}) custom-call(s32[2]{0:T(128)S(1)} %get-tuple-element.40.pos, bf16[256,2048]{1,0:T(8,128)(2,1)S(1)} %copy-done.2, bf16[3,2048,512]{2,1,0:T(8,128)(2,1)S(1)} %copy-done.1), custom_call_target="tpu_custom_call" | custom-call | tf_op jit(solution)/shard_map/project/pallas_call | solution.py:82
  15.4 2.6 %collective-permute-start.1 = (bf16[256,128]{1,0:T(8,128)(2,1)}, bf16[256,128]{1,0:T(8,128)(2,1)}, u32[]{:S(2)}, u32[]{:S(2)}) collective-permute-start(bf16[256,128]{1,0:T(8,128)(2,1)} %get-tuple-element.22), channel_id=1, source_target_pairs={{0,16},{4,20},{8,24},{12,28},{16,0},{20,4},{24,8},{28,12},{1,17},{... | collective-permute-start | bytes 196616 | tf_op jit(solution)/shard_map/ppermute | solution.py:29
  18.4 1.4 %collective-permute-start.2 = (bf16[256,128]{1,0:T(8,128)(2,1)}, bf16[256,128]{1,0:T(8,128)(2,1)}, u32[]{:S(2)}, u32[]{:S(2)}) collective-permute-start(bf16[256,128]{1,0:T(8,128)(2,1)} %get-tuple-element.23), channel_id=1, source_target_pairs={{0,24},{4,28},{8,16},{12,20},{16,8},{20,12},{24,0},{28,4},{1,25},{... | collective-permute-start | bytes 196616 | tf_op jit(solution)/shard_map/ppermute | solution.py:29
  19.8 1.7 %collective-permute-start.4 = (bf16[2,256,128]{2,1,0:T(8,128)(2,1)}, bf16[2,256,128]{2,1,0:T(8,128)(2,1)S(1)}, u32[]{:S(2)}, u32[]{:S(2)}) collective-permute-start(bf16[2,256,128]{2,1,0:T(8,128)(2,1)} %copy-done.9), channel_id=1, source_target_pairs={{0,16},{4,20},{8,24},{12,28},{16,0},{20,4},{24,8},{28,12},{1,17},{... | collective-permute-start | bytes 393224 | tf_op jit(solution)/shard_map/ppermute | solution.py:29
  21.5 2.3 %collective-permute-start.5 = (bf16[2,256,128]{2,1,0:T(8,128)(2,1)}, bf16[2,256,128]{2,1,0:T(8,128)(2,1)S(1)}, u32[]{:S(2)}, u32[]{:S(2)}) collective-permute-start(bf16[2,256,128]{2,1,0:T(8,128)(2,1)} %copy-done.8), channel_id=1, source_target_pairs={{0,24},{4,28},{8,16},{12,20},{16,8},{20,12},{24,0},{28,4},{1,25},{... | collective-permute-start | bytes 393224 | tf_op jit(solution)/shard_map/ppermute | solution.py:29
  23.9 1.7 %collective-permute-done.2.refs_3_ = bf16[256,128]{1,0:T(8,128)(2,1)} collective-permute-done((bf16[256,128]{1,0:T(8,128)(2,1)}, bf16[256,128]{1,0:T(8,128)(2,1)}, u32[]{:S(2)}, u32[]{:S(2)}) %collective-permute-start.2) | collective-permute-done | bytes 65568 | tf_op jit(solution)/shard_map/ppermute | solution.py:29
  25.5 1.5 %collective-permute-start.28 = (bf16[128,2048]{1,0:T(8,128)(2,1)S(1)}, bf16[128,2048]{1,0:T(8,128)(2,1)S(1)}, u32[]{:S(2)}, u32[]{:S(2)}) collective-permute-start(bf16[128,2048]{1,0:T(8,128)(2,1)S(1)} %get-tuple-element.35), channel_id=1, source_target_pairs={{0,2},{1,3},{2,0},{3,1},{4,6},{5,7},{6,4},{7,5},{8,10},{9,11},{10,... | collective-permute-start | bytes 1572872 | tf_op jit(solution)/shard_map/ppermute | solution.py:29
  27.1 1.5 %collective-permute-start.25 = (bf16[128,2048]{1,0:T(8,128)(2,1)S(1)}, bf16[128,2048]{1,0:T(8,128)(2,1)S(1)}, u32[]{:S(2)}, u32[]{:S(2)}) collective-permute-start(bf16[128,2048]{1,0:T(8,128)(2,1)S(1)} %get-tuple-element.36), channel_id=1, source_target_pairs={{0,1},{1,0},{2,3},{3,2},{4,5},{5,4},{6,7},{7,6},{8,9},{9,8},{10,11... | collective-permute-start | bytes 1572872 | tf_op jit(solution)/shard_map/ppermute | solution.py:29
  28.6 5.8 %collective-permute-done.4.refs_6_ = bf16[2,256,128]{2,1,0:T(8,128)(2,1)S(1)} collective-permute-done((bf16[2,256,128]{2,1,0:T(8,128)(2,1)}, bf16[2,256,128]{2,1,0:T(8,128)(2,1)S(1)}, u32[]{:S(2)}, u32[]{:S(2)}) %collective-permute-start.4) | collective-permute-done | bytes 131104 | tf_op jit(solution)/shard_map/ppermute | solution.py:29
  36.8 10.6 %attend.1 = (bf16[256,128]{1,0:T(8,128)(2,1)S(1)}, bf16[256,128]{1,0:T(8,128)(2,1)S(1)}, bf16[256,128]{1,0:T(8,128)(2,1)S(1)}, bf16[256,128]{1,0:T(8,128)(2,1)S(1)}) custom-call(bf16[256,128]{1,0:T(8,128)(2,1)S(1)} %copy-done.7, bf16[256,128]{1,0:T(8,128)(2,1)} %collective-permute-done.refs_1_, bf16[256,128]{1,0:T(8,128)(2,1)} %collective-permute-done.1.refs_2_, ...), custom_call_target="tpu_custom_call" | custom-call | tf_op jit(solution)/shard_map/attend/pallas_call | solution.py:144
  47.3 2.9 %collective-permute-start.10 = (bf16[256,128]{1,0:T(8,128)(2,1)S(1)}, bf16[256,128]{1,0:T(8,128)(2,1)S(1)}, u32[]{:S(2)}, u32[]{:S(2)}) collective-permute-start(bf16[256,128]{1,0:T(8,128)(2,1)S(1)} %get-tuple-element.29), channel_id=1, source_target_pairs={{0,8},{4,12},{8,0},{12,4},{16,24},{20,28},{24,16},{28,20},{1,9},{5... | collective-permute-start | bytes 196616 | tf_op jit(solution)/shard_map/ppermute | solution.py:29
  50.5 2.1 %collective-permute-start.12 = (bf16[256,128]{1,0:T(8,128)(2,1)S(1)}, bf16[256,128]{1,0:T(8,128)(2,1)S(1)}, u32[]{:S(2)}, u32[]{:S(2)}) collective-permute-start(bf16[256,128]{1,0:T(8,128)(2,1)S(1)} %get-tuple-element.31), channel_id=1, source_target_pairs={{0,24},{4,28},{8,16},{12,20},{16,8},{20,12},{24,0},{28,4},{1,25},{... | collective-permute-start | bytes 196616 | tf_op jit(solution)/shard_map/ppermute | solution.py:29
  52.6 1.5 %collective-permute-start.17 = (bf16[256,128]{1,0:T(8,128)(2,1)S(1)}, bf16[256,128]{1,0:T(8,128)(2,1)S(1)}, u32[]{:S(2)}, u32[]{:S(2)}) collective-permute-start(bf16[256,128]{1,0:T(8,128)(2,1)S(1)} %get-tuple-element.28.refs_0_), channel_id=1, source_target_pairs={{0,2},{1,3},{2,0},{3,1},{4,6},{5,7},{6,4},{7,5},{8,10},{9,11},{10,... | collective-permute-start | bytes 196616 | tf_op jit(solution)/shard_map/ppermute | solution.py:29
  54.1 4.0 %collective-permute-done.11.refs_2_ = bf16[256,128]{1,0:T(8,128)(2,1)S(1)} collective-permute-done((bf16[256,128]{1,0:T(8,128)(2,1)S(1)}, bf16[256,128]{1,0:T(8,128)(2,1)S(1)}, u32[]{:S(2)}, u32[]{:S(2)}) %collective-permute-start.11) | collective-permute-done | bytes 65568 | tf_op jit(solution)/shard_map/ppermute | solution.py:29
  58.2 1.5 %collective-permute-start.13 = (bf16[256,128]{1,0:T(8,128)(2,1)S(1)}, bf16[256,128]{1,0:T(8,128)(2,1)S(1)}, u32[]{:S(2)}, u32[]{:S(2)}) collective-permute-start(bf16[256,128]{1,0:T(8,128)(2,1)S(1)} %get-tuple-element.28.refs_0_), channel_id=1, source_target_pairs={{0,1},{1,0},{2,3},{3,2},{4,5},{5,4},{6,7},{7,6},{8,9},{9,8},{10,11... | collective-permute-start | bytes 196616 | tf_op jit(solution)/shard_map/ppermute | solution.py:29
  59.7 1.5 %collective-permute-start.18 = (bf16[256,128]{1,0:T(8,128)(2,1)S(1)}, bf16[256,128]{1,0:T(8,128)(2,1)S(1)}, u32[]{:S(2)}, u32[]{:S(2)}) collective-permute-start(bf16[256,128]{1,0:T(8,128)(2,1)S(1)} %collective-permute-done.10.refs_1_), channel_id=1, source_target_pairs={{0,2},{1,3},{2,0},{3,1},{4,6},{5,7},{6,4},{7,5},{8,10},{9,11},{10,... | collective-permute-start | bytes 196616 | tf_op jit(solution)/shard_map/ppermute | solution.py:29
  62.7 1.4 %collective-permute-start.19 = (bf16[256,128]{1,0:T(8,128)(2,1)S(1)}, bf16[256,128]{1,0:T(8,128)(2,1)S(1)}, u32[]{:S(2)}, u32[]{:S(2)}) collective-permute-start(bf16[256,128]{1,0:T(8,128)(2,1)S(1)} %collective-permute-done.11.refs_2_), channel_id=1, source_target_pairs={{0,2},{1,3},{2,0},{3,1},{4,6},{5,7},{6,4},{7,5},{8,10},{9,11},{10,... | collective-permute-start | bytes 196616 | tf_op jit(solution)/shard_map/ppermute | solution.py:29
  67.0 1.4 %collective-permute-start.16 = (bf16[256,128]{1,0:T(8,128)(2,1)S(1)}, bf16[256,128]{1,0:T(8,128)(2,1)S(1)}, u32[]{:S(2)}, u32[]{:S(2)}) collective-permute-start(bf16[256,128]{1,0:T(8,128)(2,1)S(1)} %collective-permute-done.12.refs_3_), channel_id=1, source_target_pairs={{0,1},{1,0},{2,3},{3,2},{4,5},{5,4},{6,7},{7,6},{8,9},{9,8},{10,11... | collective-permute-start | bytes 196616 | tf_op jit(solution)/shard_map/ppermute | solution.py:29
  68.5 1.5 %collective-permute-start.21 = (bf16[256,128]{1,0:T(8,128)(2,1)S(1)}, bf16[256,128]{1,0:T(8,128)(2,1)S(1)}, u32[]{:S(2)}, u32[]{:S(2)}) collective-permute-start(bf16[256,128]{1,0:T(8,128)(2,1)S(1)} %collective-permute-done.13.refs_4_), channel_id=1, source_target_pairs={{0,2},{1,3},{2,0},{3,1},{4,6},{5,7},{6,4},{7,5},{8,10},{9,11},{10,... | collective-permute-start | bytes 196616 | tf_op jit(solution)/shard_map/ppermute | solution.py:29
  71.5 1.5 %collective-permute-start.23 = (bf16[256,128]{1,0:T(8,128)(2,1)S(1)}, bf16[256,128]{1,0:T(8,128)(2,1)S(1)}, u32[]{:S(2)}, u32[]{:S(2)}) collective-permute-start(bf16[256,128]{1,0:T(8,128)(2,1)S(1)} %collective-permute-done.19.refs_10_), channel_id=1, source_target_pairs={{0,1},{1,0},{2,3},{3,2},{4,5},{5,4},{6,7},{7,6},{8,9},{9,8},{10,11... | collective-permute-start | bytes 196616 | tf_op jit(solution)/shard_map/ppermute | solution.py:29
  76.6 1.4 %collective-permute-start.27 = (bf16[128,2048]{1,0:T(8,128)(2,1)S(1)}, bf16[128,2048]{1,0:T(8,128)(2,1)S(1)}, u32[]{:S(2)}, u32[]{:S(2)}) collective-permute-start(bf16[128,2048]{1,0:T(8,128)(2,1)S(1)} %get-tuple-element.36), channel_id=1, source_target_pairs={{0,2},{1,3},{2,0},{3,1},{4,6},{5,7},{6,4},{7,5},{8,10},{9,11},{10,... | collective-permute-start | bytes 1572872 | tf_op jit(solution)/shard_map/ppermute | solution.py:29
  78.1 1.7 %collective-permute-start.30 = (bf16[128,2048]{1,0:T(8,128)(2,1)S(1)}, bf16[128,2048]{1,0:T(8,128)(2,1)S(1)}, u32[]{:S(2)}, u32[]{:S(2)}) collective-permute-start(bf16[128,2048]{1,0:T(8,128)(2,1)S(1)} %collective-permute-done.28.refs_20_), channel_id=1, source_target_pairs={{0,1},{1,0},{2,3},{3,2},{4,5},{5,4},{6,7},{7,6},{8,9},{9,8},{10,11... | collective-permute-start | bytes 1572872 | tf_op jit(solution)/shard_map/ppermute | solution.py:29
  79.8 1.3 %collective-permute-start.29 = (bf16[128,2048]{1,0:T(8,128)(2,1)S(1)}, bf16[128,2048]{1,0:T(8,128)(2,1)S(1)}, u32[]{:S(2)}, u32[]{:S(2)}) collective-permute-start(bf16[128,2048]{1,0:T(8,128)(2,1)S(1)} %collective-permute-done.25.refs_17_), channel_id=1, source_target_pairs={{0,2},{1,3},{2,0},{3,1},{4,6},{5,7},{6,4},{7,5},{8,10},{9,11},{10,... | collective-permute-start | bytes 1572872 | tf_op jit(solution)/shard_map/ppermute | solution.py:29
  81.1 8.4 %collective-permute-done.26.refs_18_ = bf16[128,2048]{1,0:T(8,128)(2,1)S(1)} collective-permute-done((bf16[128,2048]{1,0:T(8,128)(2,1)S(1)}, bf16[128,2048]{1,0:T(8,128)(2,1)S(1)}, u32[]{:S(2)}, u32[]{:S(2)}) %collective-permute-start.26) | collective-permute-done | bytes 524320 | tf_op jit(solution)/shard_map/ppermute | solution.py:29
  90.1 6.4 %collective-permute-done.30.refs_22_ = bf16[128,2048]{1,0:T(8,128)(2,1)S(1)} collective-permute-done((bf16[128,2048]{1,0:T(8,128)(2,1)S(1)}, bf16[128,2048]{1,0:T(8,128)(2,1)S(1)}, u32[]{:S(2)}, u32[]{:S(2)}) %collective-permute-start.30) | collective-permute-done | bytes 524320 | tf_op jit(solution)/shard_map/ppermute | solution.py:29
  99.3 1.9 %copy-done.5 = bf16[2048,12,64]{0,2,1:T(8,128)(2,1)S(1)} copy-done((bf16[2048,12,64]{0,2,1:T(8,128)(2,1)S(1)}, bf16[2048,12,64]{0,2,1:T(8,128)(2,1)}, u32[]{:S(2)}) %copy-start.5) | copy-done | bytes 3145752
  101.1 4.2 %decode.1 = (f32[512,256]{1,0:T(8,128)S(1)}, bf16[128,256]{1,0:T(8,128)(2,1)S(1)}, bf16[128,256]{1,0:T(8,128)(2,1)S(1)}) custom-call(s32[2]{0:T(128)S(1)} %pad_add_fusion.pos, bf16[256,2048]{1,0:T(8,128)(2,1)S(1)} %copy-done.3, bf16[768,2048]{1,0:T(8,128)(2,1)S(1)} %bitcast.11, bf16[256,128]{1,0:T(8,128)(2,1)S(1)} %get-tuple-element.28.refs_0_, ...), custom_call_target="tpu_custom_call" | custom-call | tf_op jit(solution)/shard_map/decode/pallas_call | solution.py:190
  105.5 3.4 %collective-permute-start.38 = (bf16[128,256]{1,0:T(8,128)(2,1)S(1)}, bf16[128,256]{1,0:T(8,128)(2,1)S(1)}, u32[]{:S(2)}, u32[]{:S(2)}) collective-permute-start(bf16[128,256]{1,0:T(8,128)(2,1)S(1)} %get-tuple-element.34), channel_id=1, source_target_pairs={{0,28},{4,0},{8,4},{12,8},{16,12},{20,16},{24,20},{28,24},{1,29},{... | collective-permute-start | bytes 196616 | tf_op jit(solution)/shard_map/ppermute | solution.py:24
  108.9 2.3 %collective-permute-done.37 = bf16[128,256]{1,0:T(8,128)(2,1)S(1)} collective-permute-done((bf16[128,256]{1,0:T(8,128)(2,1)S(1)}, bf16[128,256]{1,0:T(8,128)(2,1)S(1)}, u32[]{:S(2)}, u32[]{:S(2)}) %collective-permute-start.37) | collective-permute-done | bytes 65568 | tf_op jit(solution)/shard_map/ppermute | solution.py:24
  (76 shorter events, 20.5 us)
Async XLA Ops:
  7.9 11.9 %collective-permute-start = (bf16[256,128]{1,0:T(8,128)(2,1)}, bf16[256,128]{1,0:T(8,128)(2,1)}, u32[]{:S(2)}, u32[]{:S(2)}) collective-permute-start(bf16[256,128]{1,0:T(8,128)(2,1)} %get-tuple-element.21), channel_id=1, source_target_pairs={{0,8},{4,12},{8,0},{12,4},{16,24},{20,28},{24,16},{28,20},{1,9},{5... | collective-permute-start | bytes 196616 | tf_op jit(solution)/shard_map/ppermute | solution.py:29
  15.4 6.1 %collective-permute-start.1 = (bf16[256,128]{1,0:T(8,128)(2,1)}, bf16[256,128]{1,0:T(8,128)(2,1)}, u32[]{:S(2)}, u32[]{:S(2)}) collective-permute-start(bf16[256,128]{1,0:T(8,128)(2,1)} %get-tuple-element.22), channel_id=1, source_target_pairs={{0,16},{4,20},{8,24},{12,28},{16,0},{20,4},{24,8},{28,12},{1,17},{... | collective-permute-start | bytes 196616 | tf_op jit(solution)/shard_map/ppermute | solution.py:29
  18.0 9.1 %collective-permute-start.3 = (bf16[2,256,128]{2,1,0:T(8,128)(2,1)}, bf16[2,256,128]{2,1,0:T(8,128)(2,1)S(1)}, u32[]{:S(2)}, u32[]{:S(2)}) collective-permute-start(bf16[2,256,128]{2,1,0:T(8,128)(2,1)} %get-tuple-element.25), channel_id=1, source_target_pairs={{0,8},{4,12},{8,0},{12,4},{16,24},{20,28},{24,16},{28,20},{1,9},{5... | collective-permute-start | bytes 393224 | tf_op jit(solution)/shard_map/ppermute | solution.py:29
  18.4 10.1 %collective-permute-start.6 = (bf16[2,256,128]{2,1,0:T(8,128)(2,1)S(1)}, bf16[2,256,128]{2,1,0:T(8,128)(2,1)S(1)}, u32[]{:S(2)}, u32[]{:S(2)}) collective-permute-start(bf16[2,256,128]{2,1,0:T(8,128)(2,1)S(1)} %get-tuple-element.24.refs_4_), channel_id=1, source_target_pairs={{0,4},{4,0},{8,12},{12,8},{16,20},{20,16},{24,28},{28,24},{1,5},{5... | collective-permute-start | bytes 393224 | tf_op jit(solution)/shard_map/ppermute | solution.py:29
  18.4 7.1 %collective-permute-start.2 = (bf16[256,128]{1,0:T(8,128)(2,1)}, bf16[256,128]{1,0:T(8,128)(2,1)}, u32[]{:S(2)}, u32[]{:S(2)}) collective-permute-start(bf16[256,128]{1,0:T(8,128)(2,1)} %get-tuple-element.23), channel_id=1, source_target_pairs={{0,24},{4,28},{8,16},{12,20},{16,8},{20,12},{24,0},{28,4},{1,25},{... | collective-permute-start | bytes 196616 | tf_op jit(solution)/shard_map/ppermute | solution.py:29
  19.8 14.6 %collective-permute-start.4 = (bf16[2,256,128]{2,1,0:T(8,128)(2,1)}, bf16[2,256,128]{2,1,0:T(8,128)(2,1)S(1)}, u32[]{:S(2)}, u32[]{:S(2)}) collective-permute-start(bf16[2,256,128]{2,1,0:T(8,128)(2,1)} %copy-done.9), channel_id=1, source_target_pairs={{0,16},{4,20},{8,24},{12,28},{16,0},{20,4},{24,8},{28,12},{1,17},{... | collective-permute-start | bytes 393224 | tf_op jit(solution)/shard_map/ppermute | solution.py:29
  21.5 12.9 %collective-permute-start.5 = (bf16[2,256,128]{2,1,0:T(8,128)(2,1)}, bf16[2,256,128]{2,1,0:T(8,128)(2,1)S(1)}, u32[]{:S(2)}, u32[]{:S(2)}) collective-permute-start(bf16[2,256,128]{2,1,0:T(8,128)(2,1)} %copy-done.8), channel_id=1, source_target_pairs={{0,24},{4,28},{8,16},{12,20},{16,8},{20,12},{24,0},{28,4},{1,25},{... | collective-permute-start | bytes 393224 | tf_op jit(solution)/shard_map/ppermute | solution.py:29
  25.5 52.4 %collective-permute-start.28 = (bf16[128,2048]{1,0:T(8,128)(2,1)S(1)}, bf16[128,2048]{1,0:T(8,128)(2,1)S(1)}, u32[]{:S(2)}, u32[]{:S(2)}) collective-permute-start(bf16[128,2048]{1,0:T(8,128)(2,1)S(1)} %get-tuple-element.35), channel_id=1, source_target_pairs={{0,2},{1,3},{2,0},{3,1},{4,6},{5,7},{6,4},{7,5},{8,10},{9,11},{10,... | collective-permute-start | bytes 1572872 | tf_op jit(solution)/shard_map/ppermute | solution.py:29
  27.1 52.7 %collective-permute-start.25 = (bf16[128,2048]{1,0:T(8,128)(2,1)S(1)}, bf16[128,2048]{1,0:T(8,128)(2,1)S(1)}, u32[]{:S(2)}, u32[]{:S(2)}) collective-permute-start(bf16[128,2048]{1,0:T(8,128)(2,1)S(1)} %get-tuple-element.36), channel_id=1, source_target_pairs={{0,1},{1,0},{2,3},{3,2},{4,5},{5,4},{6,7},{7,6},{8,9},{9,8},{10,11... | collective-permute-start | bytes 1572872 | tf_op jit(solution)/shard_map/ppermute | solution.py:29
  28.6 6.3 %collective-permute-start.7 = (bf16[2,256,128]{2,1,0:T(8,128)(2,1)S(1)}, bf16[2,256,128]{2,1,0:T(8,128)(2,1)S(1)}, u32[]{:S(2)}, u32[]{:S(2)}) collective-permute-start(bf16[2,256,128]{2,1,0:T(8,128)(2,1)S(1)} %collective-permute-done.3.refs_5_), channel_id=1, source_target_pairs={{0,4},{4,0},{8,12},{12,8},{16,20},{20,16},{24,28},{28,24},{1,5},{5... | collective-permute-start | bytes 393224 | tf_op jit(solution)/shard_map/ppermute | solution.py:29
  47.3 5.3 %collective-permute-start.10 = (bf16[256,128]{1,0:T(8,128)(2,1)S(1)}, bf16[256,128]{1,0:T(8,128)(2,1)S(1)}, u32[]{:S(2)}, u32[]{:S(2)}) collective-permute-start(bf16[256,128]{1,0:T(8,128)(2,1)S(1)} %get-tuple-element.29), channel_id=1, source_target_pairs={{0,8},{4,12},{8,0},{12,4},{16,24},{20,28},{24,16},{28,20},{1,9},{5... | collective-permute-start | bytes 196616 | tf_op jit(solution)/shard_map/ppermute | solution.py:29
  50.2 8.0 %collective-permute-start.11 = (bf16[256,128]{1,0:T(8,128)(2,1)S(1)}, bf16[256,128]{1,0:T(8,128)(2,1)S(1)}, u32[]{:S(2)}, u32[]{:S(2)}) collective-permute-start(bf16[256,128]{1,0:T(8,128)(2,1)S(1)} %get-tuple-element.30), channel_id=1, source_target_pairs={{0,16},{4,20},{8,24},{12,28},{16,0},{20,4},{24,8},{28,12},{1,17},{... | collective-permute-start | bytes 196616 | tf_op jit(solution)/shard_map/ppermute | solution.py:29
  50.5 9.1 %collective-permute-start.12 = (bf16[256,128]{1,0:T(8,128)(2,1)S(1)}, bf16[256,128]{1,0:T(8,128)(2,1)S(1)}, u32[]{:S(2)}, u32[]{:S(2)}) collective-permute-start(bf16[256,128]{1,0:T(8,128)(2,1)S(1)} %get-tuple-element.31), channel_id=1, source_target_pairs={{0,24},{4,28},{8,16},{12,20},{16,8},{20,12},{24,0},{28,4},{1,25},{... | collective-permute-start | bytes 196616 | tf_op jit(solution)/shard_map/ppermute | solution.py:29
  52.6 8.6 %collective-permute-start.17 = (bf16[256,128]{1,0:T(8,128)(2,1)S(1)}, bf16[256,128]{1,0:T(8,128)(2,1)S(1)}, u32[]{:S(2)}, u32[]{:S(2)}) collective-permute-start(bf16[256,128]{1,0:T(8,128)(2,1)S(1)} %get-tuple-element.28.refs_0_), channel_id=1, source_target_pairs={{0,2},{1,3},{2,0},{3,1},{4,6},{5,7},{6,4},{7,5},{8,10},{9,11},{10,... | collective-permute-start | bytes 196616 | tf_op jit(solution)/shard_map/ppermute | solution.py:29
  58.2 4.6 %collective-permute-start.13 = (bf16[256,128]{1,0:T(8,128)(2,1)S(1)}, bf16[256,128]{1,0:T(8,128)(2,1)S(1)}, u32[]{:S(2)}, u32[]{:S(2)}) collective-permute-start(bf16[256,128]{1,0:T(8,128)(2,1)S(1)} %get-tuple-element.28.refs_0_), channel_id=1, source_target_pairs={{0,1},{1,0},{2,3},{3,2},{4,5},{5,4},{6,7},{7,6},{8,9},{9,8},{10,11... | collective-permute-start | bytes 196616 | tf_op jit(solution)/shard_map/ppermute | solution.py:29
  59.7 4.6 %collective-permute-start.18 = (bf16[256,128]{1,0:T(8,128)(2,1)S(1)}, bf16[256,128]{1,0:T(8,128)(2,1)S(1)}, u32[]{:S(2)}, u32[]{:S(2)}) collective-permute-start(bf16[256,128]{1,0:T(8,128)(2,1)S(1)} %collective-permute-done.10.refs_1_), channel_id=1, source_target_pairs={{0,2},{1,3},{2,0},{3,1},{4,6},{5,7},{6,4},{7,5},{8,10},{9,11},{10,... | collective-permute-start | bytes 196616 | tf_op jit(solution)/shard_map/ppermute | solution.py:29
  65.5 4.7 %collective-permute-start.20 = (bf16[256,128]{1,0:T(8,128)(2,1)S(1)}, bf16[256,128]{1,0:T(8,128)(2,1)S(1)}, u32[]{:S(2)}, u32[]{:S(2)}) collective-permute-start(bf16[256,128]{1,0:T(8,128)(2,1)S(1)} %collective-permute-done.12.refs_3_), channel_id=1, source_target_pairs={{0,2},{1,3},{2,0},{3,1},{4,6},{5,7},{6,4},{7,5},{8,10},{9,11},{10,... | collective-permute-start | bytes 196616 | tf_op jit(solution)/shard_map/ppermute | solution.py:29
  67.0 4.5 %collective-permute-start.16 = (bf16[256,128]{1,0:T(8,128)(2,1)S(1)}, bf16[256,128]{1,0:T(8,128)(2,1)S(1)}, u32[]{:S(2)}, u32[]{:S(2)}) collective-permute-start(bf16[256,128]{1,0:T(8,128)(2,1)S(1)} %collective-permute-done.12.refs_3_), channel_id=1, source_target_pairs={{0,1},{1,0},{2,3},{3,2},{4,5},{5,4},{6,7},{7,6},{8,9},{9,8},{10,11... | collective-permute-start | bytes 196616 | tf_op jit(solution)/shard_map/ppermute | solution.py:29
  68.5 4.5 %collective-permute-start.21 = (bf16[256,128]{1,0:T(8,128)(2,1)S(1)}, bf16[256,128]{1,0:T(8,128)(2,1)S(1)}, u32[]{:S(2)}, u32[]{:S(2)}) collective-permute-start(bf16[256,128]{1,0:T(8,128)(2,1)S(1)} %collective-permute-done.13.refs_4_), channel_id=1, source_target_pairs={{0,2},{1,3},{2,0},{3,1},{4,6},{5,7},{6,4},{7,5},{8,10},{9,11},{10,... | collective-permute-start | bytes 196616 | tf_op jit(solution)/shard_map/ppermute | solution.py:29
  70.2 5.0 %collective-permute-start.22 = (bf16[256,128]{1,0:T(8,128)(2,1)S(1)}, bf16[256,128]{1,0:T(8,128)(2,1)S(1)}, u32[]{:S(2)}, u32[]{:S(2)}) collective-permute-start(bf16[256,128]{1,0:T(8,128)(2,1)S(1)} %collective-permute-done.14.refs_5_), channel_id=1, source_target_pairs={{0,2},{1,3},{2,0},{3,1},{4,6},{5,7},{6,4},{7,5},{8,10},{9,11},{10,... | collective-permute-start | bytes 196616 | tf_op jit(solution)/shard_map/ppermute | solution.py:29
  71.5 5.0 %collective-permute-start.23 = (bf16[256,128]{1,0:T(8,128)(2,1)S(1)}, bf16[256,128]{1,0:T(8,128)(2,1)S(1)}, u32[]{:S(2)}, u32[]{:S(2)}) collective-permute-start(bf16[256,128]{1,0:T(8,128)(2,1)S(1)} %collective-permute-done.19.refs_10_), channel_id=1, source_target_pairs={{0,1},{1,0},{2,3},{3,2},{4,5},{5,4},{6,7},{7,6},{8,9},{9,8},{10,11... | collective-permute-start | bytes 196616 | tf_op jit(solution)/shard_map/ppermute | solution.py:29
  73.0 5.0 %collective-permute-start.24 = (bf16[256,128]{1,0:T(8,128)(2,1)S(1)}, bf16[256,128]{1,0:T(8,128)(2,1)S(1)}, u32[]{:S(2)}, u32[]{:S(2)}) collective-permute-start(bf16[256,128]{1,0:T(8,128)(2,1)S(1)} %collective-permute-done.20.refs_11_), channel_id=1, source_target_pairs={{0,1},{1,0},{2,3},{3,2},{4,5},{5,4},{6,7},{7,6},{8,9},{9,8},{10,11... | collective-permute-start | bytes 196616 | tf_op jit(solution)/shard_map/ppermute | solution.py:29
  75.2 14.3 %collective-permute-start.26 = (bf16[128,2048]{1,0:T(8,128)(2,1)S(1)}, bf16[128,2048]{1,0:T(8,128)(2,1)S(1)}, u32[]{:S(2)}, u32[]{:S(2)}) collective-permute-start(bf16[128,2048]{1,0:T(8,128)(2,1)S(1)} %get-tuple-element.35), channel_id=1, source_target_pairs={{0,1},{1,0},{2,3},{3,2},{4,5},{5,4},{6,7},{7,6},{8,9},{9,8},{10,11... | collective-permute-start | bytes 1572872 | tf_op jit(solution)/shard_map/ppermute | solution.py:29
  76.6 13.0 %collective-permute-start.27 = (bf16[128,2048]{1,0:T(8,128)(2,1)S(1)}, bf16[128,2048]{1,0:T(8,128)(2,1)S(1)}, u32[]{:S(2)}, u32[]{:S(2)}) collective-permute-start(bf16[128,2048]{1,0:T(8,128)(2,1)S(1)} %get-tuple-element.36), channel_id=1, source_target_pairs={{0,2},{1,3},{2,0},{3,1},{4,6},{5,7},{6,4},{7,5},{8,10},{9,11},{10,... | collective-permute-start | bytes 1572872 | tf_op jit(solution)/shard_map/ppermute | solution.py:29
  77.9 12.1 %collective-permute-start.34 = (bf16[128,2048]{1,0:T(8,128)(2,1)S(1)}, bf16[128,2048]{1,0:T(8,128)(2,1)S(1)}, u32[]{:S(2)}, u32[]{:S(2)}) collective-permute-start(bf16[128,2048]{1,0:T(8,128)(2,1)S(1)} %collective-permute-done.28.refs_20_), channel_id=1, source_target_pairs={{0,4},{4,0},{8,12},{12,8},{16,20},{20,16},{24,28},{28,24},{1,5},{5... | collective-permute-start | bytes 1572872 | tf_op jit(solution)/shard_map/ppermute | solution.py:29
  78.1 18.5 %collective-permute-start.30 = (bf16[128,2048]{1,0:T(8,128)(2,1)S(1)}, bf16[128,2048]{1,0:T(8,128)(2,1)S(1)}, u32[]{:S(2)}, u32[]{:S(2)}) collective-permute-start(bf16[128,2048]{1,0:T(8,128)(2,1)S(1)} %collective-permute-done.28.refs_20_), channel_id=1, source_target_pairs={{0,1},{1,0},{2,3},{3,2},{4,5},{5,4},{6,7},{7,6},{8,9},{9,8},{10,11... | collective-permute-start | bytes 1572872 | tf_op jit(solution)/shard_map/ppermute | solution.py:29
  79.8 17.2 %collective-permute-start.29 = (bf16[128,2048]{1,0:T(8,128)(2,1)S(1)}, bf16[128,2048]{1,0:T(8,128)(2,1)S(1)}, u32[]{:S(2)}, u32[]{:S(2)}) collective-permute-start(bf16[128,2048]{1,0:T(8,128)(2,1)S(1)} %collective-permute-done.25.refs_17_), channel_id=1, source_target_pairs={{0,2},{1,3},{2,0},{3,1},{4,6},{5,7},{6,4},{7,5},{8,10},{9,11},{10,... | collective-permute-start | bytes 1572872 | tf_op jit(solution)/shard_map/ppermute | solution.py:29
  89.6 7.6 %collective-permute-start.31 = (bf16[128,2048]{1,0:T(8,128)(2,1)S(1)}, bf16[128,2048]{1,0:T(8,128)(2,1)S(1)}, u32[]{:S(2)}, u32[]{:S(2)}) collective-permute-start(bf16[128,2048]{1,0:T(8,128)(2,1)S(1)} %collective-permute-done.25.refs_17_), channel_id=1, source_target_pairs={{0,4},{4,0},{8,12},{12,8},{16,20},{20,16},{24,28},{28,24},{1,5},{5... | collective-permute-start | bytes 1572872 | tf_op jit(solution)/shard_map/ppermute | solution.py:29
  89.6 7.6 %collective-permute-start.32 = (bf16[128,2048]{1,0:T(8,128)(2,1)S(1)}, bf16[128,2048]{1,0:T(8,128)(2,1)S(1)}, u32[]{:S(2)}, u32[]{:S(2)}) collective-permute-start(bf16[128,2048]{1,0:T(8,128)(2,1)S(1)} %collective-permute-done.26.refs_18_), channel_id=1, source_target_pairs={{0,4},{4,0},{8,12},{12,8},{16,20},{20,16},{24,28},{28,24},{1,5},{5... | collective-permute-start | bytes 1572872 | tf_op jit(solution)/shard_map/ppermute | solution.py:29
  90.1 7.1 %collective-permute-start.33 = (bf16[128,2048]{1,0:T(8,128)(2,1)S(1)}, bf16[128,2048]{1,0:T(8,128)(2,1)S(1)}, u32[]{:S(2)}, u32[]{:S(2)}) collective-permute-start(bf16[128,2048]{1,0:T(8,128)(2,1)S(1)} %collective-permute-done.27.refs_19_), channel_id=1, source_target_pairs={{0,4},{4,0},{8,12},{12,8},{16,20},{20,16},{24,28},{28,24},{1,5},{5... | collective-permute-start | bytes 1572872 | tf_op jit(solution)/shard_map/ppermute | solution.py:29
  105.3 5.9 %collective-permute-start.37 = (bf16[128,256]{1,0:T(8,128)(2,1)S(1)}, bf16[128,256]{1,0:T(8,128)(2,1)S(1)}, u32[]{:S(2)}, u32[]{:S(2)}) collective-permute-start(bf16[128,256]{1,0:T(8,128)(2,1)S(1)} %get-tuple-element.33), channel_id=1, source_target_pairs={{0,4},{4,8},{8,12},{12,16},{16,20},{20,24},{24,28},{28,0},{1,5},{5... | collective-permute-start | bytes 196616 | tf_op jit(solution)/shard_map/ppermute | solution.py:24
  105.5 5.7 %collective-permute-start.38 = (bf16[128,256]{1,0:T(8,128)(2,1)S(1)}, bf16[128,256]{1,0:T(8,128)(2,1)S(1)}, u32[]{:S(2)}, u32[]{:S(2)}) collective-permute-start(bf16[128,256]{1,0:T(8,128)(2,1)S(1)} %get-tuple-element.34), channel_id=1, source_target_pairs={{0,28},{4,0},{8,4},{12,8},{16,12},{20,16},{24,20},{28,24},{1,29},{... | collective-permute-start | bytes 196616 | tf_op jit(solution)/shard_map/ppermute | solution.py:24
  (17 other events, 132.1 us)

commit v2 on v0

v2 whole, which is shorter than its diff:
```python
import functools
import math

import jax
import jax.numpy as jnp
from jax import lax
from jax.experimental import pallas as pl
from jax.experimental.pallas import tpu as pltpu
from jax.sharding import PartitionSpec as P

HD = 64
PATCH = 8
OV = 2
LANES = 128

eps = 1e-05
bf16 = jnp.bfloat16
f32 = jnp.float32


def passed_along(value, axis, steps):
    count = lax.axis_size(axis)
    pairs = [(source, (source + steps) % count) for source in range(count)]
    return lax.ppermute(value, axis, pairs)


def swapped(value, axis, bits):
    count = lax.axis_size(axis)
    return lax.ppermute(value, axis, [(i, i ^ bits) for i in range(count)])


def rms_scale(values):
    return values * lax.rsqrt(jnp.mean(values * values, axis=-1, keepdims=True) + eps)


def project_kernel(pos, x_hbm, w_hbm, out_hbm, *refs):
    packs, half_hbm = refs[:4], refs[4]
    x_ref, w_ref, x_sem, w_sem, half_sem = refs[5:]
    z, core = pos[0], pos[1]
    rows = x_ref.shape[0]
    pairs = [(z // 2) ^ 1, z // 2]
    copies = []
    for i, pair in enumerate(pairs):
        for k in range(3):
            cols = pl.ds(pl.multiple_of(pair * 2 * LANES, 2 * LANES), 2 * LANES)
            n = 3 * i + k
            copies.append(pltpu.make_async_copy(w_hbm.at[k, :, cols], w_ref.at[n], w_sem.at[n]))
    x_copy = pltpu.make_async_copy(x_hbm, x_ref, x_sem)
    x_copy.start()
    for copy in copies:
        copy.start()
    half = half_hbm.shape[0]
    half_copy = pltpu.make_async_copy(
        out_hbm.at[pl.ds(pl.multiple_of(core * half, half), half)], half_hbm, half_sem
    )
    half_copy.start()
    x_copy.wait()
    x = x_ref[...].astype(f32)
    scale = lax.rsqrt(jnp.mean(x * x, axis=-1, keepdims=True) + eps)
    q_scale = scale * (HD ** (-0.5) * math.log2(math.e))
    odd = z % 2
    for i in range(2):
        even_pack, odd_pack = packs[2 * (1 - i)], packs[2 * (1 - i) + 1]
        for k in range(3):
            copies[3 * i + k].wait()
            out = jnp.dot(x_ref[...], w_ref[3 * i + k], preferred_element_type=f32)
            out = (out * (q_scale if k == 0 else scale)).astype(bf16)
            left, right = out[:, :LANES], out[:, LANES:]
            part = pl.ds(k * rows, rows)
            even_pack[part] = jnp.where(odd == 0, left, right)
            odd_pack[part] = jnp.where(odd == 0, right, left)
    half_copy.wait()


def project(pos, tokens, w_qkv, w_out):
    rows, width = tokens.shape
    hbm = pl.BlockSpec(memory_space=pltpu.HBM)
    vmem = pl.BlockSpec(memory_space=pltpu.VMEM)
    pack = jax.ShapeDtypeStruct((3 * rows, LANES), bf16)
    return pl.pallas_call(
        project_kernel,
        in_specs=[pl.BlockSpec(memory_space=pltpu.SMEM), hbm, hbm, hbm],
        out_specs=[vmem] * 4 + [hbm],
        out_shape=[pack] * 4 + [jax.ShapeDtypeStruct((w_out.shape[0] // 2, width), bf16)],
        scratch_shapes=[
            pltpu.VMEM((rows, width), bf16),
            pltpu.VMEM((6, width, 2 * LANES), bf16),
            pltpu.SemaphoreType.DMA(()),
            pltpu.SemaphoreType.DMA((6,)),
            pltpu.SemaphoreType.DMA(()),
        ],
        compiler_params=pltpu.CompilerParams(vmem_limit_bytes=60 * 2**20),
        name="project",
    )(pos, tokens, w_qkv, w_out)


def attention_kernel(*refs):
    packs, outs = refs[:8], refs[8:10]
    k_all, v_lo, v_hi, q_all = refs[10:]
    rows = packs[0].shape[0] // 3
    low = lax.broadcasted_iota(jnp.int32, (1, LANES), 1) < HD
    one = jnp.ones((), bf16)
    zero = jnp.zeros((), bf16)
    for i, pack in enumerate(packs):
        part = pl.ds(i * rows, rows)
        k_all[part] = pack[rows : 2 * rows]
        v = pack[2 * rows :]
        v_lo[part] = jnp.where(low, v, one)
        v_hi[part] = jnp.where(low, one, v)
    for i in range(2):
        q_all[pl.ds(i * rows, rows)] = packs[i][:rows]

    def score(q):
        return lax.dot_general(
            q, k_all[...], (((1,), (1,)), ((), ())), preferred_element_type=f32
        )

    def weigh(scores):
        return jnp.exp2(scores - jnp.max(scores, axis=-1, keepdims=True)).astype(bf16)

    q = q_all[...]
    lo_scores = score(jnp.where(low, q, zero))
    hi_scores = score(jnp.where(low, zero, q))
    lo_weights, hi_weights = weigh(lo_scores), weigh(hi_scores)
    lo = jnp.dot(lo_weights, v_lo[...], preferred_element_type=f32)
    hi = jnp.dot(hi_weights, v_hi[...], preferred_element_type=f32)
    top = jnp.where(low, lo, hi)
    bottom = pltpu.roll(jnp.where(low, hi, lo), HD, 1)
    attended = (top / bottom).astype(bf16)
    for i in range(2):
        outs[i][...] = attended[i * rows : (i + 1) * rows]


def attend(packs):
    rows = packs[0].shape[0] // 3
    keys = rows * len(packs)
    vmem = pl.BlockSpec(memory_space=pltpu.VMEM)
    return pl.pallas_call(
        attention_kernel,
        in_specs=[vmem] * len(packs),
        out_specs=[vmem] * 2,
        out_shape=[jax.ShapeDtypeStruct((rows, LANES), bf16)] * 2,
        scratch_shapes=[pltpu.VMEM((keys, LANES), bf16)] * 3 + [pltpu.VMEM((2 * rows, LANES), bf16)],
        compiler_params=pltpu.CompilerParams(vmem_limit_bytes=24 * 2**20),
        name="attend",
    )(*packs)


def mix_kernel(pos, x_ref, o0, o1, o2, own, n1, f2, n2, f1, total, att):
    z, core = pos[0], pos[1]
    rows, width = x_ref.shape
    local = own.shape[0]
    for s in range(4):
        place = z ^ s
        part = pl.ds(s * rows, rows)
        att[:, pl.ds(pl.multiple_of(place * LANES, LANES), LANES)] = o0[part]
        place = place ^ (2 * core)
        for i, o in enumerate((o1, o2)):
            at = pl.multiple_of((i + 1) * local + place * LANES, LANES)
            att[:, pl.ds(at, LANES)] = o[part]
    step = 512
    for n in range(0, width, step):
        w = jnp.concatenate([part[:, n : n + step] for part in (own, n1, f2, n2, f1)], axis=0)
        mixed = jnp.dot(att[...], w, preferred_element_type=f32)
        total[:, n : n + step] = x_ref[:, n : n + step].astype(f32) + mixed


def mix(pos, tokens, outs, parts):
    rows, width = tokens.shape
    vmem = pl.BlockSpec(memory_space=pltpu.VMEM)
    return pl.pallas_call(
        mix_kernel,
        in_specs=[pl.BlockSpec(memory_space=pltpu.SMEM)] + [vmem] * 9,
        out_specs=vmem,
        out_shape=jax.ShapeDtypeStruct((rows, width), f32),
        scratch_shapes=[pltpu.VMEM((rows, 3 * parts[0].shape[0]), bf16)],
        compiler_params=pltpu.CompilerParams(vmem_limit_bytes=12 * 2**20),
        name="mix",
    )(pos, tokens, *outs, *parts)


def decode_kernel(pos, total, o3, n3, f3, dec_ref, main, up, down, att, hidden):
    z, core = pos[0], pos[1]
    rows, width = total.shape
    for s in range(4):
        place = z ^ s ^ (2 * core)
        att[:, pl.ds(pl.multiple_of(place * LANES, LANES), LANES)] = o3[pl.ds(s * rows, rows)]
    step = 512
    squares = jnp.zeros((rows, LANES), f32)
    for n in range(0, width, step):
        w = jnp.concatenate([part[:, n : n + step] for part in (n3, f3)], axis=0)
        mixed = total[:, n : n + step] + jnp.dot(att[...], w, preferred_element_type=f32)
        hidden[:, n : n + step] = mixed
        for i in range(0, step, LANES):
            squares += mixed[:, i : i + LANES] * mixed[:, i : i + LANES]
    scale = lax.rsqrt(jnp.sum(squares, axis=-1, keepdims=True) * (1.0 / width) + eps)
    ext = lax.dot_general(
        dec_ref[...],
        (hidden[...] * scale).astype(bf16),
        (((1,), (1,)), ((), ())),
        preferred_element_type=f32,
    )
    cells = main.shape[0] // PATCH
    main[...] = ext[OV * cells : (OV + PATCH) * cells]
    down[...] = ext[: OV * cells].astype(bf16)
    up[...] = ext[(OV + PATCH) * cells :].astype(bf16)


def decode(pos, total, o3, n3, f3, w_dec):
    rows, width = total.shape
    wide = w_dec.shape[0]
    cells = wide // (PATCH + 2 * OV)
    vmem = pl.BlockSpec(memory_space=pltpu.VMEM)
    edge = jax.ShapeDtypeStruct((OV * cells, rows), bf16)
    return pl.pallas_call(
        decode_kernel,
        in_specs=[pl.BlockSpec(memory_space=pltpu.SMEM)] + [vmem] * 5,
        out_specs=[vmem] * 3,
        out_shape=[jax.ShapeDtypeStruct((PATCH * cells, rows), f32), edge, edge],
        scratch_shapes=[
            pltpu.VMEM((rows, n3.shape[0] + f3.shape[0]), bf16),
            pltpu.VMEM((rows, width), f32),
        ],
        compiler_params=pltpu.CompilerParams(vmem_limit_bytes=12 * 2**20),
        name="decode",
    )(pos, total, o3, n3, f3, w_dec)


def gathered_kernel(*refs):
    rows = refs[0].shape[0]
    for i, part in enumerate(refs[:-1]):
        refs[-1][pl.ds(i * rows, rows)] = part[...]


def gathered(parts):
    rows, width = parts[0].shape
    vmem = pl.BlockSpec(memory_space=pltpu.VMEM)
    return pl.pallas_call(
        gathered_kernel,
        in_specs=[vmem] * len(parts),
        out_specs=vmem,
        out_shape=jax.ShapeDtypeStruct((len(parts) * rows, width), bf16),
        compiler_params=pltpu.CompilerParams(vmem_limit_bytes=4 * 2**20),
        name="gathered",
    )(*parts)


def first_way(value):
    count = lax.axis_size("ctx") * lax.axis_size("head")
    pairs = [(i, i ^ (1 if (i // 4) % 2 == 0 else 2)) for i in range(count)]
    return lax.ppermute(value, ("ctx", "head"), pairs)


def second_way(value):
    count = lax.axis_size("ctx") * lax.axis_size("head")
    pairs = [(i, i ^ (2 if (i // 4) % 2 == 0 else 1)) for i in range(count)]
    return lax.ppermute(value, ("ctx", "head"), pairs)


def fast_body(tokens, w_qkv, w_out, w_dec):
    rows = tokens.shape[0]
    ctx = lax.axis_index("ctx")
    pos = jnp.stack([ctx // 2, ctx % 2])

    p0, p1, p2, p3, half = project(pos, tokens, w_qkv, w_out)
    r2, r3, r1 = swapped(p2, "ctx", 4), swapped(p3, "ctx", 6), swapped(p1, "ctx", 2)


    n1, n2 = first_way(half), second_way(half)
    c0, c1, c2, c3 = (swapped(part, "ctx", 1) for part in (p0, r1, r2, r3))
    n1, n2, c0, c1, c2, c3 = lax.optimization_barrier((n1, n2, c0, c1, c2, c3))
    n3 = second_way(n1)

    o2, o3 = attend([r2, r3, p0, r1, c0, c1, c2, c3])
    o0, o1 = attend([p0, r1, r2, r3, c0, c1, c2, c3])
    own = gathered([o0, swapped(o1, "ctx", 2), swapped(o2, "ctx", 4), swapped(o3, "ctx", 6)])
    own, n1, n2 = lax.optimization_barrier((own, n1, n2))
    a1, a2 = first_way(own), second_way(own)
    f1, f2 = (swapped(part, "ctx", 1) for part in (n1, n2))
    a1, n3 = lax.optimization_barrier((a1, n3))
    a3 = second_way(a1)
    f3 = swapped(n3, "ctx", 1)
    total = mix(pos, tokens, [own, a1, a2], [w_out, n1, f2, n2, f1])

    dec = w_dec.transpose(1, 2, 0)
    dec = dec.reshape(-1, dec.shape[2])
    main, up, down = decode(pos, total, a3, n3, f3, dec)
    from_before = passed_along(up, "ctx", 1).astype(f32)
    from_after = passed_along(down, "ctx", -1).astype(f32)
    edge = up.shape[0]
    field = jnp.concatenate(
        [main[:edge] + from_before, main[edge:-edge], main[-edge:] + from_after], axis=0
    )
    return field.reshape(PATCH, -1, rows).transpose(2, 0, 1)


def general_body(tokens, w_qkv, w_out, w_dec):
    rows = tokens.shape[0]
    local_heads = w_qkv.shape[2] // HD
    xf = tokens.astype(f32)
    normed = rms_scale(xf).astype(bf16)
    projected = jnp.einsum("td,kdc->ktc", normed, w_qkv, preferred_element_type=f32).astype(bf16)
    queries = projected[0].reshape(rows, local_heads, HD)
    keyvals = projected[1:]
    scale = HD ** (-0.5)

    def block_update(carry, block):
        best, total, accum = carry
        keys = block[0].reshape(-1, local_heads, HD)
        values = block[1].reshape(-1, local_heads, HD)
        scores = jnp.einsum("thd,rhd->thr", queries, keys, preferred_element_type=f32) * scale
        fresh = jnp.maximum(best, jnp.max(scores, axis=-1))
        shrink = jnp.exp(best - fresh)
        weights = jnp.exp(scores - fresh[..., None])
        total = total * shrink + jnp.sum(weights, axis=-1)
        accum = accum * shrink[..., None] + jnp.einsum(
            "thr,rhd->thd", weights.astype(bf16), values, preferred_element_type=f32
        )
        return (fresh, total, accum)

    initial = (
        jnp.full((rows, local_heads), -1e30, f32),
        jnp.zeros((rows, local_heads), f32),
        jnp.zeros((rows, local_heads, HD), f32),
    )
    piece = lax.all_gather(keyvals, "ctx", axis=1, tiled=True)
    length = piece.shape[1]
    span = math.gcd(length, 1024)

    def one_block(index, inner):
        block = lax.dynamic_slice_in_dim(piece, index * span, span, 1)
        return block_update(inner, block)

    best, total, accum = lax.fori_loop(0, length // span, one_block, initial)
    attended = (accum / total[..., None]).astype(bf16).reshape(rows, local_heads * HD)
    partial_out = jnp.dot(attended, w_out, preferred_element_type=f32)
    mixed = lax.psum(partial_out.astype(bf16), "head").astype(f32)
    hidden = rms_scale(xf + mixed).astype(bf16)
    extended = jnp.dot(hidden, w_dec.reshape(w_dec.shape[0], -1), preferred_element_type=f32)
    extended = extended.reshape(rows, w_dec.shape[1], w_dec.shape[2])
    from_before = passed_along(extended[:, PATCH + OV :].astype(bf16), "ctx", 1).astype(f32)
    from_after = passed_along(extended[:, :OV].astype(bf16), "ctx", -1).astype(f32)
    middle = extended[:, OV : OV + PATCH]
    return jnp.concatenate(
        [
            middle[:, :OV] + from_before,
            middle[:, OV : PATCH - OV],
            middle[:, PATCH - OV :] + from_after,
        ],
        axis=1,
    )


def body(tokens, w_qkv, w_out, w_dec):
    fits = lax.axis_size("ctx") == 8 and lax.axis_size("head") == 4
    fits = fits and w_qkv.shape[2] == 4 * LANES and tokens.shape[0] % 256 == 0
    run = fast_body if fits else general_body
    return run(tokens, w_qkv, w_out, w_dec)


def solution(mesh):
    return jax.shard_map(
        body,
        mesh=mesh,
        in_specs=(P("ctx", None), P(None, None, "head"), P("head", None), P(None, None, "head")),
        out_specs=P("ctx", None, "head"),
        check_vma=False,
    )
```

time: 167 us -> 104 us (0.62)
  waiting for transfers between devices: 101 us -> 33.1 us
  Pallas kernels: 0 us -> 44.9 us
  local copies, waits for them, and re-layouts: 21.1 us -> 0.97 us
  starting transfers between devices: 3.63 us -> 23.1 us
  matrix products: 19.2 us -> 0 us
  between operations: 13.5 us -> 0.12 us
  other arithmetic: 8.36 us -> 1.41 us
    psum x1 -> x0, waiting for transfers between devices: 51.4 us -> none  [body(): lax.psum(partial_out.astype(jnp.bfloat16), 'head').astype(jnp.float32)]
    all_gather x1 -> x0, waiting for transfers between devices: 47.2 us -> none  [body(): piece = lax.all_gather(keyvals, 'ctx', axis=1, tiled=True)]
    pallas_call x0 -> x6, Pallas kernels: none -> 44.9 us  [the longest x1 34.5 us: project(): pl.pallas_call(project_kernel, in_specs=[pl.BlockSpec(memory_space=pltpu....]
    ppermute x0 -> x19, waiting for transfers between devices: none -> 31.2 us  [the longest x13 20 us: swapped(): return lax.ppermute(value, axis, [(i, i ^ bits) for i in range(count)])]
    ppermute x0 -> x19, starting transfers between devices: none -> 19.5 us  [the longest x13 9.78 us: swapped(): return lax.ppermute(value, axis, [(i, i ^ bits) for i in range(count)])]
    dot_general x7 -> x0, matrix products: 19.2 us -> none  [the longest x2 5.08 us: block_update(): jnp.einsum('thd,rhd->thr', queries, keys, preferred_element_type=jnp.floa...]
    while x18 -> x0, local copies, waits for them, and re-layouts: 10.6 us -> none
    slice x7 -> x1, local copies, waits for them, and re-layouts: 9.62 us -> 0.02 us  [fast_body(): main[edge:-edge]]
  transfers between devices with their start and end apart: 4 -> 21, of which waited for: 3 -> 13; matrix products, arithmetic and copies ran while one was open for 2% -> 0% of each run, Pallas kernels for 0% -> 8%
where the time goes in v2:
time: 104 us
  Pallas kernels  44.9 us (43%)
  waiting for transfers between devices  33.1 us (32%)
  starting transfers between devices  23.1 us (22%)
  other arithmetic  1.41 us (1%)
    pallas_call x1, Pallas kernels, project(): pl.pallas_call(project_kernel, in_specs=[pl.BlockSpec(memory_space=pltpu....  34.5 us
    ppermute x13, waiting for transfers between devices, swapped(): return lax.ppermute(value, axis, [(i, i ^ bits) for i in range(count)])  20 us
    ppermute x13, starting transfers between devices, swapped(): return lax.ppermute(value, axis, [(i, i ^ bits) for i in range(count)])  9.78 us
    ppermute x4, starting transfers between devices, second_way(): return lax.ppermute(value, ('ctx', 'head'), pairs)  7.44 us
    ppermute x4, waiting for transfers between devices, second_way(): return lax.ppermute(value, ('ctx', 'head'), pairs)  5.97 us
    pallas_call x2, Pallas kernels, attend(): pl.pallas_call(attention_kernel, in_specs=[vmem] * len(packs), out_specs=...  5.38 us
    ppermute x2, waiting for transfers between devices, first_way(): return lax.ppermute(value, ('ctx', 'head'), pairs)  5.18 us
    ppermute x2, starting transfers between devices, passed_along(): return lax.ppermute(value, axis, pairs)  3.59 us
  transfers between devices with their start and end apart: 21, of which 13 were waited for; matrix products, arithmetic and copies ran while one was open for 0% of the time, Pallas kernels for 8%

profile of v2, /device:TPU:0, one launch (start us, length us, event | category | flops | bytes accessed | tf_op | source)
XLA Modules:
  0.0 103.6 jit_solution(16333266584342277864)
XLA Ops:
  0.0 0.6 pad_add_fusion.pos
  0.6 34.5 %project.1 = (bf16[768,128]{1,0:T(8,128)(2,1)}, bf16[768,128]{1,0:T(8,128)(2,1)}, bf16[768,128]{1,0:T(8,128)(2,1)}, bf16[768,128]{1,0:T(8,128)(2,1)}, bf16[256,2048]{1,0:T(8,128)(2,1)}) custom-call(s32[2]{0:T(128)} %pad_add_fusion.pos, bf16[256,2048]{1,0:T(8,128)(2,1)} %x_ref.1, bf16[3,2048,512]{2,1,0:T(8,128)(2,1)} %w_hbm.1, bf16[512,2048]{1,0:T(8,128)(2,1)} %own.1), custom_call_target="tpu_custom_call" | custom-call | tf_op jit(solution)/shard_map/project/pallas_call | solution.py:80
  35.1 3.0 %collective-permute-start.4 = (bf16[256,2048]{1,0:T(8,128)(2,1)}, bf16[256,2048]{1,0:T(8,128)(2,1)S(1)}, u32[]{:S(2)}, u32[]{:S(2)}) collective-permute-start(bf16[256,2048]{1,0:T(8,128)(2,1)} %get-tuple-element.32), channel_id=1, source_target_pairs={{0,2},{1,3},{2,0},{3,1},{4,5},{5,4},{6,7},{7,6},{8,10},{9,11},{10,... | collective-permute-start | bytes 3145736 | tf_op jit(solution)/shard_map/ppermute | solution.py:257
  38.2 1.5 %collective-permute-start.3 = (bf16[256,2048]{1,0:T(8,128)(2,1)}, bf16[256,2048]{1,0:T(8,128)(2,1)S(1)}, u32[]{:S(2)}, u32[]{:S(2)}) collective-permute-start(bf16[256,2048]{1,0:T(8,128)(2,1)} %get-tuple-element.32), channel_id=1, source_target_pairs={{0,1},{1,0},{2,3},{3,2},{4,6},{5,7},{6,4},{7,5},{8,9},{9,8},{10,11... | collective-permute-start | bytes 3145736 | tf_op jit(solution)/shard_map/ppermute | solution.py:251
  39.7 1.6 %collective-permute-start = (bf16[768,128]{1,0:T(8,128)(2,1)}, bf16[768,128]{1,0:T(8,128)(2,1)S(1)}, u32[]{:S(2)}, u32[]{:S(2)}) collective-permute-start(bf16[768,128]{1,0:T(8,128)(2,1)} %get-tuple-element.29), channel_id=1, source_target_pairs={{0,8},{4,12},{8,0},{12,4},{16,24},{20,28},{24,16},{28,20},{1,9},{5... | collective-permute-start | bytes 589832 | tf_op jit(solution)/shard_map/ppermute | solution.py:29
  41.2 2.6 %collective-permute-start.1 = (bf16[768,128]{1,0:T(8,128)(2,1)}, bf16[768,128]{1,0:T(8,128)(2,1)S(1)}, u32[]{:S(2)}, u32[]{:S(2)}) collective-permute-start(bf16[768,128]{1,0:T(8,128)(2,1)} %get-tuple-element.30), channel_id=1, source_target_pairs={{0,16},{4,20},{8,24},{12,28},{16,0},{20,4},{24,8},{28,12},{1,17},{... | collective-permute-start | bytes 589832 | tf_op jit(solution)/shard_map/ppermute | solution.py:29
  44.1 4.8 %collective-permute-done.refs_1_.refs_3_ = bf16[768,128]{1,0:T(8,128)(2,1)S(1)} collective-permute-done((bf16[768,128]{1,0:T(8,128)(2,1)}, bf16[768,128]{1,0:T(8,128)(2,1)S(1)}, u32[]{:S(2)}, u32[]{:S(2)}) %collective-permute-start) | collective-permute-done | bytes 196640 | tf_op jit(solution)/shard_map/ppermute | solution.py:29
  48.8 9.8 %collective-permute-done.1.refs_2_.refs_0_ = bf16[768,128]{1,0:T(8,128)(2,1)S(1)} collective-permute-done((bf16[768,128]{1,0:T(8,128)(2,1)}, bf16[768,128]{1,0:T(8,128)(2,1)S(1)}, u32[]{:S(2)}, u32[]{:S(2)}) %collective-permute-start.1) | collective-permute-done | bytes 196640 | tf_op jit(solution)/shard_map/ppermute | solution.py:29
  58.6 0.5 collective-permute-start.7
  59.2 0.9 collective-permute-done.6.refs_5_
  60.6 1.3 %collective-permute-done.4.n2 = bf16[256,2048]{1,0:T(8,128)(2,1)S(1)} collective-permute-done((bf16[256,2048]{1,0:T(8,128)(2,1)}, bf16[256,2048]{1,0:T(8,128)(2,1)S(1)}, u32[]{:S(2)}, u32[]{:S(2)}) %collective-permute-start.4) | collective-permute-done | bytes 1048608 | tf_op jit(solution)/shard_map/ppermute | solution.py:257
  62.0 2.4 %collective-permute-start.13 = (bf16[256,2048]{1,0:T(8,128)(2,1)S(1)}, bf16[256,2048]{1,0:T(8,128)(2,1)S(1)}, u32[]{:S(2)}, u32[]{:S(2)}) collective-permute-start(bf16[256,2048]{1,0:T(8,128)(2,1)S(1)} %collective-permute-done.3.n1), channel_id=1, source_target_pairs={{0,2},{1,3},{2,0},{3,1},{4,5},{5,4},{6,7},{7,6},{8,10},{9,11},{10,... | collective-permute-start | bytes 3145736 | tf_op jit(solution)/shard_map/ppermute | solution.py:257
  64.3 0.9 copy-done.3
  65.3 2.7 %attend.3 = (bf16[256,128]{1,0:T(8,128)(2,1)S(1)}, bf16[256,128]{1,0:T(8,128)(2,1)S(1)}) custom-call(bf16[768,128]{1,0:T(8,128)(2,1)S(1)} %collective-permute-done.1.refs_2_.refs_0_, bf16[768,128]{1,0:T(8,128)(2,1)S(1)} %collective-permute-done.2.refs_3_.refs_1_, bf16[768,128]{1,0:T(8,128)(2,1)S(1)} %copy-done.3, ...), custom_call_target="tpu_custom_call" | custom-call | tf_op jit(solution)/shard_map/attend/pallas_call | solution.py:138
  68.0 2.6 %collective-permute-start.10 = (bf16[256,128]{1,0:T(8,128)(2,1)S(1)}, bf16[256,128]{1,0:T(8,128)(2,1)S(1)}, u32[]{:S(2)}, u32[]{:S(2)}) collective-permute-start(bf16[256,128]{1,0:T(8,128)(2,1)S(1)} %get-tuple-element.39), channel_id=1, source_target_pairs={{0,16},{4,20},{8,24},{12,28},{16,0},{20,4},{24,8},{28,12},{1,17},{... | collective-permute-start | bytes 196616 | tf_op jit(solution)/shard_map/ppermute | solution.py:29
  70.6 1.3 %collective-permute-start.11 = (bf16[256,128]{1,0:T(8,128)(2,1)S(1)}, bf16[256,128]{1,0:T(8,128)(2,1)S(1)}, u32[]{:S(2)}, u32[]{:S(2)}) collective-permute-start(bf16[256,128]{1,0:T(8,128)(2,1)S(1)} %get-tuple-element.40), channel_id=1, source_target_pairs={{0,24},{4,28},{8,16},{12,20},{16,8},{20,12},{24,0},{28,4},{1,25},{... | collective-permute-start | bytes 196616 | tf_op jit(solution)/shard_map/ppermute | solution.py:29
  72.0 2.7 %attend.2 = (bf16[256,128]{1,0:T(8,128)(2,1)S(1)}, bf16[256,128]{1,0:T(8,128)(2,1)S(1)}) custom-call(bf16[768,128]{1,0:T(8,128)(2,1)S(1)} %copy-done.3, bf16[768,128]{1,0:T(8,128)(2,1)S(1)} %collective-permute-done.refs_1_.refs_3_, bf16[768,128]{1,0:T(8,128)(2,1)S(1)} %collective-permute-done.1.refs_2_.refs_0_, ...), custom_call_target="tpu_custom_call" | custom-call | tf_op jit(solution)/shard_map/attend/pallas_call | solution.py:138
  74.7 0.3 collective-permute-start.9
  75.0 0.3 collective-permute-done.10.refs_2_
  75.3 1.7 %collective-permute-done.11.refs_3_ = bf16[256,128]{1,0:T(8,128)(2,1)S(1)} collective-permute-done((bf16[256,128]{1,0:T(8,128)(2,1)S(1)}, bf16[256,128]{1,0:T(8,128)(2,1)S(1)}, u32[]{:S(2)}, u32[]{:S(2)}) %collective-permute-start.11) | collective-permute-done | bytes 65568 | tf_op jit(solution)/shard_map/ppermute | solution.py:29
  76.9 2.0 %collective-permute-done.9.refs_1_ = bf16[256,128]{1,0:T(8,128)(2,1)S(1)} collective-permute-done((bf16[256,128]{1,0:T(8,128)(2,1)S(1)}, bf16[256,128]{1,0:T(8,128)(2,1)S(1)}, u32[]{:S(2)}, u32[]{:S(2)}) %collective-permute-start.9) | collective-permute-done | bytes 65568 | tf_op jit(solution)/shard_map/ppermute | solution.py:29
  79.0 0.8 collective-permute-start.12
  79.8 0.5 collective-permute-start.15
  80.3 5.2 %collective-permute-done.12.o1 = bf16[1024,128]{1,0:T(8,128)(2,1)S(1)} collective-permute-done((bf16[1024,128]{1,0:T(8,128)(2,1)S(1)}, bf16[1024,128]{1,0:T(8,128)(2,1)S(1)}, u32[]{:S(2)}, u32[]{:S(2)}) %collective-permute-start.12) | collective-permute-done | bytes 262176 | tf_op jit(solution)/shard_map/ppermute | solution.py:251
  85.5 0.5 collective-permute-start.14
  86.0 1.5 %collective-permute-start.17 = (bf16[1024,128]{1,0:T(8,128)(2,1)S(1)}, bf16[1024,128]{1,0:T(8,128)(2,1)S(1)}, u32[]{:S(2)}, u32[]{:S(2)}) collective-permute-start(bf16[1024,128]{1,0:T(8,128)(2,1)S(1)} %collective-permute-done.12.o1), channel_id=1, source_target_pairs={{0,2},{1,3},{2,0},{3,1},{4,5},{5,4},{6,7},{7,6},{8,10},{9,11},{10,... | collective-permute-start | bytes 786440 | tf_op jit(solution)/shard_map/ppermute | solution.py:257
  87.5 4.3 %collective-permute-done.14.o2 = bf16[1024,128]{1,0:T(8,128)(2,1)S(1)} collective-permute-done((bf16[1024,128]{1,0:T(8,128)(2,1)S(1)}, bf16[1024,128]{1,0:T(8,128)(2,1)S(1)}, u32[]{:S(2)}, u32[]{:S(2)}) %collective-permute-start.14) | collective-permute-done | bytes 262176 | tf_op jit(solution)/shard_map/ppermute | solution.py:257
  91.9 2.5 %mix.1.total = f32[256,2048]{1,0:T(8,128)S(1)} custom-call(s32[2]{0:T(128)S(1)} %copy-done.4, bf16[256,2048]{1,0:T(8,128)(2,1)S(1)} %copy-done.1, bf16[1024,128]{1,0:T(8,128)(2,1)S(1)} %gathered.1.o0, bf16[1024,128]{1,0:T(8,128)(2,1)S(1)} %collective-permute-done.12.o1, bf16[1024,128]{1,0:T(8,128)(2,1)S(1)} %collective-permute-done.14.o2, ...), custom_call_target="tpu_custom_call" | custom-call | tf_op jit(solution)/shard_map/mix/pallas_call | solution.py:171
  94.7 2.5 %decode.1 = (f32[512,256]{1,0:T(8,128)S(1)}, bf16[128,256]{1,0:T(8,128)(2,1)S(1)}, bf16[128,256]{1,0:T(8,128)(2,1)S(1)}) custom-call(s32[2]{0:T(128)S(1)} %copy-done.4, f32[256,2048]{1,0:T(8,128)S(1)} %mix.1.total, bf16[1024,128]{1,0:T(8,128)(2,1)S(1)} %collective-permute-done.17.o3, bf16[256,2048]{1,0:T(8,128)(2,1)S(1)} %collective-permute-done.13.n3, ...), custom_call_target="tpu_custom_call" | custom-call | tf_op jit(solution)/shard_map/decode/pallas_call | solution.py:215
  97.2 3.5 %collective-permute-start.20 = (bf16[128,256]{1,0:T(8,128)(2,1)S(1)}, bf16[128,256]{1,0:T(8,128)(2,1)S(1)}, u32[]{:S(2)}, u32[]{:S(2)}) collective-permute-start(bf16[128,256]{1,0:T(8,128)(2,1)S(1)} %get-tuple-element.50), channel_id=1, source_target_pairs={{0,28},{4,0},{8,4},{12,8},{16,12},{20,16},{24,20},{28,24},{1,29},{... | collective-permute-start | bytes 196616 | tf_op jit(solution)/shard_map/ppermute | solution.py:24
  100.7 2.0 %collective-permute-done.19 = bf16[128,256]{1,0:T(8,128)(2,1)S(1)} collective-permute-done((bf16[128,256]{1,0:T(8,128)(2,1)S(1)}, bf16[128,256]{1,0:T(8,128)(2,1)S(1)}, u32[]{:S(2)}, u32[]{:S(2)}) %collective-permute-start.19) | collective-permute-done | bytes 65568 | tf_op jit(solution)/shard_map/ppermute | solution.py:24
  102.7 0.8 pad_maximum_fusion
  (30 shorter events, 1.3 us)
Async XLA Ops:
  0.6 91.3 %copy-start.4 = (s32[2]{0:T(128)S(1)}, s32[2]{0:T(128)}, u32[]{:S(2)}) copy-start(s32[2]{0:T(128)} %pad_add_fusion.pos) | copy-start | bytes 28
  35.1 56.7 %copy-start = (bf16[512,2048]{1,0:T(8,128)(2,1)S(1)}, bf16[512,2048]{1,0:T(8,128)(2,1)}, u32[]{:S(2)}) copy-start(bf16[512,2048]{1,0:T(8,128)(2,1)} %own.1) | copy-start | bytes 6291460
  35.1 56.7 %copy-start.1 = (bf16[256,2048]{1,0:T(8,128)(2,1)S(1)}, bf16[256,2048]{1,0:T(8,128)(2,1)}, u32[]{:S(2)}) copy-start(bf16[256,2048]{1,0:T(8,128)(2,1)} %x_ref.1) | copy-start | bytes 3145732
  35.1 26.8 %collective-permute-start.4 = (bf16[256,2048]{1,0:T(8,128)(2,1)}, bf16[256,2048]{1,0:T(8,128)(2,1)S(1)}, u32[]{:S(2)}, u32[]{:S(2)}) collective-permute-start(bf16[256,2048]{1,0:T(8,128)(2,1)} %get-tuple-element.32), channel_id=1, source_target_pairs={{0,2},{1,3},{2,0},{3,1},{4,5},{5,4},{6,7},{7,6},{8,10},{9,11},{10,... | collective-permute-start | bytes 3145736 | tf_op jit(solution)/shard_map/ppermute | solution.py:257
  38.2 23.8 %collective-permute-start.3 = (bf16[256,2048]{1,0:T(8,128)(2,1)}, bf16[256,2048]{1,0:T(8,128)(2,1)S(1)}, u32[]{:S(2)}, u32[]{:S(2)}) collective-permute-start(bf16[256,2048]{1,0:T(8,128)(2,1)} %get-tuple-element.32), channel_id=1, source_target_pairs={{0,1},{1,0},{2,3},{3,2},{4,6},{5,7},{6,4},{7,5},{8,9},{9,8},{10,11... | collective-permute-start | bytes 3145736 | tf_op jit(solution)/shard_map/ppermute | solution.py:251
  39.7 9.2 %collective-permute-start = (bf16[768,128]{1,0:T(8,128)(2,1)}, bf16[768,128]{1,0:T(8,128)(2,1)S(1)}, u32[]{:S(2)}, u32[]{:S(2)}) collective-permute-start(bf16[768,128]{1,0:T(8,128)(2,1)} %get-tuple-element.29), channel_id=1, source_target_pairs={{0,8},{4,12},{8,0},{12,4},{16,24},{20,28},{24,16},{28,20},{1,9},{5... | collective-permute-start | bytes 589832 | tf_op jit(solution)/shard_map/ppermute | solution.py:29
  41.2 17.4 %collective-permute-start.1 = (bf16[768,128]{1,0:T(8,128)(2,1)}, bf16[768,128]{1,0:T(8,128)(2,1)S(1)}, u32[]{:S(2)}, u32[]{:S(2)}) collective-permute-start(bf16[768,128]{1,0:T(8,128)(2,1)} %get-tuple-element.30), channel_id=1, source_target_pairs={{0,16},{4,20},{8,24},{12,28},{16,0},{20,4},{24,8},{28,12},{1,17},{... | collective-permute-start | bytes 589832 | tf_op jit(solution)/shard_map/ppermute | solution.py:29
  43.8 14.8 %collective-permute-start.2 = (bf16[768,128]{1,0:T(8,128)(2,1)}, bf16[768,128]{1,0:T(8,128)(2,1)S(1)}, u32[]{:S(2)}, u32[]{:S(2)}) collective-permute-start(bf16[768,128]{1,0:T(8,128)(2,1)} %get-tuple-element.31), channel_id=1, source_target_pairs={{0,24},{4,28},{8,16},{12,20},{16,8},{20,12},{24,0},{28,4},{1,25},{... | collective-permute-start | bytes 589832 | tf_op jit(solution)/shard_map/ppermute | solution.py:29
  48.8 10.3 %collective-permute-start.5 = (bf16[768,128]{1,0:T(8,128)(2,1)}, bf16[768,128]{1,0:T(8,128)(2,1)S(1)}, u32[]{:S(2)}, u32[]{:S(2)}) collective-permute-start(bf16[768,128]{1,0:T(8,128)(2,1)} %get-tuple-element.28.refs_0_.refs_2_), channel_id=1, source_target_pairs={{0,4},{4,0},{8,12},{12,8},{16,20},{20,16},{24,28},{28,24},{1,5},{5... | collective-permute-start | bytes 589832 | tf_op jit(solution)/shard_map/ppermute | solution.py:29
  58.6 1.4 %collective-permute-start.6 = (bf16[768,128]{1,0:T(8,128)(2,1)S(1)}, bf16[768,128]{1,0:T(8,128)(2,1)S(1)}, u32[]{:S(2)}, u32[]{:S(2)}) collective-permute-start(bf16[768,128]{1,0:T(8,128)(2,1)S(1)} %collective-permute-done.refs_1_.refs_3_), channel_id=1, source_target_pairs={{0,4},{4,0},{8,12},{12,8},{16,20},{20,16},{24,28},{28,24},{1,5},{5... | collective-permute-start | bytes 589832 | tf_op jit(solution)/shard_map/ppermute | solution.py:29
  58.6 1.7 %collective-permute-start.7 = (bf16[768,128]{1,0:T(8,128)(2,1)S(1)}, bf16[768,128]{1,0:T(8,128)(2,1)S(1)}, u32[]{:S(2)}, u32[]{:S(2)}) collective-permute-start(bf16[768,128]{1,0:T(8,128)(2,1)S(1)} %collective-permute-done.1.refs_2_.refs_0_), channel_id=1, source_target_pairs={{0,4},{4,0},{8,12},{12,8},{16,20},{20,16},{24,28},{28,24},{1,5},{5... | collective-permute-start | bytes 589832 | tf_op jit(solution)/shard_map/ppermute | solution.py:29
  59.1 1.5 %collective-permute-start.8 = (bf16[768,128]{1,0:T(8,128)(2,1)S(1)}, bf16[768,128]{1,0:T(8,128)(2,1)S(1)}, u32[]{:S(2)}, u32[]{:S(2)}) collective-permute-start(bf16[768,128]{1,0:T(8,128)(2,1)S(1)} %collective-permute-done.2.refs_3_.refs_1_), channel_id=1, source_target_pairs={{0,4},{4,0},{8,12},{12,8},{16,20},{20,16},{24,28},{28,24},{1,5},{5... | collective-permute-start | bytes 589832 | tf_op jit(solution)/shard_map/ppermute | solution.py:29
  62.0 23.5 %collective-permute-start.13 = (bf16[256,2048]{1,0:T(8,128)(2,1)S(1)}, bf16[256,2048]{1,0:T(8,128)(2,1)S(1)}, u32[]{:S(2)}, u32[]{:S(2)}) collective-permute-start(bf16[256,2048]{1,0:T(8,128)(2,1)S(1)} %collective-permute-done.3.n1), channel_id=1, source_target_pairs={{0,2},{1,3},{2,0},{3,1},{4,5},{5,4},{6,7},{7,6},{8,10},{9,11},{10,... | collective-permute-start | bytes 3145736 | tf_op jit(solution)/shard_map/ppermute | solution.py:257
  64.3 0.9 copy-start.3
  68.0 7.3 %collective-permute-start.10 = (bf16[256,128]{1,0:T(8,128)(2,1)S(1)}, bf16[256,128]{1,0:T(8,128)(2,1)S(1)}, u32[]{:S(2)}, u32[]{:S(2)}) collective-permute-start(bf16[256,128]{1,0:T(8,128)(2,1)S(1)} %get-tuple-element.39), channel_id=1, source_target_pairs={{0,16},{4,20},{8,24},{12,28},{16,0},{20,4},{24,8},{28,12},{1,17},{... | collective-permute-start | bytes 196616 | tf_op jit(solution)/shard_map/ppermute | solution.py:29
  70.6 6.3 %collective-permute-start.11 = (bf16[256,128]{1,0:T(8,128)(2,1)S(1)}, bf16[256,128]{1,0:T(8,128)(2,1)S(1)}, u32[]{:S(2)}, u32[]{:S(2)}) collective-permute-start(bf16[256,128]{1,0:T(8,128)(2,1)S(1)} %get-tuple-element.40), channel_id=1, source_target_pairs={{0,24},{4,28},{8,16},{12,20},{16,8},{20,12},{24,0},{28,4},{1,25},{... | collective-permute-start | bytes 196616 | tf_op jit(solution)/shard_map/ppermute | solution.py:29
  74.7 4.3 %collective-permute-start.9 = (bf16[256,128]{1,0:T(8,128)(2,1)S(1)}, bf16[256,128]{1,0:T(8,128)(2,1)S(1)}, u32[]{:S(2)}, u32[]{:S(2)}) collective-permute-start(bf16[256,128]{1,0:T(8,128)(2,1)S(1)} %get-tuple-element.38), channel_id=1, source_target_pairs={{0,8},{4,12},{8,0},{12,4},{16,24},{20,28},{24,16},{28,20},{1,9},{5... | collective-permute-start | bytes 196616 | tf_op jit(solution)/shard_map/ppermute | solution.py:29
  79.0 15.6 %copy-start.2 = (bf16[2048,12,64]{0,2,1:T(8,128)(2,1)S(1)}, bf16[2048,12,64]{0,2,1:T(8,128)(2,1)}, u32[]{:S(2)}) copy-start(bf16[2048,12,64]{0,2,1:T(8,128)(2,1)} %param.7) | copy-start | bytes 9437188
  79.0 6.4 %collective-permute-start.12 = (bf16[1024,128]{1,0:T(8,128)(2,1)S(1)}, bf16[1024,128]{1,0:T(8,128)(2,1)S(1)}, u32[]{:S(2)}, u32[]{:S(2)}) collective-permute-start(bf16[1024,128]{1,0:T(8,128)(2,1)S(1)} %gathered.1.o0), channel_id=1, source_target_pairs={{0,1},{1,0},{2,3},{3,2},{4,6},{5,7},{6,4},{7,5},{8,9},{9,8},{10,11... | collective-permute-start | bytes 786440 | tf_op jit(solution)/shard_map/ppermute | solution.py:251
  79.8 12.1 %collective-permute-start.16 = (bf16[256,2048]{1,0:T(8,128)(2,1)S(1)}, bf16[256,2048]{1,0:T(8,128)(2,1)S(1)}, u32[]{:S(2)}, u32[]{:S(2)}) collective-permute-start(bf16[256,2048]{1,0:T(8,128)(2,1)S(1)} %collective-permute-done.3.n1), channel_id=1, source_target_pairs={{0,4},{4,0},{8,12},{12,8},{16,20},{20,16},{24,28},{28,24},{1,5},{5... | collective-permute-start | bytes 3145736 | tf_op jit(solution)/shard_map/ppermute | solution.py:29
  79.8 12.1 %collective-permute-start.15 = (bf16[256,2048]{1,0:T(8,128)(2,1)S(1)}, bf16[256,2048]{1,0:T(8,128)(2,1)S(1)}, u32[]{:S(2)}, u32[]{:S(2)}) collective-permute-start(bf16[256,2048]{1,0:T(8,128)(2,1)S(1)} %collective-permute-done.4.n2), channel_id=1, source_target_pairs={{0,4},{4,0},{8,12},{12,8},{16,20},{20,16},{24,28},{28,24},{1,5},{5... | collective-permute-start | bytes 3145736 | tf_op jit(solution)/shard_map/ppermute | solution.py:29
  85.5 9.2 %collective-permute-start.18 = (bf16[256,2048]{1,0:T(8,128)(2,1)S(1)}, bf16[256,2048]{1,0:T(8,128)(2,1)S(1)}, u32[]{:S(2)}, u32[]{:S(2)}) collective-permute-start(bf16[256,2048]{1,0:T(8,128)(2,1)S(1)} %collective-permute-done.13.n3), channel_id=1, source_target_pairs={{0,4},{4,0},{8,12},{12,8},{16,20},{20,16},{24,28},{28,24},{1,5},{5... | collective-permute-start | bytes 3145736 | tf_op jit(solution)/shard_map/ppermute | solution.py:29
  85.5 6.4 %collective-permute-start.14 = (bf16[1024,128]{1,0:T(8,128)(2,1)S(1)}, bf16[1024,128]{1,0:T(8,128)(2,1)S(1)}, u32[]{:S(2)}, u32[]{:S(2)}) collective-permute-start(bf16[1024,128]{1,0:T(8,128)(2,1)S(1)} %gathered.1.o0), channel_id=1, source_target_pairs={{0,2},{1,3},{2,0},{3,1},{4,5},{5,4},{6,7},{7,6},{8,10},{9,11},{10,... | collective-permute-start | bytes 786440 | tf_op jit(solution)/shard_map/ppermute | solution.py:257
  86.0 8.7 %collective-permute-start.17 = (bf16[1024,128]{1,0:T(8,128)(2,1)S(1)}, bf16[1024,128]{1,0:T(8,128)(2,1)S(1)}, u32[]{:S(2)}, u32[]{:S(2)}) collective-permute-start(bf16[1024,128]{1,0:T(8,128)(2,1)S(1)} %collective-permute-done.12.o1), channel_id=1, source_target_pairs={{0,2},{1,3},{2,0},{3,1},{4,5},{5,4},{6,7},{7,6},{8,10},{9,11},{10,... | collective-permute-start | bytes 786440 | tf_op jit(solution)/shard_map/ppermute | solution.py:257
  97.1 5.6 %collective-permute-start.19 = (bf16[128,256]{1,0:T(8,128)(2,1)S(1)}, bf16[128,256]{1,0:T(8,128)(2,1)S(1)}, u32[]{:S(2)}, u32[]{:S(2)}) collective-permute-start(bf16[128,256]{1,0:T(8,128)(2,1)S(1)} %get-tuple-element.49), channel_id=1, source_target_pairs={{0,4},{4,8},{8,12},{12,16},{16,20},{20,24},{24,28},{28,0},{1,5},{5... | collective-permute-start | bytes 196616 | tf_op jit(solution)/shard_map/ppermute | solution.py:24
  97.2 5.5 %collective-permute-start.20 = (bf16[128,256]{1,0:T(8,128)(2,1)S(1)}, bf16[128,256]{1,0:T(8,128)(2,1)S(1)}, u32[]{:S(2)}, u32[]{:S(2)}) collective-permute-start(bf16[128,256]{1,0:T(8,128)(2,1)S(1)} %get-tuple-element.50), channel_id=1, source_target_pairs={{0,28},{4,0},{8,4},{12,8},{16,12},{20,16},{24,20},{28,24},{1,29},{... | collective-permute-start | bytes 196616 | tf_op jit(solution)/shard_map/ppermute | solution.py:24

commit v3 on v2

--- a/solution.py
+++ b/solution.py
@@ -34,7 +34,7 @@
 
 
 def project_kernel(pos, x_hbm, w_hbm, out_hbm, *refs):
-    packs, half_hbm = refs[:4], refs[4]
+    packs, half_ref = refs[:4], refs[4]
     x_ref, w_ref, x_sem, w_sem, half_sem = refs[5:]
     z, core = pos[0], pos[1]
     rows = x_ref.shape[0]
@@ -49,9 +49,9 @@
     x_copy.start()
     for copy in copies:
         copy.start()
-    half = half_hbm.shape[0]
+    half = half_ref.shape[0]
     half_copy = pltpu.make_async_copy(
-        out_hbm.at[pl.ds(pl.multiple_of(core * half, half), half)], half_hbm, half_sem
+        out_hbm.at[pl.ds(pl.multiple_of(core * half, half), half)], half_ref, half_sem
     )
     half_copy.start()
     x_copy.wait()
@@ -80,7 +80,7 @@
     return pl.pallas_call(
         project_kernel,
         in_specs=[pl.BlockSpec(memory_space=pltpu.SMEM), hbm, hbm, hbm],
-        out_specs=[vmem] * 4 + [hbm],
+        out_specs=[vmem] * 5,
         out_shape=[pack] * 4 + [jax.ShapeDtypeStruct((w_out.shape[0] // 2, width), bf16)],
         scratch_shapes=[
             pltpu.VMEM((rows, width), bf16),

time: 104 us -> 76.9 us (0.74)
  Pallas kernels: 44.9 us -> 18.1 us
    pallas_call x1, Pallas kernels: 34.5 us -> 7.76 us  [project(): pl.pallas_call(project_kernel, in_specs=[pl.BlockSpec(memory_space=pltpu....]
  transfers between devices with their start and end apart: 21 -> 21, of which waited for: 13 -> 13; matrix products, arithmetic and copies ran while one was open for 0% -> 0% of each run, Pallas kernels for 8% -> 10%
where the time goes in v3:
time: 76.9 us; the launch traced here: 76.8 us
  waiting for transfers between devices  33.2 us (43%)
  starting transfers between devices  23.1 us (30%)
  Pallas kernels  18.1 us (24%)
  other arithmetic  1.41 us (2%)
  local copies, waits for them, and re-layouts  0.97 us (1%)
    ppermute x13, waiting for transfers between devices, swapped(): return lax.ppermute(value, axis, [(i, i ^ bits) for i in range(count)])  20 us
    ppermute x13, starting transfers between devices, swapped(): return lax.ppermute(value, axis, [(i, i ^ bits) for i in range(count)])  9.78 us
    pallas_call x1, Pallas kernels, project(): pl.pallas_call(project_kernel, in_specs=[pl.BlockSpec(memory_space=pltpu....  7.76 us
    ppermute x4, starting transfers between devices, second_way(): return lax.ppermute(value, ('ctx', 'head'), pairs)  7.44 us
    ppermute x4, waiting for transfers between devices, second_way(): return lax.ppermute(value, ('ctx', 'head'), pairs)  5.98 us
    pallas_call x2, Pallas kernels, attend(): pl.pallas_call(attention_kernel, in_specs=[vmem] * len(packs), out_specs=...  5.37 us
    ppermute x2, waiting for transfers between devices, first_way(): return lax.ppermute(value, ('ctx', 'head'), pairs)  5.17 us
    ppermute x2, starting transfers between devices, passed_along(): return lax.ppermute(value, axis, pairs)  3.59 us
  transfers between devices with their start and end apart: 21, of which 13 were waited for; matrix products, arithmetic and copies ran while one was open for 0% of the time, Pallas kernels for 10%

profile of v3, /device:TPU:0, one launch (start us, length us, event | category | flops | bytes accessed | tf_op | source)
XLA Modules:
  0.0 76.8 jit_solution(10013125976124113288)
XLA Ops:
  0.0 0.6 pad_add_fusion.pos
  0.6 7.8 %project.1 = (bf16[768,128]{1,0:T(8,128)(2,1)}, bf16[768,128]{1,0:T(8,128)(2,1)}, bf16[768,128]{1,0:T(8,128)(2,1)}, bf16[768,128]{1,0:T(8,128)(2,1)}, bf16[256,2048]{1,0:T(8,128)(2,1)}) custom-call(s32[2]{0:T(128)} %pad_add_fusion.pos, bf16[256,2048]{1,0:T(8,128)(2,1)} %x_ref.1, bf16[3,2048,512]{2,1,0:T(8,128)(2,1)} %w_hbm.1, bf16[512,2048]{1,0:T(8,128)(2,1)} %own.1), custom_call_target="tpu_custom_call" | custom-call | tf_op jit(solution)/shard_map/project/pallas_call | solution.py:80
  8.3 3.0 %collective-permute-start.4 = (bf16[256,2048]{1,0:T(8,128)(2,1)}, bf16[256,2048]{1,0:T(8,128)(2,1)S(1)}, u32[]{:S(2)}, u32[]{:S(2)}) collective-permute-start(bf16[256,2048]{1,0:T(8,128)(2,1)} %get-tuple-element.32), channel_id=1, source_target_pairs={{0,2},{1,3},{2,0},{3,1},{4,5},{5,4},{6,7},{7,6},{8,10},{9,11},{10,... | collective-permute-start | bytes 3145736 | tf_op jit(solution)/shard_map/ppermute | solution.py:257
  11.4 1.5 %collective-permute-start.3 = (bf16[256,2048]{1,0:T(8,128)(2,1)}, bf16[256,2048]{1,0:T(8,128)(2,1)S(1)}, u32[]{:S(2)}, u32[]{:S(2)}) collective-permute-start(bf16[256,2048]{1,0:T(8,128)(2,1)} %get-tuple-element.32), channel_id=1, source_target_pairs={{0,1},{1,0},{2,3},{3,2},{4,6},{5,7},{6,4},{7,5},{8,9},{9,8},{10,11... | collective-permute-start | bytes 3145736 | tf_op jit(solution)/shard_map/ppermute | solution.py:251
  12.9 1.6 %collective-permute-start = (bf16[768,128]{1,0:T(8,128)(2,1)}, bf16[768,128]{1,0:T(8,128)(2,1)S(1)}, u32[]{:S(2)}, u32[]{:S(2)}) collective-permute-start(bf16[768,128]{1,0:T(8,128)(2,1)} %get-tuple-element.29), channel_id=1, source_target_pairs={{0,8},{4,12},{8,0},{12,4},{16,24},{20,28},{24,16},{28,20},{1,9},{5... | collective-permute-start | bytes 589832 | tf_op jit(solution)/shard_map/ppermute | solution.py:29
  14.4 2.6 %collective-permute-start.1 = (bf16[768,128]{1,0:T(8,128)(2,1)}, bf16[768,128]{1,0:T(8,128)(2,1)S(1)}, u32[]{:S(2)}, u32[]{:S(2)}) collective-permute-start(bf16[768,128]{1,0:T(8,128)(2,1)} %get-tuple-element.30), channel_id=1, source_target_pairs={{0,16},{4,20},{8,24},{12,28},{16,0},{20,4},{24,8},{28,12},{1,17},{... | collective-permute-start | bytes 589832 | tf_op jit(solution)/shard_map/ppermute | solution.py:29
  17.3 4.8 %collective-permute-done.refs_1_.refs_3_ = bf16[768,128]{1,0:T(8,128)(2,1)S(1)} collective-permute-done((bf16[768,128]{1,0:T(8,128)(2,1)}, bf16[768,128]{1,0:T(8,128)(2,1)S(1)}, u32[]{:S(2)}, u32[]{:S(2)}) %collective-permute-start) | collective-permute-done | bytes 196640 | tf_op jit(solution)/shard_map/ppermute | solution.py:29
  22.0 9.8 %collective-permute-done.1.refs_2_.refs_0_ = bf16[768,128]{1,0:T(8,128)(2,1)S(1)} collective-permute-done((bf16[768,128]{1,0:T(8,128)(2,1)}, bf16[768,128]{1,0:T(8,128)(2,1)S(1)}, u32[]{:S(2)}, u32[]{:S(2)}) %collective-permute-start.1) | collective-permute-done | bytes 196640 | tf_op jit(solution)/shard_map/ppermute | solution.py:29
  31.8 0.5 collective-permute-start.7
  32.4 0.9 %collective-permute-done.6.refs_5_ = bf16[768,128]{1,0:T(8,128)(2,1)S(1)} collective-permute-done((bf16[768,128]{1,0:T(8,128)(2,1)S(1)}, bf16[768,128]{1,0:T(8,128)(2,1)S(1)}, u32[]{:S(2)}, u32[]{:S(2)}) %collective-permute-start.6) | collective-permute-done | bytes 196640 | tf_op jit(solution)/shard_map/ppermute | solution.py:29
  33.8 1.3 %collective-permute-done.4.n2 = bf16[256,2048]{1,0:T(8,128)(2,1)S(1)} collective-permute-done((bf16[256,2048]{1,0:T(8,128)(2,1)}, bf16[256,2048]{1,0:T(8,128)(2,1)S(1)}, u32[]{:S(2)}, u32[]{:S(2)}) %collective-permute-start.4) | collective-permute-done | bytes 1048608 | tf_op jit(solution)/shard_map/ppermute | solution.py:257
  35.2 2.4 %collective-permute-start.13 = (bf16[256,2048]{1,0:T(8,128)(2,1)S(1)}, bf16[256,2048]{1,0:T(8,128)(2,1)S(1)}, u32[]{:S(2)}, u32[]{:S(2)}) collective-permute-start(bf16[256,2048]{1,0:T(8,128)(2,1)S(1)} %collective-permute-done.3.n1), channel_id=1, source_target_pairs={{0,2},{1,3},{2,0},{3,1},{4,5},{5,4},{6,7},{7,6},{8,10},{9,11},{10,... | collective-permute-start | bytes 3145736 | tf_op jit(solution)/shard_map/ppermute | solution.py:257
  37.6 0.9 %copy-done.3 = bf16[768,128]{1,0:T(8,128)(2,1)S(1)} copy-done((bf16[768,128]{1,0:T(8,128)(2,1)S(1)}, bf16[768,128]{1,0:T(8,128)(2,1)}, u32[]{:S(2)}) %copy-start.3) | copy-done | bytes 196632
  38.5 2.7 %attend.3 = (bf16[256,128]{1,0:T(8,128)(2,1)S(1)}, bf16[256,128]{1,0:T(8,128)(2,1)S(1)}) custom-call(bf16[768,128]{1,0:T(8,128)(2,1)S(1)} %collective-permute-done.1.refs_2_.refs_0_, bf16[768,128]{1,0:T(8,128)(2,1)S(1)} %collective-permute-done.2.refs_3_.refs_1_, bf16[768,128]{1,0:T(8,128)(2,1)S(1)} %copy-done.3, ...), custom_call_target="tpu_custom_call" | custom-call | tf_op jit(solution)/shard_map/attend/pallas_call | solution.py:138
  41.2 2.7 %collective-permute-start.10 = (bf16[256,128]{1,0:T(8,128)(2,1)S(1)}, bf16[256,128]{1,0:T(8,128)(2,1)S(1)}, u32[]{:S(2)}, u32[]{:S(2)}) collective-permute-start(bf16[256,128]{1,0:T(8,128)(2,1)S(1)} %get-tuple-element.39), channel_id=1, source_target_pairs={{0,16},{4,20},{8,24},{12,28},{16,0},{20,4},{24,8},{28,12},{1,17},{... | collective-permute-start | bytes 196616 | tf_op jit(solution)/shard_map/ppermute | solution.py:29
  43.8 1.3 %collective-permute-start.11 = (bf16[256,128]{1,0:T(8,128)(2,1)S(1)}, bf16[256,128]{1,0:T(8,128)(2,1)S(1)}, u32[]{:S(2)}, u32[]{:S(2)}) collective-permute-start(bf16[256,128]{1,0:T(8,128)(2,1)S(1)} %get-tuple-element.40), channel_id=1, source_target_pairs={{0,24},{4,28},{8,16},{12,20},{16,8},{20,12},{24,0},{28,4},{1,25},{... | collective-permute-start | bytes 196616 | tf_op jit(solution)/shard_map/ppermute | solution.py:29
  45.2 2.7 %attend.2 = (bf16[256,128]{1,0:T(8,128)(2,1)S(1)}, bf16[256,128]{1,0:T(8,128)(2,1)S(1)}) custom-call(bf16[768,128]{1,0:T(8,128)(2,1)S(1)} %copy-done.3, bf16[768,128]{1,0:T(8,128)(2,1)S(1)} %collective-permute-done.refs_1_.refs_3_, bf16[768,128]{1,0:T(8,128)(2,1)S(1)} %collective-permute-done.1.refs_2_.refs_0_, ...), custom_call_target="tpu_custom_call" | custom-call | tf_op jit(solution)/shard_map/attend/pallas_call | solution.py:138
  47.9 0.3 collective-permute-start.9
  48.2 0.3 collective-permute-done.10.refs_2_
  48.5 1.7 %collective-permute-done.11.refs_3_ = bf16[256,128]{1,0:T(8,128)(2,1)S(1)} collective-permute-done((bf16[256,128]{1,0:T(8,128)(2,1)S(1)}, bf16[256,128]{1,0:T(8,128)(2,1)S(1)}, u32[]{:S(2)}, u32[]{:S(2)}) %collective-permute-start.11) | collective-permute-done | bytes 65568 | tf_op jit(solution)/shard_map/ppermute | solution.py:29
  50.2 2.0 %collective-permute-done.9.refs_1_ = bf16[256,128]{1,0:T(8,128)(2,1)S(1)} collective-permute-done((bf16[256,128]{1,0:T(8,128)(2,1)S(1)}, bf16[256,128]{1,0:T(8,128)(2,1)S(1)}, u32[]{:S(2)}, u32[]{:S(2)}) %collective-permute-start.9) | collective-permute-done | bytes 65568 | tf_op jit(solution)/shard_map/ppermute | solution.py:29
  52.2 0.8 collective-permute-start.12
  53.0 0.5 collective-permute-start.15
  53.5 5.2 %collective-permute-done.12.o1 = bf16[1024,128]{1,0:T(8,128)(2,1)S(1)} collective-permute-done((bf16[1024,128]{1,0:T(8,128)(2,1)S(1)}, bf16[1024,128]{1,0:T(8,128)(2,1)S(1)}, u32[]{:S(2)}, u32[]{:S(2)}) %collective-permute-start.12) | collective-permute-done | bytes 262176 | tf_op jit(solution)/shard_map/ppermute | solution.py:251
  58.7 0.5 collective-permute-start.14
  59.2 1.5 %collective-permute-start.17 = (bf16[1024,128]{1,0:T(8,128)(2,1)S(1)}, bf16[1024,128]{1,0:T(8,128)(2,1)S(1)}, u32[]{:S(2)}, u32[]{:S(2)}) collective-permute-start(bf16[1024,128]{1,0:T(8,128)(2,1)S(1)} %collective-permute-done.12.o1), channel_id=1, source_target_pairs={{0,2},{1,3},{2,0},{3,1},{4,5},{5,4},{6,7},{7,6},{8,10},{9,11},{10,... | collective-permute-start | bytes 786440 | tf_op jit(solution)/shard_map/ppermute | solution.py:257
  60.7 4.3 %collective-permute-done.14.o2 = bf16[1024,128]{1,0:T(8,128)(2,1)S(1)} collective-permute-done((bf16[1024,128]{1,0:T(8,128)(2,1)S(1)}, bf16[1024,128]{1,0:T(8,128)(2,1)S(1)}, u32[]{:S(2)}, u32[]{:S(2)}) %collective-permute-start.14) | collective-permute-done | bytes 262176 | tf_op jit(solution)/shard_map/ppermute | solution.py:257
  65.1 2.5 %mix.1.total = f32[256,2048]{1,0:T(8,128)S(1)} custom-call(s32[2]{0:T(128)S(1)} %copy-done.4, bf16[256,2048]{1,0:T(8,128)(2,1)S(1)} %copy-done.1, bf16[1024,128]{1,0:T(8,128)(2,1)S(1)} %gathered.1.o0, bf16[1024,128]{1,0:T(8,128)(2,1)S(1)} %collective-permute-done.12.o1, bf16[1024,128]{1,0:T(8,128)(2,1)S(1)} %collective-permute-done.14.o2, ...), custom_call_target="tpu_custom_call" | custom-call | tf_op jit(solution)/shard_map/mix/pallas_call | solution.py:171
  67.9 2.5 %decode.1 = (f32[512,256]{1,0:T(8,128)S(1)}, bf16[128,256]{1,0:T(8,128)(2,1)S(1)}, bf16[128,256]{1,0:T(8,128)(2,1)S(1)}) custom-call(s32[2]{0:T(128)S(1)} %copy-done.4, f32[256,2048]{1,0:T(8,128)S(1)} %mix.1.total, bf16[1024,128]{1,0:T(8,128)(2,1)S(1)} %collective-permute-done.17.o3, bf16[256,2048]{1,0:T(8,128)(2,1)S(1)} %collective-permute-done.13.n3, ...), custom_call_target="tpu_custom_call" | custom-call | tf_op jit(solution)/shard_map/decode/pallas_call | solution.py:215
  70.4 3.5 %collective-permute-start.20 = (bf16[128,256]{1,0:T(8,128)(2,1)S(1)}, bf16[128,256]{1,0:T(8,128)(2,1)S(1)}, u32[]{:S(2)}, u32[]{:S(2)}) collective-permute-start(bf16[128,256]{1,0:T(8,128)(2,1)S(1)} %get-tuple-element.50), channel_id=1, source_target_pairs={{0,28},{4,0},{8,4},{12,8},{16,12},{20,16},{24,20},{28,24},{1,29},{... | collective-permute-start | bytes 196616 | tf_op jit(solution)/shard_map/ppermute | solution.py:24
  73.9 2.0 %collective-permute-done.19 = bf16[128,256]{1,0:T(8,128)(2,1)S(1)} collective-permute-done((bf16[128,256]{1,0:T(8,128)(2,1)S(1)}, bf16[128,256]{1,0:T(8,128)(2,1)S(1)}, u32[]{:S(2)}, u32[]{:S(2)}) %collective-permute-start.19) | collective-permute-done | bytes 65568 | tf_op jit(solution)/shard_map/ppermute | solution.py:24
  76.0 0.8 %pad_maximum_fusion = f32[512,256]{1,0:T(8,128)} fusion(f32[128,256]{1,0:T(8,128)S(1)} %get-tuple-element.52, f32[256,256]{1,0:T(8,128)S(1)} %slice.10, f32[128,256]{1,0:T(8,128)S(1)} %get-tuple-element.51), kind=kLoop, calls=%fused_computation | loop fusion | flops 262144 | bytes 1048576 | tf_op jit(solution)/shard_map/concatenate | solution.py:291
  (30 shorter events, 1.3 us)
Async XLA Ops:
  0.6 64.5 %copy-start.4 = (s32[2]{0:T(128)S(1)}, s32[2]{0:T(128)}, u32[]{:S(2)}) copy-start(s32[2]{0:T(128)} %pad_add_fusion.pos) | copy-start | bytes 28
  8.3 56.7 %copy-start = (bf16[512,2048]{1,0:T(8,128)(2,1)S(1)}, bf16[512,2048]{1,0:T(8,128)(2,1)}, u32[]{:S(2)}) copy-start(bf16[512,2048]{1,0:T(8,128)(2,1)} %own.1) | copy-start | bytes 6291460
  8.3 56.7 %copy-start.1 = (bf16[256,2048]{1,0:T(8,128)(2,1)S(1)}, bf16[256,2048]{1,0:T(8,128)(2,1)}, u32[]{:S(2)}) copy-start(bf16[256,2048]{1,0:T(8,128)(2,1)} %x_ref.1) | copy-start | bytes 3145732
  8.3 26.8 %collective-permute-start.4 = (bf16[256,2048]{1,0:T(8,128)(2,1)}, bf16[256,2048]{1,0:T(8,128)(2,1)S(1)}, u32[]{:S(2)}, u32[]{:S(2)}) collective-permute-start(bf16[256,2048]{1,0:T(8,128)(2,1)} %get-tuple-element.32), channel_id=1, source_target_pairs={{0,2},{1,3},{2,0},{3,1},{4,5},{5,4},{6,7},{7,6},{8,10},{9,11},{10,... | collective-permute-start | bytes 3145736 | tf_op jit(solution)/shard_map/ppermute | solution.py:257
  11.4 23.8 %collective-permute-start.3 = (bf16[256,2048]{1,0:T(8,128)(2,1)}, bf16[256,2048]{1,0:T(8,128)(2,1)S(1)}, u32[]{:S(2)}, u32[]{:S(2)}) collective-permute-start(bf16[256,2048]{1,0:T(8,128)(2,1)} %get-tuple-element.32), channel_id=1, source_target_pairs={{0,1},{1,0},{2,3},{3,2},{4,6},{5,7},{6,4},{7,5},{8,9},{9,8},{10,11... | collective-permute-start | bytes 3145736 | tf_op jit(solution)/shard_map/ppermute | solution.py:251
  12.9 9.2 %collective-permute-start = (bf16[768,128]{1,0:T(8,128)(2,1)}, bf16[768,128]{1,0:T(8,128)(2,1)S(1)}, u32[]{:S(2)}, u32[]{:S(2)}) collective-permute-start(bf16[768,128]{1,0:T(8,128)(2,1)} %get-tuple-element.29), channel_id=1, source_target_pairs={{0,8},{4,12},{8,0},{12,4},{16,24},{20,28},{24,16},{28,20},{1,9},{5... | collective-permute-start | bytes 589832 | tf_op jit(solution)/shard_map/ppermute | solution.py:29
  14.4 17.4 %collective-permute-start.1 = (bf16[768,128]{1,0:T(8,128)(2,1)}, bf16[768,128]{1,0:T(8,128)(2,1)S(1)}, u32[]{:S(2)}, u32[]{:S(2)}) collective-permute-start(bf16[768,128]{1,0:T(8,128)(2,1)} %get-tuple-element.30), channel_id=1, source_target_pairs={{0,16},{4,20},{8,24},{12,28},{16,0},{20,4},{24,8},{28,12},{1,17},{... | collective-permute-start | bytes 589832 | tf_op jit(solution)/shard_map/ppermute | solution.py:29
  17.0 14.8 %collective-permute-start.2 = (bf16[768,128]{1,0:T(8,128)(2,1)}, bf16[768,128]{1,0:T(8,128)(2,1)S(1)}, u32[]{:S(2)}, u32[]{:S(2)}) collective-permute-start(bf16[768,128]{1,0:T(8,128)(2,1)} %get-tuple-element.31), channel_id=1, source_target_pairs={{0,24},{4,28},{8,16},{12,20},{16,8},{20,12},{24,0},{28,4},{1,25},{... | collective-permute-start | bytes 589832 | tf_op jit(solution)/shard_map/ppermute | solution.py:29
  22.0 10.3 %collective-permute-start.5 = (bf16[768,128]{1,0:T(8,128)(2,1)}, bf16[768,128]{1,0:T(8,128)(2,1)S(1)}, u32[]{:S(2)}, u32[]{:S(2)}) collective-permute-start(bf16[768,128]{1,0:T(8,128)(2,1)} %get-tuple-element.28.refs_0_.refs_2_), channel_id=1, source_target_pairs={{0,4},{4,0},{8,12},{12,8},{16,20},{20,16},{24,28},{28,24},{1,5},{5... | collective-permute-start | bytes 589832 | tf_op jit(solution)/shard_map/ppermute | solution.py:29
  31.8 1.4 %collective-permute-start.6 = (bf16[768,128]{1,0:T(8,128)(2,1)S(1)}, bf16[768,128]{1,0:T(8,128)(2,1)S(1)}, u32[]{:S(2)}, u32[]{:S(2)}) collective-permute-start(bf16[768,128]{1,0:T(8,128)(2,1)S(1)} %collective-permute-done.refs_1_.refs_3_), channel_id=1, source_target_pairs={{0,4},{4,0},{8,12},{12,8},{16,20},{20,16},{24,28},{28,24},{1,5},{5... | collective-permute-start | bytes 589832 | tf_op jit(solution)/shard_map/ppermute | solution.py:29
  31.8 1.7 %collective-permute-start.7 = (bf16[768,128]{1,0:T(8,128)(2,1)S(1)}, bf16[768,128]{1,0:T(8,128)(2,1)S(1)}, u32[]{:S(2)}, u32[]{:S(2)}) collective-permute-start(bf16[768,128]{1,0:T(8,128)(2,1)S(1)} %collective-permute-done.1.refs_2_.refs_0_), channel_id=1, source_target_pairs={{0,4},{4,0},{8,12},{12,8},{16,20},{20,16},{24,28},{28,24},{1,5},{5... | collective-permute-start | bytes 589832 | tf_op jit(solution)/shard_map/ppermute | solution.py:29
  32.3 1.5 %collective-permute-start.8 = (bf16[768,128]{1,0:T(8,128)(2,1)S(1)}, bf16[768,128]{1,0:T(8,128)(2,1)S(1)}, u32[]{:S(2)}, u32[]{:S(2)}) collective-permute-start(bf16[768,128]{1,0:T(8,128)(2,1)S(1)} %collective-permute-done.2.refs_3_.refs_1_), channel_id=1, source_target_pairs={{0,4},{4,0},{8,12},{12,8},{16,20},{20,16},{24,28},{28,24},{1,5},{5... | collective-permute-start | bytes 589832 | tf_op jit(solution)/shard_map/ppermute | solution.py:29
  35.2 23.5 %collective-permute-start.13 = (bf16[256,2048]{1,0:T(8,128)(2,1)S(1)}, bf16[256,2048]{1,0:T(8,128)(2,1)S(1)}, u32[]{:S(2)}, u32[]{:S(2)}) collective-permute-start(bf16[256,2048]{1,0:T(8,128)(2,1)S(1)} %collective-permute-done.3.n1), channel_id=1, source_target_pairs={{0,2},{1,3},{2,0},{3,1},{4,5},{5,4},{6,7},{7,6},{8,10},{9,11},{10,... | collective-permute-start | bytes 3145736 | tf_op jit(solution)/shard_map/ppermute | solution.py:257
  37.6 0.9 %copy-start.3 = (bf16[768,128]{1,0:T(8,128)(2,1)S(1)}, bf16[768,128]{1,0:T(8,128)(2,1)}, u32[]{:S(2)}) copy-start(bf16[768,128]{1,0:T(8,128)(2,1)} %get-tuple-element.28.refs_0_.refs_2_) | copy-start | bytes 589828
  41.2 7.3 %collective-permute-start.10 = (bf16[256,128]{1,0:T(8,128)(2,1)S(1)}, bf16[256,128]{1,0:T(8,128)(2,1)S(1)}, u32[]{:S(2)}, u32[]{:S(2)}) collective-permute-start(bf16[256,128]{1,0:T(8,128)(2,1)S(1)} %get-tuple-element.39), channel_id=1, source_target_pairs={{0,16},{4,20},{8,24},{12,28},{16,0},{20,4},{24,8},{28,12},{1,17},{... | collective-permute-start | bytes 196616 | tf_op jit(solution)/shard_map/ppermute | solution.py:29
  43.8 6.3 %collective-permute-start.11 = (bf16[256,128]{1,0:T(8,128)(2,1)S(1)}, bf16[256,128]{1,0:T(8,128)(2,1)S(1)}, u32[]{:S(2)}, u32[]{:S(2)}) collective-permute-start(bf16[256,128]{1,0:T(8,128)(2,1)S(1)} %get-tuple-element.40), channel_id=1, source_target_pairs={{0,24},{4,28},{8,16},{12,20},{16,8},{20,12},{24,0},{28,4},{1,25},{... | collective-permute-start | bytes 196616 | tf_op jit(solution)/shard_map/ppermute | solution.py:29
  47.9 4.3 %collective-permute-start.9 = (bf16[256,128]{1,0:T(8,128)(2,1)S(1)}, bf16[256,128]{1,0:T(8,128)(2,1)S(1)}, u32[]{:S(2)}, u32[]{:S(2)}) collective-permute-start(bf16[256,128]{1,0:T(8,128)(2,1)S(1)} %get-tuple-element.38), channel_id=1, source_target_pairs={{0,8},{4,12},{8,0},{12,4},{16,24},{20,28},{24,16},{28,20},{1,9},{5... | collective-permute-start | bytes 196616 | tf_op jit(solution)/shard_map/ppermute | solution.py:29
  52.2 15.6 %copy-start.2 = (bf16[2048,12,64]{0,2,1:T(8,128)(2,1)S(1)}, bf16[2048,12,64]{0,2,1:T(8,128)(2,1)}, u32[]{:S(2)}) copy-start(bf16[2048,12,64]{0,2,1:T(8,128)(2,1)} %param.7) | copy-start | bytes 9437188
  52.2 6.4 %collective-permute-start.12 = (bf16[1024,128]{1,0:T(8,128)(2,1)S(1)}, bf16[1024,128]{1,0:T(8,128)(2,1)S(1)}, u32[]{:S(2)}, u32[]{:S(2)}) collective-permute-start(bf16[1024,128]{1,0:T(8,128)(2,1)S(1)} %gathered.1.o0), channel_id=1, source_target_pairs={{0,1},{1,0},{2,3},{3,2},{4,6},{5,7},{6,4},{7,5},{8,9},{9,8},{10,11... | collective-permute-start | bytes 786440 | tf_op jit(solution)/shard_map/ppermute | solution.py:251
  53.0 12.1 %collective-permute-start.16 = (bf16[256,2048]{1,0:T(8,128)(2,1)S(1)}, bf16[256,2048]{1,0:T(8,128)(2,1)S(1)}, u32[]{:S(2)}, u32[]{:S(2)}) collective-permute-start(bf16[256,2048]{1,0:T(8,128)(2,1)S(1)} %collective-permute-done.3.n1), channel_id=1, source_target_pairs={{0,4},{4,0},{8,12},{12,8},{16,20},{20,16},{24,28},{28,24},{1,5},{5... | collective-permute-start | bytes 3145736 | tf_op jit(solution)/shard_map/ppermute | solution.py:29
  53.0 12.1 %collective-permute-start.15 = (bf16[256,2048]{1,0:T(8,128)(2,1)S(1)}, bf16[256,2048]{1,0:T(8,128)(2,1)S(1)}, u32[]{:S(2)}, u32[]{:S(2)}) collective-permute-start(bf16[256,2048]{1,0:T(8,128)(2,1)S(1)} %collective-permute-done.4.n2), channel_id=1, source_target_pairs={{0,4},{4,0},{8,12},{12,8},{16,20},{20,16},{24,28},{28,24},{1,5},{5... | collective-permute-start | bytes 3145736 | tf_op jit(solution)/shard_map/ppermute | solution.py:29
  58.7 9.2 %collective-permute-start.18 = (bf16[256,2048]{1,0:T(8,128)(2,1)S(1)}, bf16[256,2048]{1,0:T(8,128)(2,1)S(1)}, u32[]{:S(2)}, u32[]{:S(2)}) collective-permute-start(bf16[256,2048]{1,0:T(8,128)(2,1)S(1)} %collective-permute-done.13.n3), channel_id=1, source_target_pairs={{0,4},{4,0},{8,12},{12,8},{16,20},{20,16},{24,28},{28,24},{1,5},{5... | collective-permute-start | bytes 3145736 | tf_op jit(solution)/shard_map/ppermute | solution.py:29
  58.7 6.4 %collective-permute-start.14 = (bf16[1024,128]{1,0:T(8,128)(2,1)S(1)}, bf16[1024,128]{1,0:T(8,128)(2,1)S(1)}, u32[]{:S(2)}, u32[]{:S(2)}) collective-permute-start(bf16[1024,128]{1,0:T(8,128)(2,1)S(1)} %gathered.1.o0), channel_id=1, source_target_pairs={{0,2},{1,3},{2,0},{3,1},{4,5},{5,4},{6,7},{7,6},{8,10},{9,11},{10,... | collective-permute-start | bytes 786440 | tf_op jit(solution)/shard_map/ppermute | solution.py:257
  59.2 8.7 %collective-permute-start.17 = (bf16[1024,128]{1,0:T(8,128)(2,1)S(1)}, bf16[1024,128]{1,0:T(8,128)(2,1)S(1)}, u32[]{:S(2)}, u32[]{:S(2)}) collective-permute-start(bf16[1024,128]{1,0:T(8,128)(2,1)S(1)} %collective-permute-done.12.o1), channel_id=1, source_target_pairs={{0,2},{1,3},{2,0},{3,1},{4,5},{5,4},{6,7},{7,6},{8,10},{9,11},{10,... | collective-permute-start | bytes 786440 | tf_op jit(solution)/shard_map/ppermute | solution.py:257
  70.3 5.6 %collective-permute-start.19 = (bf16[128,256]{1,0:T(8,128)(2,1)S(1)}, bf16[128,256]{1,0:T(8,128)(2,1)S(1)}, u32[]{:S(2)}, u32[]{:S(2)}) collective-permute-start(bf16[128,256]{1,0:T(8,128)(2,1)S(1)} %get-tuple-element.49), channel_id=1, source_target_pairs={{0,4},{4,8},{8,12},{12,16},{16,20},{20,24},{24,28},{28,0},{1,5},{5... | collective-permute-start | bytes 196616 | tf_op jit(solution)/shard_map/ppermute | solution.py:24
  70.4 5.5 %collective-permute-start.20 = (bf16[128,256]{1,0:T(8,128)(2,1)S(1)}, bf16[128,256]{1,0:T(8,128)(2,1)S(1)}, u32[]{:S(2)}, u32[]{:S(2)}) collective-permute-start(bf16[128,256]{1,0:T(8,128)(2,1)S(1)} %get-tuple-element.50), channel_id=1, source_target_pairs={{0,28},{4,0},{8,4},{12,8},{16,12},{20,16},{24,20},{28,24},{1,29},{... | collective-permute-start | bytes 196616 | tf_op jit(solution)/shard_map/ppermute | solution.py:24

commit v4 on v3

--- a/solution.py
+++ b/solution.py
@@ -33,65 +33,48 @@
     return values * lax.rsqrt(jnp.mean(values * values, axis=-1, keepdims=True) + eps)
 
 
-def project_kernel(pos, x_hbm, w_hbm, out_hbm, *refs):
-    packs, half_ref = refs[:4], refs[4]
-    x_ref, w_ref, x_sem, w_sem, half_sem = refs[5:]
-    z, core = pos[0], pos[1]
+def place():
+    ctx = lax.axis_index("ctx")
+    return lax.div(ctx, 2), lax.rem(ctx, 2)
+
+
+def project_kernel(x_ref, w_hbm, *refs):
+    packs = refs[:5]
+    w_ref, w_sem = refs[5:]
+    z, _ = place()
     rows = x_ref.shape[0]
-    pairs = [(z // 2) ^ 1, z // 2]
-    copies = []
-    for i, pair in enumerate(pairs):
-        for k in range(3):
-            cols = pl.ds(pl.multiple_of(pair * 2 * LANES, 2 * LANES), 2 * LANES)
-            n = 3 * i + k
-            copies.append(pltpu.make_async_copy(w_hbm.at[k, :, cols], w_ref.at[n], w_sem.at[n]))
-    x_copy = pltpu.make_async_copy(x_hbm, x_ref, x_sem)
-    x_copy.start()
+    copies = [pltpu.make_async_copy(w_hbm.at[k], w_ref.at[k], w_sem.at[k]) for k in range(3)]
     for copy in copies:
         copy.start()
-    half = half_ref.shape[0]
-    half_copy = pltpu.make_async_copy(
-        out_hbm.at[pl.ds(pl.multiple_of(core * half, half), half)], half_ref, half_sem
-    )
-    half_copy.start()
-    x_copy.wait()
     x = x_ref[...].astype(f32)
     scale = lax.rsqrt(jnp.mean(x * x, axis=-1, keepdims=True) + eps)
     q_scale = scale * (HD ** (-0.5) * math.log2(math.e))
-    odd = z % 2
-    for i in range(2):
-        even_pack, odd_pack = packs[2 * (1 - i)], packs[2 * (1 - i) + 1]
-        for k in range(3):
-            copies[3 * i + k].wait()
-            out = jnp.dot(x_ref[...], w_ref[3 * i + k], preferred_element_type=f32)
-            out = (out * (q_scale if k == 0 else scale)).astype(bf16)
-            left, right = out[:, :LANES], out[:, LANES:]
-            part = pl.ds(k * rows, rows)
-            even_pack[part] = jnp.where(odd == 0, left, right)
-            odd_pack[part] = jnp.where(odd == 0, right, left)
-    half_copy.wait()
-
-
-def project(pos, tokens, w_qkv, w_out):
-    rows, width = tokens.shape
-    hbm = pl.BlockSpec(memory_space=pltpu.HBM)
-    vmem = pl.BlockSpec(memory_space=pltpu.VMEM)
-    pack = jax.ShapeDtypeStruct((3 * rows, LANES), bf16)
+    odd = lax.rem(z, 2) == 1
+    upper = lax.div(z, 2) == 1
+    for k, copy in enumerate(copies):
+        copy.wait()
+        out = jnp.dot(x_ref[...], w_ref[k], preferred_element_type=f32)
+        out = (out * (q_scale if k == 0 else scale)).astype(bf16)
+        parts = [out[:, i * LANES : (i + 1) * LANES] for i in range(4)]
+        parts = [jnp.where(odd, parts[i ^ 1], parts[i]) for i in range(4)]
+        parts = [jnp.where(upper, parts[i ^ 2], parts[i]) for i in range(4)]
+        for pack, part in zip(packs, parts):
+            pack[pl.ds(k * rows, rows)] = part
+    packs[4][...] = packs[0][...]
+
+
+def project(tokens, w_qkv):
+    rows = tokens.shape[0]
+    vmem = pl.BlockSpec(memory_space=pltpu.VMEM)
     return pl.pallas_call(
         project_kernel,
-        in_specs=[pl.BlockSpec(memory_space=pltpu.SMEM), hbm, hbm, hbm],
+        in_specs=[vmem, pl.BlockSpec(memory_space=pltpu.HBM)],
         out_specs=[vmem] * 5,
-        out_shape=[pack] * 4 + [jax.ShapeDtypeStruct((w_out.shape[0] // 2, width), bf16)],
-        scratch_shapes=[
-            pltpu.VMEM((rows, width), bf16),
-            pltpu.VMEM((6, width, 2 * LANES), bf16),
-            pltpu.SemaphoreType.DMA(()),
-            pltpu.SemaphoreType.DMA((6,)),
-            pltpu.SemaphoreType.DMA(()),
-        ],
-        compiler_params=pltpu.CompilerParams(vmem_limit_bytes=60 * 2**20),
+        out_shape=[jax.ShapeDtypeStruct((3 * rows, LANES), bf16)] * 5,
+        scratch_shapes=[pltpu.VMEM(w_qkv.shape, bf16), pltpu.SemaphoreType.DMA((3,))],
+        compiler_params=pltpu.CompilerParams(vmem_limit_bytes=52 * 2**20),
         name="project",
-    )(pos, tokens, w_qkv, w_out)
+    )(tokens, w_qkv)
 
 
 def attention_kernel(*refs):
@@ -146,17 +129,17 @@
     )(*packs)
 
 
-def mix_kernel(pos, x_ref, o0, o1, o2, own, n1, f2, n2, f1, total, att):
-    z, core = pos[0], pos[1]
+def mix_kernel(x_ref, o0, o1, o2, own, n1, f2, n2, f1, total, att):
+    z, core = place()
     rows, width = x_ref.shape
     local = own.shape[0]
     for s in range(4):
-        place = z ^ s
+        spot = z ^ s
         part = pl.ds(s * rows, rows)
-        att[:, pl.ds(pl.multiple_of(place * LANES, LANES), LANES)] = o0[part]
-        place = place ^ (2 * core)
+        att[:, pl.ds(pl.multiple_of(spot * LANES, LANES), LANES)] = o0[part]
+        spot = spot ^ (2 * core)
         for i, o in enumerate((o1, o2)):
-            at = pl.multiple_of((i + 1) * local + place * LANES, LANES)
+            at = pl.multiple_of((i + 1) * local + spot * LANES, LANES)
             att[:, pl.ds(at, LANES)] = o[part]
     step = 512
     for n in range(0, width, step):
@@ -165,65 +148,113 @@
         total[:, n : n + step] = x_ref[:, n : n + step].astype(f32) + mixed
 
 
-def mix(pos, tokens, outs, parts):
+def mix(tokens, outs, parts):
     rows, width = tokens.shape
     vmem = pl.BlockSpec(memory_space=pltpu.VMEM)
     return pl.pallas_call(
         mix_kernel,
-        in_specs=[pl.BlockSpec(memory_space=pltpu.SMEM)] + [vmem] * 9,
+        in_specs=[vmem] * 9,
         out_specs=vmem,
         out_shape=jax.ShapeDtypeStruct((rows, width), f32),
         scratch_shapes=[pltpu.VMEM((rows, 3 * parts[0].shape[0]), bf16)],
         compiler_params=pltpu.CompilerParams(vmem_limit_bytes=12 * 2**20),
         name="mix",
-    )(pos, tokens, *outs, *parts)
-
-
-def decode_kernel(pos, total, o3, n3, f3, dec_ref, main, up, down, att, hidden):
-    z, core = pos[0], pos[1]
+    )(tokens, *outs, *parts)
+
+
+def edges_kernel(total, o3, n3, f3, dec_ref, hidden, inner, outer, att, held):
+    z, core = place()
     rows, width = total.shape
     for s in range(4):
-        place = z ^ s ^ (2 * core)
-        att[:, pl.ds(pl.multiple_of(place * LANES, LANES), LANES)] = o3[pl.ds(s * rows, rows)]
+        spot = z ^ s ^ (2 * core)
+        att[:, pl.ds(pl.multiple_of(spot * LANES, LANES), LANES)] = o3[pl.ds(s * rows, rows)]
     step = 512
     squares = jnp.zeros((rows, LANES), f32)
     for n in range(0, width, step):
         w = jnp.concatenate([part[:, n : n + step] for part in (n3, f3)], axis=0)
         mixed = total[:, n : n + step] + jnp.dot(att[...], w, preferred_element_type=f32)
-        hidden[:, n : n + step] = mixed
+        held[:, n : n + step] = mixed
         for i in range(0, step, LANES):
             squares += mixed[:, i : i + LANES] * mixed[:, i : i + LANES]
     scale = lax.rsqrt(jnp.sum(squares, axis=-1, keepdims=True) * (1.0 / width) + eps)
-    ext = lax.dot_general(
-        dec_ref[...],
-        (hidden[...] * scale).astype(bf16),
-        (((1,), (1,)), ((), ())),
-        preferred_element_type=f32,
-    )
-    cells = main.shape[0] // PATCH
-    main[...] = ext[OV * cells : (OV + PATCH) * cells]
-    down[...] = ext[: OV * cells].astype(bf16)
-    up[...] = ext[(OV + PATCH) * cells :].astype(bf16)
-
-
-def decode(pos, total, o3, n3, f3, w_dec):
+    hidden[...] = (held[...] * scale).astype(bf16)
+    edge = inner.shape[0]
+    last = dec_ref.shape[0] - edge
+
+    def cells(part):
+        return lax.dot_general(
+            dec_ref[part], hidden[...], (((1,), (1,)), ((), ())), preferred_element_type=f32
+        ).astype(bf16)
+
+    down = cells(pl.ds(0, edge))
+    up = cells(pl.ds(last, edge))
+    inner[...] = jnp.where(core == 0, up, down)
+    outer[...] = jnp.where(core == 0, down, up)
+
+
+def decode_edges(total, o3, n3, f3, w_dec):
     rows, width = total.shape
-    wide = w_dec.shape[0]
-    cells = wide // (PATCH + 2 * OV)
+    cells = w_dec.shape[0] // (PATCH + 2 * OV)
     vmem = pl.BlockSpec(memory_space=pltpu.VMEM)
     edge = jax.ShapeDtypeStruct((OV * cells, rows), bf16)
     return pl.pallas_call(
-        decode_kernel,
-        in_specs=[pl.BlockSpec(memory_space=pltpu.SMEM)] + [vmem] * 5,
+        edges_kernel,
+        in_specs=[vmem] * 5,
         out_specs=[vmem] * 3,
-        out_shape=[jax.ShapeDtypeStruct((PATCH * cells, rows), f32), edge, edge],
+        out_shape=[jax.ShapeDtypeStruct((rows, width), bf16), edge, edge],
         scratch_shapes=[
             pltpu.VMEM((rows, n3.shape[0] + f3.shape[0]), bf16),
             pltpu.VMEM((rows, width), f32),
         ],
         compiler_params=pltpu.CompilerParams(vmem_limit_bytes=12 * 2**20),
-        name="decode",
-    )(pos, total, o3, n3, f3, w_dec)
+        name="decode_edges",
+    )(total, o3, n3, f3, w_dec)
+
+
+def main_kernel(hidden, dec_ref, main):
+    edge = (dec_ref.shape[0] - main.shape[0]) // 2
+    main[...] = lax.dot_general(
+        dec_ref[pl.ds(edge, main.shape[0])],
+        hidden[...],
+        (((1,), (1,)), ((), ())),
+        preferred_element_type=f32,
+    )
+
+
+def decode_main(hidden, w_dec):
+    cells = w_dec.shape[0] // (PATCH + 2 * OV)
+    vmem = pl.BlockSpec(memory_space=pltpu.VMEM)
+    return pl.pallas_call(
+        main_kernel,
+        in_specs=[vmem] * 2,
+        out_specs=vmem,
+        out_shape=jax.ShapeDtypeStruct((PATCH * cells, hidden.shape[0]), f32),
+        compiler_params=pltpu.CompilerParams(vmem_limit_bytes=8 * 2**20),
+        name="decode_main",
+    )(hidden, w_dec)
+
+
+def join_kernel(main, inner, outer, field):
+    _, core = place()
+    edge = inner.shape[0]
+    rest = main.shape[0] - edge
+    before = jnp.where(core == 0, outer[...], inner[...]).astype(f32)
+    after = jnp.where(core == 0, inner[...], outer[...]).astype(f32)
+    field[:edge] = main[:edge] + before
+    field[edge:rest] = main[edge:rest]
+    field[rest:] = main[rest:] + after
+
+
+def join(main, inner, outer):
+    vmem = pl.BlockSpec(memory_space=pltpu.VMEM)
+    return pl.pallas_call(
+        join_kernel,
+        in_specs=[vmem] * 3,
+        out_specs=vmem,
+        out_shape=jax.ShapeDtypeStruct(main.shape, f32),
+        compiler_params=pltpu.CompilerParams(vmem_limit_bytes=4 * 2**20),
+        name="join",
+    )(main, inner, outer)
 
 
 def gathered_kernel(*refs):
@@ -259,15 +290,14 @@
 
 def fast_body(tokens, w_qkv, w_out, w_dec):
     rows = tokens.shape[0]
-    ctx = lax.axis_index("ctx")
-    pos = jnp.stack([ctx // 2, ctx % 2])
-
-    p0, p1, p2, p3, half = project(pos, tokens, w_qkv, w_out)
+
+    size = w_out.shape[0] // 2
+    half = lax.dynamic_slice_in_dim(w_out, lax.rem(lax.axis_index("ctx"), 2) * size, size, 0)
+    n1, n2 = first_way(half), second_way(half)
+
+    p0, p1, p2, p3, p0_sent = project(tokens, w_qkv)
     r2, r3, r1 = swapped(p2, "ctx", 4), swapped(p3, "ctx", 6), swapped(p1, "ctx", 2)
-
-
-    n1, n2 = first_way(half), second_way(half)
-    c0, c1, c2, c3 = (swapped(part, "ctx", 1) for part in (p0, r1, r2, r3))
+    c0, c1, c2, c3 = (swapped(part, "ctx", 1) for part in (p0_sent, r1, r2, r3))
     n1, n2, c0, c1, c2, c3 = lax.optimization_barrier((n1, n2, c0, c1, c2, c3))
     n3 = second_way(n1)
 
@@ -277,20 +307,19 @@
     own, n1, n2 = lax.optimization_barrier((own, n1, n2))
     a1, a2 = first_way(own), second_way(own)
     f1, f2 = (swapped(part, "ctx", 1) for part in (n1, n2))
-    a1, n3 = lax.optimization_barrier((a1, n3))
+    a1, a2, n3 = lax.optimization_barrier((a1, a2, n3))
     a3 = second_way(a1)
     f3 = swapped(n3, "ctx", 1)
-    total = mix(pos, tokens, [own, a1, a2], [w_out, n1, f2, n2, f1])
+    total = mix(tokens, [own, a1, a2], [w_out, n1, f2, n2, f1])
 
     dec = w_dec.transpose(1, 2, 0)
     dec = dec.reshape(-1, dec.shape[2])
-    main, up, down = decode(pos, total, a3, n3, f3, dec)
-    from_before = passed_along(up, "ctx", 1).astype(f32)
-    from_after = passed_along(down, "ctx", -1).astype(f32)
-    edge = up.shape[0]
-    field = jnp.concatenate(
-        [main[:edge] + from_before, main[edge:-edge], main[-edge:] + from_after], axis=0
-    )
+    hidden, inner, outer = decode_edges(total, a3, n3, f3, dec)
+    count = lax.axis_size("ctx")
+    pairs = [(i, (i - 1 + 2 * (i % 2)) % count) for i in range(count)]
+    outer = lax.ppermute(outer, "ctx", pairs)
+    inner = swapped(inner, "ctx", 1)
+    field = join(decode_main(hidden, dec), inner, outer)
     return field.reshape(PATCH, -1, rows).transpose(2, 0, 1)
 
 

time: 76.9 us -> 69.2 us (0.90)
  Pallas kernels: 18.1 us -> 14.3 us
  starting transfers between devices: 23.1 us -> 20.9 us
  other arithmetic: 1.41 us -> 0 us
  waiting for transfers between devices: 33.2 us -> 32.3 us
    ppermute x2, waiting for transfers between devices: 5.17 us -> 0.01 us  [first_way(): return lax.ppermute(value, ('ctx', 'head'), pairs)]
    pallas_call x3 -> x5, Pallas kernels: 12.7 us -> 8.93 us  [the longest x1 3.81 us: project(): pl.pallas_call(project_kernel, in_specs=[vmem, pl.BlockSpec(memory_space=...]
    ppermute x4, waiting for transfers between devices: 5.98 us -> 9.55 us  [second_way(): return lax.ppermute(value, ('ctx', 'head'), pairs)]
    ppermute x4, starting transfers between devices: 7.44 us -> 5.64 us  [second_way(): return lax.ppermute(value, ('ctx', 'head'), pairs)]
    dynamic_slice x0 -> x1, local copies, waits for them, and re-layouts: none -> 1.41 us  [fast_body(): lax.dynamic_slice_in_dim(w_out, lax.rem(lax.axis_index('ctx'), 2) * size,...]
    ppermute x2 -> x1, starting transfers between devices: 3.59 us -> 2.57 us  [fast_body(): outer = lax.ppermute(outer, 'ctx', pairs)]
    unnamed x10 -> x6, local copies, waits for them, and re-layouts: 0.95 us -> 0.02 us
    ppermute x13 -> x14, starting transfers between devices: 9.78 us -> 10.6 us  [swapped(): return lax.ppermute(value, axis, [(i, i ^ bits) for i in range(count)])]
  transfers between devices with their start and end apart: 21 -> 21, of which waited for: 13 -> 11; matrix products, arithmetic and copies ran while one was open for 0% -> 0% of each run, Pallas kernels for 10% -> 17%
where the time goes in v4:
time: 69.2 us; the launch traced here: 69 us
  waiting for transfers between devices  32.3 us (47%)
  starting transfers between devices  20.9 us (30%)
  Pallas kernels  14.3 us (21%)
  local copies, waits for them, and re-layouts  1.43 us (2%)
    ppermute x14, waiting for transfers between devices, swapped(): return lax.ppermute(value, axis, [(i, i ^ bits) for i in range(count)])  20 us
    ppermute x14, starting transfers between devices, swapped(): return lax.ppermute(value, axis, [(i, i ^ bits) for i in range(count)])  10.6 us
    ppermute x4, waiting for transfers between devices, second_way(): return lax.ppermute(value, ('ctx', 'head'), pairs)  9.55 us
    ppermute x4, starting transfers between devices, second_way(): return lax.ppermute(value, ('ctx', 'head'), pairs)  5.64 us
    pallas_call x2, Pallas kernels, attend(): pl.pallas_call(attention_kernel, in_specs=[vmem] * len(packs), out_specs=...  5.37 us
    pallas_call x1, Pallas kernels, project(): pl.pallas_call(project_kernel, in_specs=[vmem, pl.BlockSpec(memory_space=...  3.81 us
    ppermute x1, waiting for transfers between devices, fast_body(): outer = lax.ppermute(outer, 'ctx', pairs)  2.71 us
    ppermute x1, starting transfers between devices, fast_body(): outer = lax.ppermute(outer, 'ctx', pairs)  2.57 us
  transfers between devices with their start and end apart: 21, of which 11 were waited for; matrix products, arithmetic and copies ran while one was open for 0% of the time, Pallas kernels for 17%

profile of v4, /device:TPU:0, one launch (start us, length us, event | category | flops | bytes accessed | tf_op | source)
XLA Modules:
  0.0 69.0 jit_solution(5441853029147485524)
XLA Ops:
  0.0 1.4 %constant_dynamic-slice_fusion = bf16[256,2048]{1,0:T(8,128)(2,1)S(1)} fusion(bf16[512,2048]{1,0:T(8,128)(2,1)} %own.1, s32[]{:T(128)S(6)} %select_n.3), kind=kLoop, calls=%fused_computation | loop fusion | bytes 2097156 | tf_op jit(solution)/shard_map/dynamic_slice | solution.py:295
  1.4 3.0 %collective-permute-start.4 = (bf16[256,2048]{1,0:T(8,128)(2,1)S(1)}, bf16[256,2048]{1,0:T(8,128)(2,1)S(1)}, u32[]{:S(2)}, u32[]{:S(2)}) collective-permute-start(bf16[256,2048]{1,0:T(8,128)(2,1)S(1)} %constant_dynamic-slice_fusion), channel_id=1, source_target_pairs={{0,2},{1,3},{2,0},{3,1},{4,5},{5,4},{6,7},{7,6},{8,10},{9,11},{10,... | collective-permute-start | bytes 3145736 | tf_op jit(solution)/shard_map/ppermute | solution.py:288
  4.5 1.5 %collective-permute-start.3 = (bf16[256,2048]{1,0:T(8,128)(2,1)S(1)}, bf16[256,2048]{1,0:T(8,128)(2,1)S(1)}, u32[]{:S(2)}, u32[]{:S(2)}) collective-permute-start(bf16[256,2048]{1,0:T(8,128)(2,1)S(1)} %constant_dynamic-slice_fusion), channel_id=1, source_target_pairs={{0,1},{1,0},{2,3},{3,2},{4,6},{5,7},{6,4},{7,5},{8,9},{9,8},{10,11... | collective-permute-start | bytes 3145736 | tf_op jit(solution)/shard_map/ppermute | solution.py:282
  5.9 3.8 %project.1 = (bf16[768,128]{1,0:T(8,128)(2,1)S(1)}, bf16[768,128]{1,0:T(8,128)(2,1)S(1)}, bf16[768,128]{1,0:T(8,128)(2,1)S(1)}, bf16[768,128]{1,0:T(8,128)(2,1)S(1)}, bf16[768,128]{1,0:T(8,128)(2,1)S(1)}) custom-call(bf16[256,2048]{1,0:T(8,128)(2,1)S(1)} %copy-done.2, bf16[3,2048,512]{2,1,0:T(8,128)(2,1)} %w_hbm.1), custom_call_target="tpu_custom_call" | custom-call | tf_op jit(solution)/shard_map/project/pallas_call | solution.py:69
  9.8 1.6 %collective-permute-start = (bf16[768,128]{1,0:T(8,128)(2,1)S(1)}, bf16[768,128]{1,0:T(8,128)(2,1)S(1)}, u32[]{:S(2)}, u32[]{:S(2)}) collective-permute-start(bf16[768,128]{1,0:T(8,128)(2,1)S(1)} %get-tuple-element.30), channel_id=1, source_target_pairs={{0,8},{4,12},{8,0},{12,4},{16,24},{20,28},{24,16},{28,20},{1,9},{5... | collective-permute-start | bytes 589832 | tf_op jit(solution)/shard_map/ppermute | solution.py:29
  11.4 2.6 %collective-permute-start.1 = (bf16[768,128]{1,0:T(8,128)(2,1)S(1)}, bf16[768,128]{1,0:T(8,128)(2,1)S(1)}, u32[]{:S(2)}, u32[]{:S(2)}) collective-permute-start(bf16[768,128]{1,0:T(8,128)(2,1)S(1)} %get-tuple-element.31), channel_id=1, source_target_pairs={{0,16},{4,20},{8,24},{12,28},{16,0},{20,4},{24,8},{28,12},{1,17},{... | collective-permute-start | bytes 589832 | tf_op jit(solution)/shard_map/ppermute | solution.py:29
  14.2 4.6 %collective-permute-done.refs_1_.refs_3_ = bf16[768,128]{1,0:T(8,128)(2,1)S(1)} collective-permute-done((bf16[768,128]{1,0:T(8,128)(2,1)S(1)}, bf16[768,128]{1,0:T(8,128)(2,1)S(1)}, u32[]{:S(2)}, u32[]{:S(2)}) %collective-permute-start) | collective-permute-done | bytes 196640 | tf_op jit(solution)/shard_map/ppermute | solution.py:29
  18.8 9.8 %collective-permute-done.1.refs_2_.refs_0_ = bf16[768,128]{1,0:T(8,128)(2,1)S(1)} collective-permute-done((bf16[768,128]{1,0:T(8,128)(2,1)S(1)}, bf16[768,128]{1,0:T(8,128)(2,1)S(1)}, u32[]{:S(2)}, u32[]{:S(2)}) %collective-permute-start.1) | collective-permute-done | bytes 196640 | tf_op jit(solution)/shard_map/ppermute | solution.py:29
  28.6 0.5 collective-permute-start.7
  29.2 0.9 %collective-permute-done.6.refs_5_ = bf16[768,128]{1,0:T(8,128)(2,1)S(1)} collective-permute-done((bf16[768,128]{1,0:T(8,128)(2,1)S(1)}, bf16[768,128]{1,0:T(8,128)(2,1)S(1)}, u32[]{:S(2)}, u32[]{:S(2)}) %collective-permute-start.6) | collective-permute-done | bytes 196640 | tf_op jit(solution)/shard_map/ppermute | solution.py:29
  30.0 0.3 collective-permute-done.7.refs_6_
  30.3 0.3 collective-permute-done.8.refs_7_
  30.6 0.5 collective-permute-start.14
  31.1 2.7 %attend.3 = (bf16[256,128]{1,0:T(8,128)(2,1)S(1)}, bf16[256,128]{1,0:T(8,128)(2,1)S(1)}) custom-call(bf16[768,128]{1,0:T(8,128)(2,1)S(1)} %collective-permute-done.1.refs_2_.refs_0_, bf16[768,128]{1,0:T(8,128)(2,1)S(1)} %collective-permute-done.2.refs_3_.refs_1_, bf16[768,128]{1,0:T(8,128)(2,1)S(1)} %get-tuple-element.29.refs_0_.refs_2_, ...), custom_call_target="tpu_custom_call" | custom-call | tf_op jit(solution)/shard_map/attend/pallas_call | solution.py:121
  33.8 3.6 %collective-permute-start.10 = (bf16[256,128]{1,0:T(8,128)(2,1)S(1)}, bf16[256,128]{1,0:T(8,128)(2,1)S(1)}, u32[]{:S(2)}, u32[]{:S(2)}) collective-permute-start(bf16[256,128]{1,0:T(8,128)(2,1)S(1)} %get-tuple-element.40), channel_id=1, source_target_pairs={{0,16},{4,20},{8,24},{12,28},{16,0},{20,4},{24,8},{28,12},{1,17},{... | collective-permute-start | bytes 196616 | tf_op jit(solution)/shard_map/ppermute | solution.py:29
  37.4 1.3 %collective-permute-start.11 = (bf16[256,128]{1,0:T(8,128)(2,1)S(1)}, bf16[256,128]{1,0:T(8,128)(2,1)S(1)}, u32[]{:S(2)}, u32[]{:S(2)}) collective-permute-start(bf16[256,128]{1,0:T(8,128)(2,1)S(1)} %get-tuple-element.41), channel_id=1, source_target_pairs={{0,24},{4,28},{8,16},{12,20},{16,8},{20,12},{24,0},{28,4},{1,25},{... | collective-permute-start | bytes 196616 | tf_op jit(solution)/shard_map/ppermute | solution.py:29
  38.7 2.7 %attend.2 = (bf16[256,128]{1,0:T(8,128)(2,1)S(1)}, bf16[256,128]{1,0:T(8,128)(2,1)S(1)}) custom-call(bf16[768,128]{1,0:T(8,128)(2,1)S(1)} %get-tuple-element.29.refs_0_.refs_2_, bf16[768,128]{1,0:T(8,128)(2,1)S(1)} %collective-permute-done.refs_1_.refs_3_, bf16[768,128]{1,0:T(8,128)(2,1)S(1)} %collective-permute-done.1.refs_2_.refs_0_, ...), custom_call_target="tpu_custom_call" | custom-call | tf_op jit(solution)/shard_map/attend/pallas_call | solution.py:121
  41.5 0.9 %collective-permute-done.10.refs_2_ = bf16[256,128]{1,0:T(8,128)(2,1)S(1)} collective-permute-done((bf16[256,128]{1,0:T(8,128)(2,1)S(1)}, bf16[256,128]{1,0:T(8,128)(2,1)S(1)}, u32[]{:S(2)}, u32[]{:S(2)}) %collective-permute-start.10) | collective-permute-done | bytes 65568 | tf_op jit(solution)/shard_map/ppermute | solution.py:29
  42.4 1.2 %collective-permute-done.11.refs_3_ = bf16[256,128]{1,0:T(8,128)(2,1)S(1)} collective-permute-done((bf16[256,128]{1,0:T(8,128)(2,1)S(1)}, bf16[256,128]{1,0:T(8,128)(2,1)S(1)}, u32[]{:S(2)}, u32[]{:S(2)}) %collective-permute-start.11) | collective-permute-done | bytes 65568 | tf_op jit(solution)/shard_map/ppermute | solution.py:29
  43.6 2.2 %collective-permute-done.9.refs_1_ = bf16[256,128]{1,0:T(8,128)(2,1)S(1)} collective-permute-done((bf16[256,128]{1,0:T(8,128)(2,1)S(1)}, bf16[256,128]{1,0:T(8,128)(2,1)S(1)}, u32[]{:S(2)}, u32[]{:S(2)}) %collective-permute-start.9) | collective-permute-done | bytes 65568 | tf_op jit(solution)/shard_map/ppermute | solution.py:29
  45.8 1.6 %collective-permute-start.13 = (bf16[1024,128]{1,0:T(8,128)(2,1)S(1)}, bf16[1024,128]{1,0:T(8,128)(2,1)S(1)}, u32[]{:S(2)}, u32[]{:S(2)}) collective-permute-start(bf16[1024,128]{1,0:T(8,128)(2,1)S(1)} %gathered.1.o0), channel_id=1, source_target_pairs={{0,2},{1,3},{2,0},{3,1},{4,5},{5,4},{6,7},{7,6},{8,10},{9,11},{10,... | collective-permute-start | bytes 786440 | tf_op jit(solution)/shard_map/ppermute | solution.py:288
  47.4 0.6 collective-permute-start.12
  47.9 0.5 collective-permute-start.15
  48.4 5.6 %collective-permute-done.13.o2 = bf16[1024,128]{1,0:T(8,128)(2,1)S(1)} collective-permute-done((bf16[1024,128]{1,0:T(8,128)(2,1)S(1)}, bf16[1024,128]{1,0:T(8,128)(2,1)S(1)}, u32[]{:S(2)}, u32[]{:S(2)}) %collective-permute-start.13) | collective-permute-done | bytes 262176 | tf_op jit(solution)/shard_map/ppermute | solution.py:288
  54.0 0.5 collective-permute-start.17
  54.5 1.9 %mix.1.total = f32[256,2048]{1,0:T(8,128)S(1)} custom-call(bf16[256,2048]{1,0:T(8,128)(2,1)S(1)} %copy-done.2, bf16[1024,128]{1,0:T(8,128)(2,1)S(1)} %gathered.1.o0, bf16[1024,128]{1,0:T(8,128)(2,1)S(1)} %collective-permute-done.12.o1, bf16[1024,128]{1,0:T(8,128)(2,1)S(1)} %collective-permute-done.13.o2, bf16[512,2048]{1,0:T(8,128)(2,1)S(1)} %copy-done.1, ...), custom_call_target="tpu_custom_call" | custom-call | tf_op jit(solution)/shard_map/mix/pallas_call | solution.py:154
  56.5 4.0 %collective-permute-done.17.o3 = bf16[1024,128]{1,0:T(8,128)(2,1)S(1)} collective-permute-done((bf16[1024,128]{1,0:T(8,128)(2,1)S(1)}, bf16[1024,128]{1,0:T(8,128)(2,1)S(1)}, u32[]{:S(2)}, u32[]{:S(2)}) %collective-permute-start.17) | collective-permute-done | bytes 262176 | tf_op jit(solution)/shard_map/ppermute | solution.py:288
  60.5 1.6 %decode_edges.1 = (bf16[256,2048]{1,0:T(8,128)(2,1)S(1)}, bf16[128,256]{1,0:T(8,128)(2,1)S(1)}, bf16[128,256]{1,0:T(8,128)(2,1)S(1)}) custom-call(f32[256,2048]{1,0:T(8,128)S(1)} %mix.1.total, bf16[1024,128]{1,0:T(8,128)(2,1)S(1)} %collective-permute-done.17.o3, bf16[256,2048]{1,0:T(8,128)(2,1)S(1)} %collective-permute-done.14.n3, ...), custom_call_target="tpu_custom_call" | custom-call | tf_op jit(solution)/shard_map/decode_edges/pallas_call | solution.py:200
  62.2 2.6 %collective-permute-start.20 = (bf16[128,256]{1,0:T(8,128)(2,1)S(1)}, bf16[128,256]{1,0:T(8,128)(2,1)S(1)}, u32[]{:S(2)}, u32[]{:S(2)}) collective-permute-start(bf16[128,256]{1,0:T(8,128)(2,1)S(1)} %get-tuple-element.52), channel_id=1, source_target_pairs={{0,28},{4,8},{8,4},{12,16},{16,12},{20,24},{24,20},{28,0},{1,29},{... | collective-permute-start | bytes 196616 | tf_op jit(solution)/shard_map/ppermute | solution.py:320
  64.7 0.7 %decode_main.1.main = f32[512,256]{1,0:T(8,128)S(1)} custom-call(bf16[256,2048]{1,0:T(8,128)(2,1)S(1)} %get-tuple-element.50.hidden, bf16[768,2048]{1,0:T(8,128)(2,1)S(1)} %bitcast.7), custom_call_target="tpu_custom_call" | custom-call | tf_op jit(solution)/shard_map/decode_main/pallas_call | solution.py:227
  65.5 2.7 %collective-permute-done.20.outer = bf16[128,256]{1,0:T(8,128)(2,1)S(1)} collective-permute-done((bf16[128,256]{1,0:T(8,128)(2,1)S(1)}, bf16[128,256]{1,0:T(8,128)(2,1)S(1)}, u32[]{:S(2)}, u32[]{:S(2)}) %collective-permute-start.20) | collective-permute-done | bytes 65568 | tf_op jit(solution)/shard_map/ppermute | solution.py:320
  68.2 0.8 %join.1 = f32[512,256]{1,0:T(8,128)} custom-call(f32[512,256]{1,0:T(8,128)S(1)} %decode_main.1.main, bf16[128,256]{1,0:T(8,128)(2,1)S(1)} %collective-permute-done.19.inner, bf16[128,256]{1,0:T(8,128)(2,1)S(1)} %collective-permute-done.20.outer), custom_call_target="tpu_custom_call" | custom-call | tf_op jit(solution)/shard_map/join/pallas_call | solution.py:250
  (25 shorter events, 0.5 us)
Async XLA Ops:
  0.0 5.9 %copy-start.2 = (bf16[256,2048]{1,0:T(8,128)(2,1)S(1)}, bf16[256,2048]{1,0:T(8,128)(2,1)}, u32[]{:S(2)}) copy-start(bf16[256,2048]{1,0:T(8,128)(2,1)} %x_ref.3) | copy-start | bytes 3145732
  1.4 29.2 %collective-permute-start.4 = (bf16[256,2048]{1,0:T(8,128)(2,1)S(1)}, bf16[256,2048]{1,0:T(8,128)(2,1)S(1)}, u32[]{:S(2)}, u32[]{:S(2)}) collective-permute-start(bf16[256,2048]{1,0:T(8,128)(2,1)S(1)} %constant_dynamic-slice_fusion), channel_id=1, source_target_pairs={{0,2},{1,3},{2,0},{3,1},{4,5},{5,4},{6,7},{7,6},{8,10},{9,11},{10,... | collective-permute-start | bytes 3145736 | tf_op jit(solution)/shard_map/ppermute | solution.py:288
  4.5 26.1 %collective-permute-start.3 = (bf16[256,2048]{1,0:T(8,128)(2,1)S(1)}, bf16[256,2048]{1,0:T(8,128)(2,1)S(1)}, u32[]{:S(2)}, u32[]{:S(2)}) collective-permute-start(bf16[256,2048]{1,0:T(8,128)(2,1)S(1)} %constant_dynamic-slice_fusion), channel_id=1, source_target_pairs={{0,1},{1,0},{2,3},{3,2},{4,6},{5,7},{6,4},{7,5},{8,9},{9,8},{10,11... | collective-permute-start | bytes 3145736 | tf_op jit(solution)/shard_map/ppermute | solution.py:282
  9.8 44.8 %copy-start.1 = (bf16[512,2048]{1,0:T(8,128)(2,1)S(1)}, bf16[512,2048]{1,0:T(8,128)(2,1)}, u32[]{:S(2)}) copy-start(bf16[512,2048]{1,0:T(8,128)(2,1)} %own.1) | copy-start | bytes 6291460
  9.8 9.0 %collective-permute-start = (bf16[768,128]{1,0:T(8,128)(2,1)S(1)}, bf16[768,128]{1,0:T(8,128)(2,1)S(1)}, u32[]{:S(2)}, u32[]{:S(2)}) collective-permute-start(bf16[768,128]{1,0:T(8,128)(2,1)S(1)} %get-tuple-element.30), channel_id=1, source_target_pairs={{0,8},{4,12},{8,0},{12,4},{16,24},{20,28},{24,16},{28,20},{1,9},{5... | collective-permute-start | bytes 589832 | tf_op jit(solution)/shard_map/ppermute | solution.py:29
  11.4 17.2 %collective-permute-start.1 = (bf16[768,128]{1,0:T(8,128)(2,1)S(1)}, bf16[768,128]{1,0:T(8,128)(2,1)S(1)}, u32[]{:S(2)}, u32[]{:S(2)}) collective-permute-start(bf16[768,128]{1,0:T(8,128)(2,1)S(1)} %get-tuple-element.31), channel_id=1, source_target_pairs={{0,16},{4,20},{8,24},{12,28},{16,0},{20,4},{24,8},{28,12},{1,17},{... | collective-permute-start | bytes 589832 | tf_op jit(solution)/shard_map/ppermute | solution.py:29
  14.0 14.6 %collective-permute-start.2 = (bf16[768,128]{1,0:T(8,128)(2,1)S(1)}, bf16[768,128]{1,0:T(8,128)(2,1)S(1)}, u32[]{:S(2)}, u32[]{:S(2)}) collective-permute-start(bf16[768,128]{1,0:T(8,128)(2,1)S(1)} %get-tuple-element.32), channel_id=1, source_target_pairs={{0,24},{4,28},{8,16},{12,20},{16,8},{20,12},{24,0},{28,4},{1,25},{... | collective-permute-start | bytes 589832 | tf_op jit(solution)/shard_map/ppermute | solution.py:29
  18.8 10.3 %collective-permute-start.5 = (bf16[768,128]{1,0:T(8,128)(2,1)S(1)}, bf16[768,128]{1,0:T(8,128)(2,1)S(1)}, u32[]{:S(2)}, u32[]{:S(2)}) collective-permute-start(bf16[768,128]{1,0:T(8,128)(2,1)S(1)} %get-tuple-element.33), channel_id=1, source_target_pairs={{0,4},{4,0},{8,12},{12,8},{16,20},{20,16},{24,28},{28,24},{1,5},{5... | collective-permute-start | bytes 589832 | tf_op jit(solution)/shard_map/ppermute | solution.py:29
  28.6 1.4 %collective-permute-start.6 = (bf16[768,128]{1,0:T(8,128)(2,1)S(1)}, bf16[768,128]{1,0:T(8,128)(2,1)S(1)}, u32[]{:S(2)}, u32[]{:S(2)}) collective-permute-start(bf16[768,128]{1,0:T(8,128)(2,1)S(1)} %collective-permute-done.refs_1_.refs_3_), channel_id=1, source_target_pairs={{0,4},{4,0},{8,12},{12,8},{16,20},{20,16},{24,28},{28,24},{1,5},{5... | collective-permute-start | bytes 589832 | tf_op jit(solution)/shard_map/ppermute | solution.py:29
  28.6 1.7 %collective-permute-start.7 = (bf16[768,128]{1,0:T(8,128)(2,1)S(1)}, bf16[768,128]{1,0:T(8,128)(2,1)S(1)}, u32[]{:S(2)}, u32[]{:S(2)}) collective-permute-start(bf16[768,128]{1,0:T(8,128)(2,1)S(1)} %collective-permute-done.1.refs_2_.refs_0_), channel_id=1, source_target_pairs={{0,4},{4,0},{8,12},{12,8},{16,20},{20,16},{24,28},{28,24},{1,5},{5... | collective-permute-start | bytes 589832 | tf_op jit(solution)/shard_map/ppermute | solution.py:29
  29.1 1.5 %collective-permute-start.8 = (bf16[768,128]{1,0:T(8,128)(2,1)S(1)}, bf16[768,128]{1,0:T(8,128)(2,1)S(1)}, u32[]{:S(2)}, u32[]{:S(2)}) collective-permute-start(bf16[768,128]{1,0:T(8,128)(2,1)S(1)} %collective-permute-done.2.refs_3_.refs_1_), channel_id=1, source_target_pairs={{0,4},{4,0},{8,12},{12,8},{16,20},{20,16},{24,28},{28,24},{1,5},{5... | collective-permute-start | bytes 589832 | tf_op jit(solution)/shard_map/ppermute | solution.py:29
  30.6 23.4 %collective-permute-start.14 = (bf16[256,2048]{1,0:T(8,128)(2,1)S(1)}, bf16[256,2048]{1,0:T(8,128)(2,1)S(1)}, u32[]{:S(2)}, u32[]{:S(2)}) collective-permute-start(bf16[256,2048]{1,0:T(8,128)(2,1)S(1)} %collective-permute-done.3.n1), channel_id=1, source_target_pairs={{0,2},{1,3},{2,0},{3,1},{4,5},{5,4},{6,7},{7,6},{8,10},{9,11},{10,... | collective-permute-start | bytes 3145736 | tf_op jit(solution)/shard_map/ppermute | solution.py:288
  33.8 8.6 %collective-permute-start.10 = (bf16[256,128]{1,0:T(8,128)(2,1)S(1)}, bf16[256,128]{1,0:T(8,128)(2,1)S(1)}, u32[]{:S(2)}, u32[]{:S(2)}) collective-permute-start(bf16[256,128]{1,0:T(8,128)(2,1)S(1)} %get-tuple-element.40), channel_id=1, source_target_pairs={{0,16},{4,20},{8,24},{12,28},{16,0},{20,4},{24,8},{28,12},{1,17},{... | collective-permute-start | bytes 196616 | tf_op jit(solution)/shard_map/ppermute | solution.py:29
  37.4 6.2 %collective-permute-start.11 = (bf16[256,128]{1,0:T(8,128)(2,1)S(1)}, bf16[256,128]{1,0:T(8,128)(2,1)S(1)}, u32[]{:S(2)}, u32[]{:S(2)}) collective-permute-start(bf16[256,128]{1,0:T(8,128)(2,1)S(1)} %get-tuple-element.41), channel_id=1, source_target_pairs={{0,24},{4,28},{8,16},{12,20},{16,8},{20,12},{24,0},{28,4},{1,25},{... | collective-permute-start | bytes 196616 | tf_op jit(solution)/shard_map/ppermute | solution.py:29
  41.4 4.3 %collective-permute-start.9 = (bf16[256,128]{1,0:T(8,128)(2,1)S(1)}, bf16[256,128]{1,0:T(8,128)(2,1)S(1)}, u32[]{:S(2)}, u32[]{:S(2)}) collective-permute-start(bf16[256,128]{1,0:T(8,128)(2,1)S(1)} %get-tuple-element.39), channel_id=1, source_target_pairs={{0,8},{4,12},{8,0},{12,4},{16,24},{20,28},{24,16},{28,20},{1,9},{5... | collective-permute-start | bytes 196616 | tf_op jit(solution)/shard_map/ppermute | solution.py:29
  45.8 8.2 %collective-permute-start.13 = (bf16[1024,128]{1,0:T(8,128)(2,1)S(1)}, bf16[1024,128]{1,0:T(8,128)(2,1)S(1)}, u32[]{:S(2)}, u32[]{:S(2)}) collective-permute-start(bf16[1024,128]{1,0:T(8,128)(2,1)S(1)} %gathered.1.o0), channel_id=1, source_target_pairs={{0,2},{1,3},{2,0},{3,1},{4,5},{5,4},{6,7},{7,6},{8,10},{9,11},{10,... | collective-permute-start | bytes 786440 | tf_op jit(solution)/shard_map/ppermute | solution.py:288
  47.4 6.6 %collective-permute-start.12 = (bf16[1024,128]{1,0:T(8,128)(2,1)S(1)}, bf16[1024,128]{1,0:T(8,128)(2,1)S(1)}, u32[]{:S(2)}, u32[]{:S(2)}) collective-permute-start(bf16[1024,128]{1,0:T(8,128)(2,1)S(1)} %gathered.1.o0), channel_id=1, source_target_pairs={{0,1},{1,0},{2,3},{3,2},{4,6},{5,7},{6,4},{7,5},{8,9},{9,8},{10,11... | collective-permute-start | bytes 786440 | tf_op jit(solution)/shard_map/ppermute | solution.py:282
  47.9 6.6 %collective-permute-start.16 = (bf16[256,2048]{1,0:T(8,128)(2,1)S(1)}, bf16[256,2048]{1,0:T(8,128)(2,1)S(1)}, u32[]{:S(2)}, u32[]{:S(2)}) collective-permute-start(bf16[256,2048]{1,0:T(8,128)(2,1)S(1)} %collective-permute-done.3.n1), channel_id=1, source_target_pairs={{0,4},{4,0},{8,12},{12,8},{16,20},{20,16},{24,28},{28,24},{1,5},{5... | collective-permute-start | bytes 3145736 | tf_op jit(solution)/shard_map/ppermute | solution.py:29
  47.9 6.6 %collective-permute-start.15 = (bf16[256,2048]{1,0:T(8,128)(2,1)S(1)}, bf16[256,2048]{1,0:T(8,128)(2,1)S(1)}, u32[]{:S(2)}, u32[]{:S(2)}) collective-permute-start(bf16[256,2048]{1,0:T(8,128)(2,1)S(1)} %collective-permute-done.4.n2), channel_id=1, source_target_pairs={{0,4},{4,0},{8,12},{12,8},{16,20},{20,16},{24,28},{28,24},{1,5},{5... | collective-permute-start | bytes 3145736 | tf_op jit(solution)/shard_map/ppermute | solution.py:29
  54.0 6.5 %collective-permute-start.18 = (bf16[256,2048]{1,0:T(8,128)(2,1)S(1)}, bf16[256,2048]{1,0:T(8,128)(2,1)S(1)}, u32[]{:S(2)}, u32[]{:S(2)}) collective-permute-start(bf16[256,2048]{1,0:T(8,128)(2,1)S(1)} %collective-permute-done.14.n3), channel_id=1, source_target_pairs={{0,4},{4,0},{8,12},{12,8},{16,20},{20,16},{24,28},{28,24},{1,5},{5... | collective-permute-start | bytes 3145736 | tf_op jit(solution)/shard_map/ppermute | solution.py:29
  54.0 6.4 %collective-permute-start.17 = (bf16[1024,128]{1,0:T(8,128)(2,1)S(1)}, bf16[1024,128]{1,0:T(8,128)(2,1)S(1)}, u32[]{:S(2)}, u32[]{:S(2)}) collective-permute-start(bf16[1024,128]{1,0:T(8,128)(2,1)S(1)} %collective-permute-done.12.o1), channel_id=1, source_target_pairs={{0,2},{1,3},{2,0},{3,1},{4,5},{5,4},{6,7},{7,6},{8,10},{9,11},{10,... | collective-permute-start | bytes 786440 | tf_op jit(solution)/shard_map/ppermute | solution.py:288
  54.5 5.9 %copy-start = (bf16[2048,12,64]{0,2,1:T(8,128)(2,1)S(1)}, bf16[2048,12,64]{0,2,1:T(8,128)(2,1)}, u32[]{:S(2)}) copy-start(bf16[2048,12,64]{0,2,1:T(8,128)(2,1)} %param.7) | copy-start | bytes 9437188
  62.1 3.4 %collective-permute-start.19 = (bf16[128,256]{1,0:T(8,128)(2,1)S(1)}, bf16[128,256]{1,0:T(8,128)(2,1)S(1)}, u32[]{:S(2)}, u32[]{:S(2)}) collective-permute-start(bf16[128,256]{1,0:T(8,128)(2,1)S(1)} %get-tuple-element.51), channel_id=1, source_target_pairs={{0,4},{4,0},{8,12},{12,8},{16,20},{20,16},{24,28},{28,24},{1,5},{5... | collective-permute-start | bytes 196616 | tf_op jit(solution)/shard_map/ppermute | solution.py:29
  62.2 6.0 %collective-permute-start.20 = (bf16[128,256]{1,0:T(8,128)(2,1)S(1)}, bf16[128,256]{1,0:T(8,128)(2,1)S(1)}, u32[]{:S(2)}, u32[]{:S(2)}) collective-permute-start(bf16[128,256]{1,0:T(8,128)(2,1)S(1)} %get-tuple-element.52), channel_id=1, source_target_pairs={{0,28},{4,8},{8,4},{12,16},{16,12},{20,24},{24,20},{28,0},{1,29},{... | collective-permute-start | bytes 196616 | tf_op jit(solution)/shard_map/ppermute | solution.py:320

commit v5 on v4

--- a/solution.py
+++ b/solution.py
@@ -129,21 +129,17 @@
     )(*packs)
 
 
-def mix_kernel(x_ref, o0, o1, o2, own, n1, f2, n2, f1, total, att):
-    z, core = place()
+def mix_kernel(x_ref, o0, o1, o2, own, w1, w2, total, att):
+    z, _ = place()
     rows, width = x_ref.shape
     local = own.shape[0]
     for s in range(4):
-        spot = z ^ s
-        part = pl.ds(s * rows, rows)
-        att[:, pl.ds(pl.multiple_of(spot * LANES, LANES), LANES)] = o0[part]
-        spot = spot ^ (2 * core)
-        for i, o in enumerate((o1, o2)):
-            at = pl.multiple_of((i + 1) * local + spot * LANES, LANES)
-            att[:, pl.ds(at, LANES)] = o[part]
+        for i, o in enumerate((o0, o1, o2)):
+            at = pl.multiple_of(i * local + (z ^ s) * LANES, LANES)
+            att[:, pl.ds(at, LANES)] = o[pl.ds(s * rows, rows)]
     step = 512
     for n in range(0, width, step):
-        w = jnp.concatenate([part[:, n : n + step] for part in (own, n1, f2, n2, f1)], axis=0)
+        w = jnp.concatenate([part[:, n : n + step] for part in (own, w1, w2)], axis=0)
         mixed = jnp.dot(att[...], w, preferred_element_type=f32)
         total[:, n : n + step] = x_ref[:, n : n + step].astype(f32) + mixed
 
@@ -153,7 +149,7 @@
     vmem = pl.BlockSpec(memory_space=pltpu.VMEM)
     return pl.pallas_call(
         mix_kernel,
-        in_specs=[vmem] * 9,
+        in_specs=[vmem] * 7,
         out_specs=vmem,
         out_shape=jax.ShapeDtypeStruct((rows, width), f32),
         scratch_shapes=[pltpu.VMEM((rows, 3 * parts[0].shape[0]), bf16)],
@@ -291,26 +287,29 @@
 def fast_body(tokens, w_qkv, w_out, w_dec):
     rows = tokens.shape[0]
 
+    w1 = first_way(w_out)
+
+    p0, p1, p2, p3, p0_sent = project(tokens, w_qkv)
+    r2, r3 = swapped(p2, "ctx", 4), swapped(p3, "ctx", 6)
+    c0 = swapped(p0_sent, "ctx", 1)
+    p1, c0 = lax.optimization_barrier((p1, c0))
+    r1 = swapped(p1, "ctx", 2)
+    c1, c2, c3 = (swapped(part, "ctx", 1) for part in (r1, r2, r3))
+    w1, c1, c2, c3 = lax.optimization_barrier((w1, c1, c2, c3))
     size = w_out.shape[0] // 2
-    half = lax.dynamic_slice_in_dim(w_out, lax.rem(lax.axis_index("ctx"), 2) * size, size, 0)
-    n1, n2 = first_way(half), second_way(half)
-
-    p0, p1, p2, p3, p0_sent = project(tokens, w_qkv)
-    r2, r3, r1 = swapped(p2, "ctx", 4), swapped(p3, "ctx", 6), swapped(p1, "ctx", 2)
-    c0, c1, c2, c3 = (swapped(part, "ctx", 1) for part in (p0_sent, r1, r2, r3))
-    n1, n2, c0, c1, c2, c3 = lax.optimization_barrier((n1, n2, c0, c1, c2, c3))
-    n3 = second_way(n1)
+    half = lax.dynamic_slice_in_dim(w1, lax.rem(lax.axis_index("ctx"), 2) * size, size, 0)
+    n3 = second_way(half)
 
     o2, o3 = attend([r2, r3, p0, r1, c0, c1, c2, c3])
     o0, o1 = attend([p0, r1, r2, r3, c0, c1, c2, c3])
     own = gathered([o0, swapped(o1, "ctx", 2), swapped(o2, "ctx", 4), swapped(o3, "ctx", 6)])
-    own, n1, n2 = lax.optimization_barrier((own, n1, n2))
+    own, w1, n3 = lax.optimization_barrier((own, w1, n3))
     a1, a2 = first_way(own), second_way(own)
-    f1, f2 = (swapped(part, "ctx", 1) for part in (n1, n2))
+    w2 = swapped(w1, "ctx", 1)
     a1, a2, n3 = lax.optimization_barrier((a1, a2, n3))
     a3 = second_way(a1)
     f3 = swapped(n3, "ctx", 1)
-    total = mix(tokens, [own, a1, a2], [w_out, n1, f2, n2, f1])
+    total = mix(tokens, [own, a1, a2], [w_out, w1, w2])
 
     dec = w_dec.transpose(1, 2, 0)
     dec = dec.reshape(-1, dec.shape[2])

time: 69.2 us -> 71.2 us (1.029)
  Pallas kernels: 14.3 us -> 16.2 us
    ppermute x2, waiting for transfers between devices: 0.01 us -> 7.74 us  [first_way(): return lax.ppermute(value, ('ctx', 'head'), pairs)]
    ppermute x4 -> x3, waiting for transfers between devices: 9.55 us -> 3.89 us  [second_way(): return lax.ppermute(value, ('ctx', 'head'), pairs)]
    ppermute x4 -> x3, starting transfers between devices: 5.64 us -> 3.05 us  [second_way(): return lax.ppermute(value, ('ctx', 'head'), pairs)]
    pallas_call x2, Pallas kernels: 5.37 us -> 7.22 us  [attend(): pl.pallas_call(attention_kernel, in_specs=[vmem] * len(packs), out_specs=...]
    ppermute x2, starting transfers between devices: 2.04 us -> 3.54 us  [first_way(): return lax.ppermute(value, ('ctx', 'head'), pairs)]
    ppermute x14 -> x13, waiting for transfers between devices: 20 us -> 18.6 us  [swapped(): return lax.ppermute(value, axis, [(i, i ^ bits) for i in range(count)])]
    dynamic_slice x1, local copies, waits for them, and re-layouts: 1.41 us -> 0.07 us  [fast_body(): lax.dynamic_slice_in_dim(w1, lax.rem(lax.axis_index('ctx'), 2) * size, si...]
    unnamed x6 -> x8, local copies, waits for them, and re-layouts: 0.02 us -> 1.24 us
  transfers between devices with their start and end apart: 21 -> 19, of which waited for: 11 -> 9; matrix products, arithmetic and copies ran while one was open for 0% -> 0% of each run, Pallas kernels for 17% -> 19%
where the time goes in v5:
time: 71.2 us; the launch traced here: 71.1 us
  waiting for transfers between devices  32.4 us (46%)
  starting transfers between devices  21 us (29%)
  Pallas kernels  16.2 us (23%)
  local copies, waits for them, and re-layouts  1.31 us (2%)
    ppermute x13, waiting for transfers between devices, swapped(): return lax.ppermute(value, axis, [(i, i ^ bits) for i in range(count)])  18.6 us
    ppermute x13, starting transfers between devices, swapped(): return lax.ppermute(value, axis, [(i, i ^ bits) for i in range(count)])  11.5 us
    ppermute x2, waiting for transfers between devices, first_way(): return lax.ppermute(value, ('ctx', 'head'), pairs)  7.74 us
    pallas_call x2, Pallas kernels, attend(): pl.pallas_call(attention_kernel, in_specs=[vmem] * len(packs), out_specs=...  7.22 us
    ppermute x3, waiting for transfers between devices, second_way(): return lax.ppermute(value, ('ctx', 'head'), pairs)  3.89 us
    pallas_call x1, Pallas kernels, project(): pl.pallas_call(project_kernel, in_specs=[vmem, pl.BlockSpec(memory_space=...  3.81 us
    ppermute x2, starting transfers between devices, first_way(): return lax.ppermute(value, ('ctx', 'head'), pairs)  3.54 us
    ppermute x3, starting transfers between devices, second_way(): return lax.ppermute(value, ('ctx', 'head'), pairs)  3.05 us
  transfers between devices with their start and end apart: 19, of which 9 were waited for; matrix products, arithmetic and copies ran while one was open for 0% of the time, Pallas kernels for 19%

profile of v5, /device:TPU:0, one launch (start us, length us, event | category | flops | bytes accessed | tf_op | source)
XLA Modules:
  0.0 71.1 jit_solution(1658084013621907201)
XLA Ops:
  0.0 2.9 %collective-permute-start.4 = (bf16[512,2048]{1,0:T(8,128)(2,1)}, bf16[512,2048]{1,0:T(8,128)(2,1)S(1)}, u32[]{:S(2)}, u32[]{:S(2)}) collective-permute-start(bf16[512,2048]{1,0:T(8,128)(2,1)} %own.1), channel_id=1, source_target_pairs={{0,1},{1,0},{2,3},{3,2},{4,6},{5,7},{6,4},{7,5},{8,9},{9,8},{10,11... | collective-permute-start | bytes 6291464 | tf_op jit(solution)/shard_map/ppermute | solution.py:278
  2.9 1.2 %copy-done.1 = bf16[256,2048]{1,0:T(8,128)(2,1)S(1)} copy-done((bf16[256,2048]{1,0:T(8,128)(2,1)S(1)}, bf16[256,2048]{1,0:T(8,128)(2,1)}, u32[]{:S(2)}) %copy-start.1) | copy-done | bytes 1048600
  4.2 3.8 %project.1 = (bf16[768,128]{1,0:T(8,128)(2,1)S(1)}, bf16[768,128]{1,0:T(8,128)(2,1)S(1)}, bf16[768,128]{1,0:T(8,128)(2,1)S(1)}, bf16[768,128]{1,0:T(8,128)(2,1)S(1)}, bf16[768,128]{1,0:T(8,128)(2,1)S(1)}) custom-call(bf16[256,2048]{1,0:T(8,128)(2,1)S(1)} %copy-done.1, bf16[3,2048,512]{2,1,0:T(8,128)(2,1)} %w_hbm.1), custom_call_target="tpu_custom_call" | custom-call | tf_op jit(solution)/shard_map/project/pallas_call | solution.py:69
  8.0 0.1 collective-permute-start
  8.1 2.7 %collective-permute-start.2 = (bf16[768,128]{1,0:T(8,128)(2,1)S(1)}, bf16[768,128]{1,0:T(8,128)(2,1)S(1)}, u32[]{:S(2)}, u32[]{:S(2)}) collective-permute-start(bf16[768,128]{1,0:T(8,128)(2,1)S(1)} %get-tuple-element.33), channel_id=1, source_target_pairs={{0,16},{4,20},{8,24},{12,28},{16,0},{20,4},{24,8},{28,12},{1,17},{... | collective-permute-start | bytes 589832 | tf_op jit(solution)/shard_map/ppermute | solution.py:29
  10.7 1.3 %collective-permute-start.3 = (bf16[768,128]{1,0:T(8,128)(2,1)S(1)}, bf16[768,128]{1,0:T(8,128)(2,1)S(1)}, u32[]{:S(2)}, u32[]{:S(2)}) collective-permute-start(bf16[768,128]{1,0:T(8,128)(2,1)S(1)} %get-tuple-element.34), channel_id=1, source_target_pairs={{0,24},{4,28},{8,16},{12,20},{16,8},{20,12},{24,0},{28,4},{1,25},{... | collective-permute-start | bytes 589832 | tf_op jit(solution)/shard_map/ppermute | solution.py:29
  12.1 0.2 collective-permute-start.1
  12.3 12.9 %collective-permute-done.2.refs_2_.refs_0_ = bf16[768,128]{1,0:T(8,128)(2,1)S(1)} collective-permute-done((bf16[768,128]{1,0:T(8,128)(2,1)S(1)}, bf16[768,128]{1,0:T(8,128)(2,1)S(1)}, u32[]{:S(2)}, u32[]{:S(2)}) %collective-permute-start.2) | collective-permute-done | bytes 196640 | tf_op jit(solution)/shard_map/ppermute | solution.py:29
  25.2 0.5 collective-permute-start.7
  25.7 0.4 collective-permute-done.1.refs_1_.refs_3_
  26.1 0.6 collective-permute-done.6.refs_6_
  26.6 0.3 collective-permute-done.7.refs_7_
  26.9 0.7 %collective-permute-done.5.refs_5_ = bf16[768,128]{1,0:T(8,128)(2,1)} collective-permute-done((bf16[768,128]{1,0:T(8,128)(2,1)S(1)}, bf16[768,128]{1,0:T(8,128)(2,1)}, u32[]{:S(2)}, u32[]{:S(2)}) %collective-permute-start.5) | collective-permute-done | bytes 196640 | tf_op jit(solution)/shard_map/ppermute | solution.py:29
  27.8 1.6 %collective-permute-start.11 = (bf16[256,2048]{1,0:T(8,128)(2,1)S(1)}, bf16[256,2048]{1,0:T(8,128)(2,1)S(1)}, u32[]{:S(2)}, u32[]{:S(2)}) collective-permute-start(bf16[256,2048]{1,0:T(8,128)(2,1)S(1)} %constant_dynamic-slice_fusion), channel_id=1, source_target_pairs={{0,2},{1,3},{2,0},{3,1},{4,5},{5,4},{6,7},{7,6},{8,10},{9,11},{10,... | collective-permute-start | bytes 3145736 | tf_op jit(solution)/shard_map/ppermute | solution.py:284
  29.4 3.6 %attend.3 = (bf16[256,128]{1,0:T(8,128)(2,1)S(1)}, bf16[256,128]{1,0:T(8,128)(2,1)S(1)}) custom-call(bf16[768,128]{1,0:T(8,128)(2,1)S(1)} %collective-permute-done.2.refs_2_.refs_0_, bf16[768,128]{1,0:T(8,128)(2,1)S(1)} %collective-permute-done.3.refs_3_.refs_1_, bf16[768,128]{1,0:T(8,128)(2,1)S(1)} %get-tuple-element.29.refs_0_.refs_2_, ...), custom_call_target="tpu_custom_call" | custom-call | tf_op jit(solution)/shard_map/attend/pallas_call | solution.py:121
  33.0 3.7 %collective-permute-start.10 = (bf16[256,128]{1,0:T(8,128)(2,1)S(1)}, bf16[256,128]{1,0:T(8,128)(2,1)S(1)}, u32[]{:S(2)}, u32[]{:S(2)}) collective-permute-start(bf16[256,128]{1,0:T(8,128)(2,1)S(1)} %get-tuple-element.42), channel_id=1, source_target_pairs={{0,24},{4,28},{8,16},{12,20},{16,8},{20,12},{24,0},{28,4},{1,25},{... | collective-permute-start | bytes 196616 | tf_op jit(solution)/shard_map/ppermute | solution.py:29
  36.7 2.2 %collective-permute-start.9 = (bf16[256,128]{1,0:T(8,128)(2,1)S(1)}, bf16[256,128]{1,0:T(8,128)(2,1)S(1)}, u32[]{:S(2)}, u32[]{:S(2)}) collective-permute-start(bf16[256,128]{1,0:T(8,128)(2,1)S(1)} %get-tuple-element.41), channel_id=1, source_target_pairs={{0,16},{4,20},{8,24},{12,28},{16,0},{20,4},{24,8},{28,12},{1,17},{... | collective-permute-start | bytes 196616 | tf_op jit(solution)/shard_map/ppermute | solution.py:29
  38.9 3.6 %attend.2 = (bf16[256,128]{1,0:T(8,128)(2,1)S(1)}, bf16[256,128]{1,0:T(8,128)(2,1)S(1)}) custom-call(bf16[768,128]{1,0:T(8,128)(2,1)S(1)} %get-tuple-element.29.refs_0_.refs_2_, bf16[768,128]{1,0:T(8,128)(2,1)S(1)} %collective-permute-done.1.refs_1_.refs_3_, bf16[768,128]{1,0:T(8,128)(2,1)S(1)} %collective-permute-done.2.refs_2_.refs_0_, ...), custom_call_target="tpu_custom_call" | custom-call | tf_op jit(solution)/shard_map/attend/pallas_call | solution.py:121
  42.5 0.6 collective-permute-start.8
  43.0 3.8 %collective-permute-done.8.refs_1_ = bf16[256,128]{1,0:T(8,128)(2,1)S(1)} collective-permute-done((bf16[256,128]{1,0:T(8,128)(2,1)S(1)}, bf16[256,128]{1,0:T(8,128)(2,1)S(1)}, u32[]{:S(2)}, u32[]{:S(2)}) %collective-permute-start.8) | collective-permute-done | bytes 65568 | tf_op jit(solution)/shard_map/ppermute | solution.py:29
  46.9 0.6 collective-permute-start.12
  47.5 0.9 %collective-permute-start.13 = (bf16[1024,128]{1,0:T(8,128)(2,1)S(1)}, bf16[1024,128]{1,0:T(8,128)(2,1)S(1)}, u32[]{:S(2)}, u32[]{:S(2)}) collective-permute-start(bf16[1024,128]{1,0:T(8,128)(2,1)S(1)} %gathered.1.o0), channel_id=1, source_target_pairs={{0,2},{1,3},{2,0},{3,1},{4,5},{5,4},{6,7},{7,6},{8,10},{9,11},{10,... | collective-permute-start | bytes 786440 | tf_op jit(solution)/shard_map/ppermute | solution.py:284
  48.4 7.7 %collective-permute-done.12.o1 = bf16[1024,128]{1,0:T(8,128)(2,1)S(1)} collective-permute-done((bf16[1024,128]{1,0:T(8,128)(2,1)S(1)}, bf16[1024,128]{1,0:T(8,128)(2,1)S(1)}, u32[]{:S(2)}, u32[]{:S(2)}) %collective-permute-start.12) | collective-permute-done | bytes 262176 | tf_op jit(solution)/shard_map/ppermute | solution.py:278
  56.2 0.1 collective-permute-start.16
  56.2 0.5 collective-permute-start.15
  56.8 1.9 %mix.1.total = f32[256,2048]{1,0:T(8,128)S(1)} custom-call(bf16[256,2048]{1,0:T(8,128)(2,1)S(1)} %copy-done.2, bf16[1024,128]{1,0:T(8,128)(2,1)S(1)} %gathered.1.o0, bf16[1024,128]{1,0:T(8,128)(2,1)S(1)} %collective-permute-done.12.o1, bf16[1024,128]{1,0:T(8,128)(2,1)S(1)} %collective-permute-done.13.o2, bf16[512,2048]{1,0:T(8,128)(2,1)S(1)} %copy-done.3, ...), custom_call_target="tpu_custom_call" | custom-call | tf_op jit(solution)/shard_map/mix/pallas_call | solution.py:150
  58.7 3.9 %collective-permute-done.15.o3 = bf16[1024,128]{1,0:T(8,128)(2,1)S(1)} collective-permute-done((bf16[1024,128]{1,0:T(8,128)(2,1)S(1)}, bf16[1024,128]{1,0:T(8,128)(2,1)S(1)}, u32[]{:S(2)}, u32[]{:S(2)}) %collective-permute-start.15) | collective-permute-done | bytes 262176 | tf_op jit(solution)/shard_map/ppermute | solution.py:284
  62.6 1.6 %decode_edges.1 = (bf16[256,2048]{1,0:T(8,128)(2,1)S(1)}, bf16[128,256]{1,0:T(8,128)(2,1)S(1)}, bf16[128,256]{1,0:T(8,128)(2,1)S(1)}) custom-call(f32[256,2048]{1,0:T(8,128)S(1)} %mix.1.total, bf16[1024,128]{1,0:T(8,128)(2,1)S(1)} %collective-permute-done.15.o3, bf16[256,2048]{1,0:T(8,128)(2,1)S(1)} %collective-permute-done.11.n3, ...), custom_call_target="tpu_custom_call" | custom-call | tf_op jit(solution)/shard_map/decode_edges/pallas_call | solution.py:196
  64.3 3.0 %collective-permute-start.18 = (bf16[128,256]{1,0:T(8,128)(2,1)S(1)}, bf16[128,256]{1,0:T(8,128)(2,1)S(1)}, u32[]{:S(2)}, u32[]{:S(2)}) collective-permute-start(bf16[128,256]{1,0:T(8,128)(2,1)S(1)} %get-tuple-element.52), channel_id=1, source_target_pairs={{0,28},{4,8},{8,4},{12,16},{16,12},{20,24},{24,20},{28,0},{1,29},{... | collective-permute-start | bytes 196616 | tf_op jit(solution)/shard_map/ppermute | solution.py:319
  67.3 0.7 %decode_main.1.main = f32[512,256]{1,0:T(8,128)S(1)} custom-call(bf16[256,2048]{1,0:T(8,128)(2,1)S(1)} %get-tuple-element.50.hidden, bf16[768,2048]{1,0:T(8,128)(2,1)S(1)} %bitcast.7), custom_call_target="tpu_custom_call" | custom-call | tf_op jit(solution)/shard_map/decode_main/pallas_call | solution.py:223
  68.1 2.2 %collective-permute-done.18.outer = bf16[128,256]{1,0:T(8,128)(2,1)S(1)} collective-permute-done((bf16[128,256]{1,0:T(8,128)(2,1)S(1)}, bf16[128,256]{1,0:T(8,128)(2,1)S(1)}, u32[]{:S(2)}, u32[]{:S(2)}) %collective-permute-start.18) | collective-permute-done | bytes 65568 | tf_op jit(solution)/shard_map/ppermute | solution.py:319
  70.2 0.8 %join.1 = f32[512,256]{1,0:T(8,128)} custom-call(f32[512,256]{1,0:T(8,128)S(1)} %decode_main.1.main, bf16[128,256]{1,0:T(8,128)(2,1)S(1)} %collective-permute-done.17.inner, bf16[128,256]{1,0:T(8,128)(2,1)S(1)} %collective-permute-done.18.outer), custom_call_target="tpu_custom_call" | custom-call | tf_op jit(solution)/shard_map/join/pallas_call | solution.py:246
  (23 shorter events, 0.3 us)
Async XLA Ops:
  0.0 27.7 %collective-permute-start.4 = (bf16[512,2048]{1,0:T(8,128)(2,1)}, bf16[512,2048]{1,0:T(8,128)(2,1)S(1)}, u32[]{:S(2)}, u32[]{:S(2)}) collective-permute-start(bf16[512,2048]{1,0:T(8,128)(2,1)} %own.1), channel_id=1, source_target_pairs={{0,1},{1,0},{2,3},{3,2},{4,6},{5,7},{6,4},{7,5},{8,9},{9,8},{10,11... | collective-permute-start | bytes 6291464 | tf_op jit(solution)/shard_map/ppermute | solution.py:278
  2.9 1.2 %copy-start.1 = (bf16[256,2048]{1,0:T(8,128)(2,1)S(1)}, bf16[256,2048]{1,0:T(8,128)(2,1)}, u32[]{:S(2)}) copy-start(bf16[256,2048]{1,0:T(8,128)(2,1)} %x_ref.3) | copy-start | bytes 3145732
  8.0 4.1 %collective-permute-start = (bf16[768,128]{1,0:T(8,128)(2,1)S(1)}, bf16[768,128]{1,0:T(8,128)(2,1)S(1)}, u32[]{:S(2)}, u32[]{:S(2)}) collective-permute-start(bf16[768,128]{1,0:T(8,128)(2,1)S(1)} %get-tuple-element.31), channel_id=1, source_target_pairs={{0,4},{4,0},{8,12},{12,8},{16,20},{20,16},{24,28},{28,24},{1,5},{5... | collective-permute-start | bytes 589832 | tf_op jit(solution)/shard_map/ppermute | solution.py:29
  8.1 17.1 %collective-permute-start.2 = (bf16[768,128]{1,0:T(8,128)(2,1)S(1)}, bf16[768,128]{1,0:T(8,128)(2,1)S(1)}, u32[]{:S(2)}, u32[]{:S(2)}) collective-permute-start(bf16[768,128]{1,0:T(8,128)(2,1)S(1)} %get-tuple-element.33), channel_id=1, source_target_pairs={{0,16},{4,20},{8,24},{12,28},{16,0},{20,4},{24,8},{28,12},{1,17},{... | collective-permute-start | bytes 589832 | tf_op jit(solution)/shard_map/ppermute | solution.py:29
  10.7 14.5 %collective-permute-start.3 = (bf16[768,128]{1,0:T(8,128)(2,1)S(1)}, bf16[768,128]{1,0:T(8,128)(2,1)S(1)}, u32[]{:S(2)}, u32[]{:S(2)}) collective-permute-start(bf16[768,128]{1,0:T(8,128)(2,1)S(1)} %get-tuple-element.34), channel_id=1, source_target_pairs={{0,24},{4,28},{8,16},{12,20},{16,8},{20,12},{24,0},{28,4},{1,25},{... | collective-permute-start | bytes 589832 | tf_op jit(solution)/shard_map/ppermute | solution.py:29
  12.1 14.0 %collective-permute-start.1 = (bf16[768,128]{1,0:T(8,128)(2,1)S(1)}, bf16[768,128]{1,0:T(8,128)(2,1)S(1)}, u32[]{:S(2)}, u32[]{:S(2)}) collective-permute-start(bf16[768,128]{1,0:T(8,128)(2,1)S(1)} %get-tuple-element.32), channel_id=1, source_target_pairs={{0,8},{4,12},{8,0},{12,4},{16,24},{20,28},{24,16},{28,20},{1,9},{5... | collective-permute-start | bytes 589832 | tf_op jit(solution)/shard_map/ppermute | solution.py:29
  25.2 1.4 %collective-permute-start.6 = (bf16[768,128]{1,0:T(8,128)(2,1)S(1)}, bf16[768,128]{1,0:T(8,128)(2,1)S(1)}, u32[]{:S(2)}, u32[]{:S(2)}) collective-permute-start(bf16[768,128]{1,0:T(8,128)(2,1)S(1)} %collective-permute-done.2.refs_2_.refs_0_), channel_id=1, source_target_pairs={{0,4},{4,0},{8,12},{12,8},{16,20},{20,16},{24,28},{28,24},{1,5},{5... | collective-permute-start | bytes 589832 | tf_op jit(solution)/shard_map/ppermute | solution.py:29
  25.2 1.7 %collective-permute-start.7 = (bf16[768,128]{1,0:T(8,128)(2,1)S(1)}, bf16[768,128]{1,0:T(8,128)(2,1)S(1)}, u32[]{:S(2)}, u32[]{:S(2)}) collective-permute-start(bf16[768,128]{1,0:T(8,128)(2,1)S(1)} %collective-permute-done.3.refs_3_.refs_1_), channel_id=1, source_target_pairs={{0,4},{4,0},{8,12},{12,8},{16,20},{20,16},{24,28},{28,24},{1,5},{5... | collective-permute-start | bytes 589832 | tf_op jit(solution)/shard_map/ppermute | solution.py:29
  26.1 1.6 %collective-permute-start.5 = (bf16[768,128]{1,0:T(8,128)(2,1)S(1)}, bf16[768,128]{1,0:T(8,128)(2,1)}, u32[]{:S(2)}, u32[]{:S(2)}) collective-permute-start(bf16[768,128]{1,0:T(8,128)(2,1)S(1)} %collective-permute-done.1.refs_1_.refs_3_), channel_id=1, source_target_pairs={{0,4},{4,0},{8,12},{12,8},{16,20},{20,16},{24,28},{28,24},{1,5},{5... | collective-permute-start | bytes 589832 | tf_op jit(solution)/shard_map/ppermute | solution.py:29
  27.7 29.1 %copy-start.2 = (bf16[256,2048]{1,0:T(8,128)(2,1)S(1)}, bf16[256,2048]{1,0:T(8,128)(2,1)}, u32[]{:S(2)}) copy-start(bf16[256,2048]{1,0:T(8,128)(2,1)} %x_ref.3) | copy-start | bytes 3145732
  27.7 29.1 %copy-start.3 = (bf16[512,2048]{1,0:T(8,128)(2,1)S(1)}, bf16[512,2048]{1,0:T(8,128)(2,1)}, u32[]{:S(2)}) copy-start(bf16[512,2048]{1,0:T(8,128)(2,1)} %own.1) | copy-start | bytes 6291460
  27.8 19.1 %collective-permute-start.11 = (bf16[256,2048]{1,0:T(8,128)(2,1)S(1)}, bf16[256,2048]{1,0:T(8,128)(2,1)S(1)}, u32[]{:S(2)}, u32[]{:S(2)}) collective-permute-start(bf16[256,2048]{1,0:T(8,128)(2,1)S(1)} %constant_dynamic-slice_fusion), channel_id=1, source_target_pairs={{0,2},{1,3},{2,0},{3,1},{4,5},{5,4},{6,7},{7,6},{8,10},{9,11},{10,... | collective-permute-start | bytes 3145736 | tf_op jit(solution)/shard_map/ppermute | solution.py:284
  33.0 10.0 %collective-permute-start.10 = (bf16[256,128]{1,0:T(8,128)(2,1)S(1)}, bf16[256,128]{1,0:T(8,128)(2,1)S(1)}, u32[]{:S(2)}, u32[]{:S(2)}) collective-permute-start(bf16[256,128]{1,0:T(8,128)(2,1)S(1)} %get-tuple-element.42), channel_id=1, source_target_pairs={{0,24},{4,28},{8,16},{12,20},{16,8},{20,12},{24,0},{28,4},{1,25},{... | collective-permute-start | bytes 196616 | tf_op jit(solution)/shard_map/ppermute | solution.py:29
  36.7 6.4 %collective-permute-start.9 = (bf16[256,128]{1,0:T(8,128)(2,1)S(1)}, bf16[256,128]{1,0:T(8,128)(2,1)S(1)}, u32[]{:S(2)}, u32[]{:S(2)}) collective-permute-start(bf16[256,128]{1,0:T(8,128)(2,1)S(1)} %get-tuple-element.41), channel_id=1, source_target_pairs={{0,16},{4,20},{8,24},{12,28},{16,0},{20,4},{24,8},{28,12},{1,17},{... | collective-permute-start | bytes 196616 | tf_op jit(solution)/shard_map/ppermute | solution.py:29
  42.5 4.3 %collective-permute-start.8 = (bf16[256,128]{1,0:T(8,128)(2,1)S(1)}, bf16[256,128]{1,0:T(8,128)(2,1)S(1)}, u32[]{:S(2)}, u32[]{:S(2)}) collective-permute-start(bf16[256,128]{1,0:T(8,128)(2,1)S(1)} %get-tuple-element.40), channel_id=1, source_target_pairs={{0,8},{4,12},{8,0},{12,4},{16,24},{20,28},{24,16},{28,20},{1,9},{5... | collective-permute-start | bytes 196616 | tf_op jit(solution)/shard_map/ppermute | solution.py:29
  46.8 10.0 %collective-permute-start.14 = (bf16[512,2048]{1,0:T(8,128)(2,1)S(1)}, bf16[512,2048]{1,0:T(8,128)(2,1)S(1)}, u32[]{:S(2)}, u32[]{:S(2)}) collective-permute-start(bf16[512,2048]{1,0:T(8,128)(2,1)S(1)} %collective-permute-done.4.w1), channel_id=1, source_target_pairs={{0,4},{4,0},{8,12},{12,8},{16,20},{20,16},{24,28},{28,24},{1,5},{5... | collective-permute-start | bytes 6291464 | tf_op jit(solution)/shard_map/ppermute | solution.py:29
  46.9 9.2 %collective-permute-start.12 = (bf16[1024,128]{1,0:T(8,128)(2,1)S(1)}, bf16[1024,128]{1,0:T(8,128)(2,1)S(1)}, u32[]{:S(2)}, u32[]{:S(2)}) collective-permute-start(bf16[1024,128]{1,0:T(8,128)(2,1)S(1)} %gathered.1.o0), channel_id=1, source_target_pairs={{0,1},{1,0},{2,3},{3,2},{4,6},{5,7},{6,4},{7,5},{8,9},{9,8},{10,11... | collective-permute-start | bytes 786440 | tf_op jit(solution)/shard_map/ppermute | solution.py:278
  47.5 8.6 %collective-permute-start.13 = (bf16[1024,128]{1,0:T(8,128)(2,1)S(1)}, bf16[1024,128]{1,0:T(8,128)(2,1)S(1)}, u32[]{:S(2)}, u32[]{:S(2)}) collective-permute-start(bf16[1024,128]{1,0:T(8,128)(2,1)S(1)} %gathered.1.o0), channel_id=1, source_target_pairs={{0,2},{1,3},{2,0},{3,1},{4,5},{5,4},{6,7},{7,6},{8,10},{9,11},{10,... | collective-permute-start | bytes 786440 | tf_op jit(solution)/shard_map/ppermute | solution.py:284
  56.2 6.5 %collective-permute-start.16 = (bf16[256,2048]{1,0:T(8,128)(2,1)S(1)}, bf16[256,2048]{1,0:T(8,128)(2,1)S(1)}, u32[]{:S(2)}, u32[]{:S(2)}) collective-permute-start(bf16[256,2048]{1,0:T(8,128)(2,1)S(1)} %collective-permute-done.11.n3), channel_id=1, source_target_pairs={{0,4},{4,0},{8,12},{12,8},{16,20},{20,16},{24,28},{28,24},{1,5},{5... | collective-permute-start | bytes 3145736 | tf_op jit(solution)/shard_map/ppermute | solution.py:29
  56.2 6.4 %collective-permute-start.15 = (bf16[1024,128]{1,0:T(8,128)(2,1)S(1)}, bf16[1024,128]{1,0:T(8,128)(2,1)S(1)}, u32[]{:S(2)}, u32[]{:S(2)}) collective-permute-start(bf16[1024,128]{1,0:T(8,128)(2,1)S(1)} %collective-permute-done.12.o1), channel_id=1, source_target_pairs={{0,2},{1,3},{2,0},{3,1},{4,5},{5,4},{6,7},{7,6},{8,10},{9,11},{10,... | collective-permute-start | bytes 786440 | tf_op jit(solution)/shard_map/ppermute | solution.py:284
  56.8 5.8 %copy-start = (bf16[2048,12,64]{0,2,1:T(8,128)(2,1)S(1)}, bf16[2048,12,64]{0,2,1:T(8,128)(2,1)}, u32[]{:S(2)}) copy-start(bf16[2048,12,64]{0,2,1:T(8,128)(2,1)} %param.7) | copy-start | bytes 9437188
  64.3 3.8 %collective-permute-start.17 = (bf16[128,256]{1,0:T(8,128)(2,1)S(1)}, bf16[128,256]{1,0:T(8,128)(2,1)S(1)}, u32[]{:S(2)}, u32[]{:S(2)}) collective-permute-start(bf16[128,256]{1,0:T(8,128)(2,1)S(1)} %get-tuple-element.51), channel_id=1, source_target_pairs={{0,4},{4,0},{8,12},{12,8},{16,20},{20,16},{24,28},{28,24},{1,5},{5... | collective-permute-start | bytes 196616 | tf_op jit(solution)/shard_map/ppermute | solution.py:29
  64.3 5.9 %collective-permute-start.18 = (bf16[128,256]{1,0:T(8,128)(2,1)S(1)}, bf16[128,256]{1,0:T(8,128)(2,1)S(1)}, u32[]{:S(2)}, u32[]{:S(2)}) collective-permute-start(bf16[128,256]{1,0:T(8,128)(2,1)S(1)} %get-tuple-element.52), channel_id=1, source_target_pairs={{0,28},{4,8},{8,4},{12,16},{16,12},{20,24},{24,20},{28,0},{1,29},{... | collective-permute-start | bytes 196616 | tf_op jit(solution)/shard_map/ppermute | solution.py:319

commit v6 on v5

--- a/solution.py
+++ b/solution.py
@@ -38,14 +38,17 @@
     return lax.div(ctx, 2), lax.rem(ctx, 2)
 
 
-def project_kernel(x_ref, w_hbm, *refs):
-    packs = refs[:5]
-    w_ref, w_sem = refs[5:]
+def project_kernel(x_hbm, w_hbm, *refs):
+    packs = refs[:4]
+    x_ref, w_ref, x_sem, w_sem = refs[4:]
     z, _ = place()
     rows = x_ref.shape[0]
+    x_copy = pltpu.make_async_copy(x_hbm, x_ref, x_sem)
+    x_copy.start()
     copies = [pltpu.make_async_copy(w_hbm.at[k], w_ref.at[k], w_sem.at[k]) for k in range(3)]
     for copy in copies:
         copy.start()
+    x_copy.wait()
     x = x_ref[...].astype(f32)
     scale = lax.rsqrt(jnp.mean(x * x, axis=-1, keepdims=True) + eps)
     q_scale = scale * (HD ** (-0.5) * math.log2(math.e))
@@ -60,19 +63,24 @@
         parts = [jnp.where(upper, parts[i ^ 2], parts[i]) for i in range(4)]
         for pack, part in zip(packs, parts):
             pack[pl.ds(k * rows, rows)] = part
-    packs[4][...] = packs[0][...]
 
 
 def project(tokens, w_qkv):
-    rows = tokens.shape[0]
+    rows, width = tokens.shape
+    hbm = pl.BlockSpec(memory_space=pltpu.HBM)
     vmem = pl.BlockSpec(memory_space=pltpu.VMEM)
     return pl.pallas_call(
         project_kernel,
-        in_specs=[vmem, pl.BlockSpec(memory_space=pltpu.HBM)],
-        out_specs=[vmem] * 5,
-        out_shape=[jax.ShapeDtypeStruct((3 * rows, LANES), bf16)] * 5,
-        scratch_shapes=[pltpu.VMEM(w_qkv.shape, bf16), pltpu.SemaphoreType.DMA((3,))],
-        compiler_params=pltpu.CompilerParams(vmem_limit_bytes=52 * 2**20),
+        in_specs=[hbm] * 2,
+        out_specs=[vmem] * 4,
+        out_shape=[jax.ShapeDtypeStruct((3 * rows, LANES), bf16)] * 4,
+        scratch_shapes=[
+            pltpu.VMEM((rows, width), bf16),
+            pltpu.VMEM(w_qkv.shape, bf16),
+            pltpu.SemaphoreType.DMA(()),
+            pltpu.SemaphoreType.DMA((3,)),
+        ],
+        compiler_params=pltpu.CompilerParams(vmem_limit_bytes=53 * 2**20),
         name="project",
     )(tokens, w_qkv)
 
@@ -289,9 +297,9 @@
 
     w1 = first_way(w_out)
 
-    p0, p1, p2, p3, p0_sent = project(tokens, w_qkv)
+    p0, p1, p2, p3 = project(tokens, w_qkv)
     r2, r3 = swapped(p2, "ctx", 4), swapped(p3, "ctx", 6)
-    c0 = swapped(p0_sent, "ctx", 1)
+    c0 = swapped(p0, "ctx", 1)
     p1, c0 = lax.optimization_barrier((p1, c0))
     r1 = swapped(p1, "ctx", 2)
     c1, c2, c3 = (swapped(part, "ctx", 1) for part in (r1, r2, r3))
@@ -303,7 +311,7 @@
     o2, o3 = attend([r2, r3, p0, r1, c0, c1, c2, c3])
     o0, o1 = attend([p0, r1, r2, r3, c0, c1, c2, c3])
     own = gathered([o0, swapped(o1, "ctx", 2), swapped(o2, "ctx", 4), swapped(o3, "ctx", 6)])
-    own, w1, n3 = lax.optimization_barrier((own, w1, n3))
+    own, n3 = lax.optimization_barrier((own, n3))
     a1, a2 = first_way(own), second_way(own)
     w2 = swapped(w1, "ctx", 1)
     a1, a2, n3 = lax.optimization_barrier((a1, a2, n3))

time: 71.2 us -> 69.2 us (0.972)
  waiting for transfers between devices: 32.4 us -> 29.5 us
  local copies, waits for them, and re-layouts: 1.31 us -> 0.09 us
  Pallas kernels: 16.2 us -> 17.3 us
  starting transfers between devices: 21 us -> 22 us
    ppermute x2, waiting for transfers between devices: 7.74 us -> 5.63 us  [first_way(): return lax.ppermute(value, ('ctx', 'head'), pairs)]
    ppermute x3, starting transfers between devices: 3.05 us -> 4.56 us  [second_way(): return lax.ppermute(value, ('ctx', 'head'), pairs)]
    unnamed x8 -> x6, local copies, waits for them, and re-layouts: 1.24 us -> 0.02 us
    pallas_call x1, Pallas kernels: 3.81 us -> 4.98 us  [project(): pl.pallas_call(project_kernel, in_specs=[hbm] * 2, out_specs=[vmem] * 4,...]
    ppermute x3, waiting for transfers between devices: 3.89 us -> 3 us  [second_way(): return lax.ppermute(value, ('ctx', 'head'), pairs)]
  transfers between devices with their start and end apart: 19 -> 19, of which waited for: 9 -> 10; matrix products, arithmetic and copies ran while one was open for 0% -> 0% of each run, Pallas kernels for 19% -> 22%
where the time goes in v6:
time: 69.2 us; the launch traced here: 69 us
  waiting for transfers between devices  29.5 us (43%)
  starting transfers between devices  22 us (32%)
  Pallas kernels  17.3 us (25%)
    ppermute x13, waiting for transfers between devices, swapped(): return lax.ppermute(value, axis, [(i, i ^ bits) for i in range(count)])  18.6 us
    ppermute x13, starting transfers between devices, swapped(): return lax.ppermute(value, axis, [(i, i ^ bits) for i in range(count)])  11.3 us
    pallas_call x2, Pallas kernels, attend(): pl.pallas_call(attention_kernel, in_specs=[vmem] * len(packs), out_specs=...  7.21 us
    ppermute x2, waiting for transfers between devices, first_way(): return lax.ppermute(value, ('ctx', 'head'), pairs)  5.63 us
    pallas_call x1, Pallas kernels, project(): pl.pallas_call(project_kernel, in_specs=[hbm] * 2, out_specs=[vmem] * 4,...  4.98 us
    ppermute x3, starting transfers between devices, second_way(): return lax.ppermute(value, ('ctx', 'head'), pairs)  4.56 us
    ppermute x2, starting transfers between devices, first_way(): return lax.ppermute(value, ('ctx', 'head'), pairs)  3.54 us
    ppermute x3, waiting for transfers between devices, second_way(): return lax.ppermute(value, ('ctx', 'head'), pairs)  3 us
  transfers between devices with their start and end apart: 19, of which 10 were waited for; matrix products, arithmetic and copies ran while one was open for 0% of the time, Pallas kernels for 22%

profile of v6, /device:TPU:0, one launch (start us, length us, event | category | flops | bytes accessed | tf_op | source)
XLA Modules:
  0.0 69.0 jit_solution(10960580261154702889)
XLA Ops:
  0.0 2.9 %collective-permute-start.4 = (bf16[512,2048]{1,0:T(8,128)(2,1)}, bf16[512,2048]{1,0:T(8,128)(2,1)S(1)}, u32[]{:S(2)}, u32[]{:S(2)}) collective-permute-start(bf16[512,2048]{1,0:T(8,128)(2,1)} %own.1), channel_id=1, source_target_pairs={{0,1},{1,0},{2,3},{3,2},{4,6},{5,7},{6,4},{7,5},{8,9},{9,8},{10,11... | collective-permute-start | bytes 6291464 | tf_op jit(solution)/shard_map/ppermute | solution.py:286
  2.9 5.0 %project.1 = (bf16[768,128]{1,0:T(8,128)(2,1)S(1)}, bf16[768,128]{1,0:T(8,128)(2,1)S(1)}, bf16[768,128]{1,0:T(8,128)(2,1)S(1)}, bf16[768,128]{1,0:T(8,128)(2,1)S(1)}) custom-call(bf16[256,2048]{1,0:T(8,128)(2,1)} %x_ref.1, bf16[3,2048,512]{2,1,0:T(8,128)(2,1)} %w_hbm.1), custom_call_target="tpu_custom_call" | custom-call | tf_op jit(solution)/shard_map/project/pallas_call | solution.py:72
  7.9 0.1 collective-permute-start
  8.0 2.7 %collective-permute-start.2 = (bf16[768,128]{1,0:T(8,128)(2,1)S(1)}, bf16[768,128]{1,0:T(8,128)(2,1)S(1)}, u32[]{:S(2)}, u32[]{:S(2)}) collective-permute-start(bf16[768,128]{1,0:T(8,128)(2,1)S(1)} %get-tuple-element.30), channel_id=1, source_target_pairs={{0,16},{4,20},{8,24},{12,28},{16,0},{20,4},{24,8},{28,12},{1,17},{... | collective-permute-start | bytes 589832 | tf_op jit(solution)/shard_map/ppermute | solution.py:29
  10.7 1.3 %collective-permute-start.3 = (bf16[768,128]{1,0:T(8,128)(2,1)S(1)}, bf16[768,128]{1,0:T(8,128)(2,1)S(1)}, u32[]{:S(2)}, u32[]{:S(2)}) collective-permute-start(bf16[768,128]{1,0:T(8,128)(2,1)S(1)} %get-tuple-element.31), channel_id=1, source_target_pairs={{0,24},{4,28},{8,16},{12,20},{16,8},{20,12},{24,0},{28,4},{1,25},{... | collective-permute-start | bytes 589832 | tf_op jit(solution)/shard_map/ppermute | solution.py:29
  12.0 0.2 collective-permute-start.1
  12.2 12.9 %collective-permute-done.2.refs_2_.refs_0_ = bf16[768,128]{1,0:T(8,128)(2,1)S(1)} collective-permute-done((bf16[768,128]{1,0:T(8,128)(2,1)S(1)}, bf16[768,128]{1,0:T(8,128)(2,1)S(1)}, u32[]{:S(2)}, u32[]{:S(2)}) %collective-permute-start.2) | collective-permute-done | bytes 196640 | tf_op jit(solution)/shard_map/ppermute | solution.py:29
  25.2 0.5 collective-permute-start.7
  25.7 0.4 collective-permute-done.1.refs_1_.refs_3_
  26.0 0.6 collective-permute-done.6.refs_6_
  26.6 0.3 collective-permute-done.7.refs_7_
  26.9 0.7 %collective-permute-done.5.refs_5_ = bf16[768,128]{1,0:T(8,128)(2,1)} collective-permute-done((bf16[768,128]{1,0:T(8,128)(2,1)S(1)}, bf16[768,128]{1,0:T(8,128)(2,1)}, u32[]{:S(2)}, u32[]{:S(2)}) %collective-permute-start.5) | collective-permute-done | bytes 196640 | tf_op jit(solution)/shard_map/ppermute | solution.py:29
  27.7 1.7 %collective-permute-start.11 = (bf16[256,2048]{1,0:T(8,128)(2,1)S(1)}, bf16[256,2048]{1,0:T(8,128)(2,1)S(1)}, u32[]{:S(2)}, u32[]{:S(2)}) collective-permute-start(bf16[256,2048]{1,0:T(8,128)(2,1)S(1)} %constant_dynamic-slice_fusion), channel_id=1, source_target_pairs={{0,2},{1,3},{2,0},{3,1},{4,5},{5,4},{6,7},{7,6},{8,10},{9,11},{10,... | collective-permute-start | bytes 3145736 | tf_op jit(solution)/shard_map/ppermute | solution.py:292
  29.4 3.6 %attend.3 = (bf16[256,128]{1,0:T(8,128)(2,1)S(1)}, bf16[256,128]{1,0:T(8,128)(2,1)S(1)}) custom-call(bf16[768,128]{1,0:T(8,128)(2,1)S(1)} %collective-permute-done.2.refs_2_.refs_0_, bf16[768,128]{1,0:T(8,128)(2,1)S(1)} %collective-permute-done.3.refs_3_.refs_1_, bf16[768,128]{1,0:T(8,128)(2,1)S(1)} %get-tuple-element.27.refs_0_.refs_2_, ...), custom_call_target="tpu_custom_call" | custom-call | tf_op jit(solution)/shard_map/attend/pallas_call | solution.py:129
  33.0 3.7 %collective-permute-start.10 = (bf16[256,128]{1,0:T(8,128)(2,1)S(1)}, bf16[256,128]{1,0:T(8,128)(2,1)S(1)}, u32[]{:S(2)}, u32[]{:S(2)}) collective-permute-start(bf16[256,128]{1,0:T(8,128)(2,1)S(1)} %get-tuple-element.39), channel_id=1, source_target_pairs={{0,24},{4,28},{8,16},{12,20},{16,8},{20,12},{24,0},{28,4},{1,25},{... | collective-permute-start | bytes 196616 | tf_op jit(solution)/shard_map/ppermute | solution.py:29
  36.7 2.1 %collective-permute-start.9 = (bf16[256,128]{1,0:T(8,128)(2,1)S(1)}, bf16[256,128]{1,0:T(8,128)(2,1)S(1)}, u32[]{:S(2)}, u32[]{:S(2)}) collective-permute-start(bf16[256,128]{1,0:T(8,128)(2,1)S(1)} %get-tuple-element.38), channel_id=1, source_target_pairs={{0,16},{4,20},{8,24},{12,28},{16,0},{20,4},{24,8},{28,12},{1,17},{... | collective-permute-start | bytes 196616 | tf_op jit(solution)/shard_map/ppermute | solution.py:29
  38.8 3.6 %attend.2 = (bf16[256,128]{1,0:T(8,128)(2,1)S(1)}, bf16[256,128]{1,0:T(8,128)(2,1)S(1)}) custom-call(bf16[768,128]{1,0:T(8,128)(2,1)S(1)} %get-tuple-element.27.refs_0_.refs_2_, bf16[768,128]{1,0:T(8,128)(2,1)S(1)} %collective-permute-done.1.refs_1_.refs_3_, bf16[768,128]{1,0:T(8,128)(2,1)S(1)} %collective-permute-done.2.refs_2_.refs_0_, ...), custom_call_target="tpu_custom_call" | custom-call | tf_op jit(solution)/shard_map/attend/pallas_call | solution.py:129
  42.4 0.6 collective-permute-start.8
  43.0 1.3 %collective-permute-done.9.refs_2_ = bf16[256,128]{1,0:T(8,128)(2,1)S(1)} collective-permute-done((bf16[256,128]{1,0:T(8,128)(2,1)S(1)}, bf16[256,128]{1,0:T(8,128)(2,1)S(1)}, u32[]{:S(2)}, u32[]{:S(2)}) %collective-permute-start.9) | collective-permute-done | bytes 65568 | tf_op jit(solution)/shard_map/ppermute | solution.py:29
  44.3 2.5 %collective-permute-done.8.refs_1_ = bf16[256,128]{1,0:T(8,128)(2,1)S(1)} collective-permute-done((bf16[256,128]{1,0:T(8,128)(2,1)S(1)}, bf16[256,128]{1,0:T(8,128)(2,1)S(1)}, u32[]{:S(2)}, u32[]{:S(2)}) %collective-permute-start.8) | collective-permute-done | bytes 65568 | tf_op jit(solution)/shard_map/ppermute | solution.py:29
  46.8 0.6 collective-permute-start.12
  47.4 1.4 %collective-permute-start.13 = (bf16[1024,128]{1,0:T(8,128)(2,1)S(1)}, bf16[1024,128]{1,0:T(8,128)(2,1)S(1)}, u32[]{:S(2)}, u32[]{:S(2)}) collective-permute-start(bf16[1024,128]{1,0:T(8,128)(2,1)S(1)} %gathered.1.o0), channel_id=1, source_target_pairs={{0,2},{1,3},{2,0},{3,1},{4,5},{5,4},{6,7},{7,6},{8,10},{9,11},{10,... | collective-permute-start | bytes 786440 | tf_op jit(solution)/shard_map/ppermute | solution.py:292
  48.8 5.6 %collective-permute-done.12.o1 = bf16[1024,128]{1,0:T(8,128)(2,1)S(1)} collective-permute-done((bf16[1024,128]{1,0:T(8,128)(2,1)S(1)}, bf16[1024,128]{1,0:T(8,128)(2,1)S(1)}, u32[]{:S(2)}, u32[]{:S(2)}) %collective-permute-start.12) | collective-permute-done | bytes 262176 | tf_op jit(solution)/shard_map/ppermute | solution.py:286
  54.4 1.4 %collective-permute-start.15 = (bf16[1024,128]{1,0:T(8,128)(2,1)S(1)}, bf16[1024,128]{1,0:T(8,128)(2,1)S(1)}, u32[]{:S(2)}, u32[]{:S(2)}) collective-permute-start(bf16[1024,128]{1,0:T(8,128)(2,1)S(1)} %collective-permute-done.12.o1), channel_id=1, source_target_pairs={{0,2},{1,3},{2,0},{3,1},{4,5},{5,4},{6,7},{7,6},{8,10},{9,11},{10,... | collective-permute-start | bytes 786440 | tf_op jit(solution)/shard_map/ppermute | solution.py:292
  55.9 1.9 %mix.1.total = f32[256,2048]{1,0:T(8,128)S(1)} custom-call(bf16[256,2048]{1,0:T(8,128)(2,1)S(1)} %copy-done.1, bf16[1024,128]{1,0:T(8,128)(2,1)S(1)} %gathered.1.o0, bf16[1024,128]{1,0:T(8,128)(2,1)S(1)} %collective-permute-done.12.o1, bf16[1024,128]{1,0:T(8,128)(2,1)S(1)} %collective-permute-done.13.o2, bf16[512,2048]{1,0:T(8,128)(2,1)S(1)} %copy-done.2, ...), custom_call_target="tpu_custom_call" | custom-call | tf_op jit(solution)/shard_map/mix/pallas_call | solution.py:158
  57.8 3.0 %collective-permute-done.15.o3 = bf16[1024,128]{1,0:T(8,128)(2,1)S(1)} collective-permute-done((bf16[1024,128]{1,0:T(8,128)(2,1)S(1)}, bf16[1024,128]{1,0:T(8,128)(2,1)S(1)}, u32[]{:S(2)}, u32[]{:S(2)}) %collective-permute-start.15) | collective-permute-done | bytes 262176 | tf_op jit(solution)/shard_map/ppermute | solution.py:292
  60.8 1.6 %decode_edges.1 = (bf16[256,2048]{1,0:T(8,128)(2,1)S(1)}, bf16[128,256]{1,0:T(8,128)(2,1)S(1)}, bf16[128,256]{1,0:T(8,128)(2,1)S(1)}) custom-call(f32[256,2048]{1,0:T(8,128)S(1)} %mix.1.total, bf16[1024,128]{1,0:T(8,128)(2,1)S(1)} %collective-permute-done.15.o3, bf16[256,2048]{1,0:T(8,128)(2,1)S(1)} %collective-permute-done.11.n3, ...), custom_call_target="tpu_custom_call" | custom-call | tf_op jit(solution)/shard_map/decode_edges/pallas_call | solution.py:204
  62.5 0.1 collective-permute-start.17
  62.5 2.7 %collective-permute-start.18 = (bf16[128,256]{1,0:T(8,128)(2,1)S(1)}, bf16[128,256]{1,0:T(8,128)(2,1)S(1)}, u32[]{:S(2)}, u32[]{:S(2)}) collective-permute-start(bf16[128,256]{1,0:T(8,128)(2,1)S(1)} %get-tuple-element.48), channel_id=1, source_target_pairs={{0,28},{4,8},{8,4},{12,16},{16,12},{20,24},{24,20},{28,0},{1,29},{... | collective-permute-start | bytes 196616 | tf_op jit(solution)/shard_map/ppermute | solution.py:327
  65.2 0.7 %decode_main.1.main = f32[512,256]{1,0:T(8,128)S(1)} custom-call(bf16[256,2048]{1,0:T(8,128)(2,1)S(1)} %get-tuple-element.46.hidden, bf16[768,2048]{1,0:T(8,128)(2,1)S(1)} %bitcast.7), custom_call_target="tpu_custom_call" | custom-call | tf_op jit(solution)/shard_map/decode_main/pallas_call | solution.py:231
  66.0 2.2 %collective-permute-done.18.outer = bf16[128,256]{1,0:T(8,128)(2,1)S(1)} collective-permute-done((bf16[128,256]{1,0:T(8,128)(2,1)S(1)}, bf16[128,256]{1,0:T(8,128)(2,1)S(1)}, u32[]{:S(2)}, u32[]{:S(2)}) %collective-permute-start.18) | collective-permute-done | bytes 65568 | tf_op jit(solution)/shard_map/ppermute | solution.py:327
  68.2 0.8 %join.1 = f32[512,256]{1,0:T(8,128)} custom-call(f32[512,256]{1,0:T(8,128)S(1)} %decode_main.1.main, bf16[128,256]{1,0:T(8,128)(2,1)S(1)} %collective-permute-done.17.inner, bf16[128,256]{1,0:T(8,128)(2,1)S(1)} %collective-permute-done.18.outer), custom_call_target="tpu_custom_call" | custom-call | tf_op jit(solution)/shard_map/join/pallas_call | solution.py:254
  (21 shorter events, 0.1 us)
Async XLA Ops:
  0.0 27.6 %collective-permute-start.4 = (bf16[512,2048]{1,0:T(8,128)(2,1)}, bf16[512,2048]{1,0:T(8,128)(2,1)S(1)}, u32[]{:S(2)}, u32[]{:S(2)}) collective-permute-start(bf16[512,2048]{1,0:T(8,128)(2,1)} %own.1), channel_id=1, source_target_pairs={{0,1},{1,0},{2,3},{3,2},{4,6},{5,7},{6,4},{7,5},{8,9},{9,8},{10,11... | collective-permute-start | bytes 6291464 | tf_op jit(solution)/shard_map/ppermute | solution.py:286
  7.9 4.1 %collective-permute-start = (bf16[768,128]{1,0:T(8,128)(2,1)S(1)}, bf16[768,128]{1,0:T(8,128)(2,1)S(1)}, u32[]{:S(2)}, u32[]{:S(2)}) collective-permute-start(bf16[768,128]{1,0:T(8,128)(2,1)S(1)} %get-tuple-element.27.refs_0_.refs_2_), channel_id=1, source_target_pairs={{0,4},{4,0},{8,12},{12,8},{16,20},{20,16},{24,28},{28,24},{1,5},{5... | collective-permute-start | bytes 589832 | tf_op jit(solution)/shard_map/ppermute | solution.py:29
  8.0 17.1 %collective-permute-start.2 = (bf16[768,128]{1,0:T(8,128)(2,1)S(1)}, bf16[768,128]{1,0:T(8,128)(2,1)S(1)}, u32[]{:S(2)}, u32[]{:S(2)}) collective-permute-start(bf16[768,128]{1,0:T(8,128)(2,1)S(1)} %get-tuple-element.30), channel_id=1, source_target_pairs={{0,16},{4,20},{8,24},{12,28},{16,0},{20,4},{24,8},{28,12},{1,17},{... | collective-permute-start | bytes 589832 | tf_op jit(solution)/shard_map/ppermute | solution.py:29
  10.7 14.5 %collective-permute-start.3 = (bf16[768,128]{1,0:T(8,128)(2,1)S(1)}, bf16[768,128]{1,0:T(8,128)(2,1)S(1)}, u32[]{:S(2)}, u32[]{:S(2)}) collective-permute-start(bf16[768,128]{1,0:T(8,128)(2,1)S(1)} %get-tuple-element.31), channel_id=1, source_target_pairs={{0,24},{4,28},{8,16},{12,20},{16,8},{20,12},{24,0},{28,4},{1,25},{... | collective-permute-start | bytes 589832 | tf_op jit(solution)/shard_map/ppermute | solution.py:29
  12.0 14.0 %collective-permute-start.1 = (bf16[768,128]{1,0:T(8,128)(2,1)S(1)}, bf16[768,128]{1,0:T(8,128)(2,1)S(1)}, u32[]{:S(2)}, u32[]{:S(2)}) collective-permute-start(bf16[768,128]{1,0:T(8,128)(2,1)S(1)} %get-tuple-element.29), channel_id=1, source_target_pairs={{0,8},{4,12},{8,0},{12,4},{16,24},{20,28},{24,16},{28,20},{1,9},{5... | collective-permute-start | bytes 589832 | tf_op jit(solution)/shard_map/ppermute | solution.py:29
  25.1 1.4 %collective-permute-start.6 = (bf16[768,128]{1,0:T(8,128)(2,1)S(1)}, bf16[768,128]{1,0:T(8,128)(2,1)S(1)}, u32[]{:S(2)}, u32[]{:S(2)}) collective-permute-start(bf16[768,128]{1,0:T(8,128)(2,1)S(1)} %collective-permute-done.2.refs_2_.refs_0_), channel_id=1, source_target_pairs={{0,4},{4,0},{8,12},{12,8},{16,20},{20,16},{24,28},{28,24},{1,5},{5... | collective-permute-start | bytes 589832 | tf_op jit(solution)/shard_map/ppermute | solution.py:29
  25.2 1.7 %collective-permute-start.7 = (bf16[768,128]{1,0:T(8,128)(2,1)S(1)}, bf16[768,128]{1,0:T(8,128)(2,1)S(1)}, u32[]{:S(2)}, u32[]{:S(2)}) collective-permute-start(bf16[768,128]{1,0:T(8,128)(2,1)S(1)} %collective-permute-done.3.refs_3_.refs_1_), channel_id=1, source_target_pairs={{0,4},{4,0},{8,12},{12,8},{16,20},{20,16},{24,28},{28,24},{1,5},{5... | collective-permute-start | bytes 589832 | tf_op jit(solution)/shard_map/ppermute | solution.py:29
  26.0 1.6 %collective-permute-start.5 = (bf16[768,128]{1,0:T(8,128)(2,1)S(1)}, bf16[768,128]{1,0:T(8,128)(2,1)}, u32[]{:S(2)}, u32[]{:S(2)}) collective-permute-start(bf16[768,128]{1,0:T(8,128)(2,1)S(1)} %collective-permute-done.1.refs_1_.refs_3_), channel_id=1, source_target_pairs={{0,4},{4,0},{8,12},{12,8},{16,20},{20,16},{24,28},{28,24},{1,5},{5... | collective-permute-start | bytes 589832 | tf_op jit(solution)/shard_map/ppermute | solution.py:29
  27.7 28.2 %copy-start.1 = (bf16[256,2048]{1,0:T(8,128)(2,1)S(1)}, bf16[256,2048]{1,0:T(8,128)(2,1)}, u32[]{:S(2)}) copy-start(bf16[256,2048]{1,0:T(8,128)(2,1)} %x_ref.1) | copy-start | bytes 3145732
  27.7 28.2 %copy-start.2 = (bf16[512,2048]{1,0:T(8,128)(2,1)S(1)}, bf16[512,2048]{1,0:T(8,128)(2,1)}, u32[]{:S(2)}) copy-start(bf16[512,2048]{1,0:T(8,128)(2,1)} %own.1) | copy-start | bytes 6291460
  27.7 19.1 %collective-permute-start.11 = (bf16[256,2048]{1,0:T(8,128)(2,1)S(1)}, bf16[256,2048]{1,0:T(8,128)(2,1)S(1)}, u32[]{:S(2)}, u32[]{:S(2)}) collective-permute-start(bf16[256,2048]{1,0:T(8,128)(2,1)S(1)} %constant_dynamic-slice_fusion), channel_id=1, source_target_pairs={{0,2},{1,3},{2,0},{3,1},{4,5},{5,4},{6,7},{7,6},{8,10},{9,11},{10,... | collective-permute-start | bytes 3145736 | tf_op jit(solution)/shard_map/ppermute | solution.py:292
  29.4 26.5 %collective-permute-start.14 = (bf16[512,2048]{1,0:T(8,128)(2,1)S(1)}, bf16[512,2048]{1,0:T(8,128)(2,1)S(1)}, u32[]{:S(2)}, u32[]{:S(2)}) collective-permute-start(bf16[512,2048]{1,0:T(8,128)(2,1)S(1)} %collective-permute-done.4.w1), channel_id=1, source_target_pairs={{0,4},{4,0},{8,12},{12,8},{16,20},{20,16},{24,28},{28,24},{1,5},{5... | collective-permute-start | bytes 6291464 | tf_op jit(solution)/shard_map/ppermute | solution.py:29
  33.0 10.0 %collective-permute-start.10 = (bf16[256,128]{1,0:T(8,128)(2,1)S(1)}, bf16[256,128]{1,0:T(8,128)(2,1)S(1)}, u32[]{:S(2)}, u32[]{:S(2)}) collective-permute-start(bf16[256,128]{1,0:T(8,128)(2,1)S(1)} %get-tuple-element.39), channel_id=1, source_target_pairs={{0,24},{4,28},{8,16},{12,20},{16,8},{20,12},{24,0},{28,4},{1,25},{... | collective-permute-start | bytes 196616 | tf_op jit(solution)/shard_map/ppermute | solution.py:29
  36.7 7.6 %collective-permute-start.9 = (bf16[256,128]{1,0:T(8,128)(2,1)S(1)}, bf16[256,128]{1,0:T(8,128)(2,1)S(1)}, u32[]{:S(2)}, u32[]{:S(2)}) collective-permute-start(bf16[256,128]{1,0:T(8,128)(2,1)S(1)} %get-tuple-element.38), channel_id=1, source_target_pairs={{0,16},{4,20},{8,24},{12,28},{16,0},{20,4},{24,8},{28,12},{1,17},{... | collective-permute-start | bytes 196616 | tf_op jit(solution)/shard_map/ppermute | solution.py:29
  42.4 4.3 %collective-permute-start.8 = (bf16[256,128]{1,0:T(8,128)(2,1)S(1)}, bf16[256,128]{1,0:T(8,128)(2,1)S(1)}, u32[]{:S(2)}, u32[]{:S(2)}) collective-permute-start(bf16[256,128]{1,0:T(8,128)(2,1)S(1)} %get-tuple-element.37), channel_id=1, source_target_pairs={{0,8},{4,12},{8,0},{12,4},{16,24},{20,28},{24,16},{28,20},{1,9},{5... | collective-permute-start | bytes 196616 | tf_op jit(solution)/shard_map/ppermute | solution.py:29
  46.8 7.7 %collective-permute-start.12 = (bf16[1024,128]{1,0:T(8,128)(2,1)S(1)}, bf16[1024,128]{1,0:T(8,128)(2,1)S(1)}, u32[]{:S(2)}, u32[]{:S(2)}) collective-permute-start(bf16[1024,128]{1,0:T(8,128)(2,1)S(1)} %gathered.1.o0), channel_id=1, source_target_pairs={{0,1},{1,0},{2,3},{3,2},{4,6},{5,7},{6,4},{7,5},{8,9},{9,8},{10,11... | collective-permute-start | bytes 786440 | tf_op jit(solution)/shard_map/ppermute | solution.py:286
  47.4 7.1 %collective-permute-start.13 = (bf16[1024,128]{1,0:T(8,128)(2,1)S(1)}, bf16[1024,128]{1,0:T(8,128)(2,1)S(1)}, u32[]{:S(2)}, u32[]{:S(2)}) collective-permute-start(bf16[1024,128]{1,0:T(8,128)(2,1)S(1)} %gathered.1.o0), channel_id=1, source_target_pairs={{0,2},{1,3},{2,0},{3,1},{4,5},{5,4},{6,7},{7,6},{8,10},{9,11},{10,... | collective-permute-start | bytes 786440 | tf_op jit(solution)/shard_map/ppermute | solution.py:292
  54.4 6.4 %collective-permute-start.16 = (bf16[256,2048]{1,0:T(8,128)(2,1)S(1)}, bf16[256,2048]{1,0:T(8,128)(2,1)S(1)}, u32[]{:S(2)}, u32[]{:S(2)}) collective-permute-start(bf16[256,2048]{1,0:T(8,128)(2,1)S(1)} %collective-permute-done.11.n3), channel_id=1, source_target_pairs={{0,4},{4,0},{8,12},{12,8},{16,20},{20,16},{24,28},{28,24},{1,5},{5... | collective-permute-start | bytes 3145736 | tf_op jit(solution)/shard_map/ppermute | solution.py:29
  54.4 6.4 %collective-permute-start.15 = (bf16[1024,128]{1,0:T(8,128)(2,1)S(1)}, bf16[1024,128]{1,0:T(8,128)(2,1)S(1)}, u32[]{:S(2)}, u32[]{:S(2)}) collective-permute-start(bf16[1024,128]{1,0:T(8,128)(2,1)S(1)} %collective-permute-done.12.o1), channel_id=1, source_target_pairs={{0,2},{1,3},{2,0},{3,1},{4,5},{5,4},{6,7},{7,6},{8,10},{9,11},{10,... | collective-permute-start | bytes 786440 | tf_op jit(solution)/shard_map/ppermute | solution.py:292
  55.9 4.9 %copy-start = (bf16[2048,12,64]{0,2,1:T(8,128)(2,1)S(1)}, bf16[2048,12,64]{0,2,1:T(8,128)(2,1)}, u32[]{:S(2)}) copy-start(bf16[2048,12,64]{0,2,1:T(8,128)(2,1)} %param.7) | copy-start | bytes 9437188
  62.5 3.5 %collective-permute-start.17 = (bf16[128,256]{1,0:T(8,128)(2,1)S(1)}, bf16[128,256]{1,0:T(8,128)(2,1)S(1)}, u32[]{:S(2)}, u32[]{:S(2)}) collective-permute-start(bf16[128,256]{1,0:T(8,128)(2,1)S(1)} %get-tuple-element.47), channel_id=1, source_target_pairs={{0,4},{4,0},{8,12},{12,8},{16,20},{20,16},{24,28},{28,24},{1,5},{5... | collective-permute-start | bytes 196616 | tf_op jit(solution)/shard_map/ppermute | solution.py:29
  62.5 5.7 %collective-permute-start.18 = (bf16[128,256]{1,0:T(8,128)(2,1)S(1)}, bf16[128,256]{1,0:T(8,128)(2,1)S(1)}, u32[]{:S(2)}, u32[]{:S(2)}) collective-permute-start(bf16[128,256]{1,0:T(8,128)(2,1)S(1)} %get-tuple-element.48), channel_id=1, source_target_pairs={{0,28},{4,8},{8,4},{12,16},{16,12},{20,24},{24,20},{28,0},{1,29},{... | collective-permute-start | bytes 196616 | tf_op jit(solution)/shard_map/ppermute | solution.py:327

commit v7 on v6

--- a/solution.py
+++ b/solution.py
@@ -46,9 +46,10 @@
     x_copy = pltpu.make_async_copy(x_hbm, x_ref, x_sem)
     x_copy.start()
     copies = [pltpu.make_async_copy(w_hbm.at[k], w_ref.at[k], w_sem.at[k]) for k in range(3)]
-    for copy in copies:
-        copy.start()
+    copies[0].start()
     x_copy.wait()
+    copies[1].start()
+    copies[2].start()
     x = x_ref[...].astype(f32)
     scale = lax.rsqrt(jnp.mean(x * x, axis=-1, keepdims=True) + eps)
     q_scale = scale * (HD ** (-0.5) * math.log2(math.e))
@@ -280,6 +281,25 @@
     )(*parts)
 
 
+def halved_kernel(block, half):
+    _, core = place()
+    rows = half.shape[0]
+    half[...] = block[pl.ds(pl.multiple_of(core * rows, rows), rows)]
+
+
+def halved(block):
+    rows, width = block.shape
+    vmem = pl.BlockSpec(memory_space=pltpu.VMEM)
+    return pl.pallas_call(
+        halved_kernel,
+        in_specs=[vmem],
+        out_specs=vmem,
+        out_shape=jax.ShapeDtypeStruct((rows // 2, width), bf16),
+        compiler_params=pltpu.CompilerParams(vmem_limit_bytes=4 * 2**20),
+        name="halved",
+    )(block)
+
+
 def first_way(value):
     count = lax.axis_size("ctx") * lax.axis_size("head")
     pairs = [(i, i ^ (1 if (i // 4) % 2 == 0 else 2)) for i in range(count)]
@@ -304,16 +324,15 @@
     r1 = swapped(p1, "ctx", 2)
     c1, c2, c3 = (swapped(part, "ctx", 1) for part in (r1, r2, r3))
     w1, c1, c2, c3 = lax.optimization_barrier((w1, c1, c2, c3))
-    size = w_out.shape[0] // 2
-    half = lax.dynamic_slice_in_dim(w1, lax.rem(lax.axis_index("ctx"), 2) * size, size, 0)
-    n3 = second_way(half)
+    n3 = second_way(halved(w1))
 
     o2, o3 = attend([r2, r3, p0, r1, c0, c1, c2, c3])
+    w1, o2, o3 = lax.optimization_barrier((w1, o2, o3))
+    w2 = swapped(w1, "ctx", 1)
     o0, o1 = attend([p0, r1, r2, r3, c0, c1, c2, c3])
     own = gathered([o0, swapped(o1, "ctx", 2), swapped(o2, "ctx", 4), swapped(o3, "ctx", 6)])
     own, n3 = lax.optimization_barrier((own, n3))
     a1, a2 = first_way(own), second_way(own)
-    w2 = swapped(w1, "ctx", 1)
     a1, a2, n3 = lax.optimization_barrier((a1, a2, n3))
     a3 = second_way(a1)
     f3 = swapped(n3, "ctx", 1)

time: 69.2 us -> 67.3 us (0.973)
  Pallas kernels: 17.3 us -> 15 us
  starting transfers between devices: 22 us -> 23.2 us
  waiting for transfers between devices: 29.5 us -> 28.8 us
    pallas_call x2, Pallas kernels: 7.21 us -> 5.38 us  [attend(): pl.pallas_call(attention_kernel, in_specs=[vmem] * len(packs), out_specs=...]
    ppermute x1, starting transfers between devices: 2.67 us -> 3.95 us  [fast_body(): outer = lax.ppermute(outer, 'ctx', pairs)]
    ppermute x1, waiting for transfers between devices: 2.23 us -> 1.2 us  [fast_body(): outer = lax.ppermute(outer, 'ctx', pairs)]
    ppermute x2, starting transfers between devices: 3.54 us -> 4.32 us  [first_way(): return lax.ppermute(value, ('ctx', 'head'), pairs)]
  transfers between devices with their start and end apart: 19 -> 19, of which waited for: 10 -> 11; matrix products, arithmetic and copies ran while one was open for 0% -> 0% of each run, Pallas kernels for 22% -> 19%
where the time goes in v7:
time: 67.3 us; the launch traced here: 67.1 us
  waiting for transfers between devices  28.8 us (43%)
  starting transfers between devices  23.2 us (34%)
  Pallas kernels  15 us (22%)
    ppermute x13, waiting for transfers between devices, swapped(): return lax.ppermute(value, axis, [(i, i ^ bits) for i in range(count)])  18.5 us
    ppermute x13, starting transfers between devices, swapped(): return lax.ppermute(value, axis, [(i, i ^ bits) for i in range(count)])  10.6 us
    ppermute x2, waiting for transfers between devices, first_way(): return lax.ppermute(value, ('ctx', 'head'), pairs)  6.31 us
    pallas_call x2, Pallas kernels, attend(): pl.pallas_call(attention_kernel, in_specs=[vmem] * len(packs), out_specs=...  5.38 us
    pallas_call x1, Pallas kernels, project(): pl.pallas_call(project_kernel, in_specs=[hbm] * 2, out_specs=[vmem] * 4,...  4.43 us
    ppermute x2, starting transfers between devices, first_way(): return lax.ppermute(value, ('ctx', 'head'), pairs)  4.32 us
    ppermute x3, starting transfers between devices, second_way(): return lax.ppermute(value, ('ctx', 'head'), pairs)  4.29 us
    ppermute x1, starting transfers between devices, fast_body(): outer = lax.ppermute(outer, 'ctx', pairs)  3.95 us
  transfers between devices with their start and end apart: 19, of which 11 were waited for; matrix products, arithmetic and copies ran while one was open for 0% of the time, Pallas kernels for 19%

profile of v7, /device:TPU:0, one launch (start us, length us, event | category | flops | bytes accessed | tf_op | source)
XLA Modules:
  0.0 67.1 jit_solution(4002528609896575765)
XLA Ops:
  0.0 2.9 %collective-permute-start.4 = (bf16[512,2048]{1,0:T(8,128)(2,1)}, bf16[512,2048]{1,0:T(8,128)(2,1)S(1)}, u32[]{:S(2)}, u32[]{:S(2)}) collective-permute-start(bf16[512,2048]{1,0:T(8,128)(2,1)} %own.1), channel_id=1, source_target_pairs={{0,1},{1,0},{2,3},{3,2},{4,6},{5,7},{6,4},{7,5},{8,9},{9,8},{10,11... | collective-permute-start | bytes 6291464 | tf_op jit(solution)/shard_map/ppermute | solution.py:306
  2.9 4.4 %project.1 = (bf16[768,128]{1,0:T(8,128)(2,1)S(1)}, bf16[768,128]{1,0:T(8,128)(2,1)S(1)}, bf16[768,128]{1,0:T(8,128)(2,1)S(1)}, bf16[768,128]{1,0:T(8,128)(2,1)S(1)}) custom-call(bf16[256,2048]{1,0:T(8,128)(2,1)} %x_ref.1, bf16[3,2048,512]{2,1,0:T(8,128)(2,1)} %w_hbm.1), custom_call_target="tpu_custom_call" | custom-call | tf_op jit(solution)/shard_map/project/pallas_call | solution.py:73
  7.5 2.7 %collective-permute-start.2 = (bf16[768,128]{1,0:T(8,128)(2,1)S(1)}, bf16[768,128]{1,0:T(8,128)(2,1)S(1)}, u32[]{:S(2)}, u32[]{:S(2)}) collective-permute-start(bf16[768,128]{1,0:T(8,128)(2,1)S(1)} %get-tuple-element.33), channel_id=1, source_target_pairs={{0,16},{4,20},{8,24},{12,28},{16,0},{20,4},{24,8},{28,12},{1,17},{... | collective-permute-start | bytes 589832 | tf_op jit(solution)/shard_map/ppermute | solution.py:29
  10.1 1.3 %collective-permute-start.3 = (bf16[768,128]{1,0:T(8,128)(2,1)S(1)}, bf16[768,128]{1,0:T(8,128)(2,1)S(1)}, u32[]{:S(2)}, u32[]{:S(2)}) collective-permute-start(bf16[768,128]{1,0:T(8,128)(2,1)S(1)} %get-tuple-element.34), channel_id=1, source_target_pairs={{0,24},{4,28},{8,16},{12,20},{16,8},{20,12},{24,0},{28,4},{1,25},{... | collective-permute-start | bytes 589832 | tf_op jit(solution)/shard_map/ppermute | solution.py:29
  11.5 0.2 collective-permute-start.1
  11.7 12.9 %collective-permute-done.2.refs_2_.refs_0_ = bf16[768,128]{1,0:T(8,128)(2,1)S(1)} collective-permute-done((bf16[768,128]{1,0:T(8,128)(2,1)S(1)}, bf16[768,128]{1,0:T(8,128)(2,1)S(1)}, u32[]{:S(2)}, u32[]{:S(2)}) %collective-permute-start.2) | collective-permute-done | bytes 196640 | tf_op jit(solution)/shard_map/ppermute | solution.py:29
  24.6 0.5 collective-permute-start.7
  25.1 0.4 collective-permute-done.1.refs_1_.refs_3_
  25.5 0.6 collective-permute-done.6.refs_6_
  26.0 0.3 collective-permute-done.7.refs_7_
  26.3 0.6 collective-permute-done.5.refs_5_
  26.9 0.2 collective-permute-done.4.block.w1
  27.3 2.1 %collective-permute-start.11 = (bf16[256,2048]{1,0:T(8,128)(2,1)S(1)}, bf16[256,2048]{1,0:T(8,128)(2,1)S(1)}, u32[]{:S(2)}, u32[]{:S(2)}) collective-permute-start(bf16[256,2048]{1,0:T(8,128)(2,1)S(1)} %halved.1), channel_id=1, source_target_pairs={{0,2},{1,3},{2,0},{3,1},{4,5},{5,4},{6,7},{7,6},{8,10},{9,11},{10,... | collective-permute-start | bytes 3145736 | tf_op jit(solution)/shard_map/ppermute | solution.py:312
  29.4 2.7 %attend.3 = (bf16[256,128]{1,0:T(8,128)(2,1)S(1)}, bf16[256,128]{1,0:T(8,128)(2,1)S(1)}) custom-call(bf16[768,128]{1,0:T(8,128)(2,1)S(1)} %collective-permute-done.2.refs_2_.refs_0_, bf16[768,128]{1,0:T(8,128)(2,1)S(1)} %collective-permute-done.3.refs_3_.refs_1_, bf16[768,128]{1,0:T(8,128)(2,1)S(1)} %get-tuple-element.30.refs_0_.refs_2_, ...), custom_call_target="tpu_custom_call" | custom-call | tf_op jit(solution)/shard_map/attend/pallas_call | solution.py:130
  32.1 0.1 collective-permute-start.14
  32.2 3.7 %collective-permute-start.10 = (bf16[256,128]{1,0:T(8,128)(2,1)S(1)}, bf16[256,128]{1,0:T(8,128)(2,1)S(1)}, u32[]{:S(2)}, u32[]{:S(2)}) collective-permute-start(bf16[256,128]{1,0:T(8,128)(2,1)S(1)} %get-tuple-element.45), channel_id=1, source_target_pairs={{0,24},{4,28},{8,16},{12,20},{16,8},{20,12},{24,0},{28,4},{1,25},{... | collective-permute-start | bytes 196616 | tf_op jit(solution)/shard_map/ppermute | solution.py:29
  35.8 1.5 %collective-permute-start.9 = (bf16[256,128]{1,0:T(8,128)(2,1)S(1)}, bf16[256,128]{1,0:T(8,128)(2,1)S(1)}, u32[]{:S(2)}, u32[]{:S(2)}) collective-permute-start(bf16[256,128]{1,0:T(8,128)(2,1)S(1)} %get-tuple-element.44), channel_id=1, source_target_pairs={{0,16},{4,20},{8,24},{12,28},{16,0},{20,4},{24,8},{28,12},{1,17},{... | collective-permute-start | bytes 196616 | tf_op jit(solution)/shard_map/ppermute | solution.py:29
  37.3 2.7 %attend.2 = (bf16[256,128]{1,0:T(8,128)(2,1)S(1)}, bf16[256,128]{1,0:T(8,128)(2,1)S(1)}) custom-call(bf16[768,128]{1,0:T(8,128)(2,1)S(1)} %get-tuple-element.30.refs_0_.refs_2_, bf16[768,128]{1,0:T(8,128)(2,1)S(1)} %collective-permute-done.1.refs_1_.refs_3_, bf16[768,128]{1,0:T(8,128)(2,1)S(1)} %collective-permute-done.2.refs_2_.refs_0_, ...), custom_call_target="tpu_custom_call" | custom-call | tf_op jit(solution)/shard_map/attend/pallas_call | solution.py:130
  40.0 0.6 collective-permute-start.8
  40.5 2.2 %collective-permute-done.9.refs_2_ = bf16[256,128]{1,0:T(8,128)(2,1)S(1)} collective-permute-done((bf16[256,128]{1,0:T(8,128)(2,1)S(1)}, bf16[256,128]{1,0:T(8,128)(2,1)S(1)}, u32[]{:S(2)}, u32[]{:S(2)}) %collective-permute-start.9) | collective-permute-done | bytes 65568 | tf_op jit(solution)/shard_map/ppermute | solution.py:29
  42.7 1.6 %collective-permute-done.8.refs_1_ = bf16[256,128]{1,0:T(8,128)(2,1)S(1)} collective-permute-done((bf16[256,128]{1,0:T(8,128)(2,1)S(1)}, bf16[256,128]{1,0:T(8,128)(2,1)S(1)}, u32[]{:S(2)}, u32[]{:S(2)}) %collective-permute-start.8) | collective-permute-done | bytes 65568 | tf_op jit(solution)/shard_map/ppermute | solution.py:29
  44.3 1.4 %collective-permute-start.12 = (bf16[1024,128]{1,0:T(8,128)(2,1)S(1)}, bf16[1024,128]{1,0:T(8,128)(2,1)S(1)}, u32[]{:S(2)}, u32[]{:S(2)}) collective-permute-start(bf16[1024,128]{1,0:T(8,128)(2,1)S(1)} %gathered.1.o0), channel_id=1, source_target_pairs={{0,1},{1,0},{2,3},{3,2},{4,6},{5,7},{6,4},{7,5},{8,9},{9,8},{10,11... | collective-permute-start | bytes 786440 | tf_op jit(solution)/shard_map/ppermute | solution.py:306
  45.7 0.5 collective-permute-start.13
  46.2 6.1 %collective-permute-done.12.o1 = bf16[1024,128]{1,0:T(8,128)(2,1)S(1)} collective-permute-done((bf16[1024,128]{1,0:T(8,128)(2,1)S(1)}, bf16[1024,128]{1,0:T(8,128)(2,1)S(1)}, u32[]{:S(2)}, u32[]{:S(2)}) %collective-permute-start.12) | collective-permute-done | bytes 262176 | tf_op jit(solution)/shard_map/ppermute | solution.py:306
  52.3 1.7 %collective-permute-start.15 = (bf16[1024,128]{1,0:T(8,128)(2,1)S(1)}, bf16[1024,128]{1,0:T(8,128)(2,1)S(1)}, u32[]{:S(2)}, u32[]{:S(2)}) collective-permute-start(bf16[1024,128]{1,0:T(8,128)(2,1)S(1)} %collective-permute-done.12.o1), channel_id=1, source_target_pairs={{0,2},{1,3},{2,0},{3,1},{4,5},{5,4},{6,7},{7,6},{8,10},{9,11},{10,... | collective-permute-start | bytes 786440 | tf_op jit(solution)/shard_map/ppermute | solution.py:312
  54.0 1.9 %mix.1.total = f32[256,2048]{1,0:T(8,128)S(1)} custom-call(bf16[256,2048]{1,0:T(8,128)(2,1)S(1)} %copy-done.1, bf16[1024,128]{1,0:T(8,128)(2,1)S(1)} %gathered.1.o0, bf16[1024,128]{1,0:T(8,128)(2,1)S(1)} %collective-permute-done.12.o1, bf16[1024,128]{1,0:T(8,128)(2,1)S(1)} %collective-permute-done.13.o2, bf16[512,2048]{1,0:T(8,128)(2,1)S(1)} %copy-done.2, ...), custom_call_target="tpu_custom_call" | custom-call | tf_op jit(solution)/shard_map/mix/pallas_call | solution.py:159
  55.9 2.8 %collective-permute-done.15.o3 = bf16[1024,128]{1,0:T(8,128)(2,1)S(1)} collective-permute-done((bf16[1024,128]{1,0:T(8,128)(2,1)S(1)}, bf16[1024,128]{1,0:T(8,128)(2,1)S(1)}, u32[]{:S(2)}, u32[]{:S(2)}) %collective-permute-start.15) | collective-permute-done | bytes 262176 | tf_op jit(solution)/shard_map/ppermute | solution.py:312
  58.7 1.6 %decode_edges.1 = (bf16[256,2048]{1,0:T(8,128)(2,1)S(1)}, bf16[128,256]{1,0:T(8,128)(2,1)S(1)}, bf16[128,256]{1,0:T(8,128)(2,1)S(1)}) custom-call(f32[256,2048]{1,0:T(8,128)S(1)} %mix.1.total, bf16[1024,128]{1,0:T(8,128)(2,1)S(1)} %collective-permute-done.15.o3, bf16[256,2048]{1,0:T(8,128)(2,1)S(1)} %collective-permute-done.11.n3, ...), custom_call_target="tpu_custom_call" | custom-call | tf_op jit(solution)/shard_map/decode_edges/pallas_call | solution.py:205
  60.4 4.0 %collective-permute-start.18 = (bf16[128,256]{1,0:T(8,128)(2,1)S(1)}, bf16[128,256]{1,0:T(8,128)(2,1)S(1)}, u32[]{:S(2)}, u32[]{:S(2)}) collective-permute-start(bf16[128,256]{1,0:T(8,128)(2,1)S(1)} %get-tuple-element.54), channel_id=1, source_target_pairs={{0,28},{4,8},{8,4},{12,16},{16,12},{20,24},{24,20},{28,0},{1,29},{... | collective-permute-start | bytes 196616 | tf_op jit(solution)/shard_map/ppermute | solution.py:346
  64.3 0.7 %decode_main.1.main = f32[512,256]{1,0:T(8,128)S(1)} custom-call(bf16[256,2048]{1,0:T(8,128)(2,1)S(1)} %get-tuple-element.52.hidden, bf16[768,2048]{1,0:T(8,128)(2,1)S(1)} %bitcast.7), custom_call_target="tpu_custom_call" | custom-call | tf_op jit(solution)/shard_map/decode_main/pallas_call | solution.py:232
  65.1 1.2 %collective-permute-done.18.outer = bf16[128,256]{1,0:T(8,128)(2,1)S(1)} collective-permute-done((bf16[128,256]{1,0:T(8,128)(2,1)S(1)}, bf16[128,256]{1,0:T(8,128)(2,1)S(1)}, u32[]{:S(2)}, u32[]{:S(2)}) %collective-permute-start.18) | collective-permute-done | bytes 65568 | tf_op jit(solution)/shard_map/ppermute | solution.py:346
  66.3 0.8 %join.1 = f32[512,256]{1,0:T(8,128)} custom-call(f32[512,256]{1,0:T(8,128)S(1)} %decode_main.1.main, bf16[128,256]{1,0:T(8,128)(2,1)S(1)} %collective-permute-done.17.inner, bf16[128,256]{1,0:T(8,128)(2,1)S(1)} %collective-permute-done.18.outer), custom_call_target="tpu_custom_call" | custom-call | tf_op jit(solution)/shard_map/join/pallas_call | solution.py:255
  (21 shorter events, 0.3 us)
Async XLA Ops:
  0.0 27.2 %collective-permute-start.4 = (bf16[512,2048]{1,0:T(8,128)(2,1)}, bf16[512,2048]{1,0:T(8,128)(2,1)S(1)}, u32[]{:S(2)}, u32[]{:S(2)}) collective-permute-start(bf16[512,2048]{1,0:T(8,128)(2,1)} %own.1), channel_id=1, source_target_pairs={{0,1},{1,0},{2,3},{3,2},{4,6},{5,7},{6,4},{7,5},{8,9},{9,8},{10,11... | collective-permute-start | bytes 6291464 | tf_op jit(solution)/shard_map/ppermute | solution.py:306
  7.4 4.1 %collective-permute-start = (bf16[768,128]{1,0:T(8,128)(2,1)S(1)}, bf16[768,128]{1,0:T(8,128)(2,1)S(1)}, u32[]{:S(2)}, u32[]{:S(2)}) collective-permute-start(bf16[768,128]{1,0:T(8,128)(2,1)S(1)} %get-tuple-element.30.refs_0_.refs_2_), channel_id=1, source_target_pairs={{0,4},{4,0},{8,12},{12,8},{16,20},{20,16},{24,28},{28,24},{1,5},{5... | collective-permute-start | bytes 589832 | tf_op jit(solution)/shard_map/ppermute | solution.py:29
  7.5 17.1 %collective-permute-start.2 = (bf16[768,128]{1,0:T(8,128)(2,1)S(1)}, bf16[768,128]{1,0:T(8,128)(2,1)S(1)}, u32[]{:S(2)}, u32[]{:S(2)}) collective-permute-start(bf16[768,128]{1,0:T(8,128)(2,1)S(1)} %get-tuple-element.33), channel_id=1, source_target_pairs={{0,16},{4,20},{8,24},{12,28},{16,0},{20,4},{24,8},{28,12},{1,17},{... | collective-permute-start | bytes 589832 | tf_op jit(solution)/shard_map/ppermute | solution.py:29
  10.1 14.5 %collective-permute-start.3 = (bf16[768,128]{1,0:T(8,128)(2,1)S(1)}, bf16[768,128]{1,0:T(8,128)(2,1)S(1)}, u32[]{:S(2)}, u32[]{:S(2)}) collective-permute-start(bf16[768,128]{1,0:T(8,128)(2,1)S(1)} %get-tuple-element.34), channel_id=1, source_target_pairs={{0,24},{4,28},{8,16},{12,20},{16,8},{20,12},{24,0},{28,4},{1,25},{... | collective-permute-start | bytes 589832 | tf_op jit(solution)/shard_map/ppermute | solution.py:29
  11.5 14.0 %collective-permute-start.1 = (bf16[768,128]{1,0:T(8,128)(2,1)S(1)}, bf16[768,128]{1,0:T(8,128)(2,1)S(1)}, u32[]{:S(2)}, u32[]{:S(2)}) collective-permute-start(bf16[768,128]{1,0:T(8,128)(2,1)S(1)} %get-tuple-element.32), channel_id=1, source_target_pairs={{0,8},{4,12},{8,0},{12,4},{16,24},{20,28},{24,16},{28,20},{1,9},{5... | collective-permute-start | bytes 589832 | tf_op jit(solution)/shard_map/ppermute | solution.py:29
  24.6 1.4 %collective-permute-start.6 = (bf16[768,128]{1,0:T(8,128)(2,1)S(1)}, bf16[768,128]{1,0:T(8,128)(2,1)S(1)}, u32[]{:S(2)}, u32[]{:S(2)}) collective-permute-start(bf16[768,128]{1,0:T(8,128)(2,1)S(1)} %collective-permute-done.2.refs_2_.refs_0_), channel_id=1, source_target_pairs={{0,4},{4,0},{8,12},{12,8},{16,20},{20,16},{24,28},{28,24},{1,5},{5... | collective-permute-start | bytes 589832 | tf_op jit(solution)/shard_map/ppermute | solution.py:29
  24.6 1.7 %collective-permute-start.7 = (bf16[768,128]{1,0:T(8,128)(2,1)S(1)}, bf16[768,128]{1,0:T(8,128)(2,1)S(1)}, u32[]{:S(2)}, u32[]{:S(2)}) collective-permute-start(bf16[768,128]{1,0:T(8,128)(2,1)S(1)} %collective-permute-done.3.refs_3_.refs_1_), channel_id=1, source_target_pairs={{0,4},{4,0},{8,12},{12,8},{16,20},{20,16},{24,28},{28,24},{1,5},{5... | collective-permute-start | bytes 589832 | tf_op jit(solution)/shard_map/ppermute | solution.py:29
  25.5 1.4 %collective-permute-start.5 = (bf16[768,128]{1,0:T(8,128)(2,1)S(1)}, bf16[768,128]{1,0:T(8,128)(2,1)S(1)}, u32[]{:S(2)}, u32[]{:S(2)}) collective-permute-start(bf16[768,128]{1,0:T(8,128)(2,1)S(1)} %collective-permute-done.1.refs_1_.refs_3_), channel_id=1, source_target_pairs={{0,4},{4,0},{8,12},{12,8},{16,20},{20,16},{24,28},{28,24},{1,5},{5... | collective-permute-start | bytes 589832 | tf_op jit(solution)/shard_map/ppermute | solution.py:29
  27.2 26.7 %copy-start.1 = (bf16[256,2048]{1,0:T(8,128)(2,1)S(1)}, bf16[256,2048]{1,0:T(8,128)(2,1)}, u32[]{:S(2)}) copy-start(bf16[256,2048]{1,0:T(8,128)(2,1)} %x_ref.1) | copy-start | bytes 3145732
  27.2 26.7 %copy-start.2 = (bf16[512,2048]{1,0:T(8,128)(2,1)S(1)}, bf16[512,2048]{1,0:T(8,128)(2,1)}, u32[]{:S(2)}) copy-start(bf16[512,2048]{1,0:T(8,128)(2,1)} %own.1) | copy-start | bytes 6291460
  27.3 17.1 %collective-permute-start.11 = (bf16[256,2048]{1,0:T(8,128)(2,1)S(1)}, bf16[256,2048]{1,0:T(8,128)(2,1)S(1)}, u32[]{:S(2)}, u32[]{:S(2)}) collective-permute-start(bf16[256,2048]{1,0:T(8,128)(2,1)S(1)} %halved.1), channel_id=1, source_target_pairs={{0,2},{1,3},{2,0},{3,1},{4,5},{5,4},{6,7},{7,6},{8,10},{9,11},{10,... | collective-permute-start | bytes 3145736 | tf_op jit(solution)/shard_map/ppermute | solution.py:312
  32.1 21.9 %collective-permute-start.14 = (bf16[512,2048]{1,0:T(8,128)(2,1)S(1)}, bf16[512,2048]{1,0:T(8,128)(2,1)S(1)}, u32[]{:S(2)}, u32[]{:S(2)}) collective-permute-start(bf16[512,2048]{1,0:T(8,128)(2,1)S(1)} %collective-permute-done.4.block.w1), channel_id=1, source_target_pairs={{0,4},{4,0},{8,12},{12,8},{16,20},{20,16},{24,28},{28,24},{1,5},{5... | collective-permute-start | bytes 6291464 | tf_op jit(solution)/shard_map/ppermute | solution.py:29
  32.2 8.4 %collective-permute-start.10 = (bf16[256,128]{1,0:T(8,128)(2,1)S(1)}, bf16[256,128]{1,0:T(8,128)(2,1)S(1)}, u32[]{:S(2)}, u32[]{:S(2)}) collective-permute-start(bf16[256,128]{1,0:T(8,128)(2,1)S(1)} %get-tuple-element.45), channel_id=1, source_target_pairs={{0,24},{4,28},{8,16},{12,20},{16,8},{20,12},{24,0},{28,4},{1,25},{... | collective-permute-start | bytes 196616 | tf_op jit(solution)/shard_map/ppermute | solution.py:29
  35.8 6.9 %collective-permute-start.9 = (bf16[256,128]{1,0:T(8,128)(2,1)S(1)}, bf16[256,128]{1,0:T(8,128)(2,1)S(1)}, u32[]{:S(2)}, u32[]{:S(2)}) collective-permute-start(bf16[256,128]{1,0:T(8,128)(2,1)S(1)} %get-tuple-element.44), channel_id=1, source_target_pairs={{0,16},{4,20},{8,24},{12,28},{16,0},{20,4},{24,8},{28,12},{1,17},{... | collective-permute-start | bytes 196616 | tf_op jit(solution)/shard_map/ppermute | solution.py:29
  40.0 4.3 %collective-permute-start.8 = (bf16[256,128]{1,0:T(8,128)(2,1)S(1)}, bf16[256,128]{1,0:T(8,128)(2,1)S(1)}, u32[]{:S(2)}, u32[]{:S(2)}) collective-permute-start(bf16[256,128]{1,0:T(8,128)(2,1)S(1)} %get-tuple-element.40), channel_id=1, source_target_pairs={{0,8},{4,12},{8,0},{12,4},{16,24},{20,28},{24,16},{28,20},{1,9},{5... | collective-permute-start | bytes 196616 | tf_op jit(solution)/shard_map/ppermute | solution.py:29
  44.3 8.0 %collective-permute-start.12 = (bf16[1024,128]{1,0:T(8,128)(2,1)S(1)}, bf16[1024,128]{1,0:T(8,128)(2,1)S(1)}, u32[]{:S(2)}, u32[]{:S(2)}) collective-permute-start(bf16[1024,128]{1,0:T(8,128)(2,1)S(1)} %gathered.1.o0), channel_id=1, source_target_pairs={{0,1},{1,0},{2,3},{3,2},{4,6},{5,7},{6,4},{7,5},{8,9},{9,8},{10,11... | collective-permute-start | bytes 786440 | tf_op jit(solution)/shard_map/ppermute | solution.py:306
  45.7 6.6 %collective-permute-start.13 = (bf16[1024,128]{1,0:T(8,128)(2,1)S(1)}, bf16[1024,128]{1,0:T(8,128)(2,1)S(1)}, u32[]{:S(2)}, u32[]{:S(2)}) collective-permute-start(bf16[1024,128]{1,0:T(8,128)(2,1)S(1)} %gathered.1.o0), channel_id=1, source_target_pairs={{0,2},{1,3},{2,0},{3,1},{4,5},{5,4},{6,7},{7,6},{8,10},{9,11},{10,... | collective-permute-start | bytes 786440 | tf_op jit(solution)/shard_map/ppermute | solution.py:312
  52.3 6.4 %collective-permute-start.16 = (bf16[256,2048]{1,0:T(8,128)(2,1)S(1)}, bf16[256,2048]{1,0:T(8,128)(2,1)S(1)}, u32[]{:S(2)}, u32[]{:S(2)}) collective-permute-start(bf16[256,2048]{1,0:T(8,128)(2,1)S(1)} %collective-permute-done.11.n3), channel_id=1, source_target_pairs={{0,4},{4,0},{8,12},{12,8},{16,20},{20,16},{24,28},{28,24},{1,5},{5... | collective-permute-start | bytes 3145736 | tf_op jit(solution)/shard_map/ppermute | solution.py:29
  52.3 6.4 %collective-permute-start.15 = (bf16[1024,128]{1,0:T(8,128)(2,1)S(1)}, bf16[1024,128]{1,0:T(8,128)(2,1)S(1)}, u32[]{:S(2)}, u32[]{:S(2)}) collective-permute-start(bf16[1024,128]{1,0:T(8,128)(2,1)S(1)} %collective-permute-done.12.o1), channel_id=1, source_target_pairs={{0,2},{1,3},{2,0},{3,1},{4,5},{5,4},{6,7},{7,6},{8,10},{9,11},{10,... | collective-permute-start | bytes 786440 | tf_op jit(solution)/shard_map/ppermute | solution.py:312
  54.0 4.7 %copy-start = (bf16[2048,12,64]{0,2,1:T(8,128)(2,1)S(1)}, bf16[2048,12,64]{0,2,1:T(8,128)(2,1)}, u32[]{:S(2)}) copy-start(bf16[2048,12,64]{0,2,1:T(8,128)(2,1)} %param.7) | copy-start | bytes 9437188
  60.3 4.8 %collective-permute-start.17 = (bf16[128,256]{1,0:T(8,128)(2,1)S(1)}, bf16[128,256]{1,0:T(8,128)(2,1)S(1)}, u32[]{:S(2)}, u32[]{:S(2)}) collective-permute-start(bf16[128,256]{1,0:T(8,128)(2,1)S(1)} %get-tuple-element.53), channel_id=1, source_target_pairs={{0,4},{4,0},{8,12},{12,8},{16,20},{20,16},{24,28},{28,24},{1,5},{5... | collective-permute-start | bytes 196616 | tf_op jit(solution)/shard_map/ppermute | solution.py:29
  60.4 5.9 %collective-permute-start.18 = (bf16[128,256]{1,0:T(8,128)(2,1)S(1)}, bf16[128,256]{1,0:T(8,128)(2,1)S(1)}, u32[]{:S(2)}, u32[]{:S(2)}) collective-permute-start(bf16[128,256]{1,0:T(8,128)(2,1)S(1)} %get-tuple-element.54), channel_id=1, source_target_pairs={{0,28},{4,8},{8,4},{12,16},{16,12},{20,24},{24,20},{28,0},{1,29},{... | collective-permute-start | bytes 196616 | tf_op jit(solution)/shard_map/ppermute | solution.py:346

commit v8 on v7

--- a/solution.py
+++ b/solution.py
@@ -86,56 +86,46 @@
     )(tokens, w_qkv)
 
 
-def attention_kernel(*refs):
-    packs, outs = refs[:8], refs[8:10]
-    k_all, v_lo, v_hi, q_all = refs[10:]
-    rows = packs[0].shape[0] // 3
+def attention_kernel(count, *refs):
+    queries, packs, outs = refs[:count], refs[count : count + 8], refs[count + 8 :]
+    rows = outs[0].shape[0]
     low = lax.broadcasted_iota(jnp.int32, (1, LANES), 1) < HD
     one = jnp.ones((), bf16)
     zero = jnp.zeros((), bf16)
-    for i, pack in enumerate(packs):
-        part = pl.ds(i * rows, rows)
-        k_all[part] = pack[rows : 2 * rows]
-        v = pack[2 * rows :]
-        v_lo[part] = jnp.where(low, v, one)
-        v_hi[part] = jnp.where(low, one, v)
-    for i in range(2):
-        q_all[pl.ds(i * rows, rows)] = packs[i][:rows]
-
-    def score(q):
-        return lax.dot_general(
-            q, k_all[...], (((1,), (1,)), ((), ())), preferred_element_type=f32
-        )
+    q = jnp.concatenate([pack[:rows] for pack in queries], axis=0)
+    k = jnp.concatenate([pack[rows : 2 * rows] for pack in packs], axis=0)
+    v = jnp.concatenate([pack[2 * rows :] for pack in packs], axis=0)
+
+    def score(part):
+        return lax.dot_general(part, k, (((1,), (1,)), ((), ())), preferred_element_type=f32)
 
     def weigh(scores):
         return jnp.exp2(scores - jnp.max(scores, axis=-1, keepdims=True)).astype(bf16)
 
-    q = q_all[...]
     lo_scores = score(jnp.where(low, q, zero))
     hi_scores = score(jnp.where(low, zero, q))
     lo_weights, hi_weights = weigh(lo_scores), weigh(hi_scores)
-    lo = jnp.dot(lo_weights, v_lo[...], preferred_element_type=f32)
-    hi = jnp.dot(hi_weights, v_hi[...], preferred_element_type=f32)
+    lo = jnp.dot(lo_weights, jnp.where(low, v, one), preferred_element_type=f32)
+    hi = jnp.dot(hi_weights, jnp.where(low, one, v), preferred_element_type=f32)
     top = jnp.where(low, lo, hi)
     bottom = pltpu.roll(jnp.where(low, hi, lo), HD, 1)
     attended = (top / bottom).astype(bf16)
-    for i in range(2):
-        outs[i][...] = attended[i * rows : (i + 1) * rows]
-
-
-def attend(packs):
+    for i, out in enumerate(outs):
+        out[...] = attended[i * rows : (i + 1) * rows]
+
+
+def attend(queries, packs):
     rows = packs[0].shape[0] // 3
-    keys = rows * len(packs)
-    vmem = pl.BlockSpec(memory_space=pltpu.VMEM)
-    return pl.pallas_call(
-        attention_kernel,
-        in_specs=[vmem] * len(packs),
-        out_specs=[vmem] * 2,
-        out_shape=[jax.ShapeDtypeStruct((rows, LANES), bf16)] * 2,
-        scratch_shapes=[pltpu.VMEM((keys, LANES), bf16)] * 3 + [pltpu.VMEM((2 * rows, LANES), bf16)],
+    vmem = pl.BlockSpec(memory_space=pltpu.VMEM)
+    count = len(queries)
+    return pl.pallas_call(
+        functools.partial(attention_kernel, count),
+        in_specs=[vmem] * (count + len(packs)),
+        out_specs=[vmem] * count,
+        out_shape=[jax.ShapeDtypeStruct((rows, LANES), bf16)] * count,
         compiler_params=pltpu.CompilerParams(vmem_limit_bytes=24 * 2**20),
         name="attend",
-    )(*packs)
+    )(*queries, *packs)
 
 
 def mix_kernel(x_ref, o0, o1, o2, own, w1, w2, total, att):
@@ -326,10 +316,13 @@
     w1, c1, c2, c3 = lax.optimization_barrier((w1, c1, c2, c3))
     n3 = second_way(halved(w1))
 
-    o2, o3 = attend([r2, r3, p0, r1, c0, c1, c2, c3])
+    packs = [p0, r1, r2, r3, c0, c1, c2, c3]
+    o2, o3 = attend([r2, r3], packs)
     w1, o2, o3 = lax.optimization_barrier((w1, o2, o3))
     w2 = swapped(w1, "ctx", 1)
-    o0, o1 = attend([p0, r1, r2, r3, c0, c1, c2, c3])
+    (o1,) = attend([r1], packs)
+    p0, o1 = lax.optimization_barrier((p0, o1))
+    (o0,) = attend([p0], packs)
     own = gathered([o0, swapped(o1, "ctx", 2), swapped(o2, "ctx", 4), swapped(o3, "ctx", 6)])
     own, n3 = lax.optimization_barrier((own, n3))
     a1, a2 = first_way(own), second_way(own)

time: 67.3 us -> 66 us (0.981)
  waiting for transfers between devices: 28.8 us -> 27.7 us
    ppermute x13, waiting for transfers between devices: 18.5 us -> 17.4 us  [swapped(): return lax.ppermute(value, axis, [(i, i ^ bits) for i in range(count)])]
    ppermute x2, waiting for transfers between devices: 6.31 us -> 5.27 us  [first_way(): return lax.ppermute(value, ('ctx', 'head'), pairs)]
    ppermute x3, waiting for transfers between devices: 2.77 us -> 3.75 us  [second_way(): return lax.ppermute(value, ('ctx', 'head'), pairs)]
    pallas_call x2 -> x3, Pallas kernels: 5.38 us -> 5.35 us  [attend(): pl.pallas_call(functools.partial(attention_kernel, count), in_specs=[vmem...]
  transfers between devices with their start and end apart: 19 -> 19, of which waited for: 11 -> 12; matrix products, arithmetic and copies ran while one was open for 0% -> 0% of each run, Pallas kernels for 19% -> 19%
where the time goes in v8:
time: 66 us; the launch traced here: 65.7 us
  waiting for transfers between devices  27.7 us (42%)
  starting transfers between devices  22.9 us (35%)
  Pallas kernels  15 us (23%)
    ppermute x13, waiting for transfers between devices, swapped(): return lax.ppermute(value, axis, [(i, i ^ bits) for i in range(count)])  17.4 us
    ppermute x13, starting transfers between devices, swapped(): return lax.ppermute(value, axis, [(i, i ^ bits) for i in range(count)])  10.7 us
    pallas_call x3, Pallas kernels, attend(): pl.pallas_call(functools.partial(attention_kernel, count), in_specs=[vmem...  5.35 us
    ppermute x2, waiting for transfers between devices, first_way(): return lax.ppermute(value, ('ctx', 'head'), pairs)  5.27 us
    ppermute x2, starting transfers between devices, first_way(): return lax.ppermute(value, ('ctx', 'head'), pairs)  4.49 us
    pallas_call x1, Pallas kernels, project(): pl.pallas_call(project_kernel, in_specs=[hbm] * 2, out_specs=[vmem] * 4,...  4.43 us
    ppermute x3, starting transfers between devices, second_way(): return lax.ppermute(value, ('ctx', 'head'), pairs)  4.14 us
    ppermute x3, waiting for transfers between devices, second_way(): return lax.ppermute(value, ('ctx', 'head'), pairs)  3.75 us
  transfers between devices with their start and end apart: 19, of which 12 were waited for; matrix products, arithmetic and copies ran while one was open for 0% of the time, Pallas kernels for 19%

profile of v8, /device:TPU:0, one launch (start us, length us, event | category | flops | bytes accessed | tf_op | source)
XLA Modules:
  0.0 65.7 jit_solution(6074775259121468845)
XLA Ops:
  0.0 2.9 %collective-permute-start.4 = (bf16[512,2048]{1,0:T(8,128)(2,1)}, bf16[512,2048]{1,0:T(8,128)(2,1)S(1)}, u32[]{:S(2)}, u32[]{:S(2)}) collective-permute-start(bf16[512,2048]{1,0:T(8,128)(2,1)} %own.1), channel_id=1, source_target_pairs={{0,1},{1,0},{2,3},{3,2},{4,6},{5,7},{6,4},{7,5},{8,9},{9,8},{10,11... | collective-permute-start | bytes 6291464 | tf_op jit(solution)/shard_map/ppermute | solution.py:296
  2.9 4.4 %project.1 = (bf16[768,128]{1,0:T(8,128)(2,1)S(1)}, bf16[768,128]{1,0:T(8,128)(2,1)S(1)}, bf16[768,128]{1,0:T(8,128)(2,1)S(1)}, bf16[768,128]{1,0:T(8,128)(2,1)S(1)}) custom-call(bf16[256,2048]{1,0:T(8,128)(2,1)} %x_ref.1, bf16[3,2048,512]{2,1,0:T(8,128)(2,1)} %w_hbm.1), custom_call_target="tpu_custom_call" | custom-call | tf_op jit(solution)/shard_map/project/pallas_call | solution.py:73
  7.5 2.7 %collective-permute-start.2 = (bf16[768,128]{1,0:T(8,128)(2,1)S(1)}, bf16[768,128]{1,0:T(8,128)(2,1)S(1)}, u32[]{:S(2)}, u32[]{:S(2)}) collective-permute-start(bf16[768,128]{1,0:T(8,128)(2,1)S(1)} %get-tuple-element.33), channel_id=1, source_target_pairs={{0,16},{4,20},{8,24},{12,28},{16,0},{20,4},{24,8},{28,12},{1,17},{... | collective-permute-start | bytes 589832 | tf_op jit(solution)/shard_map/ppermute | solution.py:29
  10.1 1.3 %collective-permute-start.3 = (bf16[768,128]{1,0:T(8,128)(2,1)S(1)}, bf16[768,128]{1,0:T(8,128)(2,1)S(1)}, u32[]{:S(2)}, u32[]{:S(2)}) collective-permute-start(bf16[768,128]{1,0:T(8,128)(2,1)S(1)} %get-tuple-element.34), channel_id=1, source_target_pairs={{0,24},{4,28},{8,16},{12,20},{16,8},{20,12},{24,0},{28,4},{1,25},{... | collective-permute-start | bytes 589832 | tf_op jit(solution)/shard_map/ppermute | solution.py:29
  11.7 12.9 %collective-permute-done.2.refs_3_.refs_0_.refs_4_ = bf16[768,128]{1,0:T(8,128)(2,1)S(1)} collective-permute-done((bf16[768,128]{1,0:T(8,128)(2,1)S(1)}, bf16[768,128]{1,0:T(8,128)(2,1)S(1)}, u32[]{:S(2)}, u32[]{:S(2)}) %collective-permute-start.2) | collective-permute-done | bytes 196640 | tf_op jit(solution)/shard_map/ppermute | solution.py:29
  24.6 0.5 collective-permute-start.7
  25.1 0.4 collective-permute-done.1.refs_0_.refs_2_.refs_3_
  25.5 0.6 collective-permute-done.6.refs_7_.refs_8_
  26.0 0.3 collective-permute-done.7.refs_8_.refs_9_
  26.3 0.6 collective-permute-done.5.refs_6_.refs_7_
  26.9 0.2 collective-permute-done.4.block.w1
  27.2 2.1 %collective-permute-start.11 = (bf16[256,2048]{1,0:T(8,128)(2,1)S(1)}, bf16[256,2048]{1,0:T(8,128)(2,1)S(1)}, u32[]{:S(2)}, u32[]{:S(2)}) collective-permute-start(bf16[256,2048]{1,0:T(8,128)(2,1)S(1)} %halved.1), channel_id=1, source_target_pairs={{0,2},{1,3},{2,0},{3,1},{4,5},{5,4},{6,7},{7,6},{8,10},{9,11},{10,... | collective-permute-start | bytes 3145736 | tf_op jit(solution)/shard_map/ppermute | solution.py:302
  29.4 2.5 %attend.5 = (bf16[256,128]{1,0:T(8,128)(2,1)S(1)}, bf16[256,128]{1,0:T(8,128)(2,1)S(1)}) custom-call(bf16[768,128]{1,0:T(8,128)(2,1)S(1)} %collective-permute-done.2.refs_3_.refs_0_.refs_4_, bf16[768,128]{1,0:T(8,128)(2,1)S(1)} %collective-permute-done.3.refs_4_.refs_1_.refs_5_, bf16[768,128]{1,0:T(8,128)(2,1)S(1)} %get-tuple-element.39.refs_1_.refs_0_.refs_2_, ...), custom_call_target="tpu_custom_call" | custom-call | tf_op jit(solution)/shard_map/attend/pallas_call | solution.py:121
  32.0 3.7 %collective-permute-start.10 = (bf16[256,128]{1,0:T(8,128)(2,1)S(1)}, bf16[256,128]{1,0:T(8,128)(2,1)S(1)}, u32[]{:S(2)}, u32[]{:S(2)}) collective-permute-start(bf16[256,128]{1,0:T(8,128)(2,1)S(1)} %get-tuple-element.45), channel_id=1, source_target_pairs={{0,24},{4,28},{8,16},{12,20},{16,8},{20,12},{24,0},{28,4},{1,25},{... | collective-permute-start | bytes 196616 | tf_op jit(solution)/shard_map/ppermute | solution.py:29
  35.6 1.5 %collective-permute-start.9 = (bf16[256,128]{1,0:T(8,128)(2,1)S(1)}, bf16[256,128]{1,0:T(8,128)(2,1)S(1)}, u32[]{:S(2)}, u32[]{:S(2)}) collective-permute-start(bf16[256,128]{1,0:T(8,128)(2,1)S(1)} %get-tuple-element.44), channel_id=1, source_target_pairs={{0,16},{4,20},{8,24},{12,28},{16,0},{20,4},{24,8},{28,12},{1,17},{... | collective-permute-start | bytes 196616 | tf_op jit(solution)/shard_map/ppermute | solution.py:29
  37.1 1.4 %attend.3 = bf16[256,128]{1,0:T(8,128)(2,1)S(1)} custom-call(bf16[768,128]{1,0:T(8,128)(2,1)S(1)} %collective-permute-done.1.refs_0_.refs_2_.refs_3_, bf16[768,128]{1,0:T(8,128)(2,1)S(1)} %get-tuple-element.39.refs_1_.refs_0_.refs_2_, bf16[768,128]{1,0:T(8,128)(2,1)S(1)} %collective-permute-done.1.refs_0_.refs_2_.refs_3_, ...), custom_call_target="tpu_custom_call" | custom-call | tf_op jit(solution)/shard_map/attend/pallas_call | solution.py:121
  38.5 0.6 collective-permute-start.8
  39.1 1.4 %attend.4.refs_0_ = bf16[256,128]{1,0:T(8,128)(2,1)S(1)} custom-call(bf16[768,128]{1,0:T(8,128)(2,1)S(1)} %get-tuple-element.39.refs_1_.refs_0_.refs_2_, bf16[768,128]{1,0:T(8,128)(2,1)S(1)} %get-tuple-element.39.refs_1_.refs_0_.refs_2_, bf16[768,128]{1,0:T(8,128)(2,1)S(1)} %collective-permute-done.1.refs_0_.refs_2_.refs_3_, ...), custom_call_target="tpu_custom_call" | custom-call | tf_op jit(solution)/shard_map/attend/pallas_call | solution.py:121
  40.5 2.1 %collective-permute-done.9.refs_2_ = bf16[256,128]{1,0:T(8,128)(2,1)S(1)} collective-permute-done((bf16[256,128]{1,0:T(8,128)(2,1)S(1)}, bf16[256,128]{1,0:T(8,128)(2,1)S(1)}, u32[]{:S(2)}, u32[]{:S(2)}) %collective-permute-start.9) | collective-permute-done | bytes 65568 | tf_op jit(solution)/shard_map/ppermute | solution.py:29
  42.6 0.6 collective-permute-done.8.refs_1_
  43.2 1.6 %collective-permute-start.12 = (bf16[1024,128]{1,0:T(8,128)(2,1)S(1)}, bf16[1024,128]{1,0:T(8,128)(2,1)S(1)}, u32[]{:S(2)}, u32[]{:S(2)}) collective-permute-start(bf16[1024,128]{1,0:T(8,128)(2,1)S(1)} %gathered.1.o0), channel_id=1, source_target_pairs={{0,1},{1,0},{2,3},{3,2},{4,6},{5,7},{6,4},{7,5},{8,9},{9,8},{10,11... | collective-permute-start | bytes 786440 | tf_op jit(solution)/shard_map/ppermute | solution.py:296
  44.8 0.9 %collective-permute-start.13 = (bf16[1024,128]{1,0:T(8,128)(2,1)S(1)}, bf16[1024,128]{1,0:T(8,128)(2,1)S(1)}, u32[]{:S(2)}, u32[]{:S(2)}) collective-permute-start(bf16[1024,128]{1,0:T(8,128)(2,1)S(1)} %gathered.1.o0), channel_id=1, source_target_pairs={{0,2},{1,3},{2,0},{3,1},{4,5},{5,4},{6,7},{7,6},{8,10},{9,11},{10,... | collective-permute-start | bytes 786440 | tf_op jit(solution)/shard_map/ppermute | solution.py:302
  45.6 5.0 %collective-permute-done.12.o1 = bf16[1024,128]{1,0:T(8,128)(2,1)S(1)} collective-permute-done((bf16[1024,128]{1,0:T(8,128)(2,1)S(1)}, bf16[1024,128]{1,0:T(8,128)(2,1)S(1)}, u32[]{:S(2)}, u32[]{:S(2)}) %collective-permute-start.12) | collective-permute-done | bytes 262176 | tf_op jit(solution)/shard_map/ppermute | solution.py:296
  50.7 0.5 collective-permute-done.13.o2
  51.2 1.2 %collective-permute-start.15 = (bf16[1024,128]{1,0:T(8,128)(2,1)S(1)}, bf16[1024,128]{1,0:T(8,128)(2,1)S(1)}, u32[]{:S(2)}, u32[]{:S(2)}) collective-permute-start(bf16[1024,128]{1,0:T(8,128)(2,1)S(1)} %collective-permute-done.12.o1), channel_id=1, source_target_pairs={{0,2},{1,3},{2,0},{3,1},{4,5},{5,4},{6,7},{7,6},{8,10},{9,11},{10,... | collective-permute-start | bytes 786440 | tf_op jit(solution)/shard_map/ppermute | solution.py:302
  52.4 1.9 %mix.1.total = f32[256,2048]{1,0:T(8,128)S(1)} custom-call(bf16[256,2048]{1,0:T(8,128)(2,1)S(1)} %copy-done.1, bf16[1024,128]{1,0:T(8,128)(2,1)S(1)} %gathered.1.o0, bf16[1024,128]{1,0:T(8,128)(2,1)S(1)} %collective-permute-done.12.o1, bf16[1024,128]{1,0:T(8,128)(2,1)S(1)} %collective-permute-done.13.o2, bf16[512,2048]{1,0:T(8,128)(2,1)S(1)} %copy-done.2, ...), custom_call_target="tpu_custom_call" | custom-call | tf_op jit(solution)/shard_map/mix/pallas_call | solution.py:149
  54.3 3.3 %collective-permute-done.15.o3 = bf16[1024,128]{1,0:T(8,128)(2,1)S(1)} collective-permute-done((bf16[1024,128]{1,0:T(8,128)(2,1)S(1)}, bf16[1024,128]{1,0:T(8,128)(2,1)S(1)}, u32[]{:S(2)}, u32[]{:S(2)}) %collective-permute-start.15) | collective-permute-done | bytes 262176 | tf_op jit(solution)/shard_map/ppermute | solution.py:302
  57.5 1.6 %decode_edges.1 = (bf16[256,2048]{1,0:T(8,128)(2,1)S(1)}, bf16[128,256]{1,0:T(8,128)(2,1)S(1)}, bf16[128,256]{1,0:T(8,128)(2,1)S(1)}) custom-call(f32[256,2048]{1,0:T(8,128)S(1)} %mix.1.total, bf16[1024,128]{1,0:T(8,128)(2,1)S(1)} %collective-permute-done.15.o3, bf16[256,2048]{1,0:T(8,128)(2,1)S(1)} %collective-permute-done.11.n3, ...), custom_call_target="tpu_custom_call" | custom-call | tf_op jit(solution)/shard_map/decode_edges/pallas_call | solution.py:195
  59.3 3.6 %collective-permute-start.18 = (bf16[128,256]{1,0:T(8,128)(2,1)S(1)}, bf16[128,256]{1,0:T(8,128)(2,1)S(1)}, u32[]{:S(2)}, u32[]{:S(2)}) collective-permute-start(bf16[128,256]{1,0:T(8,128)(2,1)S(1)} %get-tuple-element.54), channel_id=1, source_target_pairs={{0,28},{4,8},{8,4},{12,16},{16,12},{20,24},{24,20},{28,0},{1,29},{... | collective-permute-start | bytes 196616 | tf_op jit(solution)/shard_map/ppermute | solution.py:339
  62.9 0.7 %decode_main.1.main = f32[512,256]{1,0:T(8,128)S(1)} custom-call(bf16[256,2048]{1,0:T(8,128)(2,1)S(1)} %get-tuple-element.52.hidden, bf16[768,2048]{1,0:T(8,128)(2,1)S(1)} %bitcast.7), custom_call_target="tpu_custom_call" | custom-call | tf_op jit(solution)/shard_map/decode_main/pallas_call | solution.py:222
  63.7 1.3 %collective-permute-done.18.outer = bf16[128,256]{1,0:T(8,128)(2,1)S(1)} collective-permute-done((bf16[128,256]{1,0:T(8,128)(2,1)S(1)}, bf16[128,256]{1,0:T(8,128)(2,1)S(1)}, u32[]{:S(2)}, u32[]{:S(2)}) %collective-permute-start.18) | collective-permute-done | bytes 65568 | tf_op jit(solution)/shard_map/ppermute | solution.py:339
  64.9 0.8 %join.1 = f32[512,256]{1,0:T(8,128)} custom-call(f32[512,256]{1,0:T(8,128)S(1)} %decode_main.1.main, bf16[128,256]{1,0:T(8,128)(2,1)S(1)} %collective-permute-done.17.inner, bf16[128,256]{1,0:T(8,128)(2,1)S(1)} %collective-permute-done.18.outer), custom_call_target="tpu_custom_call" | custom-call | tf_op jit(solution)/shard_map/join/pallas_call | solution.py:245
  (22 shorter events, 0.6 us)
Async XLA Ops:
  0.0 27.2 %collective-permute-start.4 = (bf16[512,2048]{1,0:T(8,128)(2,1)}, bf16[512,2048]{1,0:T(8,128)(2,1)S(1)}, u32[]{:S(2)}, u32[]{:S(2)}) collective-permute-start(bf16[512,2048]{1,0:T(8,128)(2,1)} %own.1), channel_id=1, source_target_pairs={{0,1},{1,0},{2,3},{3,2},{4,6},{5,7},{6,4},{7,5},{8,9},{9,8},{10,11... | collective-permute-start | bytes 6291464 | tf_op jit(solution)/shard_map/ppermute | solution.py:296
  7.4 4.1 %collective-permute-start = (bf16[768,128]{1,0:T(8,128)(2,1)S(1)}, bf16[768,128]{1,0:T(8,128)(2,1)S(1)}, u32[]{:S(2)}, u32[]{:S(2)}) collective-permute-start(bf16[768,128]{1,0:T(8,128)(2,1)S(1)} %get-tuple-element.39.refs_1_.refs_0_.refs_2_), channel_id=1, source_target_pairs={{0,4},{4,0},{8,12},{12,8},{16,20},{20,16},{24,28},{28,24},{1,5},{5... | collective-permute-start | bytes 589832 | tf_op jit(solution)/shard_map/ppermute | solution.py:29
  7.5 17.1 %collective-permute-start.2 = (bf16[768,128]{1,0:T(8,128)(2,1)S(1)}, bf16[768,128]{1,0:T(8,128)(2,1)S(1)}, u32[]{:S(2)}, u32[]{:S(2)}) collective-permute-start(bf16[768,128]{1,0:T(8,128)(2,1)S(1)} %get-tuple-element.33), channel_id=1, source_target_pairs={{0,16},{4,20},{8,24},{12,28},{16,0},{20,4},{24,8},{28,12},{1,17},{... | collective-permute-start | bytes 589832 | tf_op jit(solution)/shard_map/ppermute | solution.py:29
  10.1 14.5 %collective-permute-start.3 = (bf16[768,128]{1,0:T(8,128)(2,1)S(1)}, bf16[768,128]{1,0:T(8,128)(2,1)S(1)}, u32[]{:S(2)}, u32[]{:S(2)}) collective-permute-start(bf16[768,128]{1,0:T(8,128)(2,1)S(1)} %get-tuple-element.34), channel_id=1, source_target_pairs={{0,24},{4,28},{8,16},{12,20},{16,8},{20,12},{24,0},{28,4},{1,25},{... | collective-permute-start | bytes 589832 | tf_op jit(solution)/shard_map/ppermute | solution.py:29
  11.5 14.0 %collective-permute-start.1 = (bf16[768,128]{1,0:T(8,128)(2,1)S(1)}, bf16[768,128]{1,0:T(8,128)(2,1)S(1)}, u32[]{:S(2)}, u32[]{:S(2)}) collective-permute-start(bf16[768,128]{1,0:T(8,128)(2,1)S(1)} %get-tuple-element.32), channel_id=1, source_target_pairs={{0,8},{4,12},{8,0},{12,4},{16,24},{20,28},{24,16},{28,20},{1,9},{5... | collective-permute-start | bytes 589832 | tf_op jit(solution)/shard_map/ppermute | solution.py:29
  24.6 1.4 %collective-permute-start.6 = (bf16[768,128]{1,0:T(8,128)(2,1)S(1)}, bf16[768,128]{1,0:T(8,128)(2,1)S(1)}, u32[]{:S(2)}, u32[]{:S(2)}) collective-permute-start(bf16[768,128]{1,0:T(8,128)(2,1)S(1)} %collective-permute-done.2.refs_3_.refs_0_.refs_4_), channel_id=1, source_target_pairs={{0,4},{4,0},{8,12},{12,8},{16,20},{20,16},{24,28},{28,24},{1,5},{5... | collective-permute-start | bytes 589832 | tf_op jit(solution)/shard_map/ppermute | solution.py:29
  24.6 1.7 %collective-permute-start.7 = (bf16[768,128]{1,0:T(8,128)(2,1)S(1)}, bf16[768,128]{1,0:T(8,128)(2,1)S(1)}, u32[]{:S(2)}, u32[]{:S(2)}) collective-permute-start(bf16[768,128]{1,0:T(8,128)(2,1)S(1)} %collective-permute-done.3.refs_4_.refs_1_.refs_5_), channel_id=1, source_target_pairs={{0,4},{4,0},{8,12},{12,8},{16,20},{20,16},{24,28},{28,24},{1,5},{5... | collective-permute-start | bytes 589832 | tf_op jit(solution)/shard_map/ppermute | solution.py:29
  25.5 1.4 %collective-permute-start.5 = (bf16[768,128]{1,0:T(8,128)(2,1)S(1)}, bf16[768,128]{1,0:T(8,128)(2,1)S(1)}, u32[]{:S(2)}, u32[]{:S(2)}) collective-permute-start(bf16[768,128]{1,0:T(8,128)(2,1)S(1)} %collective-permute-done.1.refs_0_.refs_2_.refs_3_), channel_id=1, source_target_pairs={{0,4},{4,0},{8,12},{12,8},{16,20},{20,16},{24,28},{28,24},{1,5},{5... | collective-permute-start | bytes 589832 | tf_op jit(solution)/shard_map/ppermute | solution.py:29
  27.2 16.0 %collective-permute-start.11 = (bf16[256,2048]{1,0:T(8,128)(2,1)S(1)}, bf16[256,2048]{1,0:T(8,128)(2,1)S(1)}, u32[]{:S(2)}, u32[]{:S(2)}) collective-permute-start(bf16[256,2048]{1,0:T(8,128)(2,1)S(1)} %halved.1), channel_id=1, source_target_pairs={{0,2},{1,3},{2,0},{3,1},{4,5},{5,4},{6,7},{7,6},{8,10},{9,11},{10,... | collective-permute-start | bytes 3145736 | tf_op jit(solution)/shard_map/ppermute | solution.py:302
  31.9 20.5 %copy-start.1 = (bf16[256,2048]{1,0:T(8,128)(2,1)S(1)}, bf16[256,2048]{1,0:T(8,128)(2,1)}, u32[]{:S(2)}) copy-start(bf16[256,2048]{1,0:T(8,128)(2,1)} %x_ref.1) | copy-start | bytes 3145732
  31.9 20.5 %copy-start.2 = (bf16[512,2048]{1,0:T(8,128)(2,1)S(1)}, bf16[512,2048]{1,0:T(8,128)(2,1)}, u32[]{:S(2)}) copy-start(bf16[512,2048]{1,0:T(8,128)(2,1)} %own.1) | copy-start | bytes 6291460
  31.9 20.5 %collective-permute-start.14 = (bf16[512,2048]{1,0:T(8,128)(2,1)S(1)}, bf16[512,2048]{1,0:T(8,128)(2,1)S(1)}, u32[]{:S(2)}, u32[]{:S(2)}) collective-permute-start(bf16[512,2048]{1,0:T(8,128)(2,1)S(1)} %collective-permute-done.4.block.w1), channel_id=1, source_target_pairs={{0,4},{4,0},{8,12},{12,8},{16,20},{20,16},{24,28},{28,24},{1,5},{5... | collective-permute-start | bytes 6291464 | tf_op jit(solution)/shard_map/ppermute | solution.py:29
  32.0 8.6 %collective-permute-start.10 = (bf16[256,128]{1,0:T(8,128)(2,1)S(1)}, bf16[256,128]{1,0:T(8,128)(2,1)S(1)}, u32[]{:S(2)}, u32[]{:S(2)}) collective-permute-start(bf16[256,128]{1,0:T(8,128)(2,1)S(1)} %get-tuple-element.45), channel_id=1, source_target_pairs={{0,24},{4,28},{8,16},{12,20},{16,8},{20,12},{24,0},{28,4},{1,25},{... | collective-permute-start | bytes 196616 | tf_op jit(solution)/shard_map/ppermute | solution.py:29
  35.6 7.0 %collective-permute-start.9 = (bf16[256,128]{1,0:T(8,128)(2,1)S(1)}, bf16[256,128]{1,0:T(8,128)(2,1)S(1)}, u32[]{:S(2)}, u32[]{:S(2)}) collective-permute-start(bf16[256,128]{1,0:T(8,128)(2,1)S(1)} %get-tuple-element.44), channel_id=1, source_target_pairs={{0,16},{4,20},{8,24},{12,28},{16,0},{20,4},{24,8},{28,12},{1,17},{... | collective-permute-start | bytes 196616 | tf_op jit(solution)/shard_map/ppermute | solution.py:29
  38.5 4.7 %collective-permute-start.8 = (bf16[256,128]{1,0:T(8,128)(2,1)S(1)}, bf16[256,128]{1,0:T(8,128)(2,1)S(1)}, u32[]{:S(2)}, u32[]{:S(2)}) collective-permute-start(bf16[256,128]{1,0:T(8,128)(2,1)S(1)} %attend.3), channel_id=1, source_target_pairs={{0,8},{4,12},{8,0},{12,4},{16,24},{20,28},{24,16},{28,20},{1,9},{5... | collective-permute-start | bytes 196616 | tf_op jit(solution)/shard_map/ppermute | solution.py:29
  43.2 7.4 %collective-permute-start.12 = (bf16[1024,128]{1,0:T(8,128)(2,1)S(1)}, bf16[1024,128]{1,0:T(8,128)(2,1)S(1)}, u32[]{:S(2)}, u32[]{:S(2)}) collective-permute-start(bf16[1024,128]{1,0:T(8,128)(2,1)S(1)} %gathered.1.o0), channel_id=1, source_target_pairs={{0,1},{1,0},{2,3},{3,2},{4,6},{5,7},{6,4},{7,5},{8,9},{9,8},{10,11... | collective-permute-start | bytes 786440 | tf_op jit(solution)/shard_map/ppermute | solution.py:296
  44.8 6.4 %collective-permute-start.13 = (bf16[1024,128]{1,0:T(8,128)(2,1)S(1)}, bf16[1024,128]{1,0:T(8,128)(2,1)S(1)}, u32[]{:S(2)}, u32[]{:S(2)}) collective-permute-start(bf16[1024,128]{1,0:T(8,128)(2,1)S(1)} %gathered.1.o0), channel_id=1, source_target_pairs={{0,2},{1,3},{2,0},{3,1},{4,5},{5,4},{6,7},{7,6},{8,10},{9,11},{10,... | collective-permute-start | bytes 786440 | tf_op jit(solution)/shard_map/ppermute | solution.py:302
  51.2 6.4 %collective-permute-start.16 = (bf16[256,2048]{1,0:T(8,128)(2,1)S(1)}, bf16[256,2048]{1,0:T(8,128)(2,1)S(1)}, u32[]{:S(2)}, u32[]{:S(2)}) collective-permute-start(bf16[256,2048]{1,0:T(8,128)(2,1)S(1)} %collective-permute-done.11.n3), channel_id=1, source_target_pairs={{0,4},{4,0},{8,12},{12,8},{16,20},{20,16},{24,28},{28,24},{1,5},{5... | collective-permute-start | bytes 3145736 | tf_op jit(solution)/shard_map/ppermute | solution.py:29
  51.2 6.4 %collective-permute-start.15 = (bf16[1024,128]{1,0:T(8,128)(2,1)S(1)}, bf16[1024,128]{1,0:T(8,128)(2,1)S(1)}, u32[]{:S(2)}, u32[]{:S(2)}) collective-permute-start(bf16[1024,128]{1,0:T(8,128)(2,1)S(1)} %collective-permute-done.12.o1), channel_id=1, source_target_pairs={{0,2},{1,3},{2,0},{3,1},{4,5},{5,4},{6,7},{7,6},{8,10},{9,11},{10,... | collective-permute-start | bytes 786440 | tf_op jit(solution)/shard_map/ppermute | solution.py:302
  52.4 5.2 %copy-start = (bf16[2048,12,64]{0,2,1:T(8,128)(2,1)S(1)}, bf16[2048,12,64]{0,2,1:T(8,128)(2,1)}, u32[]{:S(2)}) copy-start(bf16[2048,12,64]{0,2,1:T(8,128)(2,1)} %param.7) | copy-start | bytes 9437188
  59.2 4.5 %collective-permute-start.17 = (bf16[128,256]{1,0:T(8,128)(2,1)S(1)}, bf16[128,256]{1,0:T(8,128)(2,1)S(1)}, u32[]{:S(2)}, u32[]{:S(2)}) collective-permute-start(bf16[128,256]{1,0:T(8,128)(2,1)S(1)} %get-tuple-element.53), channel_id=1, source_target_pairs={{0,4},{4,0},{8,12},{12,8},{16,20},{20,16},{24,28},{28,24},{1,5},{5... | collective-permute-start | bytes 196616 | tf_op jit(solution)/shard_map/ppermute | solution.py:29
  59.3 5.6 %collective-permute-start.18 = (bf16[128,256]{1,0:T(8,128)(2,1)S(1)}, bf16[128,256]{1,0:T(8,128)(2,1)S(1)}, u32[]{:S(2)}, u32[]{:S(2)}) collective-permute-start(bf16[128,256]{1,0:T(8,128)(2,1)S(1)} %get-tuple-element.54), channel_id=1, source_target_pairs={{0,28},{4,8},{8,4},{12,16},{16,12},{20,24},{24,20},{28,0},{1,29},{... | collective-permute-start | bytes 196616 | tf_op jit(solution)/shard_map/ppermute | solution.py:339

commit v9 on v8

--- a/solution.py
+++ b/solution.py
@@ -157,7 +157,7 @@
     )(tokens, *outs, *parts)
 
 
-def edges_kernel(total, o3, n3, f3, dec_ref, hidden, inner, outer, att, held):
+def edges_kernel(total, o3, n3, f3, dec_ref, hidden, scale, inner, outer, att):
     z, core = place()
     rows, width = total.shape
     for s in range(4):
@@ -168,18 +168,20 @@
     for n in range(0, width, step):
         w = jnp.concatenate([part[:, n : n + step] for part in (n3, f3)], axis=0)
         mixed = total[:, n : n + step] + jnp.dot(att[...], w, preferred_element_type=f32)
-        held[:, n : n + step] = mixed
+        hidden[:, n : n + step] = mixed.astype(bf16)
         for i in range(0, step, LANES):
             squares += mixed[:, i : i + LANES] * mixed[:, i : i + LANES]
-    scale = lax.rsqrt(jnp.sum(squares, axis=-1, keepdims=True) * (1.0 / width) + eps)
-    hidden[...] = (held[...] * scale).astype(bf16)
+    mean = jnp.sum(squares.T, axis=0, keepdims=True) * (1.0 / width)
+    factor = lax.rsqrt(mean + eps)
+    scale[...] = jnp.broadcast_to(factor, scale.shape)
     edge = inner.shape[0]
     last = dec_ref.shape[0] - edge
 
     def cells(part):
-        return lax.dot_general(
+        out = lax.dot_general(
             dec_ref[part], hidden[...], (((1,), (1,)), ((), ())), preferred_element_type=f32
-        ).astype(bf16)
+        )
+        return (out * factor).astype(bf16)
 
     down = cells(pl.ds(0, edge))
     up = cells(pl.ds(last, edge))
@@ -195,61 +197,86 @@
     return pl.pallas_call(
         edges_kernel,
         in_specs=[vmem] * 5,
-        out_specs=[vmem] * 3,
-        out_shape=[jax.ShapeDtypeStruct((rows, width), bf16), edge, edge],
-        scratch_shapes=[
-            pltpu.VMEM((rows, n3.shape[0] + f3.shape[0]), bf16),
-            pltpu.VMEM((rows, width), f32),
+        out_specs=[vmem] * 4,
+        out_shape=[
+            jax.ShapeDtypeStruct((rows, width), bf16),
+            jax.ShapeDtypeStruct((8, rows), f32),
+            edge,
+            edge,
         ],
+        scratch_shapes=[pltpu.VMEM((rows, n3.shape[0] + f3.shape[0]), bf16)],
         compiler_params=pltpu.CompilerParams(vmem_limit_bytes=12 * 2**20),
         name="decode_edges",
     )(total, o3, n3, f3, w_dec)
 
 
-def main_kernel(hidden, dec_ref, main):
-    edge = (dec_ref.shape[0] - main.shape[0]) // 2
-    main[...] = lax.dot_general(
-        dec_ref[pl.ds(edge, main.shape[0])],
+def main_kernel(hidden, scale, dec_ref, field, ends, main, sem):
+    cells = main.shape[0]
+    edge = (dec_ref.shape[0] - cells) // 2
+    main[...] = scale[:1] * lax.dot_general(
+        dec_ref[pl.ds(edge, cells)],
         hidden[...],
         (((1,), (1,)), ((), ())),
         preferred_element_type=f32,
     )
-
-
-def decode_main(hidden, w_dec):
+    middle = pl.ds(edge, cells - 2 * edge)
+    copy = pltpu.make_async_copy(main.at[middle], field.at[middle], sem)
+    copy.start()
+    ends[:edge] = main[:edge]
+    ends[edge:] = main[cells - edge :]
+    copy.wait()
+
+
+def decode_main(hidden, scale, w_dec):
+    rows = hidden.shape[0]
     cells = w_dec.shape[0] // (PATCH + 2 * OV)
     vmem = pl.BlockSpec(memory_space=pltpu.VMEM)
     return pl.pallas_call(
         main_kernel,
-        in_specs=[vmem] * 2,
-        out_specs=vmem,
-        out_shape=jax.ShapeDtypeStruct((PATCH * cells, hidden.shape[0]), f32),
+        in_specs=[vmem] * 3,
+        out_specs=[pl.BlockSpec(memory_space=pltpu.HBM), vmem],
+        out_shape=[
+            jax.ShapeDtypeStruct((PATCH * cells, rows), f32),
+            jax.ShapeDtypeStruct((2 * OV * cells, rows), f32),
+        ],
+        scratch_shapes=[
+            pltpu.VMEM((PATCH * cells, rows), f32),
+            pltpu.SemaphoreType.DMA(()),
+        ],
         compiler_params=pltpu.CompilerParams(vmem_limit_bytes=8 * 2**20),
         name="decode_main",
-    )(hidden, w_dec)
-
-
-def join_kernel(main, inner, outer, field):
+    )(hidden, scale, w_dec)
+
+
+def join_kernel(middle, ends, inner, outer, field, before, after, sems):
+    del middle
     _, core = place()
     edge = inner.shape[0]
-    rest = main.shape[0] - edge
-    before = jnp.where(core == 0, outer[...], inner[...]).astype(f32)
-    after = jnp.where(core == 0, inner[...], outer[...]).astype(f32)
-    field[:edge] = main[:edge] + before
-    field[edge:rest] = main[edge:rest]
-    field[rest:] = main[rest:] + after
-
-
-def join(main, inner, outer):
-    vmem = pl.BlockSpec(memory_space=pltpu.VMEM)
+    last = field.shape[0] - edge
+    before[...] = ends[:edge] + jnp.where(core == 0, outer[...], inner[...]).astype(f32)
+    first = pltpu.make_async_copy(before, field.at[pl.ds(0, edge)], sems.at[0])
+    first.start()
+    after[...] = ends[edge:] + jnp.where(core == 0, inner[...], outer[...]).astype(f32)
+    second = pltpu.make_async_copy(after, field.at[pl.ds(last, edge)], sems.at[1])
+    second.start()
+    first.wait()
+    second.wait()
+
+
+def join(field, ends, inner, outer):
+    hbm = pl.BlockSpec(memory_space=pltpu.HBM)
+    vmem = pl.BlockSpec(memory_space=pltpu.VMEM)
+    part = pltpu.VMEM(inner.shape, f32)
     return pl.pallas_call(
         join_kernel,
-        in_specs=[vmem] * 3,
-        out_specs=vmem,
-        out_shape=jax.ShapeDtypeStruct(main.shape, f32),
+        in_specs=[hbm, vmem, vmem, vmem],
+        out_specs=hbm,
+        out_shape=jax.ShapeDtypeStruct(field.shape, f32),
+        scratch_shapes=[part, part, pltpu.SemaphoreType.DMA((2,))],
+        input_output_aliases={0: 0},
         compiler_params=pltpu.CompilerParams(vmem_limit_bytes=4 * 2**20),
         name="join",
-    )(main, inner, outer)
+    )(field, ends, inner, outer)
 
 
 def gathered_kernel(*refs):
@@ -324,7 +351,6 @@
     p0, o1 = lax.optimization_barrier((p0, o1))
     (o0,) = attend([p0], packs)
     own = gathered([o0, swapped(o1, "ctx", 2), swapped(o2, "ctx", 4), swapped(o3, "ctx", 6)])
-    own, n3 = lax.optimization_barrier((own, n3))
     a1, a2 = first_way(own), second_way(own)
     a1, a2, n3 = lax.optimization_barrier((a1, a2, n3))
     a3 = second_way(a1)
@@ -333,12 +359,13 @@
 
     dec = w_dec.transpose(1, 2, 0)
     dec = dec.reshape(-1, dec.shape[2])
-    hidden, inner, outer = decode_edges(total, a3, n3, f3, dec)
+    hidden, scale, inner, outer = decode_edges(total, a3, n3, f3, dec)
     count = lax.axis_size("ctx")
     pairs = [(i, (i - 1 + 2 * (i % 2)) % count) for i in range(count)]
     outer = lax.ppermute(outer, "ctx", pairs)
     inner = swapped(inner, "ctx", 1)
-    field = join(decode_main(hidden, dec), inner, outer)
+    field, ends = decode_main(hidden, scale, dec)
+    field = join(field, ends, inner, outer)
     return field.reshape(PATCH, -1, rows).transpose(2, 0, 1)
 
 

time: 66 us -> 65.6 us (level)
  waiting for transfers between devices: 27.7 us -> 27 us
    ppermute x1, waiting for transfers between devices: 1.25 us -> 0.58 us  [fast_body(): outer = lax.ppermute(outer, 'ctx', pairs)]
  transfers between devices with their start and end apart: 19 -> 19, of which waited for: 12 -> 12; matrix products, arithmetic and copies ran while one was open for 0% -> 0% of each run, Pallas kernels for 19% -> 16%
where the time goes in v9:
time: 65.6 us; the launch traced here: 65.4 us
  waiting for transfers between devices  27 us (41%)
  starting transfers between devices  22.9 us (35%)
  Pallas kernels  15.4 us (23%)
    ppermute x13, waiting for transfers between devices, swapped(): return lax.ppermute(value, axis, [(i, i ^ bits) for i in range(count)])  17.3 us
    ppermute x13, starting transfers between devices, swapped(): return lax.ppermute(value, axis, [(i, i ^ bits) for i in range(count)])  10.5 us
    ppermute x2, waiting for transfers between devices, first_way(): return lax.ppermute(value, ('ctx', 'head'), pairs)  5.74 us
    pallas_call x3, Pallas kernels, attend(): pl.pallas_call(functools.partial(attention_kernel, count), in_specs=[vmem...  5.35 us
    ppermute x2, starting transfers between devices, first_way(): return lax.ppermute(value, ('ctx', 'head'), pairs)  4.51 us
    pallas_call x1, Pallas kernels, project(): pl.pallas_call(project_kernel, in_specs=[hbm] * 2, out_specs=[vmem] * 4,...  4.43 us
    ppermute x3, starting transfers between devices, second_way(): return lax.ppermute(value, ('ctx', 'head'), pairs)  4.05 us
    ppermute x1, starting transfers between devices, fast_body(): outer = lax.ppermute(outer, 'ctx', pairs)  3.82 us
  transfers between devices with their start and end apart: 19, of which 12 were waited for; matrix products, arithmetic and copies ran while one was open for 0% of the time, Pallas kernels for 16%

profile of v9, /device:TPU:0, one launch (start us, length us, event | category | flops | bytes accessed | tf_op | source)
XLA Modules:
  0.0 65.4 jit_solution(4480338854783789623)
XLA Ops:
  0.0 2.9 %collective-permute-start.4 = (bf16[512,2048]{1,0:T(8,128)(2,1)}, bf16[512,2048]{1,0:T(8,128)(2,1)S(1)}, u32[]{:S(2)}, u32[]{:S(2)}) collective-permute-start(bf16[512,2048]{1,0:T(8,128)(2,1)} %own.1), channel_id=1, source_target_pairs={{0,1},{1,0},{2,3},{3,2},{4,6},{5,7},{6,4},{7,5},{8,9},{9,8},{10,11... | collective-permute-start | bytes 6291464 | tf_op jit(solution)/shard_map/ppermute | solution.py:323
  2.9 4.4 %project.1 = (bf16[768,128]{1,0:T(8,128)(2,1)S(1)}, bf16[768,128]{1,0:T(8,128)(2,1)S(1)}, bf16[768,128]{1,0:T(8,128)(2,1)S(1)}, bf16[768,128]{1,0:T(8,128)(2,1)S(1)}) custom-call(bf16[256,2048]{1,0:T(8,128)(2,1)} %x_ref.1, bf16[3,2048,512]{2,1,0:T(8,128)(2,1)} %w_hbm.1), custom_call_target="tpu_custom_call" | custom-call | tf_op jit(solution)/shard_map/project/pallas_call | solution.py:73
  7.5 2.7 %collective-permute-start.2 = (bf16[768,128]{1,0:T(8,128)(2,1)S(1)}, bf16[768,128]{1,0:T(8,128)(2,1)S(1)}, u32[]{:S(2)}, u32[]{:S(2)}) collective-permute-start(bf16[768,128]{1,0:T(8,128)(2,1)S(1)} %get-tuple-element.34), channel_id=1, source_target_pairs={{0,16},{4,20},{8,24},{12,28},{16,0},{20,4},{24,8},{28,12},{1,17},{... | collective-permute-start | bytes 589832 | tf_op jit(solution)/shard_map/ppermute | solution.py:29
  10.1 1.3 %collective-permute-start.3 = (bf16[768,128]{1,0:T(8,128)(2,1)S(1)}, bf16[768,128]{1,0:T(8,128)(2,1)S(1)}, u32[]{:S(2)}, u32[]{:S(2)}) collective-permute-start(bf16[768,128]{1,0:T(8,128)(2,1)S(1)} %get-tuple-element.35), channel_id=1, source_target_pairs={{0,24},{4,28},{8,16},{12,20},{16,8},{20,12},{24,0},{28,4},{1,25},{... | collective-permute-start | bytes 589832 | tf_op jit(solution)/shard_map/ppermute | solution.py:29
  11.7 12.9 %collective-permute-done.2.refs_3_.refs_0_.refs_4_ = bf16[768,128]{1,0:T(8,128)(2,1)S(1)} collective-permute-done((bf16[768,128]{1,0:T(8,128)(2,1)S(1)}, bf16[768,128]{1,0:T(8,128)(2,1)S(1)}, u32[]{:S(2)}, u32[]{:S(2)}) %collective-permute-start.2) | collective-permute-done | bytes 196640 | tf_op jit(solution)/shard_map/ppermute | solution.py:29
  24.6 0.5 collective-permute-start.7
  25.1 0.4 collective-permute-done.1.refs_0_.refs_2_.refs_3_
  25.5 0.6 collective-permute-done.6.refs_7_.refs_8_
  26.0 0.3 collective-permute-done.7.refs_8_.refs_9_
  26.3 0.6 collective-permute-done.5.refs_6_.refs_7_
  26.9 0.2 collective-permute-done.4.block.w1
  27.2 2.5 %attend.5 = (bf16[256,128]{1,0:T(8,128)(2,1)S(1)}, bf16[256,128]{1,0:T(8,128)(2,1)S(1)}) custom-call(bf16[768,128]{1,0:T(8,128)(2,1)S(1)} %collective-permute-done.2.refs_3_.refs_0_.refs_4_, bf16[768,128]{1,0:T(8,128)(2,1)S(1)} %collective-permute-done.3.refs_4_.refs_1_.refs_5_, bf16[768,128]{1,0:T(8,128)(2,1)S(1)} %get-tuple-element.40.refs_1_.refs_0_.refs_2_, ...), custom_call_target="tpu_custom_call" | custom-call | tf_op jit(solution)/shard_map/attend/pallas_call | solution.py:121
  29.8 2.1 %collective-permute-start.13 = (bf16[256,2048]{1,0:T(8,128)(2,1)S(1)}, bf16[256,2048]{1,0:T(8,128)(2,1)S(1)}, u32[]{:S(2)}, u32[]{:S(2)}) collective-permute-start(bf16[256,2048]{1,0:T(8,128)(2,1)S(1)} %halved.1), channel_id=1, source_target_pairs={{0,2},{1,3},{2,0},{3,1},{4,5},{5,4},{6,7},{7,6},{8,10},{9,11},{10,... | collective-permute-start | bytes 3145736 | tf_op jit(solution)/shard_map/ppermute | solution.py:329
  31.9 3.6 %collective-permute-start.10 = (bf16[256,128]{1,0:T(8,128)(2,1)S(1)}, bf16[256,128]{1,0:T(8,128)(2,1)S(1)}, u32[]{:S(2)}, u32[]{:S(2)}) collective-permute-start(bf16[256,128]{1,0:T(8,128)(2,1)S(1)} %get-tuple-element.46), channel_id=1, source_target_pairs={{0,24},{4,28},{8,16},{12,20},{16,8},{20,12},{24,0},{28,4},{1,25},{... | collective-permute-start | bytes 196616 | tf_op jit(solution)/shard_map/ppermute | solution.py:29
  35.5 1.4 %collective-permute-start.9 = (bf16[256,128]{1,0:T(8,128)(2,1)S(1)}, bf16[256,128]{1,0:T(8,128)(2,1)S(1)}, u32[]{:S(2)}, u32[]{:S(2)}) collective-permute-start(bf16[256,128]{1,0:T(8,128)(2,1)S(1)} %get-tuple-element.45), channel_id=1, source_target_pairs={{0,16},{4,20},{8,24},{12,28},{16,0},{20,4},{24,8},{28,12},{1,17},{... | collective-permute-start | bytes 196616 | tf_op jit(solution)/shard_map/ppermute | solution.py:29
  36.9 1.4 %attend.3 = bf16[256,128]{1,0:T(8,128)(2,1)S(1)} custom-call(bf16[768,128]{1,0:T(8,128)(2,1)S(1)} %collective-permute-done.1.refs_0_.refs_2_.refs_3_, bf16[768,128]{1,0:T(8,128)(2,1)S(1)} %get-tuple-element.40.refs_1_.refs_0_.refs_2_, bf16[768,128]{1,0:T(8,128)(2,1)S(1)} %collective-permute-done.1.refs_0_.refs_2_.refs_3_, ...), custom_call_target="tpu_custom_call" | custom-call | tf_op jit(solution)/shard_map/attend/pallas_call | solution.py:121
  38.3 0.6 collective-permute-start.8
  38.9 1.4 %attend.4.refs_0_ = bf16[256,128]{1,0:T(8,128)(2,1)S(1)} custom-call(bf16[768,128]{1,0:T(8,128)(2,1)S(1)} %get-tuple-element.40.refs_1_.refs_0_.refs_2_, bf16[768,128]{1,0:T(8,128)(2,1)S(1)} %get-tuple-element.40.refs_1_.refs_0_.refs_2_, bf16[768,128]{1,0:T(8,128)(2,1)S(1)} %collective-permute-done.1.refs_0_.refs_2_.refs_3_, ...), custom_call_target="tpu_custom_call" | custom-call | tf_op jit(solution)/shard_map/attend/pallas_call | solution.py:121
  40.4 2.2 %collective-permute-done.9.refs_2_ = bf16[256,128]{1,0:T(8,128)(2,1)S(1)} collective-permute-done((bf16[256,128]{1,0:T(8,128)(2,1)S(1)}, bf16[256,128]{1,0:T(8,128)(2,1)S(1)}, u32[]{:S(2)}, u32[]{:S(2)}) %collective-permute-start.9) | collective-permute-done | bytes 65568 | tf_op jit(solution)/shard_map/ppermute | solution.py:29
  42.6 0.4 collective-permute-done.8.refs_1_
  43.0 1.6 %collective-permute-start.11 = (bf16[1024,128]{1,0:T(8,128)(2,1)S(1)}, bf16[1024,128]{1,0:T(8,128)(2,1)S(1)}, u32[]{:S(2)}, u32[]{:S(2)}) collective-permute-start(bf16[1024,128]{1,0:T(8,128)(2,1)S(1)} %gathered.1.o0), channel_id=1, source_target_pairs={{0,1},{1,0},{2,3},{3,2},{4,6},{5,7},{6,4},{7,5},{8,9},{9,8},{10,11... | collective-permute-start | bytes 786440 | tf_op jit(solution)/shard_map/ppermute | solution.py:323
  44.6 0.5 collective-permute-start.12
  45.1 5.5 %collective-permute-done.11.o1 = bf16[1024,128]{1,0:T(8,128)(2,1)S(1)} collective-permute-done((bf16[1024,128]{1,0:T(8,128)(2,1)S(1)}, bf16[1024,128]{1,0:T(8,128)(2,1)S(1)}, u32[]{:S(2)}, u32[]{:S(2)}) %collective-permute-start.11) | collective-permute-done | bytes 262176 | tf_op jit(solution)/shard_map/ppermute | solution.py:323
  50.6 0.3 collective-permute-done.12.o2
  51.0 1.4 %collective-permute-start.15 = (bf16[1024,128]{1,0:T(8,128)(2,1)S(1)}, bf16[1024,128]{1,0:T(8,128)(2,1)S(1)}, u32[]{:S(2)}, u32[]{:S(2)}) collective-permute-start(bf16[1024,128]{1,0:T(8,128)(2,1)S(1)} %collective-permute-done.11.o1), channel_id=1, source_target_pairs={{0,2},{1,3},{2,0},{3,1},{4,5},{5,4},{6,7},{7,6},{8,10},{9,11},{10,... | collective-permute-start | bytes 786440 | tf_op jit(solution)/shard_map/ppermute | solution.py:329
  52.4 1.9 %mix.1.total = f32[256,2048]{1,0:T(8,128)S(1)} custom-call(bf16[256,2048]{1,0:T(8,128)(2,1)S(1)} %copy-done.1, bf16[1024,128]{1,0:T(8,128)(2,1)S(1)} %gathered.1.o0, bf16[1024,128]{1,0:T(8,128)(2,1)S(1)} %collective-permute-done.11.o1, bf16[1024,128]{1,0:T(8,128)(2,1)S(1)} %collective-permute-done.12.o2, bf16[512,2048]{1,0:T(8,128)(2,1)S(1)} %copy-done.2, ...), custom_call_target="tpu_custom_call" | custom-call | tf_op jit(solution)/shard_map/mix/pallas_call | solution.py:149
  54.3 3.0 %collective-permute-done.15.o3 = bf16[1024,128]{1,0:T(8,128)(2,1)S(1)} collective-permute-done((bf16[1024,128]{1,0:T(8,128)(2,1)S(1)}, bf16[1024,128]{1,0:T(8,128)(2,1)S(1)}, u32[]{:S(2)}, u32[]{:S(2)}) %collective-permute-start.15) | collective-permute-done | bytes 262176 | tf_op jit(solution)/shard_map/ppermute | solution.py:329
  57.4 1.4 %decode_edges.1 = (bf16[256,2048]{1,0:T(8,128)(2,1)S(1)}, f32[8,256]{1,0:T(8,128)S(1)}, bf16[128,256]{1,0:T(8,128)(2,1)S(1)}, bf16[128,256]{1,0:T(8,128)(2,1)S(1)}) custom-call(f32[256,2048]{1,0:T(8,128)S(1)} %mix.1.total, bf16[1024,128]{1,0:T(8,128)(2,1)S(1)} %collective-permute-done.15.o3, bf16[256,2048]{1,0:T(8,128)(2,1)S(1)} %collective-permute-done.13.n3, ...), custom_call_target="tpu_custom_call" | custom-call | tf_op jit(solution)/shard_map/decode_edges/pallas_call | solution.py:197
  58.8 3.8 %collective-permute-start.18 = (bf16[128,256]{1,0:T(8,128)(2,1)S(1)}, bf16[128,256]{1,0:T(8,128)(2,1)S(1)}, u32[]{:S(2)}, u32[]{:S(2)}) collective-permute-start(bf16[128,256]{1,0:T(8,128)(2,1)S(1)} %get-tuple-element.56), channel_id=1, source_target_pairs={{0,28},{4,8},{8,4},{12,16},{16,12},{20,24},{24,20},{28,0},{1,29},{... | collective-permute-start | bytes 196616 | tf_op jit(solution)/shard_map/ppermute | solution.py:365
  62.6 1.5 %decode_main.1 = (f32[512,256]{1,0:T(8,128)}, f32[256,256]{1,0:T(8,128)S(1)}) custom-call(bf16[256,2048]{1,0:T(8,128)(2,1)S(1)} %get-tuple-element.51.hidden, f32[8,256]{1,0:T(8,128)S(1)} %get-tuple-element.52.scale, bf16[768,2048]{1,0:T(8,128)(2,1)S(1)} %bitcast.7), custom_call_target="tpu_custom_call" | custom-call | tf_op jit(solution)/shard_map/decode_main/pallas_call | solution.py:234
  64.1 0.6 collective-permute-done.18.outer
  64.7 0.7 %join.1 = f32[512,256]{1,0:T(8,128)} custom-call(f32[512,256]{1,0:T(8,128)} %get-tuple-element.53.middle, f32[256,256]{1,0:T(8,128)S(1)} %get-tuple-element.54.ends, bf16[128,256]{1,0:T(8,128)(2,1)S(1)} %collective-permute-done.17.inner, bf16[128,256]{1,0:T(8,128)(2,1)S(1)} %collective-permute-done.18.outer), custom_call_target="tpu_custom_call", output_to_operand_aliasing={{}: (0, {})} | custom-call | tf_op jit(solution)/shard_map/join/pallas_call | solution.py:270
  (22 shorter events, 0.5 us)
Async XLA Ops:
  0.0 27.2 %collective-permute-start.4 = (bf16[512,2048]{1,0:T(8,128)(2,1)}, bf16[512,2048]{1,0:T(8,128)(2,1)S(1)}, u32[]{:S(2)}, u32[]{:S(2)}) collective-permute-start(bf16[512,2048]{1,0:T(8,128)(2,1)} %own.1), channel_id=1, source_target_pairs={{0,1},{1,0},{2,3},{3,2},{4,6},{5,7},{6,4},{7,5},{8,9},{9,8},{10,11... | collective-permute-start | bytes 6291464 | tf_op jit(solution)/shard_map/ppermute | solution.py:323
  7.4 4.1 %collective-permute-start = (bf16[768,128]{1,0:T(8,128)(2,1)S(1)}, bf16[768,128]{1,0:T(8,128)(2,1)S(1)}, u32[]{:S(2)}, u32[]{:S(2)}) collective-permute-start(bf16[768,128]{1,0:T(8,128)(2,1)S(1)} %get-tuple-element.40.refs_1_.refs_0_.refs_2_), channel_id=1, source_target_pairs={{0,4},{4,0},{8,12},{12,8},{16,20},{20,16},{24,28},{28,24},{1,5},{5... | collective-permute-start | bytes 589832 | tf_op jit(solution)/shard_map/ppermute | solution.py:29
  7.5 17.1 %collective-permute-start.2 = (bf16[768,128]{1,0:T(8,128)(2,1)S(1)}, bf16[768,128]{1,0:T(8,128)(2,1)S(1)}, u32[]{:S(2)}, u32[]{:S(2)}) collective-permute-start(bf16[768,128]{1,0:T(8,128)(2,1)S(1)} %get-tuple-element.34), channel_id=1, source_target_pairs={{0,16},{4,20},{8,24},{12,28},{16,0},{20,4},{24,8},{28,12},{1,17},{... | collective-permute-start | bytes 589832 | tf_op jit(solution)/shard_map/ppermute | solution.py:29
  10.1 14.5 %collective-permute-start.3 = (bf16[768,128]{1,0:T(8,128)(2,1)S(1)}, bf16[768,128]{1,0:T(8,128)(2,1)S(1)}, u32[]{:S(2)}, u32[]{:S(2)}) collective-permute-start(bf16[768,128]{1,0:T(8,128)(2,1)S(1)} %get-tuple-element.35), channel_id=1, source_target_pairs={{0,24},{4,28},{8,16},{12,20},{16,8},{20,12},{24,0},{28,4},{1,25},{... | collective-permute-start | bytes 589832 | tf_op jit(solution)/shard_map/ppermute | solution.py:29
  11.5 14.0 %collective-permute-start.1 = (bf16[768,128]{1,0:T(8,128)(2,1)S(1)}, bf16[768,128]{1,0:T(8,128)(2,1)S(1)}, u32[]{:S(2)}, u32[]{:S(2)}) collective-permute-start(bf16[768,128]{1,0:T(8,128)(2,1)S(1)} %get-tuple-element.33), channel_id=1, source_target_pairs={{0,8},{4,12},{8,0},{12,4},{16,24},{20,28},{24,16},{28,20},{1,9},{5... | collective-permute-start | bytes 589832 | tf_op jit(solution)/shard_map/ppermute | solution.py:29
  24.6 1.4 %collective-permute-start.6 = (bf16[768,128]{1,0:T(8,128)(2,1)S(1)}, bf16[768,128]{1,0:T(8,128)(2,1)S(1)}, u32[]{:S(2)}, u32[]{:S(2)}) collective-permute-start(bf16[768,128]{1,0:T(8,128)(2,1)S(1)} %collective-permute-done.2.refs_3_.refs_0_.refs_4_), channel_id=1, source_target_pairs={{0,4},{4,0},{8,12},{12,8},{16,20},{20,16},{24,28},{28,24},{1,5},{5... | collective-permute-start | bytes 589832 | tf_op jit(solution)/shard_map/ppermute | solution.py:29
  24.6 1.7 %collective-permute-start.7 = (bf16[768,128]{1,0:T(8,128)(2,1)S(1)}, bf16[768,128]{1,0:T(8,128)(2,1)S(1)}, u32[]{:S(2)}, u32[]{:S(2)}) collective-permute-start(bf16[768,128]{1,0:T(8,128)(2,1)S(1)} %collective-permute-done.3.refs_4_.refs_1_.refs_5_), channel_id=1, source_target_pairs={{0,4},{4,0},{8,12},{12,8},{16,20},{20,16},{24,28},{28,24},{1,5},{5... | collective-permute-start | bytes 589832 | tf_op jit(solution)/shard_map/ppermute | solution.py:29
  25.5 1.4 %collective-permute-start.5 = (bf16[768,128]{1,0:T(8,128)(2,1)S(1)}, bf16[768,128]{1,0:T(8,128)(2,1)S(1)}, u32[]{:S(2)}, u32[]{:S(2)}) collective-permute-start(bf16[768,128]{1,0:T(8,128)(2,1)S(1)} %collective-permute-done.1.refs_0_.refs_2_.refs_3_), channel_id=1, source_target_pairs={{0,4},{4,0},{8,12},{12,8},{16,20},{20,16},{24,28},{28,24},{1,5},{5... | collective-permute-start | bytes 589832 | tf_op jit(solution)/shard_map/ppermute | solution.py:29
  29.7 22.6 %copy-start.1 = (bf16[256,2048]{1,0:T(8,128)(2,1)S(1)}, bf16[256,2048]{1,0:T(8,128)(2,1)}, u32[]{:S(2)}) copy-start(bf16[256,2048]{1,0:T(8,128)(2,1)} %x_ref.1) | copy-start | bytes 3145732
  29.8 22.6 %copy-start.2 = (bf16[512,2048]{1,0:T(8,128)(2,1)S(1)}, bf16[512,2048]{1,0:T(8,128)(2,1)}, u32[]{:S(2)}) copy-start(bf16[512,2048]{1,0:T(8,128)(2,1)} %own.1) | copy-start | bytes 6291460
  29.8 21.2 %collective-permute-start.13 = (bf16[256,2048]{1,0:T(8,128)(2,1)S(1)}, bf16[256,2048]{1,0:T(8,128)(2,1)S(1)}, u32[]{:S(2)}, u32[]{:S(2)}) collective-permute-start(bf16[256,2048]{1,0:T(8,128)(2,1)S(1)} %halved.1), channel_id=1, source_target_pairs={{0,2},{1,3},{2,0},{3,1},{4,5},{5,4},{6,7},{7,6},{8,10},{9,11},{10,... | collective-permute-start | bytes 3145736 | tf_op jit(solution)/shard_map/ppermute | solution.py:329
  31.9 20.5 %collective-permute-start.14 = (bf16[512,2048]{1,0:T(8,128)(2,1)S(1)}, bf16[512,2048]{1,0:T(8,128)(2,1)S(1)}, u32[]{:S(2)}, u32[]{:S(2)}) collective-permute-start(bf16[512,2048]{1,0:T(8,128)(2,1)S(1)} %collective-permute-done.4.block.w1), channel_id=1, source_target_pairs={{0,4},{4,0},{8,12},{12,8},{16,20},{20,16},{24,28},{28,24},{1,5},{5... | collective-permute-start | bytes 6291464 | tf_op jit(solution)/shard_map/ppermute | solution.py:29
  31.9 8.5 %collective-permute-start.10 = (bf16[256,128]{1,0:T(8,128)(2,1)S(1)}, bf16[256,128]{1,0:T(8,128)(2,1)S(1)}, u32[]{:S(2)}, u32[]{:S(2)}) collective-permute-start(bf16[256,128]{1,0:T(8,128)(2,1)S(1)} %get-tuple-element.46), channel_id=1, source_target_pairs={{0,24},{4,28},{8,16},{12,20},{16,8},{20,12},{24,0},{28,4},{1,25},{... | collective-permute-start | bytes 196616 | tf_op jit(solution)/shard_map/ppermute | solution.py:29
  35.5 7.1 %collective-permute-start.9 = (bf16[256,128]{1,0:T(8,128)(2,1)S(1)}, bf16[256,128]{1,0:T(8,128)(2,1)S(1)}, u32[]{:S(2)}, u32[]{:S(2)}) collective-permute-start(bf16[256,128]{1,0:T(8,128)(2,1)S(1)} %get-tuple-element.45), channel_id=1, source_target_pairs={{0,16},{4,20},{8,24},{12,28},{16,0},{20,4},{24,8},{28,12},{1,17},{... | collective-permute-start | bytes 196616 | tf_op jit(solution)/shard_map/ppermute | solution.py:29
  38.3 4.7 %collective-permute-start.8 = (bf16[256,128]{1,0:T(8,128)(2,1)S(1)}, bf16[256,128]{1,0:T(8,128)(2,1)S(1)}, u32[]{:S(2)}, u32[]{:S(2)}) collective-permute-start(bf16[256,128]{1,0:T(8,128)(2,1)S(1)} %attend.3), channel_id=1, source_target_pairs={{0,8},{4,12},{8,0},{12,4},{16,24},{20,28},{24,16},{28,20},{1,9},{5... | collective-permute-start | bytes 196616 | tf_op jit(solution)/shard_map/ppermute | solution.py:29
  43.0 7.6 %collective-permute-start.11 = (bf16[1024,128]{1,0:T(8,128)(2,1)S(1)}, bf16[1024,128]{1,0:T(8,128)(2,1)S(1)}, u32[]{:S(2)}, u32[]{:S(2)}) collective-permute-start(bf16[1024,128]{1,0:T(8,128)(2,1)S(1)} %gathered.1.o0), channel_id=1, source_target_pairs={{0,1},{1,0},{2,3},{3,2},{4,6},{5,7},{6,4},{7,5},{8,9},{9,8},{10,11... | collective-permute-start | bytes 786440 | tf_op jit(solution)/shard_map/ppermute | solution.py:323
  44.6 6.4 %collective-permute-start.12 = (bf16[1024,128]{1,0:T(8,128)(2,1)S(1)}, bf16[1024,128]{1,0:T(8,128)(2,1)S(1)}, u32[]{:S(2)}, u32[]{:S(2)}) collective-permute-start(bf16[1024,128]{1,0:T(8,128)(2,1)S(1)} %gathered.1.o0), channel_id=1, source_target_pairs={{0,2},{1,3},{2,0},{3,1},{4,5},{5,4},{6,7},{7,6},{8,10},{9,11},{10,... | collective-permute-start | bytes 786440 | tf_op jit(solution)/shard_map/ppermute | solution.py:329
  51.0 6.4 %collective-permute-start.16 = (bf16[256,2048]{1,0:T(8,128)(2,1)S(1)}, bf16[256,2048]{1,0:T(8,128)(2,1)S(1)}, u32[]{:S(2)}, u32[]{:S(2)}) collective-permute-start(bf16[256,2048]{1,0:T(8,128)(2,1)S(1)} %collective-permute-done.13.n3), channel_id=1, source_target_pairs={{0,4},{4,0},{8,12},{12,8},{16,20},{20,16},{24,28},{28,24},{1,5},{5... | collective-permute-start | bytes 3145736 | tf_op jit(solution)/shard_map/ppermute | solution.py:29
  51.0 6.4 %collective-permute-start.15 = (bf16[1024,128]{1,0:T(8,128)(2,1)S(1)}, bf16[1024,128]{1,0:T(8,128)(2,1)S(1)}, u32[]{:S(2)}, u32[]{:S(2)}) collective-permute-start(bf16[1024,128]{1,0:T(8,128)(2,1)S(1)} %collective-permute-done.11.o1), channel_id=1, source_target_pairs={{0,2},{1,3},{2,0},{3,1},{4,5},{5,4},{6,7},{7,6},{8,10},{9,11},{10,... | collective-permute-start | bytes 786440 | tf_op jit(solution)/shard_map/ppermute | solution.py:329
  52.4 5.0 %copy-start = (bf16[2048,12,64]{0,2,1:T(8,128)(2,1)S(1)}, bf16[2048,12,64]{0,2,1:T(8,128)(2,1)}, u32[]{:S(2)}) copy-start(bf16[2048,12,64]{0,2,1:T(8,128)(2,1)} %param.7) | copy-start | bytes 9437188
  58.7 5.4 %collective-permute-start.17 = (bf16[128,256]{1,0:T(8,128)(2,1)S(1)}, bf16[128,256]{1,0:T(8,128)(2,1)S(1)}, u32[]{:S(2)}, u32[]{:S(2)}) collective-permute-start(bf16[128,256]{1,0:T(8,128)(2,1)S(1)} %get-tuple-element.55), channel_id=1, source_target_pairs={{0,4},{4,0},{8,12},{12,8},{16,20},{20,16},{24,28},{28,24},{1,5},{5... | collective-permute-start | bytes 196616 | tf_op jit(solution)/shard_map/ppermute | solution.py:29
  58.8 5.9 %collective-permute-start.18 = (bf16[128,256]{1,0:T(8,128)(2,1)S(1)}, bf16[128,256]{1,0:T(8,128)(2,1)S(1)}, u32[]{:S(2)}, u32[]{:S(2)}) collective-permute-start(bf16[128,256]{1,0:T(8,128)(2,1)S(1)} %get-tuple-element.56), channel_id=1, source_target_pairs={{0,28},{4,8},{8,4},{12,16},{16,12},{20,24},{24,20},{28,0},{1,29},{... | collective-permute-start | bytes 196616 | tf_op jit(solution)/shard_map/ppermute | solution.py:365

commit v10 on v9

--- a/solution.py
+++ b/solution.py
@@ -348,7 +348,6 @@
     w1, o2, o3 = lax.optimization_barrier((w1, o2, o3))
     w2 = swapped(w1, "ctx", 1)
     (o1,) = attend([r1], packs)
-    p0, o1 = lax.optimization_barrier((p0, o1))
     (o0,) = attend([p0], packs)
     own = gathered([o0, swapped(o1, "ctx", 2), swapped(o2, "ctx", 4), swapped(o3, "ctx", 6)])
     a1, a2 = first_way(own), second_way(own)

time: 65.6 us -> 65.6 us (level)
  no operation moved by 1% of the time
where the time goes in v10:
time: 65.6 us; the launch traced here: 65.4 us
  waiting for transfers between devices  27 us (41%)
  starting transfers between devices  22.9 us (35%)
  Pallas kernels  15.4 us (23%)
    ppermute x13, waiting for transfers between devices, swapped(): return lax.ppermute(value, axis, [(i, i ^ bits) for i in range(count)])  17.3 us
    ppermute x13, starting transfers between devices, swapped(): return lax.ppermute(value, axis, [(i, i ^ bits) for i in range(count)])  10.5 us
    ppermute x2, waiting for transfers between devices, first_way(): return lax.ppermute(value, ('ctx', 'head'), pairs)  5.74 us
    pallas_call x3, Pallas kernels, attend(): pl.pallas_call(functools.partial(attention_kernel, count), in_specs=[vmem...  5.35 us
    ppermute x2, starting transfers between devices, first_way(): return lax.ppermute(value, ('ctx', 'head'), pairs)  4.51 us
    pallas_call x1, Pallas kernels, project(): pl.pallas_call(project_kernel, in_specs=[hbm] * 2, out_specs=[vmem] * 4,...  4.43 us
    ppermute x3, starting transfers between devices, second_way(): return lax.ppermute(value, ('ctx', 'head'), pairs)  4.05 us
    ppermute x1, starting transfers between devices, fast_body(): outer = lax.ppermute(outer, 'ctx', pairs)  3.82 us
  transfers between devices with their start and end apart: 19, of which 12 were waited for; matrix products, arithmetic and copies ran while one was open for 0% of the time, Pallas kernels for 16%

profile of v10, /device:TPU:0, one launch (start us, length us, event | category | flops | bytes accessed | tf_op | source)
XLA Modules:
  0.0 65.4 jit_solution(4480338854783789623)
XLA Ops:
  0.0 2.9 %collective-permute-start.4 = (bf16[512,2048]{1,0:T(8,128)(2,1)}, bf16[512,2048]{1,0:T(8,128)(2,1)S(1)}, u32[]{:S(2)}, u32[]{:S(2)}) collective-permute-start(bf16[512,2048]{1,0:T(8,128)(2,1)} %own.1), channel_id=1, source_target_pairs={{0,1},{1,0},{2,3},{3,2},{4,6},{5,7},{6,4},{7,5},{8,9},{9,8},{10,11... | collective-permute-start | bytes 6291464 | tf_op jit(solution)/shard_map/ppermute | solution.py:323
  2.9 4.4 %project.1 = (bf16[768,128]{1,0:T(8,128)(2,1)S(1)}, bf16[768,128]{1,0:T(8,128)(2,1)S(1)}, bf16[768,128]{1,0:T(8,128)(2,1)S(1)}, bf16[768,128]{1,0:T(8,128)(2,1)S(1)}) custom-call(bf16[256,2048]{1,0:T(8,128)(2,1)} %x_ref.1, bf16[3,2048,512]{2,1,0:T(8,128)(2,1)} %w_hbm.1), custom_call_target="tpu_custom_call" | custom-call | tf_op jit(solution)/shard_map/project/pallas_call | solution.py:73
  7.5 2.7 %collective-permute-start.2 = (bf16[768,128]{1,0:T(8,128)(2,1)S(1)}, bf16[768,128]{1,0:T(8,128)(2,1)S(1)}, u32[]{:S(2)}, u32[]{:S(2)}) collective-permute-start(bf16[768,128]{1,0:T(8,128)(2,1)S(1)} %get-tuple-element.32), channel_id=1, source_target_pairs={{0,16},{4,20},{8,24},{12,28},{16,0},{20,4},{24,8},{28,12},{1,17},{... | collective-permute-start | bytes 589832 | tf_op jit(solution)/shard_map/ppermute | solution.py:29
  10.1 1.3 %collective-permute-start.3 = (bf16[768,128]{1,0:T(8,128)(2,1)S(1)}, bf16[768,128]{1,0:T(8,128)(2,1)S(1)}, u32[]{:S(2)}, u32[]{:S(2)}) collective-permute-start(bf16[768,128]{1,0:T(8,128)(2,1)S(1)} %get-tuple-element.33), channel_id=1, source_target_pairs={{0,24},{4,28},{8,16},{12,20},{16,8},{20,12},{24,0},{28,4},{1,25},{... | collective-permute-start | bytes 589832 | tf_op jit(solution)/shard_map/ppermute | solution.py:29
  11.7 12.9 %collective-permute-done.2.refs_3_.refs_0_.refs_4_ = bf16[768,128]{1,0:T(8,128)(2,1)S(1)} collective-permute-done((bf16[768,128]{1,0:T(8,128)(2,1)S(1)}, bf16[768,128]{1,0:T(8,128)(2,1)S(1)}, u32[]{:S(2)}, u32[]{:S(2)}) %collective-permute-start.2) | collective-permute-done | bytes 196640 | tf_op jit(solution)/shard_map/ppermute | solution.py:29
  24.6 0.5 collective-permute-start.7
  25.1 0.4 collective-permute-done.1.refs_2_.refs_0_.refs_3_
  25.5 0.6 collective-permute-done.6.refs_7_.refs_8_
  26.0 0.3 collective-permute-done.7.refs_8_.refs_9_
  26.3 0.6 collective-permute-done.5.refs_6_.refs_7_
  26.9 0.2 collective-permute-done.4.block.w1
  27.2 2.5 %attend.5 = (bf16[256,128]{1,0:T(8,128)(2,1)S(1)}, bf16[256,128]{1,0:T(8,128)(2,1)S(1)}) custom-call(bf16[768,128]{1,0:T(8,128)(2,1)S(1)} %collective-permute-done.2.refs_3_.refs_0_.refs_4_, bf16[768,128]{1,0:T(8,128)(2,1)S(1)} %collective-permute-done.3.refs_4_.refs_1_.refs_5_, bf16[768,128]{1,0:T(8,128)(2,1)S(1)} %get-tuple-element.29.refs_0_.refs_1_.refs_2_, ...), custom_call_target="tpu_custom_call" | custom-call | tf_op jit(solution)/shard_map/attend/pallas_call | solution.py:121
  29.8 2.1 %collective-permute-start.13 = (bf16[256,2048]{1,0:T(8,128)(2,1)S(1)}, bf16[256,2048]{1,0:T(8,128)(2,1)S(1)}, u32[]{:S(2)}, u32[]{:S(2)}) collective-permute-start(bf16[256,2048]{1,0:T(8,128)(2,1)S(1)} %halved.1), channel_id=1, source_target_pairs={{0,2},{1,3},{2,0},{3,1},{4,5},{5,4},{6,7},{7,6},{8,10},{9,11},{10,... | collective-permute-start | bytes 3145736 | tf_op jit(solution)/shard_map/ppermute | solution.py:329
  31.9 3.6 %collective-permute-start.10 = (bf16[256,128]{1,0:T(8,128)(2,1)S(1)}, bf16[256,128]{1,0:T(8,128)(2,1)S(1)}, u32[]{:S(2)}, u32[]{:S(2)}) collective-permute-start(bf16[256,128]{1,0:T(8,128)(2,1)S(1)} %get-tuple-element.42), channel_id=1, source_target_pairs={{0,24},{4,28},{8,16},{12,20},{16,8},{20,12},{24,0},{28,4},{1,25},{... | collective-permute-start | bytes 196616 | tf_op jit(solution)/shard_map/ppermute | solution.py:29
  35.5 1.4 %collective-permute-start.9 = (bf16[256,128]{1,0:T(8,128)(2,1)S(1)}, bf16[256,128]{1,0:T(8,128)(2,1)S(1)}, u32[]{:S(2)}, u32[]{:S(2)}) collective-permute-start(bf16[256,128]{1,0:T(8,128)(2,1)S(1)} %get-tuple-element.41), channel_id=1, source_target_pairs={{0,16},{4,20},{8,24},{12,28},{16,0},{20,4},{24,8},{28,12},{1,17},{... | collective-permute-start | bytes 196616 | tf_op jit(solution)/shard_map/ppermute | solution.py:29
  36.9 1.4 %attend.4 = bf16[256,128]{1,0:T(8,128)(2,1)S(1)} custom-call(bf16[768,128]{1,0:T(8,128)(2,1)S(1)} %collective-permute-done.1.refs_2_.refs_0_.refs_3_, bf16[768,128]{1,0:T(8,128)(2,1)S(1)} %get-tuple-element.29.refs_0_.refs_1_.refs_2_, bf16[768,128]{1,0:T(8,128)(2,1)S(1)} %collective-permute-done.1.refs_2_.refs_0_.refs_3_, ...), custom_call_target="tpu_custom_call" | custom-call | tf_op jit(solution)/shard_map/attend/pallas_call | solution.py:121
  38.3 0.6 collective-permute-start.8
  38.9 1.4 %attend.3.refs_0_ = bf16[256,128]{1,0:T(8,128)(2,1)S(1)} custom-call(bf16[768,128]{1,0:T(8,128)(2,1)S(1)} %get-tuple-element.29.refs_0_.refs_1_.refs_2_, bf16[768,128]{1,0:T(8,128)(2,1)S(1)} %get-tuple-element.29.refs_0_.refs_1_.refs_2_, bf16[768,128]{1,0:T(8,128)(2,1)S(1)} %collective-permute-done.1.refs_2_.refs_0_.refs_3_, ...), custom_call_target="tpu_custom_call" | custom-call | tf_op jit(solution)/shard_map/attend/pallas_call | solution.py:121
  40.4 2.2 %collective-permute-done.9.refs_2_ = bf16[256,128]{1,0:T(8,128)(2,1)S(1)} collective-permute-done((bf16[256,128]{1,0:T(8,128)(2,1)S(1)}, bf16[256,128]{1,0:T(8,128)(2,1)S(1)}, u32[]{:S(2)}, u32[]{:S(2)}) %collective-permute-start.9) | collective-permute-done | bytes 65568 | tf_op jit(solution)/shard_map/ppermute | solution.py:29
  42.6 0.4 collective-permute-done.8.refs_1_
  43.0 1.6 %collective-permute-start.11 = (bf16[1024,128]{1,0:T(8,128)(2,1)S(1)}, bf16[1024,128]{1,0:T(8,128)(2,1)S(1)}, u32[]{:S(2)}, u32[]{:S(2)}) collective-permute-start(bf16[1024,128]{1,0:T(8,128)(2,1)S(1)} %gathered.1.o0), channel_id=1, source_target_pairs={{0,1},{1,0},{2,3},{3,2},{4,6},{5,7},{6,4},{7,5},{8,9},{9,8},{10,11... | collective-permute-start | bytes 786440 | tf_op jit(solution)/shard_map/ppermute | solution.py:323
  44.6 0.5 collective-permute-start.12
  45.1 5.5 %collective-permute-done.11.o1 = bf16[1024,128]{1,0:T(8,128)(2,1)S(1)} collective-permute-done((bf16[1024,128]{1,0:T(8,128)(2,1)S(1)}, bf16[1024,128]{1,0:T(8,128)(2,1)S(1)}, u32[]{:S(2)}, u32[]{:S(2)}) %collective-permute-start.11) | collective-permute-done | bytes 262176 | tf_op jit(solution)/shard_map/ppermute | solution.py:323
  50.6 0.3 collective-permute-done.12.o2
  51.0 1.4 %collective-permute-start.15 = (bf16[1024,128]{1,0:T(8,128)(2,1)S(1)}, bf16[1024,128]{1,0:T(8,128)(2,1)S(1)}, u32[]{:S(2)}, u32[]{:S(2)}) collective-permute-start(bf16[1024,128]{1,0:T(8,128)(2,1)S(1)} %collective-permute-done.11.o1), channel_id=1, source_target_pairs={{0,2},{1,3},{2,0},{3,1},{4,5},{5,4},{6,7},{7,6},{8,10},{9,11},{10,... | collective-permute-start | bytes 786440 | tf_op jit(solution)/shard_map/ppermute | solution.py:329
  52.4 1.9 %mix.1.total = f32[256,2048]{1,0:T(8,128)S(1)} custom-call(bf16[256,2048]{1,0:T(8,128)(2,1)S(1)} %copy-done.1, bf16[1024,128]{1,0:T(8,128)(2,1)S(1)} %gathered.1.o0, bf16[1024,128]{1,0:T(8,128)(2,1)S(1)} %collective-permute-done.11.o1, bf16[1024,128]{1,0:T(8,128)(2,1)S(1)} %collective-permute-done.12.o2, bf16[512,2048]{1,0:T(8,128)(2,1)S(1)} %copy-done.2, ...), custom_call_target="tpu_custom_call" | custom-call | tf_op jit(solution)/shard_map/mix/pallas_call | solution.py:149
  54.3 3.0 %collective-permute-done.15.o3 = bf16[1024,128]{1,0:T(8,128)(2,1)S(1)} collective-permute-done((bf16[1024,128]{1,0:T(8,128)(2,1)S(1)}, bf16[1024,128]{1,0:T(8,128)(2,1)S(1)}, u32[]{:S(2)}, u32[]{:S(2)}) %collective-permute-start.15) | collective-permute-done | bytes 262176 | tf_op jit(solution)/shard_map/ppermute | solution.py:329
  57.4 1.4 %decode_edges.1 = (bf16[256,2048]{1,0:T(8,128)(2,1)S(1)}, f32[8,256]{1,0:T(8,128)S(1)}, bf16[128,256]{1,0:T(8,128)(2,1)S(1)}, bf16[128,256]{1,0:T(8,128)(2,1)S(1)}) custom-call(f32[256,2048]{1,0:T(8,128)S(1)} %mix.1.total, bf16[1024,128]{1,0:T(8,128)(2,1)S(1)} %collective-permute-done.15.o3, bf16[256,2048]{1,0:T(8,128)(2,1)S(1)} %collective-permute-done.13.n3, ...), custom_call_target="tpu_custom_call" | custom-call | tf_op jit(solution)/shard_map/decode_edges/pallas_call | solution.py:197
  58.8 3.8 %collective-permute-start.18 = (bf16[128,256]{1,0:T(8,128)(2,1)S(1)}, bf16[128,256]{1,0:T(8,128)(2,1)S(1)}, u32[]{:S(2)}, u32[]{:S(2)}) collective-permute-start(bf16[128,256]{1,0:T(8,128)(2,1)S(1)} %get-tuple-element.52), channel_id=1, source_target_pairs={{0,28},{4,8},{8,4},{12,16},{16,12},{20,24},{24,20},{28,0},{1,29},{... | collective-permute-start | bytes 196616 | tf_op jit(solution)/shard_map/ppermute | solution.py:364
  62.6 1.5 %decode_main.1 = (f32[512,256]{1,0:T(8,128)}, f32[256,256]{1,0:T(8,128)S(1)}) custom-call(bf16[256,2048]{1,0:T(8,128)(2,1)S(1)} %get-tuple-element.47.hidden, f32[8,256]{1,0:T(8,128)S(1)} %get-tuple-element.48.scale, bf16[768,2048]{1,0:T(8,128)(2,1)S(1)} %bitcast.7), custom_call_target="tpu_custom_call" | custom-call | tf_op jit(solution)/shard_map/decode_main/pallas_call | solution.py:234
  64.1 0.6 collective-permute-done.18.outer
  64.7 0.7 %join.1 = f32[512,256]{1,0:T(8,128)} custom-call(f32[512,256]{1,0:T(8,128)} %get-tuple-element.49.middle, f32[256,256]{1,0:T(8,128)S(1)} %get-tuple-element.50.ends, bf16[128,256]{1,0:T(8,128)(2,1)S(1)} %collective-permute-done.17.inner, bf16[128,256]{1,0:T(8,128)(2,1)S(1)} %collective-permute-done.18.outer), custom_call_target="tpu_custom_call", output_to_operand_aliasing={{}: (0, {})} | custom-call | tf_op jit(solution)/shard_map/join/pallas_call | solution.py:270
  (22 shorter events, 0.5 us)
Async XLA Ops:
  0.0 27.2 %collective-permute-start.4 = (bf16[512,2048]{1,0:T(8,128)(2,1)}, bf16[512,2048]{1,0:T(8,128)(2,1)S(1)}, u32[]{:S(2)}, u32[]{:S(2)}) collective-permute-start(bf16[512,2048]{1,0:T(8,128)(2,1)} %own.1), channel_id=1, source_target_pairs={{0,1},{1,0},{2,3},{3,2},{4,6},{5,7},{6,4},{7,5},{8,9},{9,8},{10,11... | collective-permute-start | bytes 6291464 | tf_op jit(solution)/shard_map/ppermute | solution.py:323
  7.4 4.1 %collective-permute-start = (bf16[768,128]{1,0:T(8,128)(2,1)S(1)}, bf16[768,128]{1,0:T(8,128)(2,1)S(1)}, u32[]{:S(2)}, u32[]{:S(2)}) collective-permute-start(bf16[768,128]{1,0:T(8,128)(2,1)S(1)} %get-tuple-element.29.refs_0_.refs_1_.refs_2_), channel_id=1, source_target_pairs={{0,4},{4,0},{8,12},{12,8},{16,20},{20,16},{24,28},{28,24},{1,5},{5... | collective-permute-start | bytes 589832 | tf_op jit(solution)/shard_map/ppermute | solution.py:29
  7.5 17.1 %collective-permute-start.2 = (bf16[768,128]{1,0:T(8,128)(2,1)S(1)}, bf16[768,128]{1,0:T(8,128)(2,1)S(1)}, u32[]{:S(2)}, u32[]{:S(2)}) collective-permute-start(bf16[768,128]{1,0:T(8,128)(2,1)S(1)} %get-tuple-element.32), channel_id=1, source_target_pairs={{0,16},{4,20},{8,24},{12,28},{16,0},{20,4},{24,8},{28,12},{1,17},{... | collective-permute-start | bytes 589832 | tf_op jit(solution)/shard_map/ppermute | solution.py:29
  10.1 14.5 %collective-permute-start.3 = (bf16[768,128]{1,0:T(8,128)(2,1)S(1)}, bf16[768,128]{1,0:T(8,128)(2,1)S(1)}, u32[]{:S(2)}, u32[]{:S(2)}) collective-permute-start(bf16[768,128]{1,0:T(8,128)(2,1)S(1)} %get-tuple-element.33), channel_id=1, source_target_pairs={{0,24},{4,28},{8,16},{12,20},{16,8},{20,12},{24,0},{28,4},{1,25},{... | collective-permute-start | bytes 589832 | tf_op jit(solution)/shard_map/ppermute | solution.py:29
  11.5 14.0 %collective-permute-start.1 = (bf16[768,128]{1,0:T(8,128)(2,1)S(1)}, bf16[768,128]{1,0:T(8,128)(2,1)S(1)}, u32[]{:S(2)}, u32[]{:S(2)}) collective-permute-start(bf16[768,128]{1,0:T(8,128)(2,1)S(1)} %get-tuple-element.31), channel_id=1, source_target_pairs={{0,8},{4,12},{8,0},{12,4},{16,24},{20,28},{24,16},{28,20},{1,9},{5... | collective-permute-start | bytes 589832 | tf_op jit(solution)/shard_map/ppermute | solution.py:29
  24.6 1.4 %collective-permute-start.6 = (bf16[768,128]{1,0:T(8,128)(2,1)S(1)}, bf16[768,128]{1,0:T(8,128)(2,1)S(1)}, u32[]{:S(2)}, u32[]{:S(2)}) collective-permute-start(bf16[768,128]{1,0:T(8,128)(2,1)S(1)} %collective-permute-done.2.refs_3_.refs_0_.refs_4_), channel_id=1, source_target_pairs={{0,4},{4,0},{8,12},{12,8},{16,20},{20,16},{24,28},{28,24},{1,5},{5... | collective-permute-start | bytes 589832 | tf_op jit(solution)/shard_map/ppermute | solution.py:29
  24.6 1.7 %collective-permute-start.7 = (bf16[768,128]{1,0:T(8,128)(2,1)S(1)}, bf16[768,128]{1,0:T(8,128)(2,1)S(1)}, u32[]{:S(2)}, u32[]{:S(2)}) collective-permute-start(bf16[768,128]{1,0:T(8,128)(2,1)S(1)} %collective-permute-done.3.refs_4_.refs_1_.refs_5_), channel_id=1, source_target_pairs={{0,4},{4,0},{8,12},{12,8},{16,20},{20,16},{24,28},{28,24},{1,5},{5... | collective-permute-start | bytes 589832 | tf_op jit(solution)/shard_map/ppermute | solution.py:29
  25.5 1.4 %collective-permute-start.5 = (bf16[768,128]{1,0:T(8,128)(2,1)S(1)}, bf16[768,128]{1,0:T(8,128)(2,1)S(1)}, u32[]{:S(2)}, u32[]{:S(2)}) collective-permute-start(bf16[768,128]{1,0:T(8,128)(2,1)S(1)} %collective-permute-done.1.refs_2_.refs_0_.refs_3_), channel_id=1, source_target_pairs={{0,4},{4,0},{8,12},{12,8},{16,20},{20,16},{24,28},{28,24},{1,5},{5... | collective-permute-start | bytes 589832 | tf_op jit(solution)/shard_map/ppermute | solution.py:29
  29.7 22.6 %copy-start.1 = (bf16[256,2048]{1,0:T(8,128)(2,1)S(1)}, bf16[256,2048]{1,0:T(8,128)(2,1)}, u32[]{:S(2)}) copy-start(bf16[256,2048]{1,0:T(8,128)(2,1)} %x_ref.1) | copy-start | bytes 3145732
  29.8 22.6 %copy-start.2 = (bf16[512,2048]{1,0:T(8,128)(2,1)S(1)}, bf16[512,2048]{1,0:T(8,128)(2,1)}, u32[]{:S(2)}) copy-start(bf16[512,2048]{1,0:T(8,128)(2,1)} %own.1) | copy-start | bytes 6291460
  29.8 21.2 %collective-permute-start.13 = (bf16[256,2048]{1,0:T(8,128)(2,1)S(1)}, bf16[256,2048]{1,0:T(8,128)(2,1)S(1)}, u32[]{:S(2)}, u32[]{:S(2)}) collective-permute-start(bf16[256,2048]{1,0:T(8,128)(2,1)S(1)} %halved.1), channel_id=1, source_target_pairs={{0,2},{1,3},{2,0},{3,1},{4,5},{5,4},{6,7},{7,6},{8,10},{9,11},{10,... | collective-permute-start | bytes 3145736 | tf_op jit(solution)/shard_map/ppermute | solution.py:329
  31.9 20.5 %collective-permute-start.14 = (bf16[512,2048]{1,0:T(8,128)(2,1)S(1)}, bf16[512,2048]{1,0:T(8,128)(2,1)S(1)}, u32[]{:S(2)}, u32[]{:S(2)}) collective-permute-start(bf16[512,2048]{1,0:T(8,128)(2,1)S(1)} %collective-permute-done.4.block.w1), channel_id=1, source_target_pairs={{0,4},{4,0},{8,12},{12,8},{16,20},{20,16},{24,28},{28,24},{1,5},{5... | collective-permute-start | bytes 6291464 | tf_op jit(solution)/shard_map/ppermute | solution.py:29
  31.9 8.5 %collective-permute-start.10 = (bf16[256,128]{1,0:T(8,128)(2,1)S(1)}, bf16[256,128]{1,0:T(8,128)(2,1)S(1)}, u32[]{:S(2)}, u32[]{:S(2)}) collective-permute-start(bf16[256,128]{1,0:T(8,128)(2,1)S(1)} %get-tuple-element.42), channel_id=1, source_target_pairs={{0,24},{4,28},{8,16},{12,20},{16,8},{20,12},{24,0},{28,4},{1,25},{... | collective-permute-start | bytes 196616 | tf_op jit(solution)/shard_map/ppermute | solution.py:29
  35.5 7.1 %collective-permute-start.9 = (bf16[256,128]{1,0:T(8,128)(2,1)S(1)}, bf16[256,128]{1,0:T(8,128)(2,1)S(1)}, u32[]{:S(2)}, u32[]{:S(2)}) collective-permute-start(bf16[256,128]{1,0:T(8,128)(2,1)S(1)} %get-tuple-element.41), channel_id=1, source_target_pairs={{0,16},{4,20},{8,24},{12,28},{16,0},{20,4},{24,8},{28,12},{1,17},{... | collective-permute-start | bytes 196616 | tf_op jit(solution)/shard_map/ppermute | solution.py:29
  38.3 4.7 %collective-permute-start.8 = (bf16[256,128]{1,0:T(8,128)(2,1)S(1)}, bf16[256,128]{1,0:T(8,128)(2,1)S(1)}, u32[]{:S(2)}, u32[]{:S(2)}) collective-permute-start(bf16[256,128]{1,0:T(8,128)(2,1)S(1)} %attend.4), channel_id=1, source_target_pairs={{0,8},{4,12},{8,0},{12,4},{16,24},{20,28},{24,16},{28,20},{1,9},{5... | collective-permute-start | bytes 196616 | tf_op jit(solution)/shard_map/ppermute | solution.py:29
  43.0 7.6 %collective-permute-start.11 = (bf16[1024,128]{1,0:T(8,128)(2,1)S(1)}, bf16[1024,128]{1,0:T(8,128)(2,1)S(1)}, u32[]{:S(2)}, u32[]{:S(2)}) collective-permute-start(bf16[1024,128]{1,0:T(8,128)(2,1)S(1)} %gathered.1.o0), channel_id=1, source_target_pairs={{0,1},{1,0},{2,3},{3,2},{4,6},{5,7},{6,4},{7,5},{8,9},{9,8},{10,11... | collective-permute-start | bytes 786440 | tf_op jit(solution)/shard_map/ppermute | solution.py:323
  44.6 6.4 %collective-permute-start.12 = (bf16[1024,128]{1,0:T(8,128)(2,1)S(1)}, bf16[1024,128]{1,0:T(8,128)(2,1)S(1)}, u32[]{:S(2)}, u32[]{:S(2)}) collective-permute-start(bf16[1024,128]{1,0:T(8,128)(2,1)S(1)} %gathered.1.o0), channel_id=1, source_target_pairs={{0,2},{1,3},{2,0},{3,1},{4,5},{5,4},{6,7},{7,6},{8,10},{9,11},{10,... | collective-permute-start | bytes 786440 | tf_op jit(solution)/shard_map/ppermute | solution.py:329
  51.0 6.4 %collective-permute-start.16 = (bf16[256,2048]{1,0:T(8,128)(2,1)S(1)}, bf16[256,2048]{1,0:T(8,128)(2,1)S(1)}, u32[]{:S(2)}, u32[]{:S(2)}) collective-permute-start(bf16[256,2048]{1,0:T(8,128)(2,1)S(1)} %collective-permute-done.13.n3), channel_id=1, source_target_pairs={{0,4},{4,0},{8,12},{12,8},{16,20},{20,16},{24,28},{28,24},{1,5},{5... | collective-permute-start | bytes 3145736 | tf_op jit(solution)/shard_map/ppermute | solution.py:29
  51.0 6.4 %collective-permute-start.15 = (bf16[1024,128]{1,0:T(8,128)(2,1)S(1)}, bf16[1024,128]{1,0:T(8,128)(2,1)S(1)}, u32[]{:S(2)}, u32[]{:S(2)}) collective-permute-start(bf16[1024,128]{1,0:T(8,128)(2,1)S(1)} %collective-permute-done.11.o1), channel_id=1, source_target_pairs={{0,2},{1,3},{2,0},{3,1},{4,5},{5,4},{6,7},{7,6},{8,10},{9,11},{10,... | collective-permute-start | bytes 786440 | tf_op jit(solution)/shard_map/ppermute | solution.py:329
  52.4 5.0 %copy-start = (bf16[2048,12,64]{0,2,1:T(8,128)(2,1)S(1)}, bf16[2048,12,64]{0,2,1:T(8,128)(2,1)}, u32[]{:S(2)}) copy-start(bf16[2048,12,64]{0,2,1:T(8,128)(2,1)} %param.7) | copy-start | bytes 9437188
  58.7 5.4 %collective-permute-start.17 = (bf16[128,256]{1,0:T(8,128)(2,1)S(1)}, bf16[128,256]{1,0:T(8,128)(2,1)S(1)}, u32[]{:S(2)}, u32[]{:S(2)}) collective-permute-start(bf16[128,256]{1,0:T(8,128)(2,1)S(1)} %get-tuple-element.51), channel_id=1, source_target_pairs={{0,4},{4,0},{8,12},{12,8},{16,20},{20,16},{24,28},{28,24},{1,5},{5... | collective-permute-start | bytes 196616 | tf_op jit(solution)/shard_map/ppermute | solution.py:29
  58.8 5.9 %collective-permute-start.18 = (bf16[128,256]{1,0:T(8,128)(2,1)S(1)}, bf16[128,256]{1,0:T(8,128)(2,1)S(1)}, u32[]{:S(2)}, u32[]{:S(2)}) collective-permute-start(bf16[128,256]{1,0:T(8,128)(2,1)S(1)} %get-tuple-element.52), channel_id=1, source_target_pairs={{0,28},{4,8},{8,4},{12,16},{16,12},{20,24},{24,20},{28,0},{1,29},{... | collective-permute-start | bytes 196616 | tf_op jit(solution)/shard_map/ppermute | solution.py:364
